TPU v7x, 32 devices: a whole 2x2x4 slice. The times are simulated.
32 devices in a mesh: dp: 16 (over z, y, x), rep: 2 (over core).
Axes of the slice: x: 2, y: 2, z: 4, core: 2. Of those that a mesh axis runs over, the one named last changes fastest.
Arguments:
- noise_owner: int32 [16, 1024, 8], P('dp', 'rep'), may hold values from 0 to 31, all different within a row; in each aligned block of 512 rows (0 to 511, 512 to 1023, ..., all dimensions but the last counted through in order) at most 256 rows name the same one
- noise_offset: int32 [16, 1024, 8], P('dp', 'rep'), may hold values from 0 to 1571
- option_scores: float32 [16, 1024, 8], P('dp', 'rep'), may hold values from -4 to 4
- seq_lengths: int32 [16], replicated, may hold values from 1 to 1024, as said below
- time_index: int32 [16], replicated, may hold values from 0 to 999
- loss_pick: int32 [16, 2, 64], replicated, may hold values from 0 to 511
- loss_target: int32 [16, 2, 64], replicated, may hold values from 0 to 50303
- vocab_table: float32 [50304, 768], P(('dp', 'rep'))
- table_mom: float32 [50304, 768], P(('dp', 'rep')), may hold values from -4.7683716e-06 to 4.7683716e-06
- table_sq: float32 [50304, 768], P(('dp', 'rep')), may hold values from 8.596075e-15 to 3.43843e-14
- attn_proj: float32 [768, 2304], P(('dp', 'rep')), may hold values from -0.21875 to 0.21875
- proj_mom: float32 [768, 2304], P(('dp', 'rep')), may hold values from -2.3841858e-06 to 2.3841858e-06
- proj_sq: float32 [768, 2304], P(('dp', 'rep')), may hold values from 2.1490187e-15 to 8.596075e-15
- out_proj: float32 [768, 768], P(('dp', 'rep')), may hold values from -0.875 to 0.875
- outp_mom: float32 [768, 768], P(('dp', 'rep')), may hold values from -2.3841858e-06 to 2.3841858e-06
- outp_sq: float32 [768, 768], P(('dp', 'rep')), may hold values from 2.1490187e-15 to 8.596075e-15
- up_proj: float32 [768, 3072], P(('dp', 'rep')), may hold values from -0.21875 to 0.21875
- up_mom: float32 [768, 3072], P(('dp', 'rep')), may hold values from -2.3841858e-06 to 2.3841858e-06
- up_sq: float32 [768, 3072], P(('dp', 'rep')), may hold values from 2.1490187e-15 to 8.596075e-15
- down_proj: float32 [3072, 768], P(('dp', 'rep')), may hold values from -0.109375 to 0.109375
- down_mom: float32 [3072, 768], P(('dp', 'rep')), may hold values from -2.3841858e-06 to 2.3841858e-06
- down_sq: float32 [3072, 768], P(('dp', 'rep')), may hold values from 2.1490187e-15 to 8.596075e-15
- time_proj: float32 [256, 128], P(('dp', 'rep')), may hold values from -0.5 to 0.5
- time_mom: float32 [256, 128], P(('dp', 'rep')), may hold values from -2.3841858e-06 to 2.3841858e-06
- time_sq: float32 [256, 128], P(('dp', 'rep')), may hold values from 2.1490187e-15 to 8.596075e-15
- mod_proj: float32 [128, 4608], P(('dp', 'rep')), may hold values from -0.5 to 0.5
- mod_mom: float32 [128, 4608], P(('dp', 'rep')), may hold values from -2.3841858e-06 to 2.3841858e-06
- mod_sq: float32 [128, 4608], P(('dp', 'rep')), may hold values from 2.1490187e-15 to 8.596075e-15
- final_proj: float32 [128, 1536], P(('dp', 'rep')), may hold values from -0.5 to 0.5
- final_mom: float32 [128, 1536], P(('dp', 'rep')), may hold values from -2.3841858e-06 to 2.3841858e-06
- final_sq: float32 [128, 1536], P(('dp', 'rep')), may hold values from 2.1490187e-15 to 8.596075e-15
- norm_gains: float32 [3, 768], P(None, ('dp', 'rep')), may hold values from 0.5 to 1.5
- gains_mom: float32 [3, 768], P(None, ('dp', 'rep')), may hold values from -1.9073486e-05 to 1.9073486e-05
- gains_sq: float32 [3, 768], P(None, ('dp', 'rep')), may hold values from 1.375372e-13 to 5.501488e-13
Outputs:
- loss_sum: float32 [], replicated
- coefficient_aggregate: float32 [], replicated
- grad_norm: float32 [], replicated
- fresh_table: float32 [50304, 768], P(('dp', 'rep'))
- table_mom_new: float32 [50304, 768], P(('dp', 'rep'))
- table_sq_new: float32 [50304, 768], P(('dp', 'rep'))
- attn_new: float32 [768, 2304], P(('dp', 'rep'))
- attn_mom_new: float32 [768, 2304], P(('dp', 'rep'))
- attn_sq_new: float32 [768, 2304], P(('dp', 'rep'))
- outp_new: float32 [768, 768], P(('dp', 'rep'))
- outp_mom_new: float32 [768, 768], P(('dp', 'rep'))
- outp_sq_new: float32 [768, 768], P(('dp', 'rep'))
- expand_matrix_revised: float32 [768, 3072], P(('dp', 'rep'))
- up_mom_new: float32 [768, 3072], P(('dp', 'rep'))
- up_second_moment: float32 [768, 3072], P(('dp', 'rep'))
- down_new: float32 [3072, 768], P(('dp', 'rep'))
- down_mom_new: float32 [3072, 768], P(('dp', 'rep'))
- down_sq_new: float32 [3072, 768], P(('dp', 'rep'))
- time_new: float32 [256, 128], P(('dp', 'rep'))
- time_mom_new: float32 [256, 128], P(('dp', 'rep'))
- time_sq_new: float32 [256, 128], P(('dp', 'rep'))
- mod_new: float32 [128, 4608], P(('dp', 'rep'))
- mod_mom_new: float32 [128, 4608], P(('dp', 'rep'))
- mod_sq_new: float32 [128, 4608], P(('dp', 'rep'))
- final_new: float32 [128, 1536], P(('dp', 'rep'))
- final_mom_new: float32 [128, 1536], P(('dp', 'rep'))
- final_sq_new: float32 [128, 1536], P(('dp', 'rep'))
- gains_new: float32 [3, 768], P(None, ('dp', 'rep'))
- gains_mom_new: float32 [3, 768], P(None, ('dp', 'rep'))
- gains_sq_new: float32 [3, 768], P(None, ('dp', 'rep'))
Inputs may be any that keep to these rules, and one draw needn't show every extreme that they name: `noise_owner`: each position names 8 different blocks. In each aligned block of 512 positions (one half of one sequence), at most 256 positions name one value, a bound that some block reaches. `seq_lengths`: one sequence in every draw has length 1024.
All inputs are finite; a program needn't handle non-finite values.
Results may differ from a plain program's by a relative error of at most 0.006.
The roundings to bfloat16 on the way count: a program that leaves them out, or rounds other values in their place, can miss the bound.
Values may be sent and summed in bfloat16 or wider, within the bound.
No kernel may reach another device: no remote copies, remote signals or barrier semaphores. Data moves between devices by JAX's collectives and lax.ppermute only.
A program may use at most 320 MiB of HBM per device.

v0:
```python
import math

import jax
import jax.numpy as jnp
from jax import lax
from jax.sharding import PartitionSpec as P

HD = 64
TSTEPS = 1000
STEP = 5


HIGH = lax.Precision.HIGHEST
annealed_softness = 0.5


def joined(value, axis, combine):
    everything = jax.tree.map(lambda part: lax.all_gather(part, axis), value)
    leading = jax.tree.map(lambda part: part[0], everything)

    def hop(k, so_far):
        return combine(so_far, jax.tree.map(lambda part: part[k], everything))

    return lax.fori_loop(1, lax.axis_size(axis), hop, leading)


def dense(a, b):
    return jnp.dot(a, b, preferred_element_type=jnp.float32)


def dense_nt(a, b):
    return lax.dot_general(a, b, (((1,), (1,)), ((), ())), preferred_element_type=jnp.float32)


def dense_tn(a, b):
    return lax.dot_general(a, b, (((0,), (0,)), ((), ())), preferred_element_type=jnp.float32)


def exact(a, b):
    return jnp.dot(a, b, precision=HIGH, preferred_element_type=jnp.float32)


def exact_tn(a, b):
    return lax.dot_general(
        a, b, (((0,), (0,)), ((), ())), precision=HIGH, preferred_element_type=jnp.float32
    )


def normalize(x):
    center = x - jnp.mean(x, -1, keepdims=True)
    rstd = lax.rsqrt(jnp.mean(center * center, -1, keepdims=True) + 1e-06)
    return (center * rstd, rstd)


def modulate_back(grad_h, normed, rstd, gain, scale):
    dshift = jnp.sum(grad_h, 1)
    dscale = jnp.sum(grad_h * normed * gain, 1)
    dgain = jnp.sum(grad_h * normed * (1.0 + scale), (0, 1))
    grad_n = grad_h * gain * (1.0 + scale)
    grad_x = rstd * (
        grad_n
        - jnp.mean(grad_n, -1, keepdims=True)
        - normed * jnp.mean(grad_n * normed, -1, keepdims=True)
    )
    return (grad_x, dshift, dscale, dgain)


def rope_tables(pos, head):
    half = head // 2
    freqs = jnp.exp(-math.log(10000.0) * jnp.arange(half, dtype=jnp.float32) / half)
    angle = pos.astype(jnp.float32)[:, None] * freqs[None, :]
    return (jnp.cos(angle), jnp.sin(angle))


def rotate(t, cosv, sinv):
    half = t.shape[-1] // 2
    first, second = (t[..., :half], t[..., half:])
    c = cosv[:, None, :]
    s = sinv[:, None, :]
    return jnp.concatenate([first * c - second * s, first * s + second * c], -1)


def time_features(steps, width):
    tau = (steps.astype(jnp.float32) + 1.0) / TSTEPS
    half = width // 2
    freqs = jnp.exp(-math.log(10000.0) * jnp.arange(half, dtype=jnp.float32) / half)
    angle = 1000.0 * tau[:, None] * freqs[None, :]
    return jnp.concatenate([jnp.cos(angle), jnp.sin(angle)], -1)


def masked_scores(query, keyed, valid):
    scores = jnp.einsum(
        "qhd,khd->hqk", query, keyed, preferred_element_type=jnp.float32
    ) * query.shape[-1] ** (-0.5)
    return jnp.where(valid[None, None, :], scores, -1e30)


def attend(items):
    query, keyed, valued, valid = items
    scores = masked_scores(query, keyed, valid)
    top = jnp.max(scores, -1, keepdims=True)
    expo = jnp.exp(scores - top)
    total = jnp.sum(expo, -1, keepdims=True)
    probs = (expo / total).astype(jnp.bfloat16)
    mixed = jnp.einsum("hqk,khd->qhd", probs, valued, preferred_element_type=jnp.float32)
    return (mixed, top[..., 0] + jnp.log(total[..., 0]))


def attend_back(items):
    query, keyed, valued, valid, lse, grad_mix = items
    scale = query.shape[-1] ** (-0.5)
    probs = jnp.exp(masked_scores(query, keyed, valid) - lse[..., None])
    grad_p = jnp.einsum("qhd,khd->hqk", grad_mix, valued, preferred_element_type=jnp.float32)
    delta = jnp.sum(grad_p * probs, -1, keepdims=True)
    grad_s = (probs * (grad_p - delta)).astype(jnp.bfloat16)
    grad_q = jnp.einsum("hqk,khd->qhd", grad_s, keyed, preferred_element_type=jnp.float32) * scale
    grad_k = jnp.einsum("hqk,qhd->khd", grad_s, query, preferred_element_type=jnp.float32) * scale
    grad_v = jnp.einsum(
        "hqk,qhd->khd", probs.astype(jnp.bfloat16), grad_mix, preferred_element_type=jnp.float32
    )
    return (grad_q, grad_k, grad_v)


def merge_stats(first, second):
    top = jnp.maximum(first[0], second[0])
    total = first[1] * jnp.exp(first[0] - top) + second[1] * jnp.exp(second[0] - top)
    return (top, total, first[2] + second[2])


def adamw(weight, first, second, grad, rate):
    first = 0.9 * first + 0.1 * grad
    second = 0.999 * second + 0.001 * grad * grad
    step = first / (1.0 - 0.9**STEP) / (jnp.sqrt(second / (1.0 - 0.999**STEP)) + 1e-08)
    return (weight - rate * (step + 0.01 * weight), first, second)


def local(
    noise_owner,
    noise_offset,
    option_scores,
    seq_lengths,
    time_index,
    loss_pick,
    loss_target,
    vocab_table,
    table_mom,
    table_sq,
    attn_proj,
    proj_mom,
    proj_sq,
    out_proj,
    outp_mom,
    outp_sq,
    up_proj,
    up_mom,
    up_sq,
    down_proj,
    down_mom,
    down_sq,
    time_proj,
    time_mom,
    time_sq,
    mod_proj,
    mod_mom,
    mod_sq,
    final_proj,
    final_mom,
    final_sq,
    norm_gains,
    gains_mom,
    gains_sq,
):
    devices = lax.axis_size(("dp", "rep"))
    reps = lax.axis_size("rep")
    n_dp = lax.axis_size("dp")
    dp_idx = lax.axis_index("dp")
    rep_idx = lax.axis_index("rep")
    seq_dev, half, cands = noise_offset.shape
    sliced_rows, width = vocab_table.shape
    heads = width // HD
    masters = (attn_proj, out_proj, up_proj, down_proj, time_proj, mod_proj, final_proj, norm_gains)
    copies = (
        lax.all_gather(attn_proj.astype(jnp.bfloat16), ("dp", "rep"), axis=0, tiled=True),
        lax.all_gather(out_proj.astype(jnp.bfloat16), ("dp", "rep"), axis=0, tiled=True),
        lax.all_gather(up_proj.astype(jnp.bfloat16), ("dp", "rep"), axis=0, tiled=True),
        lax.all_gather(down_proj.astype(jnp.bfloat16), ("dp", "rep"), axis=0, tiled=True),
        lax.all_gather(time_proj.astype(jnp.bfloat16), ("dp", "rep"), axis=0, tiled=True),
        lax.all_gather(mod_proj.astype(jnp.bfloat16), ("dp", "rep"), axis=0, tiled=True),
        lax.all_gather(final_proj.astype(jnp.bfloat16), ("dp", "rep"), axis=0, tiled=True),
        lax.all_gather(norm_gains.astype(jnp.bfloat16), ("dp", "rep"), axis=1, tiled=True),
    )
    qkv_w, out_w, up_w, down_w, time_w, mod_w, final_w, gain_w = copies
    gain_f = gain_w.astype(jnp.float32)
    owner = noise_owner.reshape(-1)
    offset = noise_offset.reshape(-1)
    cap = seq_dev * max(2, 2 * half * cands // devices)
    member = (owner[:, None] == jnp.arange(devices, dtype=jnp.int32)[None, :]).astype(jnp.int32)
    slot = jnp.sum((jnp.cumsum(member, 0) - member) * member, 1)
    flat_slot = owner * cap + slot
    request = jnp.zeros((devices * cap,), jnp.int32).at[flat_slot].set(offset).reshape(devices, cap)
    asked = lax.all_to_all(request, ("dp", "rep"), split_axis=0, concat_axis=0, tiled=True)
    table_low = vocab_table.astype(jnp.bfloat16)
    whole_table = lax.all_gather(table_low, ("dp", "rep"), axis=0, tiled=True)
    cand_rows = whole_table[owner * sliced_rows + offset]
    mixing_coefficient = jax.nn.softmax(option_scores / annealed_softness, axis=-1)
    x0 = jnp.sum(
        cand_rows.reshape(seq_dev, half, cands, width).astype(jnp.float32)
        * mixing_coefficient[..., None],
        2,
    )
    seq_start = dp_idx * seq_dev
    lengths = lax.dynamic_slice_in_dim(seq_lengths, seq_start, seq_dev)
    feats = time_features(lax.dynamic_slice_in_dim(time_index, seq_start, seq_dev), time_w.shape[0])
    time_f = time_w.astype(jnp.float32)
    mod_f = mod_w.astype(jnp.float32)
    final_f = final_w.astype(jnp.float32)
    cond, silu_back = jax.vjp(jax.nn.silu, exact(feats, time_f))
    mods = exact(cond, mod_f)[:, None, :]
    fmods = exact(cond, final_f)[:, None, :]
    sh1, sc1, g1, sh2, sc2, g2 = jnp.split(mods, 6, -1)
    fsh, fsc = jnp.split(fmods, 2, -1)
    n1, r1 = normalize(x0)
    h1b = (n1 * gain_f[0] * (1.0 + sc1) + sh1).astype(jnp.bfloat16).reshape(-1, width)
    shaped = dense(h1b, qkv_w).reshape(seq_dev, half, 3, heads, HD)
    pos = rep_idx * half + jnp.arange(half, dtype=jnp.int32)
    cosv, sinv = rope_tables(pos, HD)
    query = rotate(shaped[:, :, 0], cosv, sinv).astype(jnp.bfloat16)
    keyed = rotate(shaped[:, :, 1], cosv, sinv).astype(jnp.bfloat16)
    valued = shaped[:, :, 2].astype(jnp.bfloat16)
    key_all, value_all = (
        lax.all_gather(keyed, "rep", axis=1, tiled=True),
        lax.all_gather(valued, "rep", axis=1, tiled=True),
    )
    valid = jnp.arange(key_all.shape[1], dtype=jnp.int32)[None, :] < lengths[:, None]
    mixed, lse_att = lax.map(attend, (query, key_all, value_all, valid))
    mixed_b = mixed.astype(jnp.bfloat16).reshape(-1, width)
    attn = dense(mixed_b, out_w).reshape(seq_dev, half, width)
    x1 = x0 + g1 * attn
    n2, r2 = normalize(x1)
    h2b = (n2 * gain_f[1] * (1.0 + sc2) + sh2).astype(jnp.bfloat16).reshape(-1, width)
    upper = dense(h2b, up_w)
    act, gelu_back = jax.vjp(lambda u: jax.nn.gelu(u, approximate=True), upper)
    act_b = act.astype(jnp.bfloat16)
    mlp = dense(act_b, down_w).reshape(seq_dev, half, width)
    x2 = x1 + g2 * mlp
    nf, rf = normalize(x2)
    final = nf * gain_f[2] * (1.0 + fsc) + fsh
    seqs_all, reps_all, picks = loss_pick.shape
    my_pick = lax.dynamic_index_in_dim(
        lax.dynamic_slice_in_dim(loss_pick, seq_start, seq_dev), rep_idx, 1, False
    )
    rows_b = (
        jnp.take_along_axis(final, my_pick[:, :, None], 1).astype(jnp.bfloat16).reshape(-1, width)
    )

    def device_order(values):
        return values.reshape(n_dp, seq_dev, reps, picks).transpose(0, 2, 1, 3).reshape(-1)

    targets = device_order(loss_target)
    positions = device_order(loss_pick + (jnp.arange(reps, dtype=jnp.int32) * half)[None, :, None])
    seq_of = device_order(
        jnp.broadcast_to(jnp.arange(seqs_all, dtype=jnp.int32)[:, None, None], loss_pick.shape)
    )
    tau = (time_index.astype(jnp.float32) + 1.0) / TSTEPS
    weight = jnp.where(positions < seq_lengths[seq_of], 1.0 / (0.1 + tau[seq_of]), 0.0)
    coefficient_aggregate = jnp.sum(weight)
    vocab_start = (dp_idx * reps + rep_idx) * sliced_rows
    hit = jnp.arange(sliced_rows, dtype=jnp.int32)[None, :] + vocab_start == targets[:, None]
    every = lax.all_gather(rows_b, ("dp", "rep"), axis=0, tiled=True)
    logits = dense_nt(every, table_low)
    top = jnp.max(logits, -1)
    sums = jnp.sum(jnp.exp(logits - top[:, None]), -1)
    tgt = jnp.sum(jnp.where(hit, logits, 0.0), -1)
    highest_everywhere, sum_all, tgt_all = joined((top, sums, tgt), ("dp", "rep"), merge_stats)
    lse = highest_everywhere + jnp.log(sum_all)
    loss_sum = jnp.sum(weight * (lse - tgt_all))
    probs = jnp.exp(logits - lse[:, None])
    dlogit = ((weight / coefficient_aggregate)[:, None] * (probs - hit.astype(jnp.float32))).astype(
        jnp.bfloat16
    )
    table_grad = dense_tn(dlogit, every)
    drows = lax.psum_scatter(
        dense(dlogit, table_low), ("dp", "rep"), scatter_dimension=0, tiled=True
    )
    spread = (jnp.arange(half, dtype=jnp.int32)[None, :, None] == my_pick[:, None, :]).astype(
        jnp.float32
    )
    grad_final = jnp.einsum(
        "snp,spd->snd", spread, drows.reshape(seq_dev, picks, width), precision=HIGH
    )
    dx2, dfsh, dfsc, dgain_f = modulate_back(grad_final, nf, rf, gain_f[2], fsc)
    dg2 = jnp.sum(dx2 * mlp, 1)
    dmlp = (dx2 * g2).astype(jnp.bfloat16).reshape(-1, width)
    d_down = dense_tn(act_b, dmlp)
    dupper = gelu_back(dense_nt(dmlp, down_w))[0].astype(jnp.bfloat16)
    d_up = dense_tn(h2b, dupper)
    dh2 = dense_nt(dupper, up_w).reshape(seq_dev, half, width)
    dn2x, dsh2, dsc2, dgain_2 = modulate_back(dh2, n2, r2, gain_f[1], sc2)
    dx1 = dx2 + dn2x
    dg1 = jnp.sum(dx1 * attn, 1)
    dattn = (dx1 * g1).astype(jnp.bfloat16).reshape(-1, width)
    d_out = dense_tn(mixed_b, dattn)
    dmixed = dense_nt(dattn, out_w).astype(jnp.bfloat16).reshape(seq_dev, half, heads, HD)
    dquery, dkey_all, dvalue_all = lax.map(
        attend_back, (query, key_all, value_all, valid, lse_att, dmixed)
    )
    dkey, dvalue = (
        lax.psum_scatter(
            dkey_all.astype(jnp.bfloat16), "rep", scatter_dimension=1, tiled=True
        ).astype(jnp.float32),
        lax.psum_scatter(
            dvalue_all.astype(jnp.bfloat16), "rep", scatter_dimension=1, tiled=True
        ).astype(jnp.float32),
    )
    dqkv = jnp.stack([rotate(dquery, cosv, -sinv), rotate(dkey, cosv, -sinv), dvalue], 2)
    dqkv = dqkv.reshape(-1, 3 * width).astype(jnp.bfloat16)
    d_qkv = dense_tn(h1b, dqkv)
    dh1 = dense_nt(dqkv, qkv_w).reshape(seq_dev, half, width)
    dn1x, dsh1, dsc1, dgain_1 = modulate_back(dh1, n1, r1, gain_f[0], sc1)
    dx0 = dx1 + dn1x
    dmods = jnp.concatenate([dsh1, dsc1, dg1, dsh2, dsc2, dg2], -1)
    dfmods = jnp.concatenate([dfsh, dfsc], -1)
    d_mod = exact_tn(cond, dmods)
    d_final = exact_tn(cond, dfmods)
    dcond = lax.dot_general(
        dmods, mod_f, (((1,), (1,)), ((), ())), precision=HIGH, preferred_element_type=jnp.float32
    )
    dcond = dcond + lax.dot_general(
        dfmods,
        final_f,
        (((1,), (1,)), ((), ())),
        precision=HIGH,
        preferred_element_type=jnp.float32,
    )
    d_time = exact_tn(feats, silu_back(dcond)[0])
    d_gains = jnp.stack([dgain_1, dgain_2, dgain_f], 0)
    cand_grads = (mixing_coefficient[..., None] * dx0[:, :, None, :]).reshape(-1, width)
    outgoing = jnp.zeros((devices * cap, width), jnp.float32).at[flat_slot].set(cand_grads)
    incoming = lax.all_to_all(
        outgoing.reshape(devices, cap, width),
        ("dp", "rep"),
        split_axis=0,
        concat_axis=0,
        tiled=True,
    )
    table_grad = table_grad + jax.ops.segment_sum(
        incoming.reshape(-1, width), asked.reshape(-1), num_segments=sliced_rows
    )
    reduced = (
        lax.psum_scatter(d_qkv, ("dp", "rep"), scatter_dimension=0, tiled=True),
        lax.psum_scatter(d_out, ("dp", "rep"), scatter_dimension=0, tiled=True),
        lax.psum_scatter(d_up, ("dp", "rep"), scatter_dimension=0, tiled=True),
        lax.psum_scatter(d_down, ("dp", "rep"), scatter_dimension=0, tiled=True),
        lax.psum_scatter(d_time, ("dp", "rep"), scatter_dimension=0, tiled=True),
        lax.psum_scatter(d_mod, ("dp", "rep"), scatter_dimension=0, tiled=True),
        lax.psum_scatter(d_final, ("dp", "rep"), scatter_dimension=0, tiled=True),
        lax.psum_scatter(d_gains, ("dp", "rep"), scatter_dimension=1, tiled=True),
    )
    local_sq = jnp.sum(table_grad * table_grad)
    for g in reduced:
        local_sq = local_sq + jnp.sum(g * g)
    grad_norm = jnp.sqrt(lax.psum(local_sq, ("dp", "rep")))
    clip = jnp.minimum(1.0, 0.01 / (grad_norm + 1e-06))
    coefficients = (vocab_table,) + masters
    moms = (
        table_mom,
        proj_mom,
        outp_mom,
        up_mom,
        down_mom,
        time_mom,
        mod_mom,
        final_mom,
        gains_mom,
    )
    sqs = (table_sq, proj_sq, outp_sq, up_sq, down_sq, time_sq, mod_sq, final_sq, gains_sq)
    rates = (0.02, 0.02, 0.02, 0.02, 0.02, 0.02, 0.02, 0.02, 0.1)
    grads = (table_grad,) + tuple(reduced)
    result = [loss_sum, coefficient_aggregate, grad_norm]
    for weight_now, first, second, grad, rate in zip(coefficients, moms, sqs, grads, rates):
        result.extend(adamw(weight_now, first, second, clip * grad, rate))
    return tuple(result)


def solution(mesh):
    return jax.shard_map(
        local,
        mesh=mesh,
        in_specs=(
            P("dp", "rep", None),
            P("dp", "rep", None),
            P("dp", "rep", None),
            P(),
            P(),
            P(),
            P(),
            P(("dp", "rep"), None),
            P(("dp", "rep"), None),
            P(("dp", "rep"), None),
            P(("dp", "rep"), None),
            P(("dp", "rep"), None),
            P(("dp", "rep"), None),
            P(("dp", "rep"), None),
            P(("dp", "rep"), None),
            P(("dp", "rep"), None),
            P(("dp", "rep"), None),
            P(("dp", "rep"), None),
            P(("dp", "rep"), None),
            P(("dp", "rep"), None),
            P(("dp", "rep"), None),
            P(("dp", "rep"), None),
            P(("dp", "rep"), None),
            P(("dp", "rep"), None),
            P(("dp", "rep"), None),
            P(("dp", "rep"), None),
            P(("dp", "rep"), None),
            P(("dp", "rep"), None),
            P(("dp", "rep"), None),
            P(("dp", "rep"), None),
            P(("dp", "rep"), None),
            P(None, ("dp", "rep")),
            P(None, ("dp", "rep")),
            P(None, ("dp", "rep")),
        ),
        out_specs=(
            P(),
            P(),
            P(),
            P(("dp", "rep"), None),
            P(("dp", "rep"), None),
            P(("dp", "rep"), None),
            P(("dp", "rep"), None),
            P(("dp", "rep"), None),
            P(("dp", "rep"), None),
            P(("dp", "rep"), None),
            P(("dp", "rep"), None),
            P(("dp", "rep"), None),
            P(("dp", "rep"), None),
            P(("dp", "rep"), None),
            P(("dp", "rep"), None),
            P(("dp", "rep"), None),
            P(("dp", "rep"), None),
            P(("dp", "rep"), None),
            P(("dp", "rep"), None),
            P(("dp", "rep"), None),
            P(("dp", "rep"), None),
            P(("dp", "rep"), None),
            P(("dp", "rep"), None),
            P(("dp", "rep"), None),
            P(("dp", "rep"), None),
            P(("dp", "rep"), None),
            P(("dp", "rep"), None),
            P(None, ("dp", "rep")),
            P(None, ("dp", "rep")),
            P(None, ("dp", "rep")),
        ),
        check_vma=False,
    )
```

profile of v0, /device:TPU:0, one launch (start us, length us, event | category | flops | bytes accessed | tf_op | source)
XLA Modules:
  0.0 2696.8 jit_solution(15806118574043067318)
XLA Ops:
  10.5 4.0 convert_bitcast_fusion.4
  17.1 43.3 %all-gather.6 = bf16[32,24,3]{1,2,0:T(4,128)(2,1)S(1)} all-gather(bf16[1,24,3]{1,2,0:T(4,128)(2,1)S(1)} %convert_bitcast_fusion.3), channel_id=1, replica_groups=mesh['dp'=16,'rep'=2] {'dp','rep'}, dimensions={0}, use_global_device_ids=true | all-gather | bytes 4752 | tf_op jit(solution)/shard_map/all_gather | solution.py:190
  61.0 36.9 %all_gather.55 = bf16[256,128]{1,0:T(8,128)(2,1)S(1)} all-gather(bf16[8,128]{1,0:T(8,128)(2,1)S(1)} %convert_element_type.192), channel_id=1, replica_groups=mesh['dp'=16,'rep'=2] {'dp','rep'}, dimensions={0}, use_global_device_ids=true | all-gather | bytes 67584 | tf_op jit(solution)/shard_map/all_gather | solution.py:187
  102.5 28.3 %all-gather.18.cloned.1.call-done = bf16[768,2304]{1,0:T(8,128)(2,1)} async-done(((bf16[24,2304]{1,0:T(8,128)(2,1)}), bf16[768,2304]{1,0:T(8,128)(2,1)}) %all-gather.18.cloned.1.call-update) | async-done | bytes 3538960 | tf_op jit(solution)/shard_map/all_gather | solution.py:183
  130.8 5.7 copy.93
  136.5 402.4 %all-gather.32.cloned.1.call-done = bf16[32,1572,768]{2,1,0:T(8,128)(2,1)} async-done(((bf16[1,1572,768]{2,1,0:T(8,128)(2,1)}), bf16[32,1572,768]{2,1,0:T(8,128)(2,1)}) %all-gather.32.cloned.1.call-update) | async-done | bytes 77266960 | tf_op jit(solution)/shard_map/all_gather | solution.py:203
  539.0 87.9 %reshape.1104 = bf16[50304,768]{1,0:T(8,128)(2,1)} reshape(bf16[32,1572,768]{2,1,0:T(8,128)(2,1)} %all-gather.32.cloned.1.call-done) | data formatting | bytes 154533888
  626.9 70.8 %gather_fusion = bf16[4096,768]{1,0:T(8,128)(2,1)} fusion(bf16[50304,768]{1,0:T(8,128)(2,1)} %reshape.1104, s32[4096]{0:T(1024)S(1)} %broadcast_clamp_fusion), kind=kCustom, calls=%fused_computation | custom fusion | bytes 12599296 | tf_op jit(solution)/shard_map/gather | solution.py:204
  697.7 17.9 fusion.7
  717.9 4.3 convolution_bitcast_fusion.1
  732.5 39.7 %all-gather.7 = bf16[32,4,1536]{2,1,0:T(4,128)(2,1)S(1)} all-gather(bf16[1,4,1536]{2,1,0:T(4,128)(2,1)S(1)} %convert_bitcast_fusion.2), channel_id=1, replica_groups=mesh['dp'=16,'rep'=2] {'dp','rep'}, dimensions={0}, use_global_device_ids=true | all-gather | bytes 405504 | tf_op jit(solution)/shard_map/all_gather | solution.py:189
  776.4 11.9 fusion.15
  788.3 11.3 fusion
  799.6 12.6 fusion.42
  812.3 3.5 fusion.121
  816.7 55.1 %all-gather.24.cloned.1.call-done = bf16[768,3072]{1,0:T(8,128)(2,1)} async-done(((bf16[24,3072]{1,0:T(8,128)(2,1)}), bf16[768,3072]{1,0:T(8,128)(2,1)}) %all-gather.24.cloned.1.call-update) | async-done | bytes 4718608 | tf_op jit(solution)/shard_map/all_gather | solution.py:185
  871.7 7.7 fusion.109
  879.5 58.2 %all-gather.26.cloned.1.call-done = bf16[3072,768]{1,0:T(8,128)(2,1)} async-done(((bf16[96,768]{1,0:T(8,128)(2,1)}), bf16[3072,768]{1,0:T(8,128)(2,1)}) %all-gather.26.cloned.1.call-update) | async-done | bytes 4718608 | tf_op jit(solution)/shard_map/all_gather | solution.py:186
  937.7 9.1 fusion.120
  949.3 2.8 gather_fusion.1
  957.2 5.9 compare_select_fusion.5
  963.3 4.4 compare_select_fusion.6
  967.9 5.6 fusion.77
  974.2 6.7 select_select_fusion
  985.7 25.9 all-gather.28.cloned.1.call-done
  1011.6 11.1 fusion.124
  1023.2 40.0 %all-gather.1 = f32[65536]{0:T(1024)S(1)} all-gather(f32[2048]{0:T(1024)S(1)} %get-tuple-element.420), channel_id=3, replica_groups=mesh['dp'=16,'rep'=2] {'dp','rep'}, dimensions={0}, use_global_device_ids=true | all-gather | bytes 270336 | tf_op jit(solution)/shard_map/all_gather | solution.py:18
  1065.7 6.8 fusion.2
  1072.5 37.4 %all-gather.2 = f32[65536]{0:T(1024)S(1)} all-gather(f32[2048]{0:T(1024)S(1)} %get-tuple-element.263), channel_id=4, replica_groups=mesh['dp'=16,'rep'=2] {'dp','rep'}, dimensions={0}, use_global_device_ids=true | all-gather | bytes 270336 | tf_op jit(solution)/shard_map/all_gather | solution.py:18
  1112.8 38.7 %all-gather.3 = f32[65536]{0:T(1024)S(1)} all-gather(f32[2048]{0:T(1024)S(1)} %get-tuple-element.262), channel_id=5, replica_groups=mesh['dp'=16,'rep'=2] {'dp','rep'}, dimensions={0}, use_global_device_ids=true | all-gather | bytes 270336 | tf_op jit(solution)/shard_map/all_gather | solution.py:18
  1154.0 94.9 %while.12 = (s32[]{:T(128)}, f32[2048]{0:T(1024)S(1)}, f32[2048]{0:T(1024)}, f32[2048]{0:T(1024)S(1)}, f32[32,2048]{1,0:T(8,128)}, /*index=5*/f32[32,2048]{1,0:T...) while((s32[]{:T(128)}, f32[2048]{0:T(1024)S(1)}, f32[2048]{0:T(1024)}, f32[2048]{0:T(1024)S(1)}, ...), condition=%wide.region_16.17_spmd, body=%wide.region_15.16_spmd.sunk | while | flops 14341 | bytes 123031 | solution.py:24
  1250.8 6.9 fusion.5
  1257.7 2.8 copy-done.7
  1260.6 10.8 fusion.100
  1272.8 109.1 %reduce-scatter.9.cloned.1.call-done = f32[64,768]{1,0:T(8,128)} async-done(((f32[2048,768]{1,0:T(8,128)}), f32[64,768]{1,0:T(8,128)}) %reduce-scatter.9.cloned.1.call-update) | async-done | bytes 196624 | tf_op jit(solution)/shard_map/reduce_scatter | solution.py:282
  1382.0 3.8 multiply_reduce_fusion.2
  1387.1 9.5 fusion.22
  1396.6 3.7 multiply_reduce_fusion.3
  1406.9 18.1 multiply_reduce_fusion
  1424.9 17.4 multiply_convert_fusion
  1442.3 4.6 copy-done
  1446.9 3.5 fusion.39
  1450.5 13.3 fusion.36
  1467.2 18.0 reduce-window.6
  1489.1 16.1 scatter_custom_fusion
  1505.2 3.8 all-to-all-start
  1509.0 10.2 multiply_bitcast_fusion
  1526.0 3.3 multiply_reduce_fusion.4
  1531.0 30.0 %scatter_custom_fusion.1 = f32[8192,768]{1,0:T(8,128)} fusion(s32[4096]{0:T(1024)S(1)} %bitcast.243, f32[]{:T(128)} %constant.136.clone.1, f32[512,768]{1,0:T(8,128)} %multiply_add_fusion.2, f32[4096]{0:T(1024)S(1)} %copy-done.48), kind=kCustom, calls=%fused_computation.31 | custom fusion | flops 3145728 | bytes 26755076 | tf_op jit(solution)/shard_map/scatter | solution.py:338
  1561.7 6.1 all-to-all-start.1
  1568.4 3.9 fusion.61
  1587.8 2.4 broadcast_multiply_fusion
  1590.4 6.9 fusion.107
  1598.0 7.2 fusion.108
  1606.7 9.8 fusion.59
  1618.4 8.8 fusion.125
  1627.2 572.3 %all-reduce.3 = f32[3,768]{1,0:T(4,128)S(1)} all-reduce(f32[3,768]{1,0:T(4,128)S(1)} %pad_maximum_fusion.5), channel_id=16, replica_groups=mesh['dp'=16,'rep'=2] {'dp','rep'}, use_global_device_ids=true, to_apply=%region_61.62.clone | all-reduce | flops 2304 | bytes 18432
  2206.0 65.4 %reduce-scatter.15.cloned.1.call-done = f32[24,2304]{1,0:T(8,128)} async-done(((f32[768,2304]{1,0:T(8,128)}), f32[24,2304]{1,0:T(8,128)}) %reduce-scatter.15.cloned.1.call-update) | async-done | bytes 221200 | tf_op jit(solution)/shard_map/reduce_scatter | solution.py:350
  2273.0 138.9 %reduce-scatter.19.cloned.1.call-done = f32[24,3072]{1,0:T(8,128)} async-done(((f32[768,3072]{1,0:T(8,128)}), f32[24,3072]{1,0:T(8,128)}) %reduce-scatter.19.cloned.1.call-update) | async-done | bytes 294928 | tf_op jit(solution)/shard_map/reduce_scatter | solution.py:352
  2413.5 139.8 %reduce-scatter.21.cloned.1.call-done = f32[96,768]{1,0:T(8,128)} async-done(((f32[3072,768]{1,0:T(8,128)}), f32[96,768]{1,0:T(8,128)}) %reduce-scatter.21.cloned.1.call-update) | async-done | bytes 294928 | tf_op jit(solution)/shard_map/reduce_scatter | solution.py:353
  2555.0 59.8 %scatter_fusion = f32[1572,768]{1,0:T(8,128)} fusion(f32[1572,768]{1,0:T(8,128)} %fusion.125, s32[8192]{0:T(1024)S(1)} %bitcast.235, f32[8192,768]{1,0:T(8,128)} %bitcast.90), kind=kCustom, calls=%fused_computation.4 | custom fusion | flops 6291456 | bytes 75530240 | tf_op jit(solution)/shard_map/scatter-add | solution.py:346
  2614.8 4.2 multiply_reduce_fusion.1
  2624.9 40.1 %psum.7 = f32[]{:T(128)} all-reduce(f32[]{:T(128)S(6)} %add.589), channel_id=1, replica_groups=mesh['dp'=16,'rep'=2] {'dp','rep'}, use_global_device_ids=true, to_apply=%region_63.64 | all-reduce | flops 1 | bytes 8 | tf_op jit(solution)/shard_map/psum | solution.py:362
  2666.0 13.5 multiply_subtract_fusion
  (593 shorter events, 211.9 us)
Async XLA Ops:
  7.2 92.6 %all-gather.34.cloned.1.call-start = ((), (), s32[]{:S(2)}) async-start(), calls=%async_computation.24 | async-start | bytes 1216512 | tf_op jit(solution)/shard_map/all_gather | solution.py:188
  8.8 122.0 %all-gather.18.cloned.1.call-start = ((), (), s32[]{:S(2)}) async-start(), calls=%async_computation.9 | async-start | bytes 3649536 | tf_op jit(solution)/shard_map/all_gather | solution.py:183
  10.5 528.5 %all-gather.32.cloned.1.call-start = ((), (), s32[]{:S(2)}) async-start(), calls=%async_computation.23 | async-start | bytes 79884288 | tf_op jit(solution)/shard_map/all_gather | solution.py:203
  14.6 761.8 %all-gather.20.cloned.1.call-start = ((), (), s32[]{:S(2)}) async-start(), calls=%async_computation.10 | async-start | bytes 2359296 | tf_op jit(solution)/shard_map/all_gather | solution.py:231
  61.0 654.6 %copy-start.47 = (f32[4096]{0:T(1024)}, f32[4096]{0:T(1024)S(1)}, u32[]{:S(2)}) copy-start(f32[4096]{0:T(1024)S(1)} %mul.1137) | copy-start | bytes 49156
  98.0 38.5 %copy-start.131 = (f32[1,128]{1,0:T(1,128)}, f32[1,128]{1,0:T(1,128)S(1)}, u32[]{:S(2)}) copy-start(f32[1,128]{1,0:T(1,128)S(1)} %get-tuple-element.430) | copy-start | bytes 1540
  98.1 619.7 %copy-start.100 = (f32[768]{0:T(1024)}, f32[768]{0:T(1024)S(1)}, u32[]{:S(2)}) copy-start(f32[768]{0:T(1024)S(1)} %get-tuple-element.287) | copy-start | bytes 9220
  98.1 773.7 %copy-start.92 = (f32[768]{0:T(1024)}, f32[768]{0:T(1024)S(1)}, u32[]{:S(2)}) copy-start(f32[768]{0:T(1024)S(1)} %get-tuple-element.286) | copy-start | bytes 9220
  98.1 849.1 %copy-start.66 = (f32[768]{0:T(1024)}, f32[768]{0:T(1024)S(1)}, u32[]{:S(2)}) copy-start(f32[768]{0:T(1024)S(1)} %get-tuple-element.285) | copy-start | bytes 9220
  98.9 676.6 %copy-start.108 = (f32[128]{0:T(128)}, f32[128]{0:T(128)S(1)}, u32[]{:S(2)}) copy-start(f32[128]{0:T(128)S(1)} %get-tuple-element.428) | copy-start | bytes 1540
  99.8 624.6 %copy-start.31 = (f32[512,32]{0,1:T(8,128)}, f32[512,32]{0,1:T(8,128)S(1)}, u32[]{:S(2)}) copy-start(f32[512,32]{0,1:T(8,128)S(1)} %get-tuple-element.382) | copy-start | bytes 196612
  101.2 35.3 %copy-start.6 = (bf16[128,4608]{1,0:T(8,128)(2,1)}, bf16[128,4608]{1,0:T(8,128)(2,1)S(1)}, u32[]{:S(2)}) copy-start(bf16[128,4608]{1,0:T(8,128)(2,1)S(1)} %reshape.1106) | copy-start | bytes 3538948
  102.5 615.4 %copy-start.103 = (f32[768]{0:T(1024)}, f32[768]{0:T(1024)S(1)}, u32[]{:S(2)}) copy-start(f32[768]{0:T(1024)S(1)} %get-tuple-element.283) | copy-start | bytes 9220
  102.5 615.4 %copy-start.126 = (f32[768]{0:T(1024)}, f32[768]{0:T(1024)S(1)}, u32[]{:S(2)}) copy-start(f32[768]{0:T(1024)S(1)} %get-tuple-element.282) | copy-start | bytes 9220
  102.5 709.8 %copy-start.68 = (f32[768]{0:T(1024)}, f32[768]{0:T(1024)S(1)}, u32[]{:S(2)}) copy-start(f32[768]{0:T(1024)S(1)} %get-tuple-element.284) | copy-start | bytes 9220
  697.7 17.9 copy-start.1
  725.0 51.4 %copy-start.15 = (bf16[512,12,32]{0,2,1:T(8,128)(2,1)}, bf16[512,12,32]{0,2,1:T(8,128)(2,1)S(1)}, u32[]{:S(2)}) copy-start(bf16[512,12,32]{0,2,1:T(8,128)(2,1)S(1)} %get-tuple-element.370) | copy-start | bytes 1179652
  726.0 47.5 %copy-start.46 = (s32[16]{0:T(128)S(1)}, s32[16]{0:T(128)}, u32[]{:S(2)}) copy-start(s32[16]{0:T(128)} %param.39) | copy-start | bytes 196
  726.0 73.6 %all-gather.30.cloned.1.call-start = ((), (), s32[]{:S(2)}) async-start(), calls=%async_computation.22 | async-start | bytes 2359296 | tf_op jit(solution)/shard_map/all_gather | solution.py:232
  728.5 83.8 %all-gather.22.cloned.1.call-start = ((), (), s32[]{:S(2)}) async-start(), calls=%async_computation.11 | async-start | bytes 1216512 | tf_op jit(solution)/shard_map/all_gather | solution.py:184
  729.2 142.6 %all-gather.24.cloned.1.call-start = ((), (), s32[]{:S(2)}) async-start(), calls=%async_computation.12 | async-start | bytes 4866048 | tf_op jit(solution)/shard_map/all_gather | solution.py:185
  729.9 207.8 %all-gather.26.cloned.1.call-start = ((), (), s32[]{:S(2)}) async-start(), calls=%async_computation.13 | async-start | bytes 4866048 | tf_op jit(solution)/shard_map/all_gather | solution.py:186
  731.7 279.9 %all-gather.28.cloned.1.call-start = ((), (), s32[]{:S(2)}) async-start(), calls=%async_computation.14 | async-start | bytes 3244032 | tf_op jit(solution)/shard_map/all_gather | solution.py:269
  772.2 16.0 copy-start.13
  774.9 24.7 copy-start.97
  776.4 170.8 %copy-start.64 = (f32[768]{0:T(1024)}, f32[768]{0:T(1024)S(1)}, u32[]{:S(2)}) copy-start(f32[768]{0:T(1024)S(1)} %get-tuple-element.297) | copy-start | bytes 9220
  815.8 63.7 %copy-start.78 = (f32[512]{0:T(512)}, f32[512]{0:T(512)S(1)}, u32[]{:S(2)}) copy-start(f32[512]{0:T(512)S(1)} %broadcast_multiply_fusion.11) | copy-start | bytes 6148
  953.7 428.3 %reduce-scatter.9.cloned.1.call-start = ((), (), s32[]{:S(2)}) async-start(), calls=%async_computation.15 | async-start | bytes 6488064 | tf_op jit(solution)/shard_map/reduce_scatter | solution.py:282
  973.5 49.1 %copy-start.55 = (f32[2048]{0:T(1024)}, f32[2048]{0:T(1024)S(1)}, u32[]{:S(2)}) copy-start(f32[2048]{0:T(1024)S(1)} %fusion.77) | copy-start | bytes 24580
  981.0 41.7 %copy-start.56 = (s32[2048]{0:T(1024)}, s32[2048]{0:T(1024)S(1)}, u32[]{:S(2)}) copy-start(s32[2048]{0:T(1024)S(1)} %select_select_fusion) | copy-start | bytes 24580
  1065.7 88.3 %slice-start = ((f32[65536]{0:T(1024)}), f32[2048]{0:T(1024)S(1)}, s32[]{:S(2)}) async-start(f32[65536]{0:T(1024)} %copy-done.28), calls=%async_computation.26 | async-start | bytes 16384 | tf_op jit(solution)/shard_map/slice | solution.py:19
  1271.3 110.6 %copy-start.65 = (f32[768]{0:T(1024)S(1)}, f32[768]{0:T(1024)}, u32[]{:S(2)}) copy-start(f32[768]{0:T(1024)} %copy-done.64) | copy-start | bytes 9220
  1271.3 110.6 %copy-start.67 = (f32[768]{0:T(1024)S(1)}, f32[768]{0:T(1024)}, u32[]{:S(2)}) copy-start(f32[768]{0:T(1024)} %copy-done.66) | copy-start | bytes 9220
  1271.3 110.6 %copy-start.71 = (f32[512]{0:T(512)S(1)}, f32[512]{0:T(512)}, u32[]{:S(2)}) copy-start(f32[512]{0:T(512)} %copy-done.70) | copy-start | bytes 6148
  1271.3 110.6 %copy-start.82 = (f32[512]{0:T(512)S(1)}, f32[512]{0:T(512)}, u32[]{:S(2)}) copy-start(f32[512]{0:T(512)} %copy-done.81) | copy-start | bytes 6148
  1271.4 247.8 %reduce-scatter.11.cloned.1.call-start = ((), (), s32[]{:S(2)}) async-start(), calls=%async_computation.16 | async-start | bytes 2359296 | tf_op jit(solution)/shard_map/reduce_scatter | solution.py:308
  1424.9 22.0 copy-start.16
  1450.4 72.9 %reduce-scatter.13.cloned.1.call-start = ((), (), s32[]{:S(2)}) async-start(), calls=%async_computation.17 | async-start | bytes 2359296 | tf_op jit(solution)/shard_map/reduce_scatter | solution.py:311
  1505.2 55.9 %all-to-all-start = ((s32[32,1,256]{2,1,0:T(1,128)}), s32[32,1,256]{2,1,0:T(1,128)S(1)}, u32[]{:S(2)}, u32[]{:S(2)}) async-start(s32[32,1,256]{2,1,0:T(1,128)} %bitcast.74), calls=%async_computation | async-start | bytes 65536 | tf_op jit(solution)/shard_map/all_to_all | solution.py:201
  1561.7 993.3 %all-to-all-start.1 = ((f32[32,256,768]{2,1,0:T(8,128)}), f32[32,256,768]{2,1,0:T(8,128)}, u32[]{:S(2)}, u32[]{:S(2)}) async-start(f32[32,256,768]{2,1,0:T(8,128)} %bitcast.221), calls=%async_computation.4 | async-start | bytes 50331648 | tf_op jit(solution)/shard_map/all_to_all | solution.py:339
  1567.7 632.5 %reduce-scatter.17.cloned.1.call-start = ((), (), s32[]{:S(2)}) async-start(), calls=%async_computation.19 | async-start | bytes 2433024 | tf_op jit(solution)/shard_map/reduce_scatter | solution.py:351
  1572.2 629.5 %all-reduce.7.cloned.1.call-start = ((), (), s32[]{:S(2)}) async-start(), calls=%async_computation.25 | async-start | bytes 6553600
  1590.3 681.1 %reduce-scatter.15.cloned.1.call-start = ((), (), s32[]{:S(2)}) async-start(), calls=%async_computation.18 | async-start | bytes 7299072 | tf_op jit(solution)/shard_map/reduce_scatter | solution.py:350
  1597.4 814.5 %reduce-scatter.19.cloned.1.call-start = ((), (), s32[]{:S(2)}) async-start(), calls=%async_computation.20 | async-start | bytes 9732096 | tf_op jit(solution)/shard_map/reduce_scatter | solution.py:352
  1605.3 948.0 %reduce-scatter.21.cloned.1.call-start = ((), (), s32[]{:S(2)}) async-start(), calls=%async_computation.21 | async-start | bytes 9732096 | tf_op jit(solution)/shard_map/reduce_scatter | solution.py:353
  1618.4 936.6 %copy-start.51 = (s32[32,1,256]{2,1,0:T(1,128)S(1)}, s32[32,1,256]{2,1,0:T(1,128)}, u32[]{:S(2)}) copy-start(s32[32,1,256]{2,1,0:T(1,128)} %copy-done.50) | copy-start | bytes 98308
  2665.8 16.9 copy-start.52
  2665.8 16.9 copy-start.73
  2665.8 16.9 copy-start.74
  2665.8 18.3 copy-start.115
  2665.8 18.3 copy-start.133
  2665.8 18.3 copy-start.134
  2665.8 19.0 copy-start.29
  2665.8 19.0 copy-start.30
  2665.8 19.0 copy-start.44
  2665.9 19.0 copy-start.45
  2665.9 19.9 copy-start.39
  2665.9 19.9 copy-start.40
  2665.9 19.9 copy-start.53
  2665.9 19.9 copy-start.54
  2665.9 20.6 copy-start.21
  2665.9 20.6 copy-start.23
  2665.9 20.6 copy-start.34
  2666.0 20.6 copy-start.35
  (97 other events, 549.7 us)
Sparse Core Ops, SparseCore 0:
  11.5 56.7 all-gather.33
  71.8 58.9 all-gather.17
  134.3 404.6 all-gather.31
  726.1 7.9 all-gather.19
  736.1 10.9 all-gather.29
  750.4 55.1 all-gather.21
  809.1 62.5 all-gather.23
  875.2 62.4 all-gather.25
  953.8 57.7 all-gather.27
  1271.5 110.4 reduce-scatter.8
  1450.5 8.2 reduce-scatter.10
  1463.9 8.0 reduce-scatter.12
  1575.3 260.8 reduce-scatter.16
  1842.5 303.4 all-reduce.6
  2152.5 118.8 reduce-scatter.14
  2277.1 134.7 reduce-scatter.18
  2418.7 134.6 reduce-scatter.20
where the time goes:
time: 2720 us; the launch traced here: 2700 us
  waiting for transfers between devices  1020 us (38%)
  blocking collectives  848 us (31%)
  other arithmetic  321 us (12%)
  local copies, waits for them, and re-layouts  289 us (11%)
  matrix products  179 us (7%)
    unnamed x1, blocking collectives  572 us
    all_gather x1, waiting for transfers between devices, local(): whole_table = lax.all_gather(table_low, ('dp', 'rep'), axis=0, tiled=True)  402 us
    reduce_scatter x1, waiting for transfers between devices, local(): lax.psum_scatter(d_down, ('dp', 'rep'), scatter_dimension=0, tiled=True)  140 us
    reduce_scatter x1, waiting for transfers between devices, local(): lax.psum_scatter(d_up, ('dp', 'rep'), scatter_dimension=0, tiled=True)  139 us
    all_gather x3, blocking collectives, joined(): everything = jax.tree.map(lambda part: lax.all_gather(part, axis), value)  116 us
    unnamed x293, local copies, waits for them, and re-layouts  116 us
    reduce_scatter x1, waiting for transfers between devices, local(): lax.psum_scatter(dense(dlogit, table_low), ('dp', 'rep'), scatter_dimensi...  109 us
    gather x1, local copies, waits for them, and re-layouts, local(): cand_rows = whole_table[owner * sliced_rows + offset]  70.8 us
  transfers between devices with their start and end apart: 19, of which 9 were waited for; matrix products, arithmetic and copies ran while one was open for 10% of the time, Pallas kernels for 0%

commit v1 on v0

v1 whole, which is shorter than its diff:
```python
import functools
import math

import jax
import jax.numpy as jnp
from jax import lax
from jax.experimental import pallas as pl
from jax.experimental.pallas import tpu as pltpu
from jax.sharding import PartitionSpec as P

HD = 64
TSTEPS = 1000
STEP = 5
PLANE = 4
LANES = 128
BOTH = ("dp", "rep")

HIGH = lax.Precision.HIGHEST
annealed_softness = 0.5
bf16 = jnp.bfloat16
f32 = jnp.float32


def dense(a, b):
    return jnp.dot(a, b, preferred_element_type=f32)


def dense_nt(a, b):
    return lax.dot_general(a, b, (((1,), (1,)), ((), ())), preferred_element_type=f32)


def dense_tn(a, b):
    return lax.dot_general(a, b, (((0,), (0,)), ((), ())), preferred_element_type=f32)


def exact(a, b):
    return jnp.dot(a, b, precision=HIGH, preferred_element_type=f32)


def exact_nt(a, b):
    return lax.dot_general(
        a, b, (((1,), (1,)), ((), ())), precision=HIGH, preferred_element_type=f32
    )


def exact_tn(a, b):
    return lax.dot_general(
        a, b, (((0,), (0,)), ((), ())), precision=HIGH, preferred_element_type=f32
    )


def normalize(x):
    center = x - jnp.mean(x, -1, keepdims=True)
    rstd = lax.rsqrt(jnp.mean(center * center, -1, keepdims=True) + 1e-06)
    return (center * rstd, rstd)


def modulate_back(grad_h, normed, rstd, gain, scale):
    dshift = jnp.sum(grad_h, 0)
    weighted = grad_h * normed
    column = jnp.sum(weighted, 0)
    dscale = column * gain
    dgain = column * (1.0 + scale[0])
    grad_n = grad_h * gain * (1.0 + scale)
    grad_x = rstd * (
        grad_n
        - jnp.mean(grad_n, -1, keepdims=True)
        - normed * jnp.mean(grad_n * normed, -1, keepdims=True)
    )
    return (grad_x, dshift, dscale, dgain)


def rope_tables(pos, head):
    half = head // 2
    freqs = jnp.exp(-math.log(10000.0) * jnp.arange(half, dtype=f32) / half)
    angle = pos.astype(f32)[:, None] * freqs[None, :]
    return (jnp.cos(angle), jnp.sin(angle))


def rotate(t, cosv, sinv):
    half = t.shape[-1] // 2
    first, second = (t[..., :half], t[..., half:])
    c = cosv[:, None, :]
    s = sinv[:, None, :]
    return jnp.concatenate([first * c - second * s, first * s + second * c], -1)


def time_features(steps, width):
    tau = (steps.astype(f32) + 1.0) / TSTEPS
    half = width // 2
    freqs = jnp.exp(-math.log(10000.0) * jnp.arange(half, dtype=f32) / half)
    angle = 1000.0 * tau[:, None] * freqs[None, :]
    return jnp.concatenate([jnp.cos(angle), jnp.sin(angle)], -1)


def masked_scores(query, keyed, valid):
    scores = jnp.einsum("qhd,khd->hqk", query, keyed, preferred_element_type=f32) * query.shape[
        -1
    ] ** (-0.5)
    return jnp.where(valid[None, None, :], scores, -1e30)


def attend(query, keyed, valued, valid):
    scores = masked_scores(query, keyed, valid)
    top = jnp.max(scores, -1, keepdims=True)
    expo = jnp.exp(scores - top)
    total = jnp.sum(expo, -1, keepdims=True)
    probs = (expo / total).astype(bf16)
    mixed = jnp.einsum("hqk,khd->qhd", probs, valued, preferred_element_type=f32)
    return (mixed, top[..., 0] + jnp.log(total[..., 0]))


def attend_back(query, keyed, valued, valid, lse, grad_mix):
    scale = query.shape[-1] ** (-0.5)
    probs = jnp.exp(masked_scores(query, keyed, valid) - lse[..., None])
    grad_p = jnp.einsum("qhd,khd->hqk", grad_mix, valued, preferred_element_type=f32)
    delta = jnp.sum(grad_p * probs, -1, keepdims=True)
    grad_s = (probs * (grad_p - delta)).astype(bf16)
    grad_q = jnp.einsum("hqk,khd->qhd", grad_s, keyed, preferred_element_type=f32) * scale
    grad_k = jnp.einsum("hqk,qhd->khd", grad_s, query, preferred_element_type=f32) * scale
    grad_v = jnp.einsum("hqk,qhd->khd", probs.astype(bf16), grad_mix, preferred_element_type=f32)
    return (grad_q, grad_k, grad_v)


def adamw(weight, first, second, grad, rate):
    first = 0.9 * first + 0.1 * grad
    second = 0.999 * second + 0.001 * grad * grad
    step = first / (1.0 - 0.9**STEP) / (jnp.sqrt(second / (1.0 - 0.999**STEP)) + 1e-08)
    return (weight - rate * (step + 0.01 * weight), first, second)


def hop(x, dl=0, dq=0, dr=0):
    reps = lax.axis_size("rep")
    lines = lax.axis_size("dp") // PLANE
    pairs = []
    for l in range(lines):
        for q in range(PLANE):
            for r in range(reps):
                to = (((l + dl) % lines) * PLANE + (q ^ dq)) * reps + (r ^ dr)
                pairs.append(((l * PLANE + q) * reps + r, to))
    return lax.ppermute(x, BOTH, pairs)


def step_line(x, way, reach):
    lines = lax.axis_size("dp") // PLANE
    pairs = []
    for l in range(lines):
        if 0 <= l + way * reach < lines:
            for q in range(PLANE):
                pairs.append((l * PLANE + q, (l + way) * PLANE + q))
    return lax.ppermute(x, "dp", pairs)


def mix_kernel(idx_ref, mix_ref, *refs, groups, cands, counts):
    pieces = refs[: len(counts)]
    out_ref, tab, stage, sem = refs[len(counts) :]

    @pl.when(pl.program_id(0) == 0)
    def _():
        def copy(j):
            return pltpu.make_async_copy(
                pieces[j], stage.at[j % 2, pl.ds(0, counts[j])], sem.at[j % 2]
            )

        copy(0).start()
        base = 0
        for j, rows in enumerate(counts):
            if j + 1 < len(counts):
                copy(j + 1).start()
            copy(j).wait()

            @pl.loop(0, rows // 16)
            def _(t, j=j, base=base):
                part = stage[j % 2, pl.ds(pl.multiple_of(t * 16, 16), 16), :].astype(f32)
                for g in range(groups):
                    tab[pl.ds((base + t * 16) * groups + g, 16, stride=groups), :] = part[
                        :, g * LANES : (g + 1) * LANES
                    ]

            base += rows

    unroll = 4

    @pl.loop(0, idx_ref.shape[-1] // cands // unroll)
    def _(block):
        for u in range(unroll):
            p = block * unroll + u
            total = None
            for c in range(cands):
                row = tab[pl.ds(idx_ref[0, 0, p * cands + c], 8), :]
                term = row * mix_ref[0, 0, p * cands + c]
                total = term if total is None else total + term
            out_ref[0, pl.ds(p * groups, 8), :] = total


def mix_rows(idx, mix, pieces, cands):
    groups = pieces[0].shape[1] // LANES
    lines, _, entries = idx.shape
    counts = tuple(piece.shape[0] for piece in pieces)
    rows = entries // cands * groups + 8
    return pl.pallas_call(
        functools.partial(mix_kernel, groups=groups, cands=cands, counts=counts),
        grid=(lines,),
        in_specs=[pl.BlockSpec((1, 1, entries), lambda i: (i, 0, 0), memory_space=pltpu.SMEM)] * 2
        + [pl.BlockSpec(memory_space=pl.ANY)] * len(pieces),
        out_specs=pl.BlockSpec((1, rows, LANES), lambda i: (i, 0, 0)),
        out_shape=jax.ShapeDtypeStruct((lines, rows, LANES), f32),
        scratch_shapes=[
            pltpu.VMEM((sum(counts) * groups + 8, LANES), f32),
            pltpu.VMEM((2, max(counts), groups * LANES), bf16),
            pltpu.SemaphoreType.DMA((2,)),
        ],
        compiler_params=pltpu.CompilerParams(vmem_limit_bytes=60 * 2**20),
        cost_estimate=pl.CostEstimate(
            flops=lines * entries * 2048, bytes_accessed=40 * 2**20, transcendentals=0
        ),
    )(idx, mix, *pieces)


def spread_kernel(cnt_ref, row_ref, pos_ref, mix_ref, *refs, groups, arrays):
    sources = refs[:arrays]
    head_ref, out_ref, sq_ref, total, rows32, stage, sem = refs[arrays:]
    per, length, _ = sources[0].shape
    n = arrays * per

    def copy(k):
        return pltpu.make_async_copy(sources[k // per].at[k % per], stage.at[k % 2], sem.at[k % 2])

    copy(0).start()

    @pl.loop(0, total.shape[0] // 64)
    def _(t):
        total[pl.ds(pl.multiple_of(t * 64, 64), 64), :] = jnp.zeros((64, LANES), f32)

    unroll = 4
    for k in range(n):
        if k + 1 < n:
            copy(k + 1).start()
        copy(k).wait()

        @pl.loop(0, length // 64)
        def _(t, k=k):
            at = pl.multiple_of(t * 64, 64)
            rows32[pl.ds(at, 64), :] = stage[k % 2, pl.ds(at, 64), :].astype(f32)

        @pl.loop(0, (cnt_ref[k] + unroll - 1) // unroll)
        def _(block, k=k):
            for u in range(unroll):
                e = block * unroll + u
                at = pl.ds(pl.multiple_of(row_ref[k, e] * 8, 8), 8)
                term = mix_ref[k, e] * rows32[pl.ds(pos_ref[k, e], 8), :]
                total[at, :] = total[at, :] + term

    vocab = out_ref.shape[0]

    def finish(at, size, start):
        squares = jnp.zeros((size, LANES), f32)
        for g in range(groups):
            columns = slice(g * LANES, (g + 1) * LANES)
            value = head_ref[pl.ds(at, size), columns] + total[pl.ds(start + g, size, stride=8), :]
            out_ref[pl.ds(at, size), columns] = value
            squares = squares + value * value
        return squares

    squares = lax.fori_loop(
        0,
        vocab // 8,
        lambda t, so_far: so_far + finish(pl.multiple_of(t * 8, 8), 8, t * 64),
        jnp.zeros((8, LANES), f32),
    )
    sq_ref[...] = squares
    if vocab % 8:
        at = vocab // 8 * 8
        sq_ref[0 : vocab % 8, :] += finish(at, vocab % 8, at * 8)


def spread_rows(cnt, row, pos, mix, sources, head, vocab):
    width = head.shape[1]
    groups = width // LANES
    length = sources[0].shape[1]
    smem = pl.BlockSpec(memory_space=pltpu.SMEM)
    vmem = pl.BlockSpec(memory_space=pltpu.VMEM)
    return pl.pallas_call(
        functools.partial(spread_kernel, groups=groups, arrays=len(sources)),
        in_specs=[smem] * 4 + [pl.BlockSpec(memory_space=pl.ANY)] * len(sources) + [vmem],
        out_specs=[vmem, vmem],
        out_shape=[
            jax.ShapeDtypeStruct((vocab, width), f32),
            jax.ShapeDtypeStruct((8, LANES), f32),
        ],
        scratch_shapes=[
            pltpu.VMEM((-(-vocab * 8 // 64) * 64, LANES), f32),
            pltpu.VMEM((length + 8, LANES), f32),
            pltpu.VMEM((2, length, LANES), bf16),
            pltpu.SemaphoreType.DMA((2,)),
        ],
        compiler_params=pltpu.CompilerParams(vmem_limit_bytes=60 * 2**20),
        cost_estimate=pl.CostEstimate(
            flops=2**28, bytes_accessed=40 * 2**20, transcendentals=0
        ),
    )(cnt, row, pos, mix, *sources, head)


def local(
    noise_owner,
    noise_offset,
    option_scores,
    seq_lengths,
    time_index,
    loss_pick,
    loss_target,
    vocab_table,
    table_mom,
    table_sq,
    attn_proj,
    proj_mom,
    proj_sq,
    out_proj,
    outp_mom,
    outp_sq,
    up_proj,
    up_mom,
    up_sq,
    down_proj,
    down_mom,
    down_sq,
    time_proj,
    time_mom,
    time_sq,
    mod_proj,
    mod_mom,
    mod_sq,
    final_proj,
    final_mom,
    final_sq,
    norm_gains,
    gains_mom,
    gains_sq,
):
    devices = lax.axis_size(BOTH)
    reps = lax.axis_size("rep")
    n_dp = lax.axis_size("dp")
    lines = n_dp // PLANE
    dp_idx = lax.axis_index("dp")
    rep_idx = lax.axis_index("rep")
    me = dp_idx * reps + rep_idx
    line = dp_idx // PLANE
    chip = dp_idx % PLANE
    _, half, cands = noise_offset.shape
    vocab, width = vocab_table.shape
    heads = width // HD
    groups = width // LANES
    swaps = [(dq, dr) for dq in range(PLANE) for dr in range(reps)]

    padded = -(-vocab // 16) * 16
    table_low = jnp.pad(vocab_table.astype(bf16), ((0, padded - vocab), (0, 0)))
    cut = padded // 32 * 16
    upper_rows, lower_rows = table_low[:cut], table_low[cut:]
    first, second = {0: upper_rows}, {0: lower_rows}
    first[1] = hop(upper_rows, dq=1)
    second[2] = hop(lower_rows, dq=2)
    first[2] = hop(upper_rows, dq=2)
    second[1] = hop(lower_rows, dq=1)
    first[3] = hop(first[1], dq=2)
    second[3] = hop(second[2], dq=1)
    pieces = []
    for dq in range(PLANE):
        pieces += [first[dq], second[dq]]
        pieces += [hop(first[dq], dr=1), hop(second[dq], dr=1)]

    owner = noise_owner.reshape(-1)
    offset = noise_offset.reshape(-1)
    mixing = jax.nn.softmax(option_scores.reshape(half, cands) / annealed_softness, axis=-1)
    packed_owner = owner.reshape(-1, LANES) * padded + offset.reshape(-1, LANES)
    packed_mix = mixing.reshape(-1, LANES)
    line_owner = jnp.stack(
        [packed_owner] + [hop(packed_owner, dl=-d) for d in range(1, lines)]
    )
    line_mix = jnp.stack([packed_mix] + [hop(packed_mix, dl=-d) for d in range(1, lines)])
    row_owner = line_owner // padded
    slot_of = (((row_owner // reps) % PLANE) ^ chip) * reps + ((row_owner % reps) ^ rep_idx)
    here = (row_owner // (reps * PLANE)) == line
    row_at = jnp.where(here, slot_of * padded + line_owner % padded, 0) * groups
    mix_here = jnp.where(here, line_mix, 0.0)
    partial = mix_rows(
        row_at.reshape(lines, 1, half * cands),
        mix_here.reshape(lines, 1, half * cands),
        pieces,
        cands,
    )[:, : half * groups]
    ahead = back = None
    for d in range(lines - 1, 0, -1):
        to_right = partial[d] if ahead is None else partial[d] + ahead
        to_left = partial[lines - d] if back is None else partial[lines - d] + back
        ahead = step_line(to_right, 1, d)
        back = step_line(to_left, -1, d)
    x0 = (partial[0] + ahead + back).reshape(half, width)

    def gather(value, axis=0):
        return lax.all_gather(value.astype(bf16), BOTH, axis=axis, tiled=True)

    small = (time_proj, mod_proj, final_proj, norm_gains)
    flat = jnp.concatenate([value.reshape(-1) for value in small])
    flat = jnp.pad(flat, (0, -flat.size % (8 * LANES))).reshape(1, -1, LANES)
    small_all = gather(flat).reshape(devices, -1)
    qkv_w = gather(attn_proj)
    out_w = gather(out_proj)
    up_w = gather(up_proj)
    down_w = gather(down_proj)
    unpacked = []
    at = 0
    for value in small:
        part = small_all[:, at : at + value.size].astype(f32).reshape((devices,) + value.shape)
        unpacked.append(part)
        at += value.size
    time_f = unpacked[0].reshape(-1, time_proj.shape[1])
    mod_f = unpacked[1].reshape(-1, mod_proj.shape[1])
    final_f = unpacked[2].reshape(-1, final_proj.shape[1])
    gain_f = unpacked[3].transpose(1, 0, 2).reshape(norm_gains.shape[0], width)

    length = lax.dynamic_slice_in_dim(seq_lengths, dp_idx, 1)
    feats = time_features(time_index, time_f.shape[0])
    cond, silu_back = jax.vjp(jax.nn.silu, exact(feats, time_f))
    my_cond = lax.dynamic_slice_in_dim(cond, dp_idx, 1)
    mods = exact(my_cond, mod_f)
    fmods = exact(my_cond, final_f)
    sh1, sc1, g1, sh2, sc2, g2 = jnp.split(mods, 6, -1)
    fsh, fsc = jnp.split(fmods, 2, -1)

    n1, r1 = normalize(x0)
    h1b = (n1 * gain_f[0] * (1.0 + sc1) + sh1).astype(bf16)
    shaped = dense(h1b, qkv_w).reshape(half, 3, heads, HD)
    pos = rep_idx * half + jnp.arange(half, dtype=jnp.int32)
    far_pos = (1 - rep_idx) * half + jnp.arange(half, dtype=jnp.int32)
    cosv, sinv = rope_tables(pos, HD)
    query = rotate(shaped[:, 0], cosv, sinv).astype(bf16)
    keyed = rotate(shaped[:, 1], cosv, sinv).astype(bf16)
    valued = shaped[:, 2].astype(bf16)
    key_all = jnp.concatenate([keyed, hop(keyed, dr=1)], 0)
    value_all = jnp.concatenate([valued, hop(valued, dr=1)], 0)
    valid = jnp.concatenate([pos, far_pos]) < length
    mixed, lse_att = attend(query, key_all, value_all, valid)
    mixed_b = mixed.astype(bf16).reshape(-1, width)
    attn = dense(mixed_b, out_w)
    x1 = x0 + g1 * attn
    n2, r2 = normalize(x1)
    h2b = (n2 * gain_f[1] * (1.0 + sc2) + sh2).astype(bf16)
    upper = dense(h2b, up_w)
    act, gelu_back = jax.vjp(lambda u: jax.nn.gelu(u, approximate=True), upper)
    act_b = act.astype(bf16)
    mlp = dense(act_b, down_w)
    x2 = x1 + g2 * mlp
    nf, rf = normalize(x2)
    final = nf * gain_f[2] * (1.0 + fsc) + fsh

    picks = loss_pick.shape[-1]
    tau = (time_index.astype(f32) + 1.0) / TSTEPS
    starts = (jnp.arange(reps, dtype=jnp.int32) * half)[None, :, None]
    weight_all = jnp.where(
        loss_pick + starts < seq_lengths[:, None, None], (1.0 / (0.1 + tau))[:, None, None], 0.0
    )
    coefficient_aggregate = jnp.sum(weight_all)

    def of_line(values):
        mine = lax.dynamic_slice(
            values.reshape(lines, PLANE, reps, picks), (0, chip, rep_idx, 0), (lines, 1, 1, picks)
        )
        return from_me(mine.reshape(lines, picks))

    def from_me(values):
        return lax.dynamic_slice_in_dim(jnp.concatenate([values, values], 0), line, lines)

    def from_start(values):
        return lax.dynamic_slice_in_dim(
            jnp.concatenate([values, values], 0), (lines - line) % lines, lines
        )

    targets = of_line(loss_target).reshape(-1)
    weight = of_line(weight_all).reshape(-1)
    my_pick = lax.dynamic_slice(loss_pick, (dp_idx, rep_idx, 0), (1, 1, picks)).reshape(picks)
    spread = (jnp.arange(half, dtype=jnp.int32)[:, None] == my_pick[None, :]).astype(f32)
    rows_b = jnp.take(final, my_pick, axis=0).astype(bf16)
    every = jnp.concatenate([rows_b] + [hop(rows_b, dl=-d) for d in range(1, lines)], 0)
    plane_table = jnp.concatenate(pieces, 0)
    logits = dense_nt(every, plane_table)
    column = jnp.arange(plane_table.shape[0], dtype=jnp.int32)
    exists = (column % padded) < vocab
    t_owner = targets // vocab
    t_slot = (((t_owner // reps) % PLANE) ^ chip) * reps + ((t_owner % reps) ^ rep_idx)
    t_column = jnp.where(
        t_owner // (reps * PLANE) == line, t_slot * padded + targets % vocab, -1
    )
    hit = column[None, :] == t_column[:, None]
    logits = jnp.where(exists[None, :], logits, -1e30)
    top = jnp.max(logits, -1)
    sums = jnp.sum(jnp.exp(logits - top[:, None]), -1)
    tgt = jnp.sum(jnp.where(hit, logits, 0.0), -1)
    stats = from_start(
        jnp.stack([value.reshape(lines, picks) for value in (top, sums, tgt)], 1)
    )
    stats_all = jnp.stack([stats] + [hop(stats, dl=-d) for d in range(1, lines)])
    tops = stats_all[:, :, 0]
    best = jnp.max(tops, 0)
    sum_all = jnp.sum(stats_all[:, :, 1] * jnp.exp(tops - best), 0)
    lse_line = best + jnp.log(sum_all)
    tgt_line = jnp.sum(stats_all[:, :, 2], 0)
    loss_here = jnp.sum(from_start(weight.reshape(lines, picks)) * (lse_line - tgt_line))
    loss_here = jnp.where(line == 0, loss_here, 0.0)
    lse = from_me(lse_line).reshape(-1)
    probs = jnp.exp(logits - lse[:, None])
    dlogit = ((weight / coefficient_aggregate)[:, None] * (probs - hit.astype(f32))).astype(bf16)
    drows_part = dense(dlogit, plane_table).reshape(lines, picks, width)
    drows = drows_part[0]
    for d in range(1, lines):
        drows = drows + hop(drows_part[d], dl=d)
    dlogit_mine = []
    rows_mine = []
    for slot, (dq, dr) in enumerate(swaps):
        block = dlogit[:, slot * padded : (slot + 1) * padded]
        dlogit_mine.append(block if slot == 0 else hop(block, dq=dq, dr=dr))
        rows_mine.append(every if slot == 0 else hop(every, dq=dq, dr=dr))
    head_grad = dense_tn(jnp.concatenate(dlogit_mine, 0), jnp.concatenate(rows_mine, 0))

    def scatter(value):
        return lax.psum_scatter(value, BOTH, scatter_dimension=0, tiled=True)

    grad_final = exact(spread, drows)
    dx2, dfsh, dfsc, dgain_f = modulate_back(grad_final, nf, rf, gain_f[2], fsc)
    dg2 = jnp.sum(dx2 * mlp, 0)
    dmlp = (dx2 * g2).astype(bf16)
    d_down = scatter(dense_tn(act_b, dmlp))
    dupper = gelu_back(dense_nt(dmlp, down_w))[0].astype(bf16)
    d_up = scatter(dense_tn(h2b, dupper))
    dh2 = dense_nt(dupper, up_w)
    dn2x, dsh2, dsc2, dgain_2 = modulate_back(dh2, n2, r2, gain_f[1], sc2)
    dx1 = dx2 + dn2x
    dg1 = jnp.sum(dx1 * attn, 0)
    dattn = (dx1 * g1).astype(bf16)
    d_out = scatter(dense_tn(mixed_b, dattn))
    dmixed = dense_nt(dattn, out_w).astype(bf16).reshape(half, heads, HD)
    dquery, dkey_all, dvalue_all = attend_back(query, key_all, value_all, valid, lse_att, dmixed)
    dkey = dkey_all[:half] + hop(dkey_all[half:].astype(bf16), dr=1).astype(f32)
    dvalue = dvalue_all[:half] + hop(dvalue_all[half:].astype(bf16), dr=1).astype(f32)
    dqkv = jnp.stack([rotate(dquery, cosv, -sinv), rotate(dkey, cosv, -sinv), dvalue], 1)
    dqkv = dqkv.reshape(-1, 3 * width).astype(bf16)
    dh1 = dense_nt(dqkv, qkv_w)
    dn1x, dsh1, dsc1, dgain_1 = modulate_back(dh1, n1, r1, gain_f[0], sc1)
    dx0 = dx1 + dn1x
    d_qkv = scatter(dense_tn(h1b, dqkv))

    cap = max(2, 2 * half * cands // devices)
    member = (owner[:, None] == jnp.arange(devices, dtype=jnp.int32)[None, :]).astype(jnp.int32)
    slot = jnp.sum((jnp.cumsum(member, 0) - member) * member, 1)
    flat_slot = owner * cap + slot
    entry = offset * half + jnp.arange(half * cands, dtype=jnp.int32) // cands + 1
    asked = jnp.zeros((devices * cap,), jnp.int32).at[flat_slot].set(entry)
    asked_mix = jnp.zeros((devices * cap,), f32).at[flat_slot].set(mixing.reshape(-1))

    def exchange(value):
        return lax.all_to_all(
            value.reshape(devices, cap), BOTH, split_axis=0, concat_axis=0, tiled=True
        )

    asked, asked_mix = exchange(asked), exchange(asked_mix)
    dx0_b = dx0.astype(bf16).reshape(half * groups, LANES)
    on_line = [dx0_b] + [hop(dx0_b, dl=-d) for d in range(1, lines)]
    stacks = [
        jnp.stack(on_line[k * lines // 4 : (k + 1) * lines // 4]) for k in range(4)
    ]
    sources = []
    order = []
    for k, stack in enumerate(stacks):
        kind = {0: stack, 1: hop(stack, dq=1), 2: hop(stack, dq=2)}
        kind[3] = hop(kind[1], dq=2) if k % 2 == 0 else hop(kind[2], dq=1)
        for dq in range(PLANE):
            for dr in range(reps):
                sources.append(kind[dq] if dr == 0 else hop(kind[dq], dr=1))
                for d in range(k * lines // 4, (k + 1) * lines // 4):
                    order.append(
                        (((line + d) % lines) * PLANE + (chip ^ dq)) * reps + (rep_idx ^ dr)
                    )
    order = jnp.stack(order)
    asked = jnp.take(asked, order, axis=0)
    asked_mix = jnp.take(asked_mix, order, axis=0)
    count = jnp.sum((asked > 0).astype(jnp.int32), 1)
    asked = jnp.maximum(asked - 1, 0)
    table_grad, table_squares = spread_rows(
        count, asked // half, (asked % half) * groups, asked_mix, sources, head_grad, vocab
    )

    sums_here = jnp.concatenate(
        [dsh1, dsc1, dg1, dsh2, dsc2, dg2, dfsh, dfsc, dgain_1, dgain_2, dgain_f]
    )
    sums_all = lax.all_gather(sums_here.reshape(1, -1, LANES), BOTH, axis=0, tiled=True)
    sums_all = sums_all.reshape(n_dp, reps, -1).sum(1)
    dmods = sums_all[:, : 6 * width]
    dfmods = sums_all[:, 6 * width : 8 * width]

    def my_columns(value, count):
        return lax.dynamic_slice_in_dim(value, me * count, count, axis=1)

    d_mod = exact_tn(my_columns(cond, mod_proj.shape[0]), dmods)
    d_final = exact_tn(my_columns(cond, final_proj.shape[0]), dfmods)
    dcond = exact_nt(dmods, mod_f) + exact_nt(dfmods, final_f)
    d_time = exact_tn(my_columns(feats, time_proj.shape[0]), silu_back(dcond)[0])
    d_gains = my_columns(
        jnp.sum(sums_all[:, 8 * width :], 0).reshape(3, width), norm_gains.shape[1]
    )

    reduced = (d_qkv, d_out, d_up, d_down, d_time, d_mod, d_final, d_gains)
    local_sq = jnp.sum(table_squares)
    for g in reduced:
        local_sq = local_sq + jnp.sum(g * g)
    totals = lax.psum(jnp.stack([local_sq, loss_here]), BOTH)
    grad_norm = jnp.sqrt(totals[0])
    loss_sum = totals[1]
    clip = jnp.minimum(1.0, 0.01 / (grad_norm + 1e-06))
    masters = (attn_proj, out_proj, up_proj, down_proj, time_proj, mod_proj, final_proj, norm_gains)
    coefficients = (vocab_table,) + masters
    moms = (
        table_mom,
        proj_mom,
        outp_mom,
        up_mom,
        down_mom,
        time_mom,
        mod_mom,
        final_mom,
        gains_mom,
    )
    sqs = (table_sq, proj_sq, outp_sq, up_sq, down_sq, time_sq, mod_sq, final_sq, gains_sq)
    rates = (0.02, 0.02, 0.02, 0.02, 0.02, 0.02, 0.02, 0.02, 0.1)
    grads = (table_grad,) + reduced
    result = [loss_sum, coefficient_aggregate, grad_norm]
    for weight_now, first_m, second_m, grad, rate in zip(coefficients, moms, sqs, grads, rates):
        result.extend(adamw(weight_now, first_m, second_m, clip * grad, rate))
    return tuple(result)


def solution(mesh):
    shard = P(BOTH, None)
    columns = P(None, BOTH)
    return jax.shard_map(
        local,
        mesh=mesh,
        in_specs=(P("dp", "rep", None),) * 3 + (P(),) * 4 + (shard,) * 24 + (columns,) * 3,
        out_specs=(P(),) * 3 + (shard,) * 24 + (columns,) * 3,
        check_vma=False,
    )
```

time: 2720 us -> 1360 us (0.50)
  blocking collectives: 848 us -> 39.8 us
  waiting for transfers between devices: 1020 us -> 570 us
  other arithmetic: 321 us -> 150 us
  starting transfers between devices: 10.6 us -> 96.2 us
  local copies, waits for them, and re-layouts: 289 us -> 208 us
  Pallas kernels: 0 us -> 79.3 us
    unnamed x1 -> x0, blocking collectives: 572 us -> none
    all_gather x9 -> x6, waiting for transfers between devices: 570 us -> 0.07 us  [the longest x5 0.05 us: gather(): return lax.all_gather(value.astype(bf16), BOTH, axis=axis, tiled=True)]
    ppermute x0 -> x84, waiting for transfers between devices: none -> 287 us  [the longest x78 205 us: hop(): return lax.ppermute(x, BOTH, pairs)]
    all_gather x6 -> x0, blocking collectives: 236 us -> none  [the longest x3 116 us: joined(): everything = jax.tree.map(lambda part: lax.all_gather(part, axis), value)]
    reduce_scatter x7 -> x4, waiting for transfers between devices: 453 us -> 268 us  [scatter(): return lax.psum_scatter(value, BOTH, scatter_dimension=0, tiled=True)]
    ppermute x0 -> x84, starting transfers between devices: none -> 88.7 us  [the longest x78 64.6 us: hop(): return lax.ppermute(x, BOTH, pairs)]
    pallas_call x0 -> x2, Pallas kernels: none -> 79.3 us  [the longest x1 41.8 us: spread_rows(): pl.pallas_call(functools.partial(spread_kernel, groups=groups, arrays=len...]
    gather x5 -> x3, local copies, waits for them, and re-layouts: 75.7 us -> 3.32 us  [the longest x1 2.12 us: local(): rows_b = jnp.take(final, my_pick, axis=0).astype(bf16)]
  transfers between devices with their start and end apart: 19 -> 96, of which waited for: 9 -> 35; matrix products, arithmetic and copies ran while one was open for 10% -> 27% of each run, Pallas kernels for 0% -> 6%
where the time goes in v1:
time: 1360 us; the launch traced here: 1350 us
  waiting for transfers between devices  570 us (42%)
  local copies, waits for them, and re-layouts  208 us (15%)
  matrix products  177 us (13%)
  other arithmetic  150 us (11%)
  starting transfers between devices  96.2 us (7%)
  Pallas kernels  79.3 us (6%)
  blocking collectives  39.8 us (3%)
  between operations  25.7 us (2%)
    reduce_scatter x4, waiting for transfers between devices, scatter(): return lax.psum_scatter(value, BOTH, scatter_dimension=0, tiled=True)  268 us
    ppermute x78, waiting for transfers between devices, hop(): return lax.ppermute(x, BOTH, pairs)  205 us
    ppermute x6, waiting for transfers between devices, step_line(): return lax.ppermute(x, 'dp', pairs)  82 us
    ppermute x78, starting transfers between devices, hop(): return lax.ppermute(x, BOTH, pairs)  64.6 us
    unnamed x389, local copies, waits for them, and re-layouts  59.9 us
    pallas_call x1, Pallas kernels, spread_rows(): pl.pallas_call(functools.partial(spread_kernel, groups=groups, arrays=len...  41.8 us
    psum x1, blocking collectives, local(): totals = lax.psum(jnp.stack([local_sq, loss_here]), BOTH)  39.8 us
    dot_general x5, matrix products, dense_tn(): lax.dot_general(a, b, (((0,), (0,)), ((), ())), preferred_element_type=f32)  37.8 us
  transfers between devices with their start and end apart: 96, of which 35 were waited for; matrix products, arithmetic and copies ran while one was open for 27% of the time, Pallas kernels for 6%

profile of v1, /device:TPU:0, one launch (start us, length us, event | category | flops | bytes accessed | tf_op | source)
XLA Modules:
  0.0 1345.5 jit_solution(14391506129076756874)
XLA Ops:
  34.1 3.8 collective-permute-done.4
  43.1 4.3 collective-permute-done.2
  47.4 4.6 collective-permute-done.1
  58.2 23.1 %collective-permute-done.13.refs_9_ = bf16[800,768]{1,0:T(8,128)(2,1)S(1)} collective-permute-done((bf16[800,768]{1,0:T(8,128)(2,1)S(1)}, bf16[800,768]{1,0:T(8,128)(2,1)S(1)}, u32[]{:S(2)}, u32[]{:S(2)}) %collective-permute-start.13) | collective-permute-done | bytes 1228832 | tf_op jit(solution)/shard_map/ppermute | solution.py:141
  84.0 24.6 %collective-permute-done.16.refs_12_ = bf16[784,768]{1,0:T(8,128)(2,1)S(1)} collective-permute-done((bf16[784,768]{1,0:T(8,128)(2,1)}, bf16[784,768]{1,0:T(8,128)(2,1)S(1)}, u32[]{:S(2)}, u32[]{:S(2)}) %collective-permute-start.16) | collective-permute-done | bytes 1204256 | tf_op jit(solution)/shard_map/ppermute | solution.py:141
  108.6 4.3 collective-permute-done.17.refs_13_
  119.3 37.6 %shard_map.553 = f32[4,3080,128]{2,1,0:T(8,128)} custom-call(s32[4,1,4096]{2,1,0:T(1,128)} %fusion.66.idx_ref, f32[4,1,4096]{2,1,0:T(1,128)} %get-tuple-element.103.mix_ref, bf16[784,768]{1,0:T(8,128)(2,1)} %get-tuple-element.125.refs_0_, bf16[800,768]{1,0:T(8,128)(2,1)} %copy-done.19, bf16[784,768]{1,0:T(8,128)(2,1)} %collective-permute-done.6.refs_2_, ...), custom_call_target="tpu_custom_call" | custom-call | flops 33554432 | bytes 41943040 | tf_op jit(solution)/shard_map/pallas_call | solution.py:201
  160.2 3.4 collective-permute-start.20
  169.4 33.4 %collective-permute-done.20 = f32[3072,128]{1,0:T(8,128)S(1)} collective-permute-done((f32[3072,128]{1,0:T(8,128)}, f32[3072,128]{1,0:T(8,128)S(1)}, u32[]{:S(2)}, u32[]{:S(2)}) %collective-permute-start.20) | collective-permute-done | bytes 1572896 | tf_op jit(solution)/shard_map/ppermute | solution.py:151
  202.8 3.8 fusion.22
  206.6 4.5 collective-permute-start.21
  227.1 35.4 %collective-permute-done.21 = f32[3072,128]{1,0:T(8,128)S(1)} collective-permute-done((f32[3072,128]{1,0:T(8,128)}, f32[3072,128]{1,0:T(8,128)S(1)}, u32[]{:S(2)}, u32[]{:S(2)}) %collective-permute-start.21) | collective-permute-done | bytes 1572896 | tf_op jit(solution)/shard_map/ppermute | solution.py:151
  262.6 4.3 fusion.151
  266.9 11.1 collective-permute-start.22
  285.3 7.5 copy.173
  294.5 5.4 slice.236
  300.8 3.7 copy.175
  312.2 5.7 copy.177
  318.9 12.3 collective-permute-done.25
  337.4 3.4 add_convert_fusion.2
  341.5 4.2 fusion.29
  366.2 12.2 fusion.6
  378.4 11.2 fusion
  391.2 12.1 fusion.23
  403.3 3.5 fusion.167
  407.2 7.3 fusion.154
  414.7 9.1 fusion.166
  428.7 3.8 collective-permute-start.28
  439.5 12.8 fusion.175
  453.6 7.7 select_reduce_fusion
  477.1 12.1 multiply_convert_fusion.1
  489.2 11.6 fusion.176
  500.9 3.8 collective-permute-start.36
  505.4 5.3 collective-permute-done.34
  510.7 8.0 collective-permute-done.35
  521.9 8.4 fusion.13
  530.5 3.5 multiply_reduce_fusion.3
  539.3 17.7 %multiply_reduce_fusion = (f32[12,512]{1,0:T(8,128)}, f32[12,512,1024]{2,1,0:T(8,128)}) fusion(f32[12,512]{1,0:T(8,128)} %log_add_fusion, f32[12,512,1024]{2,1,0:T(8,128)} %get-tuple-element.167, pred[1024]{0:T(1024)(128)(4,1)S(1)} %copy-done.142, bf16[512,12,64]{0,2,1:T(8,128)(2,1)} %bitcast.261, bf16[512,12,64]{0,2,1:T(8,128)(2,1)} %copy-done.66, ...), kind=kOutput, calls=%fused_computation.6 | convolution fusion | flops 839903232 | bytes 52741120 | tf_op jit(solution)/shard_map/qhd,khd->hqk/dot_general | solution.py:116
  557.1 17.3 %multiply_convert_fusion = bf16[12,512,1024]{2,1,0:T(8,128)(2,1)S(1)} fusion(f32[12,512,1024]{2,1,0:T(8,128)} %get-tuple-element.175, f32[12,512]{1,0:T(8,128)} %get-tuple-element.174, f32[12,512]{1,0:T(8,128)} %log_add_fusion, f32[12,512,1024]{2,1,0:T(8,128)} %get-tuple-element.167, pred[1024]{0:T(1024)(128)(4,1)S(1)} %copy-done.142), kind=kLoop, calls=%fused_computation.5 | loop fusion | flops 37748736 | bytes 62964736 | tf_op jit(solution)/shard_map/convert_element_type | solution.py:118
  580.0 10.7 fusion.15
  593.1 8.8 multiply_bitcast_fusion.1
  608.9 4.1 multiply_reduce_fusion.5
  620.2 6.9 fusion.178
  627.8 7.3 fusion.153
  636.5 9.7 fusion.36
  650.2 9.4 reduce-window.6
  662.6 3.5 collective-permute-start.82
  669.7 7.8 fusion.170
  701.6 40.2 %collective-permute-done.83 = bf16[256,768]{1,0:T(8,128)(2,1)} collective-permute-done((bf16[256,768]{1,0:T(8,128)(2,1)}, bf16[256,768]{1,0:T(8,128)(2,1)}, u32[]{:S(2)}, u32[]{:S(2)}) %collective-permute-start.83) | collective-permute-done | bytes 393248 | tf_op jit(solution)/shard_map/ppermute | solution.py:141
  746.9 16.2 %scatter_custom_fusion.1 = f32[8192]{0:T(1024)} fusion(s32[4096]{0:T(1024)} %bitcast.273, f32[4096]{0:T(1024)S(1)} %exponential_divide_fusion.2, f32[]{:T(128)} %constant.470.clone.1), kind=kCustom, calls=%fused_computation.282 | custom fusion | bytes 33280 | tf_op jit(solution)/shard_map/scatter | solution.py:557
  763.1 4.2 all-to-all-start.1
  768.1 16.2 %scatter_custom_fusion = s32[8192]{0:T(1024)} fusion(s32[4096]{0:T(1024)} %bitcast.274, s32[4096]{0:T(1024)S(1)} %fusion.81, s32[]{:T(128)} %constant.455.clone.1), kind=kCustom, calls=%fused_computation.284 | custom fusion | bytes 33280 | tf_op jit(solution)/shard_map/scatter | solution.py:556
  785.0 14.8 %all-to-all-done.1 = f32[32,1,256]{2,1,0:T(1,128)S(1)} async-done(((f32[32,1,256]{2,1,0:T(1,128)}), f32[32,1,256]{2,1,0:T(1,128)S(1)}, u32[]{:S(2)}, u32[]{:S(2)}) %all-to-all-start.1) | async-done | bytes 32800 | tf_op jit(solution)/shard_map/all_to_all | solution.py:560
  816.5 25.5 %collective-permute-done.54 = bf16[3072,128]{1,0:T(8,128)(2,1)} collective-permute-done((bf16[3072,128]{1,0:T(8,128)(2,1)}, bf16[3072,128]{1,0:T(8,128)(2,1)}, u32[]{:S(2)}, u32[]{:S(2)}) %collective-permute-start.54) | collective-permute-done | bytes 786464 | tf_op jit(solution)/shard_map/ppermute | solution.py:141
  858.1 4.8 collective-permute-done.66.refs_28_
  866.5 13.3 collective-permute-done.58.refs_20_
  905.1 16.4 %collective-permute-done.44.refs_6_ = bf16[1,3072,128]{2,1,0:T(8,128)(2,1)} collective-permute-done((bf16[1,3072,128]{2,1,0:T(8,128)(2,1)}, bf16[1,3072,128]{2,1,0:T(8,128)(2,1)}, u32[]{:S(2)}, u32[]{:S(2)}) %collective-permute-start.44) | collective-permute-done | bytes 786464 | tf_op jit(solution)/shard_map/ppermute | solution.py:141
  923.3 4.5 collective-permute-done.68.refs_30_
  930.0 10.6 fusion.177.refs_32_
  953.8 41.8 %shard_map.554 = (f32[1572,768]{1,0:T(8,128)}, f32[8,128]{1,0:T(8,128)}) custom-call(s32[32]{0:T(128)} %get-tuple-element.147.cnt_ref, s32[32,256]{1,0:T(8,128)} %get-tuple-element.146.row_ref, s32[32,256]{1,0:T(8,128)} %get-tuple-element.145.pos_ref, f32[32,256]{1,0:T(8,128)} %broadcast_select_fusion.mix_ref, bf16[1,3072,128]{2,1,0:T(8,128)(2,1)} %copy-done.43, ...), custom_call_target="tpu_custom_call" | custom-call | flops 268435456 | bytes 41943040 | tf_op jit(solution)/shard_map/pallas_call | solution.py:283
  1000.4 129.0 %reduce-scatter.9.cloned.1.call-done = f32[24,3072]{1,0:T(8,128)} async-done(((f32[768,3072]{1,0:T(8,128)}), f32[24,3072]{1,0:T(8,128)}) %reduce-scatter.9.cloned.1.call-update) | async-done | bytes 294928 | tf_op jit(solution)/shard_map/reduce_scatter | solution.py:525
  1131.7 139.1 %reduce-scatter.11.cloned.1.call-done = f32[96,768]{1,0:T(8,128)} async-done(((f32[3072,768]{1,0:T(8,128)}), f32[96,768]{1,0:T(8,128)}) %reduce-scatter.11.cloned.1.call-update) | async-done | bytes 294928 | tf_op jit(solution)/shard_map/reduce_scatter | solution.py:525
  1275.7 39.8 %psum.7 = f32[2]{0:T(128)S(1)} all-reduce(f32[2]{0:T(128)S(1)} %pad_maximum_fusion.17), channel_id=1, replica_groups=mesh['dp'=16,'rep'=2] {'dp','rep'}, use_global_device_ids=true, to_apply=%region_56.57 | all-reduce | flops 2 | bytes 16 | tf_op jit(solution)/shard_map/psum | solution.py:614
  1319.8 13.5 %multiply_subtract_fusion = (f32[1572,768]{1,0:T(8,128)}, f32[1572,768]{1,0:T(8,128)}, f32[1572,768]{1,0:T(8,128)}) fusion(f32[1572,768]{1,0:T(8,128)} %param.41, f32[1572,768]{1,0:T(8,128)} %get-tuple-element.33, f32[]{:T(128)S(6)} %min.3, f32[1572,768]{1,0:T(8,128)} %param.42, f32[1572,768]{1,0:T(8,128)} %param.43), kind=kLoop, calls=%fused_computation.34 | loop fusion | flops 19316736 | bytes 33804292 | tf_op jit(solution)/shard_map/sub | solution.py:129
  (809 shorter events, 313.8 us)
Async XLA Ops:
  7.2 278.1 %all-gather.7.cloned.1.call-start = ((), (), s32[]{:S(2)}) async-start(), calls=%async_computation.6 | async-start | bytes 1757184 | tf_op jit(solution)/shard_map/all_gather | solution.py:400
  11.1 301.1 %all-gather.9.cloned.1.call-start = ((), (), s32[]{:S(2)}) async-start(), calls=%async_computation.7 | async-start | bytes 3649536 | tf_op jit(solution)/shard_map/all_gather | solution.py:400
  12.7 390.5 %all-gather.11.cloned.1.call-start = ((), (), s32[]{:S(2)}) async-start(), calls=%async_computation.8 | async-start | bytes 1216512 | tf_op jit(solution)/shard_map/all_gather | solution.py:400
  14.3 392.8 %all-gather.13.cloned.1.call-start = ((), (), s32[]{:S(2)}) async-start(), calls=%async_computation.9 | async-start | bytes 4866048 | tf_op jit(solution)/shard_map/all_gather | solution.py:400
  16.0 398.6 %all-gather.15.cloned.1.call-start = ((), (), s32[]{:S(2)}) async-start(), calls=%async_computation.10 | async-start | bytes 4866048 | tf_op jit(solution)/shard_map/all_gather | solution.py:400
  20.3 35.8 %collective-permute-start.12 = (bf16[784,768]{1,0:T(8,128)(2,1)}, bf16[784,768]{1,0:T(8,128)(2,1)}, u32[]{:S(2)}, u32[]{:S(2)}) collective-permute-start(bf16[784,768]{1,0:T(8,128)(2,1)} %get-tuple-element.125.refs_0_), channel_id=1, source_target_pairs={{0,4},{1,5},{2,6},{3,7},{4,0},{5,1},{6,2},{7,3},{8,12},{9,13},{10,... | collective-permute-start | bytes 3612680 | tf_op jit(solution)/shard_map/ppermute | solution.py:141
  23.3 32.8 %collective-permute-start.8 = (bf16[784,768]{1,0:T(8,128)(2,1)}, bf16[784,768]{1,0:T(8,128)(2,1)}, u32[]{:S(2)}, u32[]{:S(2)}) collective-permute-start(bf16[784,768]{1,0:T(8,128)(2,1)} %get-tuple-element.125.refs_0_), channel_id=1, source_target_pairs={{0,2},{1,3},{2,0},{3,1},{4,6},{5,7},{6,4},{7,5},{8,10},{9,11},{10,... | collective-permute-start | bytes 3612680 | tf_op jit(solution)/shard_map/ppermute | solution.py:141
  24.7 31.8 %collective-permute-start.6 = (bf16[784,768]{1,0:T(8,128)(2,1)}, bf16[784,768]{1,0:T(8,128)(2,1)}, u32[]{:S(2)}, u32[]{:S(2)}) collective-permute-start(bf16[784,768]{1,0:T(8,128)(2,1)} %get-tuple-element.125.refs_0_), channel_id=1, source_target_pairs={{0,1},{1,0},{2,3},{3,2},{4,5},{5,4},{6,7},{7,6},{8,9},{9,8},{10,11... | collective-permute-start | bytes 3612680 | tf_op jit(solution)/shard_map/ppermute | solution.py:141
  26.0 55.2 %collective-permute-start.13 = (bf16[800,768]{1,0:T(8,128)(2,1)S(1)}, bf16[800,768]{1,0:T(8,128)(2,1)S(1)}, u32[]{:S(2)}, u32[]{:S(2)}) collective-permute-start(bf16[800,768]{1,0:T(8,128)(2,1)S(1)} %get-tuple-element.123.refs_1_), channel_id=1, source_target_pairs={{0,4},{1,5},{2,6},{3,7},{4,0},{5,1},{6,2},{7,3},{8,12},{9,13},{10,... | collective-permute-start | bytes 3686408 | tf_op jit(solution)/shard_map/ppermute | solution.py:141
  30.0 910.7 %all-gather.17.cloned.1.call-start = ((), (), s32[]{:S(2)}) async-start(), calls=%async_computation.15 | async-start | bytes 1216512 | tf_op jit(solution)/shard_map/all_gather | solution.py:594
  55.7 27.6 %collective-permute-start.9 = (bf16[800,768]{1,0:T(8,128)(2,1)S(1)}, bf16[800,768]{1,0:T(8,128)(2,1)S(1)}, u32[]{:S(2)}, u32[]{:S(2)}) collective-permute-start(bf16[800,768]{1,0:T(8,128)(2,1)S(1)} %get-tuple-element.123.refs_1_), channel_id=1, source_target_pairs={{0,2},{1,3},{2,0},{3,1},{4,6},{5,7},{6,4},{7,5},{8,10},{9,11},{10,... | collective-permute-start | bytes 3686408 | tf_op jit(solution)/shard_map/ppermute | solution.py:141
  56.0 27.4 %collective-permute-start.7 = (bf16[800,768]{1,0:T(8,128)(2,1)S(1)}, bf16[800,768]{1,0:T(8,128)(2,1)S(1)}, u32[]{:S(2)}, u32[]{:S(2)}) collective-permute-start(bf16[800,768]{1,0:T(8,128)(2,1)S(1)} %get-tuple-element.123.refs_1_), channel_id=1, source_target_pairs={{0,1},{1,0},{2,3},{3,2},{4,5},{5,4},{6,7},{7,6},{8,9},{9,8},{10,11... | collective-permute-start | bytes 3686408 | tf_op jit(solution)/shard_map/ppermute | solution.py:141
  56.1 27.9 %collective-permute-start.14 = (bf16[784,768]{1,0:T(8,128)(2,1)}, bf16[784,768]{1,0:T(8,128)(2,1)}, u32[]{:S(2)}, u32[]{:S(2)}) collective-permute-start(bf16[784,768]{1,0:T(8,128)(2,1)} %collective-permute-done.12.refs_8_), channel_id=1, source_target_pairs={{0,1},{1,0},{2,3},{3,2},{4,5},{5,4},{6,7},{7,6},{8,9},{9,8},{10,11... | collective-permute-start | bytes 3612680 | tf_op jit(solution)/shard_map/ppermute | solution.py:141
  56.6 52.1 %collective-permute-start.16 = (bf16[784,768]{1,0:T(8,128)(2,1)}, bf16[784,768]{1,0:T(8,128)(2,1)S(1)}, u32[]{:S(2)}, u32[]{:S(2)}) collective-permute-start(bf16[784,768]{1,0:T(8,128)(2,1)} %collective-permute-done.8.refs_4_), channel_id=1, source_target_pairs={{0,4},{1,5},{2,6},{3,7},{4,0},{5,1},{6,2},{7,3},{8,12},{9,13},{10,... | collective-permute-start | bytes 3612680 | tf_op jit(solution)/shard_map/ppermute | solution.py:141
  81.3 31.7 %collective-permute-start.17 = (bf16[800,768]{1,0:T(8,128)(2,1)S(1)}, bf16[800,768]{1,0:T(8,128)(2,1)S(1)}, u32[]{:S(2)}, u32[]{:S(2)}) collective-permute-start(bf16[800,768]{1,0:T(8,128)(2,1)S(1)} %collective-permute-done.13.refs_9_), channel_id=1, source_target_pairs={{0,2},{1,3},{2,0},{3,1},{4,6},{5,7},{6,4},{7,5},{8,10},{9,11},{10,... | collective-permute-start | bytes 3686408 | tf_op jit(solution)/shard_map/ppermute | solution.py:141
  83.4 32.6 %collective-permute-start.10 = (bf16[784,768]{1,0:T(8,128)(2,1)}, bf16[784,768]{1,0:T(8,128)(2,1)S(1)}, u32[]{:S(2)}, u32[]{:S(2)}) collective-permute-start(bf16[784,768]{1,0:T(8,128)(2,1)} %collective-permute-done.8.refs_4_), channel_id=1, source_target_pairs={{0,1},{1,0},{2,3},{3,2},{4,5},{5,4},{6,7},{7,6},{8,9},{9,8},{10,11... | collective-permute-start | bytes 3612680 | tf_op jit(solution)/shard_map/ppermute | solution.py:141
  83.5 32.5 %collective-permute-start.15 = (bf16[800,768]{1,0:T(8,128)(2,1)S(1)}, bf16[800,768]{1,0:T(8,128)(2,1)S(1)}, u32[]{:S(2)}, u32[]{:S(2)}) collective-permute-start(bf16[800,768]{1,0:T(8,128)(2,1)S(1)} %collective-permute-done.13.refs_9_), channel_id=1, source_target_pairs={{0,1},{1,0},{2,3},{3,2},{4,5},{5,4},{6,7},{7,6},{8,9},{9,8},{10,11... | collective-permute-start | bytes 3686408 | tf_op jit(solution)/shard_map/ppermute | solution.py:141
  84.0 32.0 %collective-permute-start.11 = (bf16[800,768]{1,0:T(8,128)(2,1)S(1)}, bf16[800,768]{1,0:T(8,128)(2,1)S(1)}, u32[]{:S(2)}, u32[]{:S(2)}) collective-permute-start(bf16[800,768]{1,0:T(8,128)(2,1)S(1)} %collective-permute-done.9.refs_5_), channel_id=1, source_target_pairs={{0,1},{1,0},{2,3},{3,2},{4,5},{5,4},{6,7},{7,6},{8,9},{9,8},{10,11... | collective-permute-start | bytes 3686408 | tf_op jit(solution)/shard_map/ppermute | solution.py:141
  160.2 42.6 %collective-permute-start.20 = (f32[3072,128]{1,0:T(8,128)}, f32[3072,128]{1,0:T(8,128)S(1)}, u32[]{:S(2)}, u32[]{:S(2)}) collective-permute-start(f32[3072,128]{1,0:T(8,128)} %get-tuple-element.119), channel_id=1, source_target_pairs={{0,8},{2,10},{4,12},{6,14},{1,9},{3,11},{5,13},{7,15}} | collective-permute-start | bytes 4718600 | tf_op jit(solution)/shard_map/ppermute | solution.py:151
  163.6 39.2 %collective-permute-start.23 = (f32[3072,128]{1,0:T(8,128)S(1)}, f32[3072,128]{1,0:T(8,128)}, u32[]{:S(2)}, u32[]{:S(2)}) collective-permute-start(f32[3072,128]{1,0:T(8,128)S(1)} %get-tuple-element.120), channel_id=1, source_target_pairs={{24,16},{26,18},{28,20},{30,22},{25,17},{27,19},{29,21},{31,23}} | collective-permute-start | bytes 4718600 | tf_op jit(solution)/shard_map/ppermute | solution.py:151
  206.6 56.0 %collective-permute-start.21 = (f32[3072,128]{1,0:T(8,128)}, f32[3072,128]{1,0:T(8,128)S(1)}, u32[]{:S(2)}, u32[]{:S(2)}) collective-permute-start(f32[3072,128]{1,0:T(8,128)} %get-tuple-element.117), channel_id=1, source_target_pairs={{0,8},{2,10},{4,12},{6,14},{8,16},{10,18},{12,20},{14,22},{1,9},{3... | collective-permute-start | bytes 4718600 | tf_op jit(solution)/shard_map/ppermute | solution.py:151
  211.1 51.4 %collective-permute-start.24 = (f32[3072,128]{1,0:T(8,128)}, f32[3072,128]{1,0:T(8,128)}, u32[]{:S(2)}, u32[]{:S(2)}) collective-permute-start(f32[3072,128]{1,0:T(8,128)} %get-tuple-element.118), channel_id=1, source_target_pairs={{16,8},{18,10},{20,12},{22,14},{24,16},{26,18},{28,20},{30,22},{17... | collective-permute-start | bytes 4718600 | tf_op jit(solution)/shard_map/ppermute | solution.py:151
  266.9 52.0 %collective-permute-start.22 = (f32[3072,128]{1,0:T(8,128)}, f32[3072,128]{1,0:T(8,128)}, u32[]{:S(2)}, u32[]{:S(2)}) collective-permute-start(f32[3072,128]{1,0:T(8,128)} %get-tuple-element.115), channel_id=1, source_target_pairs={{0,8},{2,10},{4,12},{6,14},{8,16},{10,18},{12,20},{14,22},{16,24},... | collective-permute-start | bytes 4718600 | tf_op jit(solution)/shard_map/ppermute | solution.py:151
  278.0 53.1 %collective-permute-start.25 = (f32[3072,128]{1,0:T(8,128)}, f32[3072,128]{1,0:T(8,128)}, u32[]{:S(2)}, u32[]{:S(2)}) collective-permute-start(f32[3072,128]{1,0:T(8,128)} %get-tuple-element.116), channel_id=1, source_target_pairs={{8,0},{10,2},{12,4},{14,6},{16,8},{18,10},{20,12},{22,14},{24,16},... | collective-permute-start | bytes 4718600 | tf_op jit(solution)/shard_map/ppermute | solution.py:151
  365.7 24.0 %collective-permute-start.26 = (bf16[512,12,64]{0,2,1:T(8,128)(2,1)S(1)}, bf16[512,12,64]{0,2,1:T(8,128)(2,1)S(1)}, u32[]{:S(2)}, u32[]{:S(2)}) collective-permute-start(bf16[512,12,64]{0,2,1:T(8,128)(2,1)S(1)} %fusion.28), channel_id=1, source_target_pairs={{0,1},{1,0},{2,3},{3,2},{4,5},{5,4},{6,7},{7,6},{8,9},{9,8},{10,11... | collective-permute-start | bytes 2359304 | tf_op jit(solution)/shard_map/ppermute | solution.py:141
  580.0 21.9 %collective-permute-start.37 = (bf16[512,12,64]{0,2,1:T(8,128)(2,1)}, bf16[512,12,64]{0,2,1:T(8,128)(2,1)}, u32[]{:S(2)}, u32[]{:S(2)}) collective-permute-start(bf16[512,12,64]{0,2,1:T(8,128)(2,1)} %slice.348), channel_id=1, source_target_pairs={{0,1},{1,0},{2,3},{3,2},{4,5},{5,4},{6,7},{7,6},{8,9},{9,8},{10,11... | collective-permute-start | bytes 2359304 | tf_op jit(solution)/shard_map/ppermute | solution.py:141
  613.8 336.6 %reduce-scatter.7.cloned.1.call-start = ((), (), s32[]{:S(2)}) async-start(), calls=%async_computation.12 | async-start | bytes 2433024 | tf_op jit(solution)/shard_map/reduce_scatter | solution.py:525
  617.3 379.5 %reduce-scatter.5.cloned.1.call-start = ((), (), s32[]{:S(2)}) async-start(), calls=%async_computation.11 | async-start | bytes 7299072 | tf_op jit(solution)/shard_map/reduce_scatter | solution.py:525
  627.2 502.2 %reduce-scatter.9.cloned.1.call-start = ((), (), s32[]{:S(2)}) async-start(), calls=%async_computation.13 | async-start | bytes 9732096 | tf_op jit(solution)/shard_map/reduce_scatter | solution.py:525
  635.1 635.6 %reduce-scatter.11.cloned.1.call-start = ((), (), s32[]{:S(2)}) async-start(), calls=%async_computation.14 | async-start | bytes 9732096 | tf_op jit(solution)/shard_map/reduce_scatter | solution.py:525
  662.6 29.3 %collective-permute-start.82 = (bf16[256,768]{1,0:T(8,128)(2,1)}, bf16[256,768]{1,0:T(8,128)(2,1)S(1)}, u32[]{:S(2)}, u32[]{:S(2)}) collective-permute-start(bf16[256,768]{1,0:T(8,128)(2,1)} %pad_maximum_fusion.10), channel_id=1, source_target_pairs={{0,6},{1,7},{2,4},{3,5},{4,2},{5,3},{6,0},{7,1},{8,14},{9,15},{10,... | collective-permute-start | bytes 1179656 | tf_op jit(solution)/shard_map/ppermute | solution.py:141
  666.2 25.7 %collective-permute-start.81 = (bf16[256,768]{1,0:T(8,128)(2,1)}, bf16[256,768]{1,0:T(8,128)(2,1)}, u32[]{:S(2)}, u32[]{:S(2)}) collective-permute-start(bf16[256,768]{1,0:T(8,128)(2,1)} %pad_maximum_fusion.10), channel_id=1, source_target_pairs={{0,5},{1,4},{2,7},{3,6},{4,1},{5,0},{6,3},{7,2},{8,13},{9,12},{10,... | collective-permute-start | bytes 1179656 | tf_op jit(solution)/shard_map/ppermute | solution.py:141
  666.2 26.5 %collective-permute-start.80 = (bf16[256,768]{1,0:T(8,128)(2,1)}, bf16[256,768]{1,0:T(8,128)(2,1)}, u32[]{:S(2)}, u32[]{:S(2)}) collective-permute-start(bf16[256,768]{1,0:T(8,128)(2,1)} %pad_maximum_fusion.10), channel_id=1, source_target_pairs={{0,4},{1,5},{2,6},{3,7},{4,0},{5,1},{6,2},{7,3},{8,12},{9,13},{10,... | collective-permute-start | bytes 1179656 | tf_op jit(solution)/shard_map/ppermute | solution.py:141
  667.6 26.2 %collective-permute-start.79 = (bf16[256,768]{1,0:T(8,128)(2,1)}, bf16[256,768]{1,0:T(8,128)(2,1)}, u32[]{:S(2)}, u32[]{:S(2)}) collective-permute-start(bf16[256,768]{1,0:T(8,128)(2,1)} %pad_maximum_fusion.10), channel_id=1, source_target_pairs={{0,3},{1,2},{2,1},{3,0},{4,7},{5,6},{6,5},{7,4},{8,11},{9,10},{10,... | collective-permute-start | bytes 1179656 | tf_op jit(solution)/shard_map/ppermute | solution.py:141
  667.6 26.6 %collective-permute-start.78 = (bf16[256,768]{1,0:T(8,128)(2,1)}, bf16[256,768]{1,0:T(8,128)(2,1)}, u32[]{:S(2)}, u32[]{:S(2)}) collective-permute-start(bf16[256,768]{1,0:T(8,128)(2,1)} %pad_maximum_fusion.10), channel_id=1, source_target_pairs={{0,2},{1,3},{2,0},{3,1},{4,6},{5,7},{6,4},{7,5},{8,10},{9,11},{10,... | collective-permute-start | bytes 1179656 | tf_op jit(solution)/shard_map/ppermute | solution.py:141
  691.9 51.7 %collective-permute-start.70 = (bf16[256,1584]{0,1:T(8,128)(2,1)}, bf16[256,1584]{0,1:T(8,128)(2,1)}, u32[]{:S(2)}, u32[]{:S(2)}) collective-permute-start(bf16[256,1584]{0,1:T(8,128)(2,1)} %copy.185), channel_id=1, source_target_pairs={{0,1},{1,0},{2,3},{3,2},{4,5},{5,4},{6,7},{7,6},{8,9},{9,8},{10,11... | collective-permute-start | bytes 2433032 | tf_op jit(solution)/shard_map/ppermute | solution.py:141
  691.9 51.8 %collective-permute-start.71 = (bf16[256,1584]{0,1:T(8,128)(2,1)}, bf16[256,1584]{0,1:T(8,128)(2,1)}, u32[]{:S(2)}, u32[]{:S(2)}) collective-permute-start(bf16[256,1584]{0,1:T(8,128)(2,1)} %copy.186), channel_id=1, source_target_pairs={{0,2},{1,3},{2,0},{3,1},{4,6},{5,7},{6,4},{7,5},{8,10},{9,11},{10,... | collective-permute-start | bytes 2433032 | tf_op jit(solution)/shard_map/ppermute | solution.py:141
  692.7 53.4 %collective-permute-start.72 = (bf16[256,1584]{0,1:T(8,128)(2,1)}, bf16[256,1584]{0,1:T(8,128)(2,1)}, u32[]{:S(2)}, u32[]{:S(2)}) collective-permute-start(bf16[256,1584]{0,1:T(8,128)(2,1)} %copy.187), channel_id=1, source_target_pairs={{0,3},{1,2},{2,1},{3,0},{4,7},{5,6},{6,5},{7,4},{8,11},{9,10},{10,... | collective-permute-start | bytes 2433032 | tf_op jit(solution)/shard_map/ppermute | solution.py:141
  694.2 47.6 %collective-permute-start.83 = (bf16[256,768]{1,0:T(8,128)(2,1)}, bf16[256,768]{1,0:T(8,128)(2,1)}, u32[]{:S(2)}, u32[]{:S(2)}) collective-permute-start(bf16[256,768]{1,0:T(8,128)(2,1)} %pad_maximum_fusion.10), channel_id=1, source_target_pairs={{0,7},{1,6},{2,5},{3,4},{4,3},{5,2},{6,1},{7,0},{8,15},{9,14},{10,... | collective-permute-start | bytes 1179656 | tf_op jit(solution)/shard_map/ppermute | solution.py:141
  700.5 102.4 %collective-permute-start.73 = (bf16[256,1584]{0,1:T(8,128)(2,1)}, bf16[256,1584]{0,1:T(8,128)(2,1)}, u32[]{:S(2)}, u32[]{:S(2)}) collective-permute-start(bf16[256,1584]{0,1:T(8,128)(2,1)} %copy.188), channel_id=1, source_target_pairs={{0,4},{1,5},{2,6},{3,7},{4,0},{5,1},{6,2},{7,3},{8,12},{9,13},{10,... | collective-permute-start | bytes 2433032 | tf_op jit(solution)/shard_map/ppermute | solution.py:141
  741.9 63.7 %collective-permute-start.74 = (bf16[256,1584]{0,1:T(8,128)(2,1)}, bf16[256,1584]{0,1:T(8,128)(2,1)S(1)}, u32[]{:S(2)}, u32[]{:S(2)}) collective-permute-start(bf16[256,1584]{0,1:T(8,128)(2,1)} %copy.189), channel_id=1, source_target_pairs={{0,5},{1,4},{2,7},{3,6},{4,1},{5,0},{6,3},{7,2},{8,13},{9,12},{10,... | collective-permute-start | bytes 2433032 | tf_op jit(solution)/shard_map/ppermute | solution.py:141
  743.6 63.6 %collective-permute-start.75 = (bf16[256,1584]{0,1:T(8,128)(2,1)}, bf16[256,1584]{0,1:T(8,128)(2,1)S(1)}, u32[]{:S(2)}, u32[]{:S(2)}) collective-permute-start(bf16[256,1584]{0,1:T(8,128)(2,1)} %copy.190), channel_id=1, source_target_pairs={{0,6},{1,7},{2,4},{3,5},{4,2},{5,3},{6,0},{7,1},{8,14},{9,15},{10,... | collective-permute-start | bytes 2433032 | tf_op jit(solution)/shard_map/ppermute | solution.py:141
  743.7 65.0 %collective-permute-start.76 = (bf16[256,1584]{0,1:T(8,128)(2,1)}, bf16[256,1584]{0,1:T(8,128)(2,1)}, u32[]{:S(2)}, u32[]{:S(2)}) collective-permute-start(bf16[256,1584]{0,1:T(8,128)(2,1)} %copy.191), channel_id=1, source_target_pairs={{0,7},{1,6},{2,5},{3,4},{4,3},{5,2},{6,1},{7,0},{8,15},{9,14},{10,... | collective-permute-start | bytes 2433032 | tf_op jit(solution)/shard_map/ppermute | solution.py:141
  746.1 64.0 %collective-permute-start.62 = (bf16[3072,128]{1,0:T(8,128)(2,1)}, bf16[3072,128]{1,0:T(8,128)(2,1)}, u32[]{:S(2)}, u32[]{:S(2)}) collective-permute-start(bf16[3072,128]{1,0:T(8,128)(2,1)} %reshape.2529), channel_id=1, source_target_pairs={{0,8},{1,9},{2,10},{3,11},{4,12},{5,13},{6,14},{7,15},{8,16},{9,17... | collective-permute-start | bytes 2359304 | tf_op jit(solution)/shard_map/ppermute | solution.py:141
  763.1 36.7 %all-to-all-start.1 = ((f32[32,1,256]{2,1,0:T(1,128)}), f32[32,1,256]{2,1,0:T(1,128)S(1)}, u32[]{:S(2)}, u32[]{:S(2)}) async-start(f32[32,1,256]{2,1,0:T(1,128)} %bitcast.70), calls=%async_computation.1 | async-start | bytes 65536 | tf_op jit(solution)/shard_map/all_to_all | solution.py:560
  802.8 39.2 %collective-permute-start.54 = (bf16[3072,128]{1,0:T(8,128)(2,1)}, bf16[3072,128]{1,0:T(8,128)(2,1)}, u32[]{:S(2)}, u32[]{:S(2)}) collective-permute-start(bf16[3072,128]{1,0:T(8,128)(2,1)} %reshape.2529), channel_id=1, source_target_pairs={{0,16},{1,17},{2,18},{3,19},{4,20},{5,21},{6,22},{7,23},{8,24},{9,... | collective-permute-start | bytes 2359304 | tf_op jit(solution)/shard_map/ppermute | solution.py:141
  805.6 38.0 %collective-permute-start.46 = (bf16[3072,128]{1,0:T(8,128)(2,1)}, bf16[3072,128]{1,0:T(8,128)(2,1)}, u32[]{:S(2)}, u32[]{:S(2)}) collective-permute-start(bf16[3072,128]{1,0:T(8,128)(2,1)} %reshape.2529), channel_id=1, source_target_pairs={{0,24},{1,25},{2,26},{3,27},{4,28},{5,29},{6,30},{7,31},{8,0},{9,1... | collective-permute-start | bytes 2359304 | tf_op jit(solution)/shard_map/ppermute | solution.py:141
  807.2 37.9 %collective-permute-start.42 = (bf16[1,3072,128]{2,1,0:T(8,128)(2,1)S(1)}, bf16[1,3072,128]{2,1,0:T(8,128)(2,1)}, u32[]{:S(2)}, u32[]{:S(2)}) collective-permute-start(bf16[1,3072,128]{2,1,0:T(8,128)(2,1)S(1)} %stack_reshape.16.refs_0_), channel_id=1, source_target_pairs={{0,4},{1,5},{2,6},{3,7},{4,0},{5,1},{6,2},{7,3},{8,12},{9,13},{10,... | collective-permute-start | bytes 2359304 | tf_op jit(solution)/shard_map/ppermute | solution.py:141
  808.7 36.4 %collective-permute-start.40 = (bf16[1,3072,128]{2,1,0:T(8,128)(2,1)S(1)}, bf16[1,3072,128]{2,1,0:T(8,128)(2,1)}, u32[]{:S(2)}, u32[]{:S(2)}) collective-permute-start(bf16[1,3072,128]{2,1,0:T(8,128)(2,1)S(1)} %stack_reshape.16.refs_0_), channel_id=1, source_target_pairs={{0,2},{1,3},{2,0},{3,1},{4,6},{5,7},{6,4},{7,5},{8,10},{9,11},{10,... | collective-permute-start | bytes 2359304 | tf_op jit(solution)/shard_map/ppermute | solution.py:141
  810.2 35.6 %collective-permute-start.39 = (bf16[1,3072,128]{2,1,0:T(8,128)(2,1)S(1)}, bf16[1,3072,128]{2,1,0:T(8,128)(2,1)}, u32[]{:S(2)}, u32[]{:S(2)}) collective-permute-start(bf16[1,3072,128]{2,1,0:T(8,128)(2,1)S(1)} %stack_reshape.16.refs_0_), channel_id=1, source_target_pairs={{0,1},{1,0},{2,3},{3,2},{4,5},{5,4},{6,7},{7,6},{8,9},{9,8},{10,11... | collective-permute-start | bytes 2359304 | tf_op jit(solution)/shard_map/ppermute | solution.py:141
  842.1 20.8 %collective-permute-start.66 = (bf16[1,3072,128]{2,1,0:T(8,128)(2,1)}, bf16[1,3072,128]{2,1,0:T(8,128)(2,1)}, u32[]{:S(2)}, u32[]{:S(2)}) collective-permute-start(bf16[1,3072,128]{2,1,0:T(8,128)(2,1)} %bitcast.125.refs_24_), channel_id=1, source_target_pairs={{0,4},{1,5},{2,6},{3,7},{4,0},{5,1},{6,2},{7,3},{8,12},{9,13},{10,... | collective-permute-start | bytes 2359304 | tf_op jit(solution)/shard_map/ppermute | solution.py:141
  843.6 20.8 %collective-permute-start.64 = (bf16[1,3072,128]{2,1,0:T(8,128)(2,1)}, bf16[1,3072,128]{2,1,0:T(8,128)(2,1)}, u32[]{:S(2)}, u32[]{:S(2)}) collective-permute-start(bf16[1,3072,128]{2,1,0:T(8,128)(2,1)} %bitcast.125.refs_24_), channel_id=1, source_target_pairs={{0,2},{1,3},{2,0},{3,1},{4,6},{5,7},{6,4},{7,5},{8,10},{9,11},{10,... | collective-permute-start | bytes 2359304 | tf_op jit(solution)/shard_map/ppermute | solution.py:141
  845.1 34.6 %collective-permute-start.58 = (bf16[1,3072,128]{2,1,0:T(8,128)(2,1)}, bf16[1,3072,128]{2,1,0:T(8,128)(2,1)}, u32[]{:S(2)}, u32[]{:S(2)}) collective-permute-start(bf16[1,3072,128]{2,1,0:T(8,128)(2,1)} %bitcast.124.refs_16_), channel_id=1, source_target_pairs={{0,4},{1,5},{2,6},{3,7},{4,0},{5,1},{6,2},{7,3},{8,12},{9,13},{10,... | collective-permute-start | bytes 2359304 | tf_op jit(solution)/shard_map/ppermute | solution.py:141
  845.7 35.5 %collective-permute-start.56 = (bf16[1,3072,128]{2,1,0:T(8,128)(2,1)}, bf16[1,3072,128]{2,1,0:T(8,128)(2,1)}, u32[]{:S(2)}, u32[]{:S(2)}) collective-permute-start(bf16[1,3072,128]{2,1,0:T(8,128)(2,1)} %bitcast.124.refs_16_), channel_id=1, source_target_pairs={{0,2},{1,3},{2,0},{3,1},{4,6},{5,7},{6,4},{7,5},{8,10},{9,11},{10,... | collective-permute-start | bytes 2359304 | tf_op jit(solution)/shard_map/ppermute | solution.py:141
  862.9 29.3 %collective-permute-start.55 = (bf16[1,3072,128]{2,1,0:T(8,128)(2,1)}, bf16[1,3072,128]{2,1,0:T(8,128)(2,1)}, u32[]{:S(2)}, u32[]{:S(2)}) collective-permute-start(bf16[1,3072,128]{2,1,0:T(8,128)(2,1)} %bitcast.124.refs_16_), channel_id=1, source_target_pairs={{0,1},{1,0},{2,3},{3,2},{4,5},{5,4},{6,7},{7,6},{8,9},{9,8},{10,11... | collective-permute-start | bytes 2359304 | tf_op jit(solution)/shard_map/ppermute | solution.py:141
  864.4 30.5 %collective-permute-start.50 = (bf16[1,3072,128]{2,1,0:T(8,128)(2,1)}, bf16[1,3072,128]{2,1,0:T(8,128)(2,1)}, u32[]{:S(2)}, u32[]{:S(2)}) collective-permute-start(bf16[1,3072,128]{2,1,0:T(8,128)(2,1)} %bitcast.123.refs_8_), channel_id=1, source_target_pairs={{0,4},{1,5},{2,6},{3,7},{4,0},{5,1},{6,2},{7,3},{8,12},{9,13},{10,... | collective-permute-start | bytes 2359304 | tf_op jit(solution)/shard_map/ppermute | solution.py:141
  864.9 31.4 %collective-permute-start.48 = (bf16[1,3072,128]{2,1,0:T(8,128)(2,1)}, bf16[1,3072,128]{2,1,0:T(8,128)(2,1)}, u32[]{:S(2)}, u32[]{:S(2)}) collective-permute-start(bf16[1,3072,128]{2,1,0:T(8,128)(2,1)} %bitcast.123.refs_8_), channel_id=1, source_target_pairs={{0,2},{1,3},{2,0},{3,1},{4,6},{5,7},{6,4},{7,5},{8,10},{9,11},{10,... | collective-permute-start | bytes 2359304 | tf_op jit(solution)/shard_map/ppermute | solution.py:141
  892.2 29.4 %collective-permute-start.44 = (bf16[1,3072,128]{2,1,0:T(8,128)(2,1)}, bf16[1,3072,128]{2,1,0:T(8,128)(2,1)}, u32[]{:S(2)}, u32[]{:S(2)}) collective-permute-start(bf16[1,3072,128]{2,1,0:T(8,128)(2,1)} %collective-permute-done.40.refs_2_), channel_id=1, source_target_pairs={{0,4},{1,5},{2,6},{3,7},{4,0},{5,1},{6,2},{7,3},{8,12},{9,13},{10,... | collective-permute-start | bytes 2359304 | tf_op jit(solution)/shard_map/ppermute | solution.py:141
  894.9 28.5 %collective-permute-start.41 = (bf16[1,3072,128]{2,1,0:T(8,128)(2,1)}, bf16[1,3072,128]{2,1,0:T(8,128)(2,1)}, u32[]{:S(2)}, u32[]{:S(2)}) collective-permute-start(bf16[1,3072,128]{2,1,0:T(8,128)(2,1)} %collective-permute-done.40.refs_2_), channel_id=1, source_target_pairs={{0,1},{1,0},{2,3},{3,2},{4,5},{5,4},{6,7},{7,6},{8,9},{9,8},{10,11... | collective-permute-start | bytes 2359304 | tf_op jit(solution)/shard_map/ppermute | solution.py:141
  896.3 31.5 %collective-permute-start.68 = (bf16[1,3072,128]{2,1,0:T(8,128)(2,1)}, bf16[1,3072,128]{2,1,0:T(8,128)(2,1)}, u32[]{:S(2)}, u32[]{:S(2)}) collective-permute-start(bf16[1,3072,128]{2,1,0:T(8,128)(2,1)} %collective-permute-done.66.refs_28_), channel_id=1, source_target_pairs={{0,2},{1,3},{2,0},{3,1},{4,6},{5,7},{6,4},{7,5},{8,10},{9,11},{10,... | collective-permute-start | bytes 2359304 | tf_op jit(solution)/shard_map/ppermute | solution.py:141
  897.7 31.8 %collective-permute-start.67 = (bf16[1,3072,128]{2,1,0:T(8,128)(2,1)}, bf16[1,3072,128]{2,1,0:T(8,128)(2,1)}, u32[]{:S(2)}, u32[]{:S(2)}) collective-permute-start(bf16[1,3072,128]{2,1,0:T(8,128)(2,1)} %collective-permute-done.66.refs_28_), channel_id=1, source_target_pairs={{0,1},{1,0},{2,3},{3,2},{4,5},{5,4},{6,7},{7,6},{8,9},{9,8},{10,11... | collective-permute-start | bytes 2359304 | tf_op jit(solution)/shard_map/ppermute | solution.py:141
  897.7 31.8 %collective-permute-start.65 = (bf16[1,3072,128]{2,1,0:T(8,128)(2,1)}, bf16[1,3072,128]{2,1,0:T(8,128)(2,1)}, u32[]{:S(2)}, u32[]{:S(2)}) collective-permute-start(bf16[1,3072,128]{2,1,0:T(8,128)(2,1)} %collective-permute-done.64.refs_26_), channel_id=1, source_target_pairs={{0,1},{1,0},{2,3},{3,2},{4,5},{5,4},{6,7},{7,6},{8,9},{9,8},{10,11... | collective-permute-start | bytes 2359304 | tf_op jit(solution)/shard_map/ppermute | solution.py:141
  921.5 25.0 %collective-permute-start.60 = (bf16[1,3072,128]{2,1,0:T(8,128)(2,1)}, bf16[1,3072,128]{2,1,0:T(8,128)(2,1)}, u32[]{:S(2)}, u32[]{:S(2)}) collective-permute-start(bf16[1,3072,128]{2,1,0:T(8,128)(2,1)} %collective-permute-done.56.refs_18_), channel_id=1, source_target_pairs={{0,4},{1,5},{2,6},{3,7},{4,0},{5,1},{6,2},{7,3},{8,12},{9,13},{10,... | collective-permute-start | bytes 2359304 | tf_op jit(solution)/shard_map/ppermute | solution.py:141
  923.3 23.7 %collective-permute-start.57 = (bf16[1,3072,128]{2,1,0:T(8,128)(2,1)}, bf16[1,3072,128]{2,1,0:T(8,128)(2,1)}, u32[]{:S(2)}, u32[]{:S(2)}) collective-permute-start(bf16[1,3072,128]{2,1,0:T(8,128)(2,1)} %collective-permute-done.56.refs_18_), channel_id=1, source_target_pairs={{0,1},{1,0},{2,3},{3,2},{4,5},{5,4},{6,7},{7,6},{8,9},{9,8},{10,11... | collective-permute-start | bytes 2359304 | tf_op jit(solution)/shard_map/ppermute | solution.py:141
  (208 other events, 7732.7 us)
Sparse Core Ops, SparseCore 0:
  11.5 61.2 all-gather.6
  76.3 61.2 all-gather.8
  141.1 53.4 all-gather.10
  197.9 71.9 all-gather.12
  273.2 66.6 all-gather.14
  614.0 54.3 all-gather.16
  673.7 152.4 reduce-scatter.6
  832.7 155.7 reduce-scatter.4
  994.4 134.9 reduce-scatter.8
  1136.1 134.5 reduce-scatter.10

commit v2 on v1

--- a/solution.py
+++ b/solution.py
@@ -77,14 +77,6 @@
     return (jnp.cos(angle), jnp.sin(angle))
 
 
-def rotate(t, cosv, sinv):
-    half = t.shape[-1] // 2
-    first, second = (t[..., :half], t[..., half:])
-    c = cosv[:, None, :]
-    s = sinv[:, None, :]
-    return jnp.concatenate([first * c - second * s, first * s + second * c], -1)
-
-
 def time_features(steps, width):
     tau = (steps.astype(f32) + 1.0) / TSTEPS
     half = width // 2
@@ -93,35 +85,172 @@
     return jnp.concatenate([jnp.cos(angle), jnp.sin(angle)], -1)
 
 
-def masked_scores(query, keyed, valid):
-    scores = jnp.einsum("qhd,khd->hqk", query, keyed, preferred_element_type=f32) * query.shape[
-        -1
-    ] ** (-0.5)
-    return jnp.where(valid[None, None, :], scores, -1e30)
-
-
-def attend(query, keyed, valued, valid):
-    scores = masked_scores(query, keyed, valid)
-    top = jnp.max(scores, -1, keepdims=True)
-    expo = jnp.exp(scores - top)
-    total = jnp.sum(expo, -1, keepdims=True)
-    probs = (expo / total).astype(bf16)
-    mixed = jnp.einsum("hqk,khd->qhd", probs, valued, preferred_element_type=f32)
-    return (mixed, top[..., 0] + jnp.log(total[..., 0]))
-
-
-def attend_back(query, keyed, valued, valid, lse, grad_mix):
-    scale = query.shape[-1] ** (-0.5)
-    probs = jnp.exp(masked_scores(query, keyed, valid) - lse[..., None])
-    grad_p = jnp.einsum("qhd,khd->hqk", grad_mix, valued, preferred_element_type=f32)
-    delta = jnp.sum(grad_p * probs, -1, keepdims=True)
-    grad_s = (probs * (grad_p - delta)).astype(bf16)
-    grad_q = jnp.einsum("hqk,khd->qhd", grad_s, keyed, preferred_element_type=f32) * scale
-    grad_k = jnp.einsum("hqk,qhd->khd", grad_s, query, preferred_element_type=f32) * scale
-    grad_v = jnp.einsum("hqk,qhd->khd", probs.astype(bf16), grad_mix, preferred_element_type=f32)
-    return (grad_q, grad_k, grad_v)
-
-
+def turn(x, cosv, sinv):
+    lane = lax.broadcasted_iota(jnp.int32, x.shape, 1)
+    quarter = HD // 2
+    swapped = jnp.where(
+        lane % HD < quarter,
+        pltpu.roll(x, LANES - quarter, axis=1),
+        pltpu.roll(x, quarter, axis=1),
+    )
+    return x * cosv + swapped * sinv
+
+
+def turn_kernel(q_ref, k_ref, v_ref, cos_ref, sin_ref, q_out, k_out, v_out):
+    cosv, sinv = cos_ref[...], sin_ref[...]
+    for start in range(0, q_ref.shape[1], LANES):
+        at = slice(start, start + LANES)
+        q_out[:, at] = turn(q_ref[:, at], cosv, sinv).astype(bf16)
+        k_out[:, at] = turn(k_ref[:, at], cosv, sinv).astype(bf16)
+    v_out[...] = v_ref[...].astype(bf16)
+
+
+def turn_rows(qkv, cosv, sinv):
+    rows, width = qkv.shape[0], qkv.shape[1] // 3
+    wide = 3 * LANES if width % (3 * LANES) == 0 else LANES
+    blocks = width // wide
+    block = lambda shift: pl.BlockSpec((rows, wide), lambda i: (0, i + shift))
+    whole = pl.BlockSpec((rows, LANES), lambda i: (0, 0))
+    return pl.pallas_call(
+        turn_kernel,
+        grid=(blocks,),
+        in_specs=[block(0), block(blocks), block(2 * blocks), whole, whole],
+        out_specs=[block(0)] * 3,
+        out_shape=[jax.ShapeDtypeStruct((rows, width), bf16)] * 3,
+        cost_estimate=pl.CostEstimate(
+            flops=rows * width * 12, bytes_accessed=rows * width * 18, transcendentals=0
+        ),
+    )(qkv, qkv, qkv, cosv, sinv)
+
+
+def key_masks(len_ref, core_ref, keys):
+    place = lax.broadcasted_iota(jnp.int32, (1, keys), 1)
+    own = place + core_ref[0] * keys
+    far = place + (1 - core_ref[0]) * keys
+    return [jnp.where(at < len_ref[0], 0.0, -1e30).astype(f32) for at in (own, far)]
+
+
+def attend_kernel(len_ref, core_ref, q_ref, k_ref, kf_ref, v_ref, vf_ref, *refs, tile):
+    out_ref, lse_ref = refs[-2:]
+    rows = q_ref.shape[0]
+    masks = key_masks(len_ref, core_ref, rows)
+    keyed = (k_ref[...], kf_ref[...])
+    valued = (v_ref[...], vf_ref[...])
+    lane = lax.broadcasted_iota(jnp.int32, (tile, LANES), 1)
+    for t in range(rows // tile):
+        at = pl.ds(t * tile, tile)
+        query = q_ref[at, :] * bf16(HD**-0.5)
+        mixed, lses = [], []
+        for head in range(LANES // HD):
+            mine = jnp.where(lane // HD == head, query, bf16(0))
+            scores = [dense_nt(mine, k) + mask for k, mask in zip(keyed, masks)]
+            top = jnp.maximum(*[jnp.max(s, 1, keepdims=True) for s in scores])
+            expo = [jnp.exp(s - top) for s in scores]
+            total = sum(jnp.sum(e, 1, keepdims=True) for e in expo)
+            inverse = 1.0 / total
+            mixed.append(sum(dense((e * inverse).astype(bf16), v) for e, v in zip(expo, valued)))
+            lses.append(top + jnp.log(total))
+        out_ref[at, :] = jnp.where(lane < HD, mixed[0], mixed[1]).astype(bf16)
+        lse_ref[at, :] = jnp.where(lane < HD, lses[0], lses[1])
+
+
+def attend(length, core, query, keyed, keyed_far, valued, valued_far, ready=()):
+    rows, width = query.shape
+    smem = pl.BlockSpec(memory_space=pltpu.SMEM)
+    block = pl.BlockSpec((rows, LANES), lambda i: (0, i))
+    return pl.pallas_call(
+        functools.partial(attend_kernel, tile=256),
+        grid=(width // LANES,),
+        in_specs=[smem, smem] + [block] * 5 + [pl.BlockSpec(memory_space=pl.ANY)] * len(ready),
+        out_specs=[block, block],
+        out_shape=[
+            jax.ShapeDtypeStruct((rows, width), bf16),
+            jax.ShapeDtypeStruct((rows, width), f32),
+        ],
+        compiler_params=pltpu.CompilerParams(vmem_limit_bytes=48 * 2**20),
+        cost_estimate=pl.CostEstimate(
+            flops=8 * rows * rows * width, bytes_accessed=rows * width * 18,
+            transcendentals=2 * rows * rows * width // HD,
+        ),
+    )(length, core, query, keyed, keyed_far, valued, valued_far, *ready)
+
+
+def attend_back_kernel(
+    len_ref,
+    core_ref,
+    q_ref,
+    k_ref,
+    kf_ref,
+    v_ref,
+    vf_ref,
+    lse_ref,
+    do_ref,
+    cos_ref,
+    sin_ref,
+    cos_far_ref,
+    sin_far_ref,
+    *refs,
+    tile,
+):
+    dq_ref, dk_ref, dkf_ref, dv_ref, dvf_ref = refs[-5:]
+    rows = q_ref.shape[0]
+    masks = key_masks(len_ref, core_ref, rows)
+    keyed = (k_ref[...], kf_ref[...])
+    valued = (v_ref[...], vf_ref[...])
+    lane = lax.broadcasted_iota(jnp.int32, (tile, LANES), 1)
+    first = lax.broadcasted_iota(jnp.int32, (rows, LANES), 1) < HD
+    dk, dv = [None, None], [None, None]
+    for t in range(rows // tile):
+        at = pl.ds(t * tile, tile)
+        query = q_ref[at, :] * bf16(HD**-0.5)
+        grad = do_ref[at, :]
+        dqs, dks, dvs = [], [[], []], [[], []]
+        for head in range(LANES // HD):
+            mine = lane // HD == head
+            q_mine = jnp.where(mine, query, bf16(0))
+            g_mine = jnp.where(mine, grad, bf16(0))
+            lse = lse_ref[at, head * HD : head * HD + 1]
+            probs = [jnp.exp(dense_nt(q_mine, k) + mask - lse) for k, mask in zip(keyed, masks)]
+            grad_p = [dense_nt(g_mine, v) for v in valued]
+            delta = sum(jnp.sum(p * g, 1, keepdims=True) for p, g in zip(probs, grad_p))
+            grad_s = [(p * (g - delta)).astype(bf16) for p, g in zip(probs, grad_p)]
+            dqs.append(sum(dense(s, k) for s, k in zip(grad_s, keyed)))
+            for side in range(2):
+                dks[side].append(dense_tn(grad_s[side], query))
+                dvs[side].append(dense_tn(probs[side].astype(bf16), grad))
+        turned = turn(jnp.where(lane < HD, dqs[0], dqs[1]), cos_ref[at, :], -sin_ref[at, :])
+        dq_ref[at, :] = (turned * HD**-0.5).astype(bf16)
+        for side in range(2):
+            part_k = jnp.where(first, *dks[side])
+            part_v = jnp.where(first, *dvs[side])
+            dk[side] = part_k if t == 0 else dk[side] + part_k
+            dv[side] = part_v if t == 0 else dv[side] + part_v
+    dk_ref[...] = turn(dk[0], cos_ref[...], -sin_ref[...])
+    dkf_ref[...] = turn(dk[1], cos_far_ref[...], -sin_far_ref[...]).astype(bf16)
+    dv_ref[...] = dv[0]
+    dvf_ref[...] = dv[1].astype(bf16)
+
+
+def attend_back(length, core, *arrays, ready=()):
+    query = arrays[0]
+    rows, width = query.shape
+    smem = pl.BlockSpec(memory_space=pltpu.SMEM)
+    block = pl.BlockSpec((rows, LANES), lambda i: (0, i))
+    return pl.pallas_call(
+        functools.partial(attend_back_kernel, tile=256),
+        grid=(width // LANES,),
+        in_specs=[smem, smem]
+        + [block] * 7
+        + [pl.BlockSpec((rows, LANES), lambda i: (0, 0))] * 4
+        + [pl.BlockSpec(memory_space=pl.ANY)] * len(ready),
+        out_specs=[block] * 5,
+        out_shape=[jax.ShapeDtypeStruct((rows, width), t) for t in (bf16, f32, bf16, f32, bf16)],
+        compiler_params=pltpu.CompilerParams(vmem_limit_bytes=48 * 2**20),
+        cost_estimate=pl.CostEstimate(
+            flops=20 * rows * rows * width, bytes_accessed=rows * width * 32,
+            transcendentals=2 * rows * rows * width // HD,
+        ),
+    )(length, core, *arrays, *ready)
 def adamw(weight, first, second, grad, rate):
     first = 0.9 * first + 0.1 * grad
     second = 0.999 * second + 0.001 * grad * grad
@@ -151,9 +280,62 @@
     return lax.ppermute(x, "dp", pairs)
 
 
+def pick_half(value, index):
+    size = value.shape[1] // 2
+    return lax.dynamic_slice_in_dim(value, index * size, size, axis=1)
+
+
+def chip_product(left, left_far, right):
+    rep_idx = lax.axis_index("rep")
+    far = hop(pick_half(right, 1 - rep_idx), dr=1)
+    return dense_tn(left, pick_half(right, rep_idx)) + dense_tn(left_far, far)
+
+
+def plane_blocks(value):
+    lines = lax.axis_size("dp") // PLANE
+    return value.reshape(lines, 2, 2, value.shape[0] // (lines * PLANE), -1)
+
+
+def split_blocks(blocks, axis, place):
+    bit = (lax.axis_index("dp") >> axis) & 1
+    far = lax.dynamic_index_in_dim(blocks, 1 - bit, place, False).astype(bf16)
+    return lax.dynamic_index_in_dim(blocks, bit, place, False), hop(far, dq=1 << axis)
+
+
+def reduce_line(blocks):
+    lines = blocks.shape[0]
+    line = lax.axis_index("dp") // PLANE
+    total = lax.dynamic_index_in_dim(blocks, line, 0, False)
+    for d in range(1, lines):
+        total = total + hop(
+            lax.dynamic_index_in_dim(blocks, (line + d) % lines, 0, False), dl=d
+        )
+    return total
+
+
+def join_cores(parts):
+    rep_idx = lax.axis_index("rep")
+    mine = lax.dynamic_index_in_dim(parts, rep_idx, 0, False)
+    far = hop(lax.dynamic_index_in_dim(parts, 1 - rep_idx, 0, False), dr=1)
+    return jnp.where(rep_idx == 0, mine, far), jnp.where(rep_idx == 0, far, mine)
+
+
+def add_up(value):
+    lines = lax.axis_size("dp") // PLANE
+    line = lax.axis_index("dp") // PLANE
+    value = value + hop(value, dr=1)
+    far = [hop(value, dq=dq) for dq in range(1, PLANE)]
+    value = (value + far[0]) + (far[1] + far[2])
+    every = jnp.stack([value] + [hop(value, dl=-d) for d in range(1, lines)])
+    every = lax.dynamic_slice_in_dim(
+        jnp.concatenate([every, every], 0), (lines - line) % lines, lines
+    )
+    return jnp.sum(every, 0)
+
+
 def mix_kernel(idx_ref, mix_ref, *refs, groups, cands, counts):
     pieces = refs[: len(counts)]
-    out_ref, tab, stage, sem = refs[len(counts) :]
+    out_ref, tab, stage, sem = refs[-4:]
 
     @pl.when(pl.program_id(0) == 0)
     def _():
@@ -217,20 +399,29 @@
     )(idx, mix, *pieces)
 
 
-def spread_kernel(cnt_ref, row_ref, pos_ref, mix_ref, *refs, groups, arrays):
+def spread_kernel(cnt_ref, row_ref, pos_ref, mix_ref, *refs, groups, arrays, last):
     sources = refs[:arrays]
-    head_ref, out_ref, sq_ref, total, rows32, stage, sem = refs[arrays:]
-    per, length, _ = sources[0].shape
-    n = arrays * per
+    if last:
+        total_in, head_ref, out_ref, sq_ref, total, rows32, stage, sem, total_sem = refs[arrays:]
+    else:
+        total, rows32, stage, sem = refs[arrays:]
+    length = sources[0].shape[1]
+    blocks = [source.at[k] for source in sources for k in range(source.shape[0])]
+    n = len(blocks)
 
     def copy(k):
-        return pltpu.make_async_copy(sources[k // per].at[k % per], stage.at[k % 2], sem.at[k % 2])
+        return pltpu.make_async_copy(blocks[k], stage.at[k % 2], sem.at[k % 2])
 
     copy(0).start()
-
-    @pl.loop(0, total.shape[0] // 64)
-    def _(t):
-        total[pl.ds(pl.multiple_of(t * 64, 64), 64), :] = jnp.zeros((64, LANES), f32)
+    if last:
+        load = pltpu.make_async_copy(total_in, total, total_sem)
+        load.start()
+        load.wait()
+    else:
+
+        @pl.loop(0, total.shape[0] // 64)
+        def _(t):
+            total[pl.ds(pl.multiple_of(t * 64, 64), 64), :] = jnp.zeros((64, LANES), f32)
 
     unroll = 4
     for k in range(n):
@@ -251,6 +442,8 @@
                 term = mix_ref[k, e] * rows32[pl.ds(pos_ref[k, e], 8), :]
                 total[at, :] = total[at, :] + term
 
+    if not last:
+        return
     vocab = out_ref.shape[0]
 
     def finish(at, size, start):
@@ -274,31 +467,48 @@
         sq_ref[0 : vocab % 8, :] += finish(at, vocab % 8, at * 8)
 
 
-def spread_rows(cnt, row, pos, mix, sources, head, vocab):
-    width = head.shape[1]
+def spread_rows(lists, sources, vocab, width, total=None, head=None):
     groups = width // LANES
     length = sources[0].shape[1]
+    total_rows = -(-vocab * 8 // 64) * 64
+    last = total is not None
     smem = pl.BlockSpec(memory_space=pltpu.SMEM)
     vmem = pl.BlockSpec(memory_space=pltpu.VMEM)
-    return pl.pallas_call(
-        functools.partial(spread_kernel, groups=groups, arrays=len(sources)),
-        in_specs=[smem] * 4 + [pl.BlockSpec(memory_space=pl.ANY)] * len(sources) + [vmem],
-        out_specs=[vmem, vmem],
-        out_shape=[
+    hbm = pl.BlockSpec(memory_space=pl.ANY)
+    scratch = [
+        pltpu.VMEM((length + 8, LANES), f32),
+        pltpu.VMEM((2, length, LANES), bf16),
+        pltpu.SemaphoreType.DMA((2,)),
+    ]
+    if last:
+        extra_specs, extra = [hbm, vmem], [total, head]
+        out_specs = [vmem, vmem]
+        out_shape = [
             jax.ShapeDtypeStruct((vocab, width), f32),
             jax.ShapeDtypeStruct((8, LANES), f32),
-        ],
-        scratch_shapes=[
-            pltpu.VMEM((-(-vocab * 8 // 64) * 64, LANES), f32),
-            pltpu.VMEM((length + 8, LANES), f32),
-            pltpu.VMEM((2, length, LANES), bf16),
-            pltpu.SemaphoreType.DMA((2,)),
-        ],
+        ]
+        scratch = [pltpu.VMEM((total_rows, LANES), f32)] + scratch + [pltpu.SemaphoreType.DMA]
+    else:
+        extra_specs, extra = [], []
+        out_specs = vmem
+        out_shape = jax.ShapeDtypeStruct((total_rows, LANES), f32)
+    entries = sum(source.shape[0] for source in sources) * lists[1].shape[1] // 2
+    return pl.pallas_call(
+        functools.partial(
+            spread_kernel,
+            groups=groups,
+            arrays=len(sources),
+            last=last,
+        ),
+        in_specs=[smem] * 4 + [hbm] * len(sources) + extra_specs,
+        out_specs=out_specs,
+        out_shape=out_shape,
+        scratch_shapes=scratch,
         compiler_params=pltpu.CompilerParams(vmem_limit_bytes=60 * 2**20),
         cost_estimate=pl.CostEstimate(
-            flops=2**28, bytes_accessed=40 * 2**20, transcendentals=0
+            flops=entries * 2048, bytes_accessed=entries * 10240, transcendentals=0
         ),
-    )(cnt, row, pos, mix, *sources, head)
+    )(*lists, *sources, *extra)
 
 
 def local(
@@ -357,44 +567,68 @@
     cut = padded // 32 * 16
     upper_rows, lower_rows = table_low[:cut], table_low[cut:]
     first, second = {0: upper_rows}, {0: lower_rows}
-    first[1] = hop(upper_rows, dq=1)
-    second[2] = hop(lower_rows, dq=2)
-    first[2] = hop(upper_rows, dq=2)
-    second[1] = hop(lower_rows, dq=1)
+    for dq in (1, 2):
+        first[dq] = hop(upper_rows, dq=dq)
+        second[dq] = hop(lower_rows, dq=dq)
+
+    owner = noise_owner.reshape(-1)
+    offset = noise_offset.reshape(-1)
+    mixing = jax.nn.softmax(option_scores.reshape(half, cands) / annealed_softness, axis=-1)
+    names = (owner * padded + offset).astype(f32).reshape(-1, LANES)
+    packed = jnp.concatenate([names, mixing.reshape(-1, LANES)], 0)
+    on_line = jnp.stack([packed] + [hop(packed, dl=-d) for d in range(1, lines)])
+    on_line, first, second = lax.optimization_barrier((on_line, first, second))
     first[3] = hop(first[1], dq=2)
     second[3] = hop(second[2], dq=1)
     pieces = []
     for dq in range(PLANE):
         pieces += [first[dq], second[dq]]
         pieces += [hop(first[dq], dr=1), hop(second[dq], dr=1)]
-
-    owner = noise_owner.reshape(-1)
-    offset = noise_offset.reshape(-1)
-    mixing = jax.nn.softmax(option_scores.reshape(half, cands) / annealed_softness, axis=-1)
-    packed_owner = owner.reshape(-1, LANES) * padded + offset.reshape(-1, LANES)
-    packed_mix = mixing.reshape(-1, LANES)
-    line_owner = jnp.stack(
-        [packed_owner] + [hop(packed_owner, dl=-d) for d in range(1, lines)]
-    )
-    line_mix = jnp.stack([packed_mix] + [hop(packed_mix, dl=-d) for d in range(1, lines)])
+    line_owner = on_line[:, : names.shape[0]].astype(jnp.int32)
+    line_mix = on_line[:, names.shape[0] :]
     row_owner = line_owner // padded
     slot_of = (((row_owner // reps) % PLANE) ^ chip) * reps + ((row_owner % reps) ^ rep_idx)
     here = (row_owner // (reps * PLANE)) == line
     row_at = jnp.where(here, slot_of * padded + line_owner % padded, 0) * groups
     mix_here = jnp.where(here, line_mix, 0.0)
-    partial = mix_rows(
-        row_at.reshape(lines, 1, half * cands),
-        mix_here.reshape(lines, 1, half * cands),
-        pieces,
-        cands,
-    )[:, : half * groups]
+    row_at = row_at.reshape(lines, 1, half * cands)
+    mix_here = mix_here.reshape(lines, 1, half * cands)
+    parts = {}
+
+    def mix_some(which):
+        out = mix_rows(
+            jnp.stack([row_at[d] for d in which]),
+            jnp.stack([mix_here[d] for d in which]),
+            pieces,
+            cands,
+        )
+        for k, d in enumerate(which):
+            parts[d] = out[k, : half * groups]
+
+    mix_some((1, lines - 1))
+    mix_some(tuple(range(2, lines - 1)) + (0,))
     ahead = back = None
     for d in range(lines - 1, 0, -1):
-        to_right = partial[d] if ahead is None else partial[d] + ahead
-        to_left = partial[lines - d] if back is None else partial[lines - d] + back
+        to_right = parts[d] if ahead is None else parts[d] + ahead
+        to_left = parts[lines - d] if back is None else parts[lines - d] + back
         ahead = step_line(to_right, 1, d)
         back = step_line(to_left, -1, d)
-    x0 = (partial[0] + ahead + back).reshape(half, width)
+        if d == lines - 1:
+            ahead, back, owner, offset = lax.optimization_barrier((ahead, back, owner, offset))
+
+    cap = max(2, 2 * half * cands // devices)
+    member = (owner[:, None] == jnp.arange(devices, dtype=jnp.int32)[None, :]).astype(jnp.int32)
+    slot = jnp.sum((jnp.cumsum(member, 0) - member) * member, 1)
+    flat_slot = owner * cap + slot
+    entry = offset * half + jnp.arange(half * cands, dtype=jnp.int32) // cands + 1
+    empty = jnp.zeros((devices * cap,), f32)
+    lists = [
+        empty.at[flat_slot].set(value).reshape(devices, cap)
+        for value in (entry.astype(f32), mixing.reshape(-1))
+    ]
+    asked = jnp.concatenate(lists, 1)
+    ahead, back, asked = lax.optimization_barrier((ahead, back, asked))
+    x0 = (parts[0] + ahead + back).reshape(half, width)
 
     def gather(value, axis=0):
         return lax.all_gather(value.astype(bf16), BOTH, axis=axis, tiled=True)
@@ -429,18 +663,17 @@
 
     n1, r1 = normalize(x0)
     h1b = (n1 * gain_f[0] * (1.0 + sc1) + sh1).astype(bf16)
-    shaped = dense(h1b, qkv_w).reshape(half, 3, heads, HD)
-    pos = rep_idx * half + jnp.arange(half, dtype=jnp.int32)
-    far_pos = (1 - rep_idx) * half + jnp.arange(half, dtype=jnp.int32)
-    cosv, sinv = rope_tables(pos, HD)
-    query = rotate(shaped[:, 0], cosv, sinv).astype(bf16)
-    keyed = rotate(shaped[:, 1], cosv, sinv).astype(bf16)
-    valued = shaped[:, 2].astype(bf16)
-    key_all = jnp.concatenate([keyed, hop(keyed, dr=1)], 0)
-    value_all = jnp.concatenate([valued, hop(valued, dr=1)], 0)
-    valid = jnp.concatenate([pos, far_pos]) < length
-    mixed, lse_att = attend(query, key_all, value_all, valid)
-    mixed_b = mixed.astype(bf16).reshape(-1, width)
+    qkv = dense(h1b, qkv_w)
+    places = jnp.arange(half, dtype=jnp.int32)
+    turns = []
+    for core in (rep_idx, 1 - rep_idx):
+        cosv, sinv = rope_tables(core * half + places, HD)
+        turns += [jnp.tile(cosv, (1, 4)), jnp.concatenate([-sinv, sinv] * 2, 1)]
+    query, keyed, valued = turn_rows(qkv, turns[0], turns[1])
+    attended = (query, keyed, hop(keyed, dr=1), valued, hop(valued, dr=1))
+    core = rep_idx.reshape(1)
+    mixed_b, lse_att = attend(length, core, *attended)
+    asked = lax.all_to_all(asked, BOTH, split_axis=0, concat_axis=0, tiled=True)
     attn = dense(mixed_b, out_w)
     x1 = x0 + g1 * attn
     n2, r2 = normalize(x1)
@@ -461,9 +694,9 @@
     )
     coefficient_aggregate = jnp.sum(weight_all)
 
-    def of_line(values):
+    def of_line(values, at_chip, at_core):
         mine = lax.dynamic_slice(
-            values.reshape(lines, PLANE, reps, picks), (0, chip, rep_idx, 0), (lines, 1, 1, picks)
+            values.reshape(lines, PLANE, reps, picks), (0, at_chip, at_core, 0), (lines, 1, 1, picks)
         )
         return from_me(mine.reshape(lines, picks))
 
@@ -475,10 +708,12 @@
             jnp.concatenate([values, values], 0), (lines - line) % lines, lines
         )
 
-    targets = of_line(loss_target).reshape(-1)
-    weight = of_line(weight_all).reshape(-1)
+    targets = of_line(loss_target, chip, rep_idx).reshape(-1)
+    weight = of_line(weight_all, chip, rep_idx).reshape(-1)
     my_pick = lax.dynamic_slice(loss_pick, (dp_idx, rep_idx, 0), (1, 1, picks)).reshape(picks)
     spread = (jnp.arange(half, dtype=jnp.int32)[:, None] == my_pick[None, :]).astype(f32)
+    final, asked = lax.optimization_barrier((final, asked))
+    asked, asked_mix = asked[:, :cap].astype(jnp.int32), asked[:, cap:]
     rows_b = jnp.take(final, my_pick, axis=0).astype(bf16)
     every = jnp.concatenate([rows_b] + [hop(rows_b, dl=-d) for d in range(1, lines)], 0)
     plane_table = jnp.concatenate(pieces, 0)
@@ -513,79 +748,132 @@
     drows = drows_part[0]
     for d in range(1, lines):
         drows = drows + hop(drows_part[d], dl=d)
-    dlogit_mine = []
-    rows_mine = []
-    for slot, (dq, dr) in enumerate(swaps):
-        block = dlogit[:, slot * padded : (slot + 1) * padded]
-        dlogit_mine.append(block if slot == 0 else hop(block, dq=dq, dr=dr))
-        rows_mine.append(every if slot == 0 else hop(every, dq=dq, dr=dr))
-    head_grad = dense_tn(jnp.concatenate(dlogit_mine, 0), jnp.concatenate(rows_mine, 0))
-
-    def scatter(value):
-        return lax.psum_scatter(value, BOTH, scatter_dimension=0, tiled=True)
+    every, lse, drows = lax.optimization_barrier((every, lse, drows))
+    lse_x, lse_y = hop(lse, dq=1), hop(lse, dq=2)
+    every_x, every_y = hop(every, dq=1), hop(every, dq=2)
+    lse_plane = jnp.stack([lse, lse_x, lse_y, hop(lse_x, dq=2)])
+    rows_plane = jnp.stack([every, every_x, every_y, hop(every_x, dq=2)])
+    lse_all = jnp.concatenate([lse_plane, hop(lse_plane, dr=1)], 0).reshape(-1)
+    rows_all = jnp.concatenate([rows_plane, hop(rows_plane, dr=1)], 0).reshape(-1, width)
+    among = [(chip ^ dq, rep_idx ^ dr) for dr in range(reps) for dq in range(PLANE)]
+    targets_all = jnp.concatenate([of_line(loss_target, q, r).reshape(-1) for q, r in among])
+    weight_rows = jnp.concatenate([of_line(weight_all, q, r).reshape(-1) for q, r in among])
 
     grad_final = exact(spread, drows)
     dx2, dfsh, dfsc, dgain_f = modulate_back(grad_final, nf, rf, gain_f[2], fsc)
     dg2 = jnp.sum(dx2 * mlp, 0)
     dmlp = (dx2 * g2).astype(bf16)
-    d_down = scatter(dense_tn(act_b, dmlp))
+    g_down = chip_product(act_b, hop(act_b, dr=1), dmlp)
     dupper = gelu_back(dense_nt(dmlp, down_w))[0].astype(bf16)
-    d_up = scatter(dense_tn(h2b, dupper))
+    g_up = chip_product(h2b, hop(h2b, dr=1), dupper)
     dh2 = dense_nt(dupper, up_w)
     dn2x, dsh2, dsc2, dgain_2 = modulate_back(dh2, n2, r2, gain_f[1], sc2)
     dx1 = dx2 + dn2x
     dg1 = jnp.sum(dx1 * attn, 0)
     dattn = (dx1 * g1).astype(bf16)
-    d_out = scatter(dense_tn(mixed_b, dattn))
-    dmixed = dense_nt(dattn, out_w).astype(bf16).reshape(half, heads, HD)
-    dquery, dkey_all, dvalue_all = attend_back(query, key_all, value_all, valid, lse_att, dmixed)
-    dkey = dkey_all[:half] + hop(dkey_all[half:].astype(bf16), dr=1).astype(f32)
-    dvalue = dvalue_all[:half] + hop(dvalue_all[half:].astype(bf16), dr=1).astype(f32)
-    dqkv = jnp.stack([rotate(dquery, cosv, -sinv), rotate(dkey, cosv, -sinv), dvalue], 1)
-    dqkv = dqkv.reshape(-1, 3 * width).astype(bf16)
+    dattn, g_down, g_up, rows_all, lse_all = lax.optimization_barrier(
+        (dattn, g_down, g_up, rows_all, lse_all)
+    )
+    down_1 = split_blocks(plane_blocks(g_down), 1, 1)
+    up_1 = split_blocks(plane_blocks(g_up), 0, 2)
+    g_out = chip_product(mixed_b, hop(mixed_b, dr=1), dattn)
+    dmixed = dense_nt(dattn, out_w).astype(bf16)
+    dquery, dkey, dkey_far, dvalue, dvalue_far = attend_back(
+        length, core, *attended, lse_att, dmixed, *turns
+    )
+    dquery, dkey, dkey_far, dvalue, dvalue_far, down_1, up_1, g_out = lax.optimization_barrier(
+        (dquery, dkey, dkey_far, dvalue, dvalue_far, down_1, up_1, g_out)
+    )
+    down_2 = split_blocks(down_1[0] + down_1[1].astype(f32), 0, 1)
+    up_2 = split_blocks(up_1[0] + up_1[1].astype(f32), 1, 1)
+    dkey = (dkey + hop(dkey_far, dr=1).astype(f32)).astype(bf16)
+    dvalue = (dvalue + hop(dvalue_far, dr=1).astype(f32)).astype(bf16)
+    dqkv = jnp.concatenate([dquery, dkey, dvalue], 1)
     dh1 = dense_nt(dqkv, qkv_w)
     dn1x, dsh1, dsc1, dgain_1 = modulate_back(dh1, n1, r1, gain_f[0], sc1)
     dx0 = dx1 + dn1x
-    d_qkv = scatter(dense_tn(h1b, dqkv))
-
-    cap = max(2, 2 * half * cands // devices)
-    member = (owner[:, None] == jnp.arange(devices, dtype=jnp.int32)[None, :]).astype(jnp.int32)
-    slot = jnp.sum((jnp.cumsum(member, 0) - member) * member, 1)
-    flat_slot = owner * cap + slot
-    entry = offset * half + jnp.arange(half * cands, dtype=jnp.int32) // cands + 1
-    asked = jnp.zeros((devices * cap,), jnp.int32).at[flat_slot].set(entry)
-    asked_mix = jnp.zeros((devices * cap,), f32).at[flat_slot].set(mixing.reshape(-1))
-
-    def exchange(value):
-        return lax.all_to_all(
-            value.reshape(devices, cap), BOTH, split_axis=0, concat_axis=0, tiled=True
+    g_qkv = chip_product(h1b, hop(h1b, dr=1), dqkv)
+
+
+    dx0_b = dx0.astype(bf16).reshape(1, half * groups, LANES)
+    dx0_b, rows_all, lse_all, down_2, up_2 = lax.optimization_barrier(
+        (dx0_b, rows_all, lse_all, down_2, up_2)
+    )
+    others = lines - 1
+    cut = -(-2 * others // 3)
+    on_line = jnp.concatenate([hop(dx0_b, dl=-d) for d in range(1, lines)], 0)
+    own_x, own_y = hop(dx0_b, dq=1), hop(dx0_b, dq=2)
+    g_last = jnp.concatenate([g_qkv, g_out], 1)
+    last_1 = split_blocks(plane_blocks(g_last), 0, 2)
+    on_line, own_x, own_y, last_1 = lax.optimization_barrier((on_line, own_x, own_y, last_1))
+    last_2 = split_blocks(last_1[0] + last_1[1].astype(f32), 1, 1)
+    own_xy = hop(own_y, dq=1)
+    line_x, line_y = hop(on_line, dq=1), hop(on_line, dq=2)
+    early = [(dx0_b, 0, 0), (own_x, 1, 0), (own_y, 2, 0), (own_xy, 3, 0), (on_line, 0, 1)]
+    order = []
+
+    def from_cores(gathered):
+        sources = []
+        for value, dq, first_d in gathered:
+            sources.extend(add_source(value, dq, first_d))
+        return sources
+
+    def add_source(value, dq, first_d):
+        for dr in range(reps):
+            for d in range(first_d, first_d + value.shape[0]):
+                order.append(
+                    (((line + d) % lines) * PLANE + (chip ^ dq)) * reps + (rep_idx ^ dr)
+                )
+        return [value, hop(value, dr=1)]
+
+    def lists_of(order):
+        order = jnp.stack(order)
+        entries = jnp.take(asked, order, axis=0)
+        count = jnp.sum((entries > 0).astype(jnp.int32), 1)
+        entries = jnp.maximum(entries - 1, 0)
+        return (
+            count,
+            entries // half,
+            (entries % half) * groups,
+            jnp.take(asked_mix, order, axis=0),
         )
 
-    asked, asked_mix = exchange(asked), exchange(asked_mix)
-    dx0_b = dx0.astype(bf16).reshape(half * groups, LANES)
-    on_line = [dx0_b] + [hop(dx0_b, dl=-d) for d in range(1, lines)]
-    stacks = [
-        jnp.stack(on_line[k * lines // 4 : (k + 1) * lines // 4]) for k in range(4)
-    ]
-    sources = []
-    order = []
-    for k, stack in enumerate(stacks):
-        kind = {0: stack, 1: hop(stack, dq=1), 2: hop(stack, dq=2)}
-        kind[3] = hop(kind[1], dq=2) if k % 2 == 0 else hop(kind[2], dq=1)
-        for dq in range(PLANE):
-            for dr in range(reps):
-                sources.append(kind[dq] if dr == 0 else hop(kind[dq], dr=1))
-                for d in range(k * lines // 4, (k + 1) * lines // 4):
-                    order.append(
-                        (((line + d) % lines) * PLANE + (chip ^ dq)) * reps + (rep_idx ^ dr)
-                    )
-    order = jnp.stack(order)
-    asked = jnp.take(asked, order, axis=0)
-    asked_mix = jnp.take(asked_mix, order, axis=0)
-    count = jnp.sum((asked > 0).astype(jnp.int32), 1)
-    asked = jnp.maximum(asked - 1, 0)
+    sources = from_cores(early)
+    begun = spread_rows(lists_of(order), sources, vocab, width)
+    order.clear()
+    line_x, line_y, begun = lax.optimization_barrier((line_x, line_y, begun))
+    shards = [two[0] + two[1].astype(f32) for two in (down_2, up_2, last_2)]
+    both = shards[1].shape[1]
+    tall = shards[0].shape[1] // both
+    pile = shards[0].reshape(lines, tall, both, -1)
+    total = reduce_line(
+        jnp.concatenate([pile[:, k] for k in range(tall)] + shards[1:], 2)
+    )
+    down_end = tall * pile.shape[3]
+    pile = jnp.stack(jnp.split(total[:, :down_end], tall, 1))
+    d_down = jnp.concatenate(join_cores(pile.reshape(reps, -1, pile.shape[2])), 1)
+    left, right = join_cores(total[:, down_end:].reshape(reps, both // reps, -1))
+    joined = []
+    at = 0
+    for columns in (up_proj.shape[1], attn_proj.shape[1], out_proj.shape[1]):
+        part = slice(at, at + columns // 2)
+        joined.append(jnp.concatenate([left[:, part], right[:, part]], 1))
+        at += columns // 2
+    d_up, d_qkv, d_out = joined
+    late = [(line_x, 1, 1), (line_y, 2, 1), (hop(line_x[:cut], dq=2), 3, 1)]
+    if cut < others:
+        late.append((hop(line_y[cut:], dq=1), 3, 1 + cut))
+    logits_mine = dense_nt(rows_all, table_low)
+    own_column = jnp.where(targets_all // vocab == me, targets_all % vocab, -1)
+    hit_mine = jnp.arange(padded, dtype=jnp.int32)[None, :] == own_column[:, None]
+    dlogit_mine = (
+        (weight_rows / coefficient_aggregate)[:, None]
+        * (jnp.exp(logits_mine - lse_all[:, None]) - hit_mine.astype(f32))
+    ).astype(bf16)
+    head_grad = dense_tn(dlogit_mine, rows_all)
+    sources = from_cores(late)
     table_grad, table_squares = spread_rows(
-        count, asked // half, (asked % half) * groups, asked_mix, sources, head_grad, vocab
+        lists_of(order), sources, vocab, width, begun, head_grad
     )
 
     sums_here = jnp.concatenate(
@@ -611,7 +899,7 @@
     local_sq = jnp.sum(table_squares)
     for g in reduced:
         local_sq = local_sq + jnp.sum(g * g)
-    totals = lax.psum(jnp.stack([local_sq, loss_here]), BOTH)
+    totals = add_up(jnp.stack([local_sq, loss_here]))
     grad_norm = jnp.sqrt(totals[0])
     loss_sum = totals[1]
     clip = jnp.minimum(1.0, 0.01 / (grad_norm + 1e-06))

time: 1360 us -> 940 us (0.69)
  waiting for transfers between devices: 570 us -> 227 us
  Pallas kernels: 79.3 us -> 153 us
  matrix products: 177 us -> 126 us
  local copies, waits for them, and re-layouts: 208 us -> 157 us
  blocking collectives: 39.8 us -> 0 us
  other arithmetic: 150 us -> 124 us
  starting transfers between devices: 96.2 us -> 114 us
    reduce_scatter x4 -> x0, waiting for transfers between devices: 268 us -> none  [scatter(): return lax.psum_scatter(value, BOTH, scatter_dimension=0, tiled=True)]
    dot_general x6 -> x0, matrix products: 63.7 us -> none  [the longest x1 17.7 us: attend_back(): jnp.einsum('qhd,khd->hqk', grad_mix, valued, preferred_element_type=f32)]
    ppermute x6, waiting for transfers between devices: 82 us -> 24.7 us  [step_line(): return lax.ppermute(x, 'dp', pairs)]
    pallas_call x0 -> x3, Pallas kernels: none -> 50.2 us  [the longest x1 27.3 us: attend_back(): pl.pallas_call(functools.partial(attend_back_kernel, tile=256), grid=(wid...]
    psum x1 -> x0, blocking collectives: 39.8 us -> none  [local(): totals = lax.psum(jnp.stack([local_sq, loss_here]), BOTH)]
    convert_element_type x4 -> x8, other arithmetic: 32.5 us -> 3.43 us  [the longest x1 1.43 us: local(): dx0_b = dx0.astype(bf16).reshape(1, half * groups, LANES)]
    slice x11 -> x12, local copies, waits for them, and re-layouts: 25.1 us -> 4.46 us  [the longest x1 2.06 us: local(): late.append((hop(line_y[cut:], dq=1), 3, 1 + cut))]
    pallas_call x1 -> x2, Pallas kernels: 37.6 us -> 54.2 us  [mix_rows(): pl.pallas_call(functools.partial(mix_kernel, groups=groups, cands=cands,...]
  transfers between devices with their start and end apart: 96 -> 96, of which waited for: 35 -> 28; matrix products, arithmetic and copies ran while one was open for 27% -> 38% of each run, Pallas kernels for 6% -> 13%
where the time goes in v2:
time: 940 us; the launch traced here: 927 us
  waiting for transfers between devices  227 us (24%)
  local copies, waits for them, and re-layouts  157 us (17%)
  Pallas kernels  153 us (16%)
  matrix products  126 us (13%)
  other arithmetic  124 us (13%)
  starting transfers between devices  114 us (12%)
  between operations  25.8 us (3%)
    ppermute x83, waiting for transfers between devices, hop(): return lax.ppermute(x, BOTH, pairs)  198 us
    ppermute x83, starting transfers between devices, hop(): return lax.ppermute(x, BOTH, pairs)  79.7 us
    unnamed x364, local copies, waits for them, and re-layouts  54.4 us
    pallas_call x2, Pallas kernels, mix_rows(): pl.pallas_call(functools.partial(mix_kernel, groups=groups, cands=cands,...  54.2 us
    pallas_call x2, Pallas kernels, spread_rows(): pl.pallas_call(functools.partial(spread_kernel, groups=groups, arrays=len...  48.1 us
    dot_general x9, matrix products, dense_tn(): lax.dot_general(a, b, (((0,), (0,)), ((), ())), preferred_element_type=f32)  42.5 us
    dot_general x5, matrix products, dense(): return jnp.dot(a, b, preferred_element_type=f32)  42.1 us
    scatter x2, local copies, waits for them, and re-layouts, local(): empty.at[flat_slot].set(value).reshape(devices, cap)  31.1 us
  transfers between devices with their start and end apart: 96, of which 28 were waited for; matrix products, arithmetic and copies ran while one was open for 38% of the time, Pallas kernels for 13%

profile of v2, /device:TPU:0, one launch (start us, length us, event | category | flops | bytes accessed | tf_op | source)
XLA Modules:
  0.0 926.8 jit_solution(15914917225843310803)
XLA Ops:
  16.1 2.6 convert_element_type.190
  18.9 3.0 collective-permute-start.3
  34.3 2.9 fusion.66
  58.3 21.4 %collective-permute-done.5.refs_5_ = bf16[800,768]{1,0:T(8,128)(2,1)} collective-permute-done((bf16[800,768]{1,0:T(8,128)(2,1)S(1)}, bf16[800,768]{1,0:T(8,128)(2,1)}, u32[]{:S(2)}, u32[]{:S(2)}) %collective-permute-start.5) | collective-permute-done | bytes 1228832 | tf_op jit(solution)/shard_map/ppermute | solution.py:270
  89.5 22.4 %collective-permute-done.13.refs_12_ = bf16[784,768]{1,0:T(8,128)(2,1)S(1)} collective-permute-done((bf16[784,768]{1,0:T(8,128)(2,1)}, bf16[784,768]{1,0:T(8,128)(2,1)S(1)}, u32[]{:S(2)}, u32[]{:S(2)}) %collective-permute-start.13) | collective-permute-done | bytes 1204256 | tf_op jit(solution)/shard_map/ppermute | solution.py:270
  111.9 3.9 collective-permute-done.14.refs_13_
  121.1 27.1 %shard_map.554 = f32[2,3080,128]{2,1,0:T(8,128)} custom-call(s32[2,1,4096]{2,1,0:T(1,128)} %pad_add_fusion.1.idx_ref, f32[2,1,4096]{2,1,0:T(1,128)} %pad_maximum_fusion.16.mix_ref, bf16[784,768]{1,0:T(8,128)(2,1)} %copy-done.16, bf16[800,768]{1,0:T(8,128)(2,1)} %copy-done.14, bf16[784,768]{1,0:T(8,128)(2,1)} %collective-permute-done.7.refs_2_, ...), custom_call_target="tpu_custom_call" | custom-call | flops 16777216 | bytes 41943040 | tf_op jit(solution)/shard_map/pallas_call | solution.py:383
  148.2 3.9 slice_bitcast_fusion.2
  152.1 4.8 collective-permute-start.17
  166.5 27.1 %shard_map.553 = f32[2,3080,128]{2,1,0:T(8,128)} custom-call(s32[2,1,4096]{2,1,0:T(1,128)} %pad_add_fusion.idx_ref, f32[2,1,4096]{2,1,0:T(1,128)} %pad_maximum_fusion.15.mix_ref, bf16[784,768]{1,0:T(8,128)(2,1)} %copy-done.16, bf16[800,768]{1,0:T(8,128)(2,1)} %copy-done.14, bf16[784,768]{1,0:T(8,128)(2,1)} %collective-permute-done.7.refs_2_, ...), custom_call_target="tpu_custom_call" | custom-call | flops 16777216 | bytes 41943040 | tf_op jit(solution)/shard_map/pallas_call | solution.py:383
  195.3 4.3 fusion.17
  200.5 6.2 collective-permute-start.19
  221.3 7.0 copy.207
  230.9 23.0 %collective-permute-done.19 = f32[3072,128]{1,0:T(8,128)} collective-permute-done((f32[3072,128]{1,0:T(8,128)}, f32[3072,128]{1,0:T(8,128)}, u32[]{:S(2)}, u32[]{:S(2)}) %collective-permute-start.19) | collective-permute-done | bytes 1572896 | tf_op jit(solution)/shard_map/ppermute | solution.py:280
  253.9 4.6 fusion.164
  258.5 13.5 %collective-permute-start.20 = (f32[3072,128]{1,0:T(8,128)}, f32[3072,128]{1,0:T(8,128)}, u32[]{:S(2)}, u32[]{:S(2)}) collective-permute-start(f32[3072,128]{1,0:T(8,128)} %get-tuple-element.223), channel_id=1, source_target_pairs={{0,8},{2,10},{4,12},{6,14},{8,16},{10,18},{12,20},{14,22},{16,24},... | collective-permute-start | bytes 4718600 | tf_op jit(solution)/shard_map/ppermute | solution.py:280
  276.0 3.8 copy.209
  281.7 9.2 reduce-window.6
  292.5 15.5 %scatter_custom_fusion.1 = f32[8192]{0:T(1024)S(1)} fusion(s32[4096]{0:T(1024)S(1)} %get-tuple-element.314, f32[4096]{0:T(1024)S(1)} %exponential_divide_fusion, f32[]{:T(128)} %constant.594.clone.1), kind=kCustom, calls=%fused_computation.379 | custom fusion | bytes 32772 | tf_op jit(solution)/shard_map/scatter | solution.py:626
  308.1 15.5 %scatter_custom_fusion = f32[8192]{0:T(1024)S(1)} fusion(s32[4096]{0:T(1024)S(1)} %get-tuple-element.314, f32[4096]{0:T(1024)S(1)} %get-tuple-element.315, f32[]{:T(128)} %constant.594.clone.1), kind=kCustom, calls=%fused_computation.381 | custom fusion | bytes 32772 | tf_op jit(solution)/shard_map/scatter | solution.py:626
  323.7 3.9 fusion.178
  333.8 6.6 fusion.188.q_ref.k_ref.v_ref
  340.5 4.8 shard_map.555
  348.1 2.7 slice.287
  356.8 4.8 all-to-all-start
  364.5 4.6 all-to-all-done
  372.2 18.1 %shard_map.556 = (bf16[512,768]{1,0:T(8,128)(2,1)S(1)}, f32[512,768]{1,0:T(8,128)}) custom-call(s32[1]{0:T(128)} %dynamic_slice.223.len_ref, s32[1]{0:T(128)} %bitcast.44.core_ref, bf16[512,768]{1,0:T(8,128)(2,1)S(1)} %copy-done.2, bf16[512,768]{1,0:T(8,128)(2,1)S(1)} %copy-done.3, bf16[512,768]{1,0:T(8,128)(2,1)S(1)} %copy-done.7, ...), custom_call_target="tpu_custom_call" | custom-call | flops 1610612736 | bytes 7077888 | tf_op jit(solution)/shard_map/pallas_call | solution.py:161
  390.3 3.7 fusion.177
  395.5 8.4 multiply_convert_fusion.3
  404.0 7.5 fusion.176
  427.2 12.2 %fusion.187 = (f32[256]{0:T(256)S(1)}, f32[256,12672]{1,0:T(8,128)}) fusion(bf16[12672,768]{1,0:T(8,128)(2,1)} %constant_dynamic-update-slice_fusion, bf16[64,768]{1,0:T(8,128)(2,1)S(1)} %collective-permute-done.27, bf16[64,768]{1,0:T(8,128)(2,1)S(1)} %collective-permute-done.26, bf16[64,768]{1,0:T(8,128)(2,1)S(1)} %collective-permute-done.25, ...), kind=kOutput, calls=%fused_computation.571 | convolution fusion | flops 4990894080 | bytes 32847232 | tf_op jit(solution)/shard_map/dot_general | solution.py:29
  439.5 6.9 exponential_reduce_fusion
  453.6 15.8 %fusion = f32[256,768]{1,0:T(8,128)S(1)} fusion(bf16[12672,768]{1,0:T(8,128)(2,1)} %constant_dynamic-update-slice_fusion, f32[256,12672]{1,0:T(8,128)} %get-tuple-element.304, f32[256]{0:T(256)S(1)} %reshape.2254, f32[256]{0:T(256)S(1)} %copy-done.149, s32[256]{0:T(256)S(1)} %copy-done.138), kind=kOutput, calls=%fused_computation.17 | convolution fusion | flops 5002297344 | bytes 33229824 | tf_op jit(solution)/shard_map/dot_general | solution.py:25
  470.3 3.5 collective-permute-start.33
  475.8 3.8 collective-permute-done.33
  479.5 10.6 %collective-permute-done.32 = f32[64,768]{1,0:T(8,128)} collective-permute-done((f32[64,768]{1,0:T(8,128)}, f32[64,768]{1,0:T(8,128)}, u32[]{:S(2)}, u32[]{:S(2)}) %collective-permute-start.32) | collective-permute-done | bytes 196640 | tf_op jit(solution)/shard_map/ppermute | solution.py:270
  492.6 3.4 multiply_reduce_fusion
  496.9 9.4 %fusion.10 = bf16[512,3072]{1,0:T(8,128)(2,1)S(1)} fusion(f32[512,3072]{1,0:T(8,128)} %get-tuple-element.301, bf16[512,768]{1,0:T(8,128)(2,1)S(1)} %multiply_convert_fusion.5, bf16[3072,768]{1,0:T(8,128)(2,1)} %all-gather.15.cloned.1.call-done), kind=kOutput, calls=%fused_computation.27 | convolution fusion | flops 2447376384 | bytes 14942208 | tf_op jit(solution)/shard_map/dot_general | solution.py:29
  506.3 3.6 multiply_reduce_fusion.2
  509.9 4.1 fusion.41
  516.7 3.6 fusion.15
  525.8 5.8 collective-permute-done.40
  543.2 4.7 convolution_add_fusion.2
  549.6 4.9 convolution_add_fusion
  564.4 27.3 %shard_map.557 = (bf16[512,768]{1,0:T(8,128)(2,1)S(1)}, f32[512,768]{1,0:T(8,128)}, bf16[512,768]{1,0:T(8,128)(2,1)S(1)}, f32[512,768]{1,0:T(8,128)}, bf16[512,768]{1,0:T(8,128)(2,1)S(1)}) custom-call(s32[1]{0:T(128)} %dynamic_slice.223.len_ref, s32[1]{0:T(128)} %bitcast.44.core_ref, bf16[512,768]{1,0:T(8,128)(2,1)S(1)} %copy-done.2, ...), custom_call_target="tpu_custom_call" | custom-call | flops 4026531840 | bytes 12582912 | tf_op jit(solution)/shard_map/pallas_call | solution.py:239
  606.8 2.9 multiply_reduce_fusion.4
  613.6 3.6 collective-permute-done.53
  619.5 3.1 collective-permute-start.54
  626.3 15.9 %fusion.20.refs_9_ = f32[1584,768]{1,0:T(8,128)} fusion(bf16[2048,768]{1,0:T(8,128)(2,1)} %bitcast.385, s32[2048]{0:T(1024)S(1)} %copy-done.134, f32[2048]{0:T(1024)S(1)} %bitcast.401, f32[2048]{0:T(1024)S(1)} %copy-done.135, bf16[1572,768]{1,0:T(8,128)(2,1)S(1)} %copy-done.19), kind=kOutput, calls=%fused_computation.91 | convolution fusion | flops 9985130496 | bytes 10450944 | tf_op jit(solution)/shard_map/dot_general | solution.py:33
  642.2 2.7 fusion.29
  645.5 3.0 convolution_add_fusion.1
  653.6 19.3 %collective-permute-done.55 = bf16[1,3072,128]{2,1,0:T(8,128)(2,1)} collective-permute-done((bf16[1,3072,128]{2,1,0:T(8,128)(2,1)}, bf16[1,3072,128]{2,1,0:T(8,128)(2,1)}, u32[]{:S(2)}, u32[]{:S(2)}) %collective-permute-start.55) | collective-permute-done | bytes 786464 | tf_op jit(solution)/shard_map/ppermute | solution.py:270
  675.0 16.4 %collective-permute-done.61 = bf16[4,2,48,1536]{3,2,0,1:T(8,128)(2,1)S(1)} collective-permute-done((bf16[4,2,48,1536]{3,2,0,1:T(8,128)(2,1)S(1)}, bf16[4,2,48,1536]{3,2,0,1:T(8,128)(2,1)S(1)}, u32[]{:S(2)}, u32[]{:S(2)}) %collective-permute-start.61) | collective-permute-done | bytes 1179680 | tf_op jit(solution)/shard_map/ppermute | solution.py:270
  697.3 11.7 %collective-permute-done.76 = bf16[4,48,1536]{2,1,0:T(8,128)(2,1)S(1)} collective-permute-done((bf16[4,48,1536]{2,1,0:T(8,128)(2,1)S(1)}, bf16[4,48,1536]{2,1,0:T(8,128)(2,1)S(1)}, u32[]{:S(2)}, u32[]{:S(2)}) %collective-permute-start.76) | collective-permute-done | bytes 589856 | tf_op jit(solution)/shard_map/ppermute | solution.py:270
  721.8 3.4 dynamic-slice_bitcast_fusion.6
  725.3 4.0 collective-permute-start.79
  732.9 19.2 %shard_map.558.refs_8_ = f32[12608,128]{1,0:T(8,128)} custom-call(s32[14]{0:T(128)} %get-tuple-element.259.cnt_ref, s32[14,256]{1,0:T(8,128)} %get-tuple-element.258.row_ref, s32[14,256]{1,0:T(8,128)} %get-tuple-element.257.pos_ref, f32[14,256]{1,0:T(8,128)} %broadcast_select_fusion.1.mix_ref, bf16[1,3072,128]{2,1,0:T(8,128)(2,1)} %reshape.2262.refs_0_, ...), custom_call_target="tpu_custom_call" | custom-call | flops 3670016 | bytes 18350080 | tf_op jit(solution)/shard_map/pallas_call | solution.py:496
  752.2 14.6 %collective-permute-done.62.refs_0_ = bf16[3,3072,128]{2,1,0:T(8,128)(2,1)} collective-permute-done((bf16[3,3072,128]{2,1,0:T(8,128)(2,1)S(1)}, bf16[3,3072,128]{2,1,0:T(8,128)(2,1)}, u32[]{:S(2)}, u32[]{:S(2)}) %collective-permute-start.62) | collective-permute-done | bytes 2359328 | tf_op jit(solution)/shard_map/ppermute | solution.py:270
  771.3 33.4 %collective-permute-done.78 = f32[48,4608]{1,0:T(8,128)} collective-permute-done((f32[48,4608]{1,0:T(8,128)}, f32[48,4608]{1,0:T(8,128)}, u32[]{:S(2)}, u32[]{:S(2)}) %collective-permute-start.78) | collective-permute-done | bytes 884768 | tf_op jit(solution)/shard_map/ppermute | solution.py:270
  813.6 13.9 %collective-permute-done.74.refs_6_ = bf16[1,3072,128]{2,1,0:T(8,128)(2,1)} collective-permute-done((bf16[1,3072,128]{2,1,0:T(8,128)(2,1)}, bf16[1,3072,128]{2,1,0:T(8,128)(2,1)}, u32[]{:S(2)}, u32[]{:S(2)}) %collective-permute-start.74) | collective-permute-done | bytes 786464 | tf_op jit(solution)/shard_map/ppermute | solution.py:270
  833.9 28.9 %shard_map.559 = (f32[1572,768]{1,0:T(8,128)}, f32[8,128]{1,0:T(8,128)}) custom-call(s32[18]{0:T(128)} %get-tuple-element.256.cnt_ref, s32[18,256]{1,0:T(8,128)} %get-tuple-element.255.row_ref, s32[18,256]{1,0:T(8,128)} %get-tuple-element.254.pos_ref, f32[18,256]{1,0:T(8,128)} %broadcast_select_fusion.mix_ref, ...), custom_call_target="tpu_custom_call" | custom-call | flops 4718592 | bytes 23592960 | tf_op jit(solution)/shard_map/pallas_call | solution.py:496
  871.3 6.6 collective-permute-start.84
  877.9 7.6 collective-permute-start.85
  905.8 10.4 %multiply_subtract_fusion = (f32[1572,768]{1,0:T(8,128)}, f32[1572,768]{1,0:T(8,128)}, f32[1572,768]{1,0:T(8,128)}) fusion(f32[1572,768]{1,0:T(8,128)} %param.41, f32[1572,768]{1,0:T(8,128)S(1)} %copy-done.47, f32[]{:T(128)S(6)} %min.3, f32[1572,768]{1,0:T(8,128)} %param.42, f32[1572,768]{1,0:T(8,128)} %param.43), kind=kLoop, calls=%fused_computation.30 | loop fusion | flops 19316736 | bytes 33804292 | tf_op jit(solution)/shard_map/sub | solution.py:258
  (847 shorter events, 274.0 us)
Async XLA Ops:
  7.2 214.1 %all-gather.7.cloned.1.call-start = ((), (), s32[]{:S(2)}) async-start(), calls=%async_computation.1 | async-start | bytes 1757184 | tf_op jit(solution)/shard_map/all_gather | solution.py:634
  11.1 322.8 %all-gather.9.cloned.1.call-start = ((), (), s32[]{:S(2)}) async-start(), calls=%async_computation.2 | async-start | bytes 3649536 | tf_op jit(solution)/shard_map/all_gather | solution.py:634
  12.7 377.5 %all-gather.11.cloned.1.call-start = ((), (), s32[]{:S(2)}) async-start(), calls=%async_computation.3 | async-start | bytes 1216512 | tf_op jit(solution)/shard_map/all_gather | solution.py:634
  14.3 381.2 %all-gather.13.cloned.1.call-start = ((), (), s32[]{:S(2)}) async-start(), calls=%async_computation.4 | async-start | bytes 4866048 | tf_op jit(solution)/shard_map/all_gather | solution.py:634
  16.0 388.0 %all-gather.15.cloned.1.call-start = ((), (), s32[]{:S(2)}) async-start(), calls=%async_computation.5 | async-start | bytes 4866048 | tf_op jit(solution)/shard_map/all_gather | solution.py:634
  18.9 39.4 %collective-permute-start.3 = (bf16[784,768]{1,0:T(8,128)(2,1)S(1)}, bf16[784,768]{1,0:T(8,128)(2,1)}, u32[]{:S(2)}, u32[]{:S(2)}) collective-permute-start(bf16[784,768]{1,0:T(8,128)(2,1)S(1)} %slice.266.refs_0_), channel_id=1, source_target_pairs={{0,2},{1,3},{2,0},{3,1},{4,6},{5,7},{6,4},{7,5},{8,10},{9,11},{10,... | collective-permute-start | bytes 3612680 | tf_op jit(solution)/shard_map/ppermute | solution.py:270
  21.9 36.4 %collective-permute-start.4 = (bf16[784,768]{1,0:T(8,128)(2,1)S(1)}, bf16[784,768]{1,0:T(8,128)(2,1)}, u32[]{:S(2)}, u32[]{:S(2)}) collective-permute-start(bf16[784,768]{1,0:T(8,128)(2,1)S(1)} %slice.266.refs_0_), channel_id=1, source_target_pairs={{0,4},{1,5},{2,6},{3,7},{4,0},{5,1},{6,2},{7,3},{8,12},{9,13},{10,... | collective-permute-start | bytes 3612680 | tf_op jit(solution)/shard_map/ppermute | solution.py:270
  23.5 56.2 %collective-permute-start.5 = (bf16[800,768]{1,0:T(8,128)(2,1)S(1)}, bf16[800,768]{1,0:T(8,128)(2,1)}, u32[]{:S(2)}, u32[]{:S(2)}) collective-permute-start(bf16[800,768]{1,0:T(8,128)(2,1)S(1)} %pad_slice_fusion.refs_1_), channel_id=1, source_target_pairs={{0,2},{1,3},{2,0},{3,1},{4,6},{5,7},{6,4},{7,5},{8,10},{9,11},{10,... | collective-permute-start | bytes 3686408 | tf_op jit(solution)/shard_map/ppermute | solution.py:270
  24.1 56.3 %collective-permute-start.6 = (bf16[800,768]{1,0:T(8,128)(2,1)S(1)}, bf16[800,768]{1,0:T(8,128)(2,1)}, u32[]{:S(2)}, u32[]{:S(2)}) collective-permute-start(bf16[800,768]{1,0:T(8,128)(2,1)S(1)} %pad_slice_fusion.refs_1_), channel_id=1, source_target_pairs={{0,4},{1,5},{2,6},{3,7},{4,0},{5,1},{6,2},{7,3},{8,12},{9,13},{10,... | collective-permute-start | bytes 3686408 | tf_op jit(solution)/shard_map/ppermute | solution.py:270
  26.4 16.7 %collective-permute-start.2 = (f32[64,128]{1,0:T(8,128)}, f32[64,128]{1,0:T(8,128)S(1)}, u32[]{:S(2)}, u32[]{:S(2)}) collective-permute-start(f32[64,128]{1,0:T(8,128)} %get-tuple-element.253), channel_id=1, source_target_pairs={{0,8},{1,9},{2,10},{3,11},{4,12},{5,13},{6,14},{7,15},{8,16},{9,17... | collective-permute-start | bytes 98312 | tf_op jit(solution)/shard_map/ppermute | solution.py:270
  80.4 31.5 %collective-permute-start.13 = (bf16[784,768]{1,0:T(8,128)(2,1)}, bf16[784,768]{1,0:T(8,128)(2,1)S(1)}, u32[]{:S(2)}, u32[]{:S(2)}) collective-permute-start(bf16[784,768]{1,0:T(8,128)(2,1)} %collective-permute-done.3.refs_4_), channel_id=1, source_target_pairs={{0,4},{1,5},{2,6},{3,7},{4,0},{5,1},{6,2},{7,3},{8,12},{9,13},{10,... | collective-permute-start | bytes 3612680 | tf_op jit(solution)/shard_map/ppermute | solution.py:270
  82.5 33.3 %collective-permute-start.14 = (bf16[800,768]{1,0:T(8,128)(2,1)}, bf16[800,768]{1,0:T(8,128)(2,1)S(1)}, u32[]{:S(2)}, u32[]{:S(2)}) collective-permute-start(bf16[800,768]{1,0:T(8,128)(2,1)} %collective-permute-done.6.refs_9_), channel_id=1, source_target_pairs={{0,2},{1,3},{2,0},{3,1},{4,6},{5,7},{6,4},{7,5},{8,10},{9,11},{10,... | collective-permute-start | bytes 3686408 | tf_op jit(solution)/shard_map/ppermute | solution.py:270
  87.3 29.9 %collective-permute-start.12 = (bf16[800,768]{1,0:T(8,128)(2,1)}, bf16[800,768]{1,0:T(8,128)(2,1)S(1)}, u32[]{:S(2)}, u32[]{:S(2)}) collective-permute-start(bf16[800,768]{1,0:T(8,128)(2,1)} %collective-permute-done.6.refs_9_), channel_id=1, source_target_pairs={{0,1},{1,0},{2,3},{3,2},{4,5},{5,4},{6,7},{7,6},{8,9},{9,8},{10,11... | collective-permute-start | bytes 3686408 | tf_op jit(solution)/shard_map/ppermute | solution.py:270
  87.4 29.8 %collective-permute-start.8 = (bf16[800,768]{1,0:T(8,128)(2,1)S(1)}, bf16[800,768]{1,0:T(8,128)(2,1)S(1)}, u32[]{:S(2)}, u32[]{:S(2)}) collective-permute-start(bf16[800,768]{1,0:T(8,128)(2,1)S(1)} %pad_slice_fusion.refs_1_), channel_id=1, source_target_pairs={{0,1},{1,0},{2,3},{3,2},{4,5},{5,4},{6,7},{7,6},{8,9},{9,8},{10,11... | collective-permute-start | bytes 3686408 | tf_op jit(solution)/shard_map/ppermute | solution.py:270
  88.4 28.7 %collective-permute-start.10 = (bf16[800,768]{1,0:T(8,128)(2,1)}, bf16[800,768]{1,0:T(8,128)(2,1)S(1)}, u32[]{:S(2)}, u32[]{:S(2)}) collective-permute-start(bf16[800,768]{1,0:T(8,128)(2,1)} %collective-permute-done.5.refs_5_), channel_id=1, source_target_pairs={{0,1},{1,0},{2,3},{3,2},{4,5},{5,4},{6,7},{7,6},{8,9},{9,8},{10,11... | collective-permute-start | bytes 3686408 | tf_op jit(solution)/shard_map/ppermute | solution.py:270
  152.1 43.2 %collective-permute-start.17 = (f32[3072,128]{1,0:T(8,128)}, f32[3072,128]{1,0:T(8,128)}, u32[]{:S(2)}, u32[]{:S(2)}) collective-permute-start(f32[3072,128]{1,0:T(8,128)} %get-tuple-element.227), channel_id=1, source_target_pairs={{0,8},{2,10},{4,12},{6,14},{1,9},{3,11},{5,13},{7,15}} | collective-permute-start | bytes 4718600 | tf_op jit(solution)/shard_map/ppermute | solution.py:280
  156.9 38.4 %collective-permute-start.18 = (f32[3072,128]{1,0:T(8,128)}, f32[3072,128]{1,0:T(8,128)}, u32[]{:S(2)}, u32[]{:S(2)}) collective-permute-start(f32[3072,128]{1,0:T(8,128)} %get-tuple-element.226), channel_id=1, source_target_pairs={{24,16},{26,18},{28,20},{30,22},{25,17},{27,19},{29,21},{31,23}} | collective-permute-start | bytes 4718600 | tf_op jit(solution)/shard_map/ppermute | solution.py:280
  199.7 31.2 %collective-permute-start.21 = (f32[3072,128]{1,0:T(8,128)}, f32[3072,128]{1,0:T(8,128)S(1)}, u32[]{:S(2)}, u32[]{:S(2)}) collective-permute-start(f32[3072,128]{1,0:T(8,128)} %get-tuple-element.224), channel_id=1, source_target_pairs={{16,8},{18,10},{20,12},{22,14},{24,16},{26,18},{28,20},{30,22},{17... | collective-permute-start | bytes 4718600 | tf_op jit(solution)/shard_map/ppermute | solution.py:280
  200.5 53.4 %collective-permute-start.19 = (f32[3072,128]{1,0:T(8,128)}, f32[3072,128]{1,0:T(8,128)}, u32[]{:S(2)}, u32[]{:S(2)}) collective-permute-start(f32[3072,128]{1,0:T(8,128)} %get-tuple-element.225), channel_id=1, source_target_pairs={{0,8},{2,10},{4,12},{6,14},{8,16},{10,18},{12,20},{14,22},{1,9},{3... | collective-permute-start | bytes 4718600 | tf_op jit(solution)/shard_map/ppermute | solution.py:280
  258.5 65.2 %collective-permute-start.20 = (f32[3072,128]{1,0:T(8,128)}, f32[3072,128]{1,0:T(8,128)}, u32[]{:S(2)}, u32[]{:S(2)}) collective-permute-start(f32[3072,128]{1,0:T(8,128)} %get-tuple-element.223), channel_id=1, source_target_pairs={{0,8},{2,10},{4,12},{6,14},{8,16},{10,18},{12,20},{14,22},{16,24},... | collective-permute-start | bytes 4718600 | tf_op jit(solution)/shard_map/ppermute | solution.py:280
  272.0 51.7 %collective-permute-start.22 = (f32[3072,128]{1,0:T(8,128)}, f32[3072,128]{1,0:T(8,128)}, u32[]{:S(2)}, u32[]{:S(2)}) collective-permute-start(f32[3072,128]{1,0:T(8,128)} %get-tuple-element.222), channel_id=1, source_target_pairs={{8,0},{10,2},{12,4},{14,6},{16,8},{18,10},{20,12},{22,14},{24,16},... | collective-permute-start | bytes 4718600 | tf_op jit(solution)/shard_map/ppermute | solution.py:280
  345.3 23.7 %collective-permute-start.23 = (bf16[512,768]{1,0:T(8,128)(2,1)}, bf16[512,768]{1,0:T(8,128)(2,1)S(1)}, u32[]{:S(2)}, u32[]{:S(2)}) collective-permute-start(bf16[512,768]{1,0:T(8,128)(2,1)} %get-tuple-element.105.k_ref), channel_id=1, source_target_pairs={{0,1},{1,0},{2,3},{3,2},{4,5},{5,4},{6,7},{7,6},{8,9},{9,8},{10,11... | collective-permute-start | bytes 2359304 | tf_op jit(solution)/shard_map/ppermute | solution.py:270
  345.4 24.6 %collective-permute-start.24 = (bf16[512,768]{1,0:T(8,128)(2,1)}, bf16[512,768]{1,0:T(8,128)(2,1)}, u32[]{:S(2)}, u32[]{:S(2)}) collective-permute-start(bf16[512,768]{1,0:T(8,128)(2,1)} %get-tuple-element.106.v_ref), channel_id=1, source_target_pairs={{0,1},{1,0},{2,3},{3,2},{4,5},{5,4},{6,7},{7,6},{8,9},{9,8},{10,11... | collective-permute-start | bytes 2359304 | tf_op jit(solution)/shard_map/ppermute | solution.py:270
  356.8 12.2 %all-to-all-start = ((f32[32,1,512]{2,1,0:T(1,128)}), f32[32,1,512]{2,1,0:T(1,128)S(1)}, u32[]{:S(2)}, u32[]{:S(2)}) async-start(f32[32,1,512]{2,1,0:T(1,128)} %all_to_all.8), calls=%async_computation | async-start | bytes 131072 | tf_op jit(solution)/shard_map/all_to_all | solution.py:676
  361.6 350.4 %all-gather.17.cloned.1.call-start = ((), (), s32[]{:S(2)}) async-start(), calls=%async_computation.6 | async-start | bytes 1216512 | tf_op jit(solution)/shard_map/all_gather | solution.py:882
  420.2 129.3 %collective-permute-start.34 = (bf16[512,3072]{1,0:T(8,128)(2,1)}, bf16[512,3072]{1,0:T(8,128)(2,1)}, u32[]{:S(2)}, u32[]{:S(2)}) collective-permute-start(bf16[512,3072]{1,0:T(8,128)(2,1)} %get-tuple-element.300), channel_id=1, source_target_pairs={{0,1},{1,0},{2,3},{3,2},{4,5},{5,4},{6,7},{7,6},{8,9},{9,8},{10,11... | collective-permute-start | bytes 9437192 | tf_op jit(solution)/shard_map/ppermute | solution.py:270
  473.8 16.3 %collective-permute-start.32 = (f32[64,768]{1,0:T(8,128)}, f32[64,768]{1,0:T(8,128)}, u32[]{:S(2)}, u32[]{:S(2)}) collective-permute-start(f32[64,768]{1,0:T(8,128)} %get-tuple-element.236), channel_id=1, source_target_pairs={{0,16},{1,17},{2,18},{3,19},{4,20},{5,21},{6,22},{7,23},{8,24},{9,... | collective-permute-start | bytes 589832 | tf_op jit(solution)/shard_map/ppermute | solution.py:270
  473.8 16.3 %collective-permute-start.31 = (f32[64,768]{1,0:T(8,128)}, f32[64,768]{1,0:T(8,128)}, u32[]{:S(2)}, u32[]{:S(2)}) collective-permute-start(f32[64,768]{1,0:T(8,128)} %get-tuple-element.234), channel_id=1, source_target_pairs={{0,8},{1,9},{2,10},{3,11},{4,12},{5,13},{6,14},{7,15},{8,16},{9,17... | collective-permute-start | bytes 589832 | tf_op jit(solution)/shard_map/ppermute | solution.py:270
  491.4 28.9 %collective-permute-start.38 = (bf16[256,768]{1,0:T(8,128)(2,1)S(1)}, bf16[256,768]{1,0:T(8,128)(2,1)S(1)}, u32[]{:S(2)}, u32[]{:S(2)}) collective-permute-start(bf16[256,768]{1,0:T(8,128)(2,1)S(1)} %pad_maximum_fusion.4), channel_id=1, source_target_pairs={{0,2},{1,3},{2,0},{3,1},{4,6},{5,7},{6,4},{7,5},{8,10},{9,11},{10,... | collective-permute-start | bytes 1179656 | tf_op jit(solution)/shard_map/ppermute | solution.py:270
  491.9 32.4 %collective-permute-start.39 = (bf16[256,768]{1,0:T(8,128)(2,1)S(1)}, bf16[256,768]{1,0:T(8,128)(2,1)S(1)}, u32[]{:S(2)}, u32[]{:S(2)}) collective-permute-start(bf16[256,768]{1,0:T(8,128)(2,1)S(1)} %pad_maximum_fusion.4), channel_id=1, source_target_pairs={{0,4},{1,5},{2,6},{3,7},{4,0},{5,1},{6,2},{7,3},{8,12},{9,13},{10,... | collective-permute-start | bytes 1179656 | tf_op jit(solution)/shard_map/ppermute | solution.py:270
  515.3 27.8 %collective-permute-start.37 = (bf16[512,1536]{1,0:T(8,128)(2,1)}, bf16[512,1536]{1,0:T(8,128)(2,1)}, u32[]{:S(2)}, u32[]{:S(2)}) collective-permute-start(bf16[512,1536]{1,0:T(8,128)(2,1)} %constant_dynamic-slice_fusion.41), channel_id=1, source_target_pairs={{0,1},{1,0},{2,3},{3,2},{4,5},{5,4},{6,7},{7,6},{8,9},{9,8},{10,11... | collective-permute-start | bytes 4718600 | tf_op jit(solution)/shard_map/ppermute | solution.py:270
  520.3 11.2 %collective-permute-start.40 = (bf16[256,768]{1,0:T(8,128)(2,1)S(1)}, bf16[256,768]{1,0:T(8,128)(2,1)S(1)}, u32[]{:S(2)}, u32[]{:S(2)}) collective-permute-start(bf16[256,768]{1,0:T(8,128)(2,1)S(1)} %collective-permute-done.38), channel_id=1, source_target_pairs={{0,4},{1,5},{2,6},{3,7},{4,0},{5,1},{6,2},{7,3},{8,12},{9,13},{10,... | collective-permute-start | bytes 1179656 | tf_op jit(solution)/shard_map/ppermute | solution.py:270
  533.0 15.0 %collective-permute-start.41 = (bf16[4,256,768]{2,1,0:T(8,128)(2,1)}, bf16[4,256,768]{2,1,0:T(8,128)(2,1)}, u32[]{:S(2)}, u32[]{:S(2)}) collective-permute-start(bf16[4,256,768]{2,1,0:T(8,128)(2,1)} %pad_maximum_fusion.3), channel_id=1, source_target_pairs={{0,1},{1,0},{2,3},{3,2},{4,5},{5,4},{6,7},{7,6},{8,9},{9,8},{10,11... | collective-permute-start | bytes 4718600 | tf_op jit(solution)/shard_map/ppermute | solution.py:270
  536.4 108.6 %collective-permute-start.59 = (bf16[512,768]{1,0:T(8,128)(2,1)}, bf16[512,768]{1,0:T(8,128)(2,1)}, u32[]{:S(2)}, u32[]{:S(2)}) collective-permute-start(bf16[512,768]{1,0:T(8,128)(2,1)} %add_convert_fusion.4), channel_id=1, source_target_pairs={{0,1},{1,0},{2,3},{3,2},{4,5},{5,4},{6,7},{7,6},{8,9},{9,8},{10,11... | collective-permute-start | bytes 2359304 | tf_op jit(solution)/shard_map/ppermute | solution.py:270
  542.7 49.0 %collective-permute-start.48 = (bf16[512,768]{1,0:T(8,128)(2,1)S(1)}, bf16[512,768]{1,0:T(8,128)(2,1)}, u32[]{:S(2)}, u32[]{:S(2)}) collective-permute-start(bf16[512,768]{1,0:T(8,128)(2,1)S(1)} %get-tuple-element.107), channel_id=1, source_target_pairs={{0,1},{1,0},{2,3},{3,2},{4,5},{5,4},{6,7},{7,6},{8,9},{9,8},{10,11... | collective-permute-start | bytes 2359304 | tf_op jit(solution)/shard_map/ppermute | solution.py:270
  555.7 39.5 %collective-permute-start.46 = (bf16[4,2,192,384]{3,2,1,0:T(8,128)(2,1)}, bf16[4,2,192,384]{3,2,1,0:T(8,128)(2,1)}, u32[]{:S(2)}, u32[]{:S(2)}) collective-permute-start(bf16[4,2,192,384]{3,2,1,0:T(8,128)(2,1)} %fusion.25), channel_id=1, source_target_pairs={{0,4},{1,5},{2,6},{3,7},{4,0},{5,1},{6,2},{7,3},{8,12},{9,13},{10,... | collective-permute-start | bytes 3538952 | tf_op jit(solution)/shard_map/ppermute | solution.py:270
  560.0 35.2 %collective-permute-start.47 = (bf16[4,2,48,1536]{3,2,1,0:T(8,128)(2,1)}, bf16[4,2,48,1536]{3,2,1,0:T(8,128)(2,1)}, u32[]{:S(2)}, u32[]{:S(2)}) collective-permute-start(bf16[4,2,48,1536]{3,2,1,0:T(8,128)(2,1)} %fusion.26), channel_id=1, source_target_pairs={{0,2},{1,3},{2,0},{3,1},{4,6},{5,7},{6,4},{7,5},{8,10},{9,11},{10,... | collective-permute-start | bytes 3538952 | tf_op jit(solution)/shard_map/ppermute | solution.py:270
  560.4 31.3 %collective-permute-start.49 = (bf16[512,384]{1,0:T(8,128)(2,1)S(1)}, bf16[512,384]{1,0:T(8,128)(2,1)S(1)}, u32[]{:S(2)}, u32[]{:S(2)}) collective-permute-start(bf16[512,384]{1,0:T(8,128)(2,1)S(1)} %constant_dynamic-slice_fusion.40), channel_id=1, source_target_pairs={{0,1},{1,0},{2,3},{3,2},{4,5},{5,4},{6,7},{7,6},{8,9},{9,8},{10,11... | collective-permute-start | bytes 1179656 | tf_op jit(solution)/shard_map/ppermute | solution.py:270
  597.5 16.2 %collective-permute-start.52 = (bf16[4,192,384]{2,1,0:T(8,128)(2,1)S(1)}, bf16[4,192,384]{2,1,0:T(8,128)(2,1)}, u32[]{:S(2)}, u32[]{:S(2)}) collective-permute-start(bf16[4,192,384]{2,1,0:T(8,128)(2,1)S(1)} %fusion.33), channel_id=1, source_target_pairs={{0,2},{1,3},{2,0},{3,1},{4,6},{5,7},{6,4},{7,5},{8,10},{9,11},{10,... | collective-permute-start | bytes 1769480 | tf_op jit(solution)/shard_map/ppermute | solution.py:270
  601.5 15.8 %collective-permute-start.53 = (bf16[4,48,1536]{2,1,0:T(8,128)(2,1)}, bf16[4,48,1536]{2,1,0:T(8,128)(2,1)}, u32[]{:S(2)}, u32[]{:S(2)}) collective-permute-start(bf16[4,48,1536]{2,1,0:T(8,128)(2,1)} %fusion.34), channel_id=1, source_target_pairs={{0,4},{1,5},{2,6},{3,7},{4,0},{5,1},{6,2},{7,3},{8,12},{9,13},{10,... | collective-permute-start | bytes 1769480 | tf_op jit(solution)/shard_map/ppermute | solution.py:270
  617.2 35.0 %collective-permute-start.56 = (bf16[1,3072,128]{2,1,0:T(8,128)(2,1)}, bf16[1,3072,128]{2,1,0:T(8,128)(2,1)}, u32[]{:S(2)}, u32[]{:S(2)}) collective-permute-start(bf16[1,3072,128]{2,1,0:T(8,128)(2,1)} %reshape.2262.refs_0_), channel_id=1, source_target_pairs={{0,8},{1,9},{2,10},{3,11},{4,12},{5,13},{6,14},{7,15},{8,16},{9,17... | collective-permute-start | bytes 2359304 | tf_op jit(solution)/shard_map/ppermute | solution.py:270
  617.6 55.3 %collective-permute-start.55 = (bf16[1,3072,128]{2,1,0:T(8,128)(2,1)}, bf16[1,3072,128]{2,1,0:T(8,128)(2,1)}, u32[]{:S(2)}, u32[]{:S(2)}) collective-permute-start(bf16[1,3072,128]{2,1,0:T(8,128)(2,1)} %reshape.2262.refs_0_), channel_id=1, source_target_pairs={{0,16},{1,17},{2,18},{3,19},{4,20},{5,21},{6,22},{7,23},{8,24},{9,... | collective-permute-start | bytes 2359304 | tf_op jit(solution)/shard_map/ppermute | solution.py:270
  619.5 53.4 %collective-permute-start.54 = (bf16[1,3072,128]{2,1,0:T(8,128)(2,1)}, bf16[1,3072,128]{2,1,0:T(8,128)(2,1)}, u32[]{:S(2)}, u32[]{:S(2)}) collective-permute-start(bf16[1,3072,128]{2,1,0:T(8,128)(2,1)} %reshape.2262.refs_0_), channel_id=1, source_target_pairs={{0,24},{1,25},{2,26},{3,27},{4,28},{5,29},{6,30},{7,31},{8,0},{9,1... | collective-permute-start | bytes 2359304 | tf_op jit(solution)/shard_map/ppermute | solution.py:270
  625.3 20.2 %collective-permute-start.60 = (bf16[512,1152]{1,0:T(8,128)(2,1)}, bf16[512,1152]{1,0:T(8,128)(2,1)}, u32[]{:S(2)}, u32[]{:S(2)}) collective-permute-start(bf16[512,1152]{1,0:T(8,128)(2,1)} %constant_dynamic-slice_fusion.39), channel_id=1, source_target_pairs={{0,1},{1,0},{2,3},{3,2},{4,5},{5,4},{6,7},{7,6},{8,9},{9,8},{10,11... | collective-permute-start | bytes 3538952 | tf_op jit(solution)/shard_map/ppermute | solution.py:270
  644.9 30.0 %collective-permute-start.57 = (bf16[1,3072,128]{2,1,0:T(8,128)(2,1)}, bf16[1,3072,128]{2,1,0:T(8,128)(2,1)}, u32[]{:S(2)}, u32[]{:S(2)}) collective-permute-start(bf16[1,3072,128]{2,1,0:T(8,128)(2,1)} %reshape.2262.refs_0_), channel_id=1, source_target_pairs={{0,2},{1,3},{2,0},{3,1},{4,6},{5,7},{6,4},{7,5},{8,10},{9,11},{10,... | collective-permute-start | bytes 2359304 | tf_op jit(solution)/shard_map/ppermute | solution.py:270
  649.3 42.1 %collective-permute-start.61 = (bf16[4,2,48,1536]{3,2,0,1:T(8,128)(2,1)S(1)}, bf16[4,2,48,1536]{3,2,0,1:T(8,128)(2,1)S(1)}, u32[]{:S(2)}, u32[]{:S(2)}) collective-permute-start(bf16[4,2,48,1536]{3,2,0,1:T(8,128)(2,1)S(1)} %fusion.27), channel_id=1, source_target_pairs={{0,2},{1,3},{2,0},{3,1},{4,6},{5,7},{6,4},{7,5},{8,10},{9,11},{10,... | collective-permute-start | bytes 3538952 | tf_op jit(solution)/shard_map/ppermute | solution.py:270
  652.2 22.8 %collective-permute-start.58 = (bf16[1,3072,128]{2,1,0:T(8,128)(2,1)}, bf16[1,3072,128]{2,1,0:T(8,128)(2,1)}, u32[]{:S(2)}, u32[]{:S(2)}) collective-permute-start(bf16[1,3072,128]{2,1,0:T(8,128)(2,1)} %reshape.2262.refs_0_), channel_id=1, source_target_pairs={{0,4},{1,5},{2,6},{3,7},{4,0},{5,1},{6,2},{7,3},{8,12},{9,13},{10,... | collective-permute-start | bytes 2359304 | tf_op jit(solution)/shard_map/ppermute | solution.py:270
  672.9 23.0 %collective-permute-start.64 = (bf16[1,3072,128]{2,1,0:T(8,128)(2,1)}, bf16[1,3072,128]{2,1,0:T(8,128)(2,1)S(1)}, u32[]{:S(2)}, u32[]{:S(2)}) collective-permute-start(bf16[1,3072,128]{2,1,0:T(8,128)(2,1)} %reshape.2262.refs_0_), channel_id=1, source_target_pairs={{0,1},{1,0},{2,3},{3,2},{4,5},{5,4},{6,7},{7,6},{8,9},{9,8},{10,11... | collective-permute-start | bytes 2359304 | tf_op jit(solution)/shard_map/ppermute | solution.py:270
  691.9 17.1 %collective-permute-start.76 = (bf16[4,48,1536]{2,1,0:T(8,128)(2,1)S(1)}, bf16[4,48,1536]{2,1,0:T(8,128)(2,1)S(1)}, u32[]{:S(2)}, u32[]{:S(2)}) collective-permute-start(bf16[4,48,1536]{2,1,0:T(8,128)(2,1)S(1)} %fusion.35), channel_id=1, source_target_pairs={{0,4},{1,5},{2,6},{3,7},{4,0},{5,1},{6,2},{7,3},{8,12},{9,13},{10,... | collective-permute-start | bytes 1769480 | tf_op jit(solution)/shard_map/ppermute | solution.py:270
  693.3 36.0 %collective-permute-start.69 = (bf16[3,3072,128]{2,1,0:T(8,128)(2,1)S(1)}, bf16[3,3072,128]{2,1,0:T(8,128)(2,1)}, u32[]{:S(2)}, u32[]{:S(2)}) collective-permute-start(bf16[3,3072,128]{2,1,0:T(8,128)(2,1)S(1)} %pad_maximum_fusion.2.refs_8_), channel_id=1, source_target_pairs={{0,1},{1,0},{2,3},{3,2},{4,5},{5,4},{6,7},{7,6},{8,9},{9,8},{10,11... | collective-permute-start | bytes 7077896 | tf_op jit(solution)/shard_map/ppermute | solution.py:270
  694.0 24.7 %collective-permute-start.65 = (bf16[1,3072,128]{2,1,0:T(8,128)(2,1)}, bf16[1,3072,128]{2,1,0:T(8,128)(2,1)}, u32[]{:S(2)}, u32[]{:S(2)}) collective-permute-start(bf16[1,3072,128]{2,1,0:T(8,128)(2,1)} %collective-permute-done.57.refs_2_), channel_id=1, source_target_pairs={{0,1},{1,0},{2,3},{3,2},{4,5},{5,4},{6,7},{7,6},{8,9},{9,8},{10,11... | collective-permute-start | bytes 2359304 | tf_op jit(solution)/shard_map/ppermute | solution.py:270
  694.5 24.2 %collective-permute-start.67 = (bf16[1,3072,128]{2,1,0:T(8,128)(2,1)}, bf16[1,3072,128]{2,1,0:T(8,128)(2,1)}, u32[]{:S(2)}, u32[]{:S(2)}) collective-permute-start(bf16[1,3072,128]{2,1,0:T(8,128)(2,1)} %collective-permute-done.58.refs_4_), channel_id=1, source_target_pairs={{0,2},{1,3},{2,0},{3,1},{4,6},{5,7},{6,4},{7,5},{8,10},{9,11},{10,... | collective-permute-start | bytes 2359304 | tf_op jit(solution)/shard_map/ppermute | solution.py:270
  695.9 70.9 %collective-permute-start.62 = (bf16[3,3072,128]{2,1,0:T(8,128)(2,1)S(1)}, bf16[3,3072,128]{2,1,0:T(8,128)(2,1)}, u32[]{:S(2)}, u32[]{:S(2)}) collective-permute-start(bf16[3,3072,128]{2,1,0:T(8,128)(2,1)S(1)} %pad_maximum_fusion.2.refs_8_), channel_id=1, source_target_pairs={{0,2},{1,3},{2,0},{3,1},{4,6},{5,7},{6,4},{7,5},{8,10},{9,11},{10,... | collective-permute-start | bytes 7077896 | tf_op jit(solution)/shard_map/ppermute | solution.py:270
  708.9 57.9 %collective-permute-start.63 = (bf16[3,3072,128]{2,1,0:T(8,128)(2,1)S(1)}, bf16[3,3072,128]{2,1,0:T(8,128)(2,1)}, u32[]{:S(2)}, u32[]{:S(2)}) collective-permute-start(bf16[3,3072,128]{2,1,0:T(8,128)(2,1)S(1)} %pad_maximum_fusion.2.refs_8_), channel_id=1, source_target_pairs={{0,4},{1,5},{2,6},{3,7},{4,0},{5,1},{6,2},{7,3},{8,12},{9,13},{10,... | collective-permute-start | bytes 7077896 | tf_op jit(solution)/shard_map/ppermute | solution.py:270
  725.3 45.5 %collective-permute-start.79 = (f32[48,4608]{1,0:T(8,128)}, f32[48,4608]{1,0:T(8,128)S(1)}, u32[]{:S(2)}, u32[]{:S(2)}) collective-permute-start(f32[48,4608]{1,0:T(8,128)} %get-tuple-element.220), channel_id=1, source_target_pairs={{0,24},{1,25},{2,26},{3,27},{4,28},{5,29},{6,30},{7,31},{8,0},{9,1... | collective-permute-start | bytes 2654216 | tf_op jit(solution)/shard_map/ppermute | solution.py:270
  729.2 75.4 %collective-permute-start.78 = (f32[48,4608]{1,0:T(8,128)}, f32[48,4608]{1,0:T(8,128)}, u32[]{:S(2)}, u32[]{:S(2)}) collective-permute-start(f32[48,4608]{1,0:T(8,128)} %get-tuple-element.221), channel_id=1, source_target_pairs={{0,16},{1,17},{2,18},{3,19},{4,20},{5,21},{6,22},{7,23},{8,24},{9,... | collective-permute-start | bytes 2654216 | tf_op jit(solution)/shard_map/ppermute | solution.py:270
  729.3 75.4 %collective-permute-start.77 = (f32[48,4608]{1,0:T(8,128)}, f32[48,4608]{1,0:T(8,128)}, u32[]{:S(2)}, u32[]{:S(2)}) collective-permute-start(f32[48,4608]{1,0:T(8,128)} %get-tuple-element.219), channel_id=1, source_target_pairs={{0,8},{1,9},{2,10},{3,11},{4,12},{5,13},{6,14},{7,15},{8,16},{9,17... | collective-permute-start | bytes 2654216 | tf_op jit(solution)/shard_map/ppermute | solution.py:270
  768.3 40.9 %collective-permute-start.72 = (bf16[2,3072,128]{2,1,0:T(8,128)(2,1)S(1)}, bf16[2,3072,128]{2,1,0:T(8,128)(2,1)}, u32[]{:S(2)}, u32[]{:S(2)}) collective-permute-start(bf16[2,3072,128]{2,1,0:T(8,128)(2,1)S(1)} %slice.237), channel_id=1, source_target_pairs={{0,4},{1,5},{2,6},{3,7},{4,0},{5,1},{6,2},{7,3},{8,12},{9,13},{10,... | collective-permute-start | bytes 4718600 | tf_op jit(solution)/shard_map/ppermute | solution.py:270
  770.7 61.5 %collective-permute-start.70 = (bf16[3,3072,128]{2,1,0:T(8,128)(2,1)}, bf16[3,3072,128]{2,1,0:T(8,128)(2,1)S(1)}, u32[]{:S(2)}, u32[]{:S(2)}) collective-permute-start(bf16[3,3072,128]{2,1,0:T(8,128)(2,1)} %collective-permute-done.62.refs_0_), channel_id=1, source_target_pairs={{0,1},{1,0},{2,3},{3,2},{4,5},{5,4},{6,7},{7,6},{8,9},{9,8},{10,11... | collective-permute-start | bytes 7077896 | tf_op jit(solution)/shard_map/ppermute | solution.py:270
  770.7 61.5 %collective-permute-start.71 = (bf16[3,3072,128]{2,1,0:T(8,128)(2,1)}, bf16[3,3072,128]{2,1,0:T(8,128)(2,1)}, u32[]{:S(2)}, u32[]{:S(2)}) collective-permute-start(bf16[3,3072,128]{2,1,0:T(8,128)(2,1)} %collective-permute-done.63.refs_2_), channel_id=1, source_target_pairs={{0,1},{1,0},{2,3},{3,2},{4,5},{5,4},{6,7},{7,6},{8,9},{9,8},{10,11... | collective-permute-start | bytes 7077896 | tf_op jit(solution)/shard_map/ppermute | solution.py:270
  808.5 19.0 %collective-permute-start.74 = (bf16[1,3072,128]{2,1,0:T(8,128)(2,1)}, bf16[1,3072,128]{2,1,0:T(8,128)(2,1)}, u32[]{:S(2)}, u32[]{:S(2)}) collective-permute-start(bf16[1,3072,128]{2,1,0:T(8,128)(2,1)} %slice.238), channel_id=1, source_target_pairs={{0,2},{1,3},{2,0},{3,1},{4,6},{5,7},{6,4},{7,5},{8,10},{9,11},{10,... | collective-permute-start | bytes 2359304 | tf_op jit(solution)/shard_map/ppermute | solution.py:270
  809.2 23.0 %collective-permute-start.73 = (bf16[2,3072,128]{2,1,0:T(8,128)(2,1)}, bf16[2,3072,128]{2,1,0:T(8,128)(2,1)}, u32[]{:S(2)}, u32[]{:S(2)}) collective-permute-start(bf16[2,3072,128]{2,1,0:T(8,128)(2,1)} %collective-permute-done.72.refs_4_), channel_id=1, source_target_pairs={{0,1},{1,0},{2,3},{3,2},{4,5},{5,4},{6,7},{7,6},{8,9},{9,8},{10,11... | collective-permute-start | bytes 4718600 | tf_op jit(solution)/shard_map/ppermute | solution.py:270
  812.7 16.5 %collective-permute-start.80 = (f32[24,3072]{1,0:T(8,128)}, f32[24,3072]{1,0:T(8,128)}, u32[]{:S(2)}, u32[]{:S(2)}) collective-permute-start(f32[24,3072]{1,0:T(8,128)} %dynamic-slice_bitcast_fusion.7), channel_id=1, source_target_pairs={{0,1},{1,0},{2,3},{3,2},{4,5},{5,4},{6,7},{7,6},{8,9},{9,8},{10,11... | collective-permute-start | bytes 884744 | tf_op jit(solution)/shard_map/ppermute | solution.py:270
  871.3 14.1 %collective-permute-start.84 = (f32[2]{0:T(128)S(1)}, f32[2]{0:T(128)S(1)}, u32[]{:S(2)}, u32[]{:S(2)}) collective-permute-start(f32[2]{0:T(128)S(1)} %fusion.227), channel_id=1, source_target_pairs={{0,4},{1,5},{2,6},{3,7},{4,0},{5,1},{6,2},{7,3},{8,12},{9,13},{10,... | collective-permute-start | bytes 32 | tf_op jit(solution)/shard_map/ppermute | solution.py:270
  (192 other events, 2409.7 us)
Sparse Core Ops, SparseCore 0:
  11.5 61.4 all-gather.6
  76.5 61.8 all-gather.8
  141.8 53.5 all-gather.10
  198.7 66.9 all-gather.12
  269.0 67.5 all-gather.14
  626.2 83.7 all-gather.16

commit v3 on v2

--- a/solution.py
+++ b/solution.py
@@ -302,15 +302,37 @@
     return lax.dynamic_index_in_dim(blocks, bit, place, False), hop(far, dq=1 << axis)
 
 
-def reduce_line(blocks):
-    lines = blocks.shape[0]
+def gather_line(value):
+    lines = lax.axis_size("dp") // PLANE
     line = lax.axis_index("dp") // PLANE
-    total = lax.dynamic_index_in_dim(blocks, line, 0, False)
-    for d in range(1, lines):
-        total = total + hop(
-            lax.dynamic_index_in_dim(blocks, (line + d) % lines, 0, False), dl=d
-        )
-    return total
+
+    def pass_on(x, way, k):
+        pairs = []
+        for l in range(lines):
+            if 0 <= l - way * (k - 1) < lines and 0 <= l + way < lines:
+                for q in range(PLANE):
+                    pairs.append((l * PLANE + q, (l + way) * PLANE + q))
+        return lax.ppermute(x, "dp", pairs)
+
+    before, after = [value], [value]
+    for k in range(1, lines):
+        before.append(pass_on(before[-1], 1, k))
+        after.append(pass_on(after[-1], -1, k))
+    return jnp.concatenate(
+        [jnp.where(line + d < lines, after[d], before[lines - d]) for d in range(1, lines)], 0
+    )
+
+
+def block_at(blocks, shift):
+    line = lax.axis_index("dp") // PLANE
+    return lax.dynamic_index_in_dim(blocks, jnp.mod(line + shift, blocks.shape[0]), 0, False)
+
+
+def reduce_step(blocks, sums, reach):
+    to_right, to_left = block_at(blocks, reach), block_at(blocks, -reach)
+    if sums is not None:
+        to_right, to_left = to_right + sums[0], to_left + sums[1]
+    return step_line(to_right, 1, reach), step_line(to_left, -1, reach)
 
 
 def join_cores(parts):
@@ -399,12 +421,14 @@
     )(idx, mix, *pieces)
 
 
-def spread_kernel(cnt_ref, row_ref, pos_ref, mix_ref, *refs, groups, arrays, last):
+def spread_kernel(cnt_ref, row_ref, pos_ref, mix_ref, *refs, groups, arrays, first, last):
     sources = refs[:arrays]
+    refs = list(refs[arrays:])
+    total_in = None if first else refs.pop(0)
     if last:
-        total_in, head_ref, out_ref, sq_ref, total, rows32, stage, sem, total_sem = refs[arrays:]
-    else:
-        total, rows32, stage, sem = refs[arrays:]
+        head_ref, out_ref, sq_ref = refs[:3]
+        refs = refs[3:]
+    total, rows32, stage, sem, total_sem = refs
     length = sources[0].shape[1]
     blocks = [source.at[k] for source in sources for k in range(source.shape[0])]
     n = len(blocks)
@@ -413,7 +437,7 @@
         return pltpu.make_async_copy(blocks[k], stage.at[k % 2], sem.at[k % 2])
 
     copy(0).start()
-    if last:
+    if not first:
         load = pltpu.make_async_copy(total_in, total, total_sem)
         load.start()
         load.wait()
@@ -471,7 +495,7 @@
     groups = width // LANES
     length = sources[0].shape[1]
     total_rows = -(-vocab * 8 // 64) * 64
-    last = total is not None
+    first, last = total is None, head is not None
     smem = pl.BlockSpec(memory_space=pltpu.SMEM)
     vmem = pl.BlockSpec(memory_space=pltpu.VMEM)
     hbm = pl.BlockSpec(memory_space=pl.ANY)
@@ -480,16 +504,17 @@
         pltpu.VMEM((2, length, LANES), bf16),
         pltpu.SemaphoreType.DMA((2,)),
     ]
+    extra_specs, extra = ([], []) if first else ([hbm], [total])
+    scratch.append(pltpu.SemaphoreType.DMA)
     if last:
-        extra_specs, extra = [hbm, vmem], [total, head]
+        extra_specs, extra = extra_specs + [vmem], extra + [head]
         out_specs = [vmem, vmem]
         out_shape = [
             jax.ShapeDtypeStruct((vocab, width), f32),
             jax.ShapeDtypeStruct((8, LANES), f32),
         ]
-        scratch = [pltpu.VMEM((total_rows, LANES), f32)] + scratch + [pltpu.SemaphoreType.DMA]
+        scratch = [pltpu.VMEM((total_rows, LANES), f32)] + scratch
     else:
-        extra_specs, extra = [], []
         out_specs = vmem
         out_shape = jax.ShapeDtypeStruct((total_rows, LANES), f32)
     entries = sum(source.shape[0] for source in sources) * lists[1].shape[1] // 2
@@ -498,6 +523,7 @@
             spread_kernel,
             groups=groups,
             arrays=len(sources),
+            first=first,
             last=last,
         ),
         in_specs=[smem] * 4 + [hbm] * len(sources) + extra_specs,
@@ -562,6 +588,23 @@
     groups = width // LANES
     swaps = [(dq, dr) for dq in range(PLANE) for dr in range(reps)]
 
+    def gather(value, axis=0):
+        return lax.all_gather(value.astype(bf16), BOTH, axis=axis, tiled=True)
+
+    few = mod_proj.shape[0]
+    gains_flat = norm_gains.reshape(-1)
+    gains_flat = jnp.pad(gains_flat, (0, few * LANES - gains_flat.size))
+    small_all = gather(
+        jnp.concatenate(
+            [mod_proj, final_proj, time_proj.reshape(few, -1), gains_flat.reshape(few, LANES)], 1
+        )
+    )
+    wide_all = gather(jnp.concatenate([attn_proj, out_proj, up_proj], 1))
+    down_w = gather(down_proj)
+    qkv_w = wide_all[:, : 3 * width]
+    out_w = wide_all[:, 3 * width : 4 * width]
+    up_w = wide_all[:, 4 * width :]
+
     padded = -(-vocab // 16) * 16
     table_low = jnp.pad(vocab_table.astype(bf16), ((0, padded - vocab), (0, 0)))
     cut = padded // 32 * 16
@@ -577,7 +620,12 @@
     names = (owner * padded + offset).astype(f32).reshape(-1, LANES)
     packed = jnp.concatenate([names, mixing.reshape(-1, LANES)], 0)
     on_line = jnp.stack([packed] + [hop(packed, dl=-d) for d in range(1, lines)])
-    on_line, first, second = lax.optimization_barrier((on_line, first, second))
+    on_line, owner, offset = lax.optimization_barrier((on_line, owner, offset))
+    cap = max(2, 2 * half * cands // devices)
+    member = (owner[:, None] == jnp.arange(devices, dtype=jnp.int32)[None, :]).astype(jnp.int32)
+    slot = jnp.sum((jnp.cumsum(member, 0) - member) * member, 1)
+    flat_slot = owner * cap + slot
+    first, second, flat_slot = lax.optimization_barrier((first, second, flat_slot))
     first[3] = hop(first[1], dq=2)
     second[3] = hop(second[2], dq=1)
     pieces = []
@@ -606,20 +654,13 @@
             parts[d] = out[k, : half * groups]
 
     mix_some((1, lines - 1))
+    far_parts = [hop(parts[d].astype(bf16), dl=d) for d in (1, lines - 1)]
     mix_some(tuple(range(2, lines - 1)) + (0,))
-    ahead = back = None
-    for d in range(lines - 1, 0, -1):
-        to_right = parts[d] if ahead is None else parts[d] + ahead
-        to_left = parts[lines - d] if back is None else parts[lines - d] + back
-        ahead = step_line(to_right, 1, d)
-        back = step_line(to_left, -1, d)
-        if d == lines - 1:
-            ahead, back, owner, offset = lax.optimization_barrier((ahead, back, owner, offset))
-
-    cap = max(2, 2 * half * cands // devices)
-    member = (owner[:, None] == jnp.arange(devices, dtype=jnp.int32)[None, :]).astype(jnp.int32)
-    slot = jnp.sum((jnp.cumsum(member, 0) - member) * member, 1)
-    flat_slot = owner * cap + slot
+    for d in range(2, lines - 1):
+        far_parts.append(hop(parts[d].astype(bf16), dl=d))
+    far_parts[:2], flat_slot, small_all = lax.optimization_barrier(
+        (far_parts[:2], flat_slot, small_all)
+    )
     entry = offset * half + jnp.arange(half * cands, dtype=jnp.int32) // cands + 1
     empty = jnp.zeros((devices * cap,), f32)
     lists = [
@@ -627,30 +668,15 @@
         for value in (entry.astype(f32), mixing.reshape(-1))
     ]
     asked = jnp.concatenate(lists, 1)
-    ahead, back, asked = lax.optimization_barrier((ahead, back, asked))
-    x0 = (parts[0] + ahead + back).reshape(half, width)
-
-    def gather(value, axis=0):
-        return lax.all_gather(value.astype(bf16), BOTH, axis=axis, tiled=True)
-
-    small = (time_proj, mod_proj, final_proj, norm_gains)
-    flat = jnp.concatenate([value.reshape(-1) for value in small])
-    flat = jnp.pad(flat, (0, -flat.size % (8 * LANES))).reshape(1, -1, LANES)
-    small_all = gather(flat).reshape(devices, -1)
-    qkv_w = gather(attn_proj)
-    out_w = gather(out_proj)
-    up_w = gather(up_proj)
-    down_w = gather(down_proj)
-    unpacked = []
-    at = 0
-    for value in small:
-        part = small_all[:, at : at + value.size].astype(f32).reshape((devices,) + value.shape)
-        unpacked.append(part)
-        at += value.size
-    time_f = unpacked[0].reshape(-1, time_proj.shape[1])
-    mod_f = unpacked[1].reshape(-1, mod_proj.shape[1])
-    final_f = unpacked[2].reshape(-1, final_proj.shape[1])
-    gain_f = unpacked[3].transpose(1, 0, 2).reshape(norm_gains.shape[0], width)
+    far_parts, asked = lax.optimization_barrier((far_parts, asked))
+    x0 = (parts[0] + sum(far.astype(f32) for far in far_parts)).reshape(half, width)
+
+    mod_f = small_all[:, : 6 * width].astype(f32)
+    final_f = small_all[:, 6 * width : 8 * width].astype(f32)
+    time_f = small_all[:, 8 * width : -LANES].astype(f32).reshape(-1, time_proj.shape[1])
+    gain_f = small_all[:, -LANES:].astype(f32).reshape(devices, -1)[:, : norm_gains.size]
+    gain_f = gain_f.reshape((devices,) + norm_gains.shape)
+    gain_f = gain_f.transpose(1, 0, 2).reshape(norm_gains.shape[0], width)
 
     length = lax.dynamic_slice_in_dim(seq_lengths, dp_idx, 1)
     feats = time_features(time_index, time_f.shape[0])
@@ -673,7 +699,7 @@
     attended = (query, keyed, hop(keyed, dr=1), valued, hop(valued, dr=1))
     core = rep_idx.reshape(1)
     mixed_b, lse_att = attend(length, core, *attended)
-    asked = lax.all_to_all(asked, BOTH, split_axis=0, concat_axis=0, tiled=True)
+    mixed_b, h1_far = lax.optimization_barrier((mixed_b, hop(h1b, dr=1)))
     attn = dense(mixed_b, out_w)
     x1 = x0 + g1 * attn
     n2, r2 = normalize(x1)
@@ -681,6 +707,9 @@
     upper = dense(h2b, up_w)
     act, gelu_back = jax.vjp(lambda u: jax.nn.gelu(u, approximate=True), upper)
     act_b = act.astype(bf16)
+    act_b, mixed_far, h2_far = lax.optimization_barrier(
+        (act_b, hop(mixed_b, dr=1), hop(h2b, dr=1))
+    )
     mlp = dense(act_b, down_w)
     x2 = x1 + g2 * mlp
     nf, rf = normalize(x2)
@@ -712,10 +741,11 @@
     weight = of_line(weight_all, chip, rep_idx).reshape(-1)
     my_pick = lax.dynamic_slice(loss_pick, (dp_idx, rep_idx, 0), (1, 1, picks)).reshape(picks)
     spread = (jnp.arange(half, dtype=jnp.int32)[:, None] == my_pick[None, :]).astype(f32)
-    final, asked = lax.optimization_barrier((final, asked))
-    asked, asked_mix = asked[:, :cap].astype(jnp.int32), asked[:, cap:]
     rows_b = jnp.take(final, my_pick, axis=0).astype(bf16)
     every = jnp.concatenate([rows_b] + [hop(rows_b, dl=-d) for d in range(1, lines)], 0)
+    asked = lax.all_to_all(asked, BOTH, split_axis=0, concat_axis=0, tiled=True)
+    every, act_far, asked = lax.optimization_barrier((every, hop(act_b, dr=1), asked))
+    asked, asked_mix = asked[:, :cap].astype(jnp.int32), asked[:, cap:]
     plane_table = jnp.concatenate(pieces, 0)
     logits = dense_nt(every, plane_table)
     column = jnp.arange(plane_table.shape[0], dtype=jnp.int32)
@@ -749,12 +779,16 @@
     for d in range(1, lines):
         drows = drows + hop(drows_part[d], dl=d)
     every, lse, drows = lax.optimization_barrier((every, lse, drows))
-    lse_x, lse_y = hop(lse, dq=1), hop(lse, dq=2)
-    every_x, every_y = hop(every, dq=1), hop(every, dq=2)
-    lse_plane = jnp.stack([lse, lse_x, lse_y, hop(lse_x, dq=2)])
-    rows_plane = jnp.stack([every, every_x, every_y, hop(every_x, dq=2)])
-    lse_all = jnp.concatenate([lse_plane, hop(lse_plane, dr=1)], 0).reshape(-1)
-    rows_all = jnp.concatenate([rows_plane, hop(rows_plane, dr=1)], 0).reshape(-1, width)
+    pieces_of_lse = []
+    for _ in range(3):
+        rounded = lax.reduce_precision(lse, 8, 7)
+        pieces_of_lse.append(rounded.astype(bf16))
+        lse = lse - rounded
+    extra = jnp.pad(jnp.stack(pieces_of_lse, 1), ((0, 0), (0, LANES - 3)))
+    told = jnp.concatenate([every, extra], 1)
+    told_x, told_y = hop(told, dq=1), hop(told, dq=2)
+    told = jnp.stack([told, told_x, told_y, hop(told_x, dq=2)])
+    told = jnp.concatenate([told, hop(told, dr=1)], 0).reshape(-1, width + LANES)
     among = [(chip ^ dq, rep_idx ^ dr) for dr in range(reps) for dq in range(PLANE)]
     targets_all = jnp.concatenate([of_line(loss_target, q, r).reshape(-1) for q, r in among])
     weight_rows = jnp.concatenate([of_line(weight_all, q, r).reshape(-1) for q, r in among])
@@ -763,20 +797,18 @@
     dx2, dfsh, dfsc, dgain_f = modulate_back(grad_final, nf, rf, gain_f[2], fsc)
     dg2 = jnp.sum(dx2 * mlp, 0)
     dmlp = (dx2 * g2).astype(bf16)
-    g_down = chip_product(act_b, hop(act_b, dr=1), dmlp)
+    g_down = chip_product(act_b, act_far, dmlp)
     dupper = gelu_back(dense_nt(dmlp, down_w))[0].astype(bf16)
-    g_up = chip_product(h2b, hop(h2b, dr=1), dupper)
+    g_up = chip_product(h2b, h2_far, dupper)
     dh2 = dense_nt(dupper, up_w)
     dn2x, dsh2, dsc2, dgain_2 = modulate_back(dh2, n2, r2, gain_f[1], sc2)
     dx1 = dx2 + dn2x
     dg1 = jnp.sum(dx1 * attn, 0)
     dattn = (dx1 * g1).astype(bf16)
-    dattn, g_down, g_up, rows_all, lse_all = lax.optimization_barrier(
-        (dattn, g_down, g_up, rows_all, lse_all)
-    )
+    dattn, g_down, g_up = lax.optimization_barrier((dattn, g_down, g_up))
     down_1 = split_blocks(plane_blocks(g_down), 1, 1)
     up_1 = split_blocks(plane_blocks(g_up), 0, 2)
-    g_out = chip_product(mixed_b, hop(mixed_b, dr=1), dattn)
+    g_out = chip_product(mixed_b, mixed_far, dattn)
     dmixed = dense_nt(dattn, out_w).astype(bf16)
     dquery, dkey, dkey_far, dvalue, dvalue_far = attend_back(
         length, core, *attended, lse_att, dmixed, *turns
@@ -792,23 +824,35 @@
     dh1 = dense_nt(dqkv, qkv_w)
     dn1x, dsh1, dsc1, dgain_1 = modulate_back(dh1, n1, r1, gain_f[0], sc1)
     dx0 = dx1 + dn1x
-    g_qkv = chip_product(h1b, hop(h1b, dr=1), dqkv)
+    g_qkv = chip_product(h1b, h1_far, dqkv)
 
 
     dx0_b = dx0.astype(bf16).reshape(1, half * groups, LANES)
-    dx0_b, rows_all, lse_all, down_2, up_2 = lax.optimization_barrier(
-        (dx0_b, rows_all, lse_all, down_2, up_2)
-    )
+    dx0_b, down_2, up_2 = lax.optimization_barrier((dx0_b, down_2, up_2))
     others = lines - 1
     cut = -(-2 * others // 3)
-    on_line = jnp.concatenate([hop(dx0_b, dl=-d) for d in range(1, lines)], 0)
+    sums_here = jnp.concatenate(
+        [dsh1, dsc1, dg1, dsh2, dsc2, dg2, dfsh, dfsc, dgain_1, dgain_2, dgain_f]
+    )
+    on_line = gather_line(dx0_b)
     own_x, own_y = hop(dx0_b, dq=1), hop(dx0_b, dq=2)
+    own_xy = hop(own_y, dq=1)
     g_last = jnp.concatenate([g_qkv, g_out], 1)
-    last_1 = split_blocks(plane_blocks(g_last), 0, 2)
-    on_line, own_x, own_y, last_1 = lax.optimization_barrier((on_line, own_x, own_y, last_1))
-    last_2 = split_blocks(last_1[0] + last_1[1].astype(f32), 1, 1)
-    own_xy = hop(own_y, dq=1)
+    last_1 = split_blocks(plane_blocks(g_last), 1, 1)
+    sums_all = lax.all_gather(sums_here.reshape(1, -1, LANES), BOTH, axis=0, tiled=True)
+    last_2 = split_blocks(last_1[0] + last_1[1].astype(f32), 0, 1)
+    on_line, own_x, own_y, own_xy, last_2, told, sums_all = lax.optimization_barrier(
+        (on_line, own_x, own_y, own_xy, last_2, told, sums_all)
+    )
+    rows_all = told[:, :width]
+    lse_all = jnp.sum(told[:, width : width + 3].astype(f32), 1)
     line_x, line_y = hop(on_line, dq=1), hop(on_line, dq=2)
+    shards = [two[0] + two[1].astype(f32) for two in (down_2, up_2, last_2)]
+    both = shards[1].shape[1]
+    tall = shards[0].shape[1] // both
+    pile = shards[0].reshape(lines, tall, both, -1)
+    blocks = jnp.concatenate([pile[:, k] for k in range(tall)] + shards[1:], 2)
+    sums = reduce_step(blocks, None, lines - 1)
     early = [(dx0_b, 0, 0), (own_x, 1, 0), (own_y, 2, 0), (own_xy, 3, 0), (on_line, 0, 1)]
     order = []
 
@@ -841,14 +885,27 @@
     sources = from_cores(early)
     begun = spread_rows(lists_of(order), sources, vocab, width)
     order.clear()
-    line_x, line_y, begun = lax.optimization_barrier((line_x, line_y, begun))
-    shards = [two[0] + two[1].astype(f32) for two in (down_2, up_2, last_2)]
-    both = shards[1].shape[1]
-    tall = shards[0].shape[1] // both
-    pile = shards[0].reshape(lines, tall, both, -1)
-    total = reduce_line(
-        jnp.concatenate([pile[:, k] for k in range(tall)] + shards[1:], 2)
-    )
+    logits_mine = dense_nt(rows_all, table_low)
+    own_column = jnp.where(targets_all // vocab == me, targets_all % vocab, -1)
+    hit_mine = jnp.arange(padded, dtype=jnp.int32)[None, :] == own_column[:, None]
+    dlogit_mine = (
+        (weight_rows / coefficient_aggregate)[:, None]
+        * (jnp.exp(logits_mine - lse_all[:, None]) - hit_mine.astype(f32))
+    ).astype(bf16)
+    head_grad = dense_tn(dlogit_mine, rows_all)
+    line_x, line_y, begun, head_grad, sums = lax.optimization_barrier(
+        (line_x, line_y, begun, head_grad, sums)
+    )
+    for d in range(lines - 2, 1, -1):
+        sums = reduce_step(blocks, sums, d)
+    near = hop(line_x[:cut], dq=2)
+    rest = [hop(line_y[cut:], dq=1)] if cut < others else []
+    sources = from_cores([(line_x, 1, 1), (line_y, 2, 1)])
+    begun = spread_rows(lists_of(order), sources, vocab, width, begun)
+    order.clear()
+    near, rest, begun, sums = lax.optimization_barrier((near, rest, begun, sums))
+    sums = reduce_step(blocks, sums, 1)
+    total = block_at(blocks, 0) + sums[0] + sums[1]
     down_end = tall * pile.shape[3]
     pile = jnp.stack(jnp.split(total[:, :down_end], tall, 1))
     d_down = jnp.concatenate(join_cores(pile.reshape(reps, -1, pile.shape[2])), 1)
@@ -860,26 +917,11 @@
         joined.append(jnp.concatenate([left[:, part], right[:, part]], 1))
         at += columns // 2
     d_up, d_qkv, d_out = joined
-    late = [(line_x, 1, 1), (line_y, 2, 1), (hop(line_x[:cut], dq=2), 3, 1)]
-    if cut < others:
-        late.append((hop(line_y[cut:], dq=1), 3, 1 + cut))
-    logits_mine = dense_nt(rows_all, table_low)
-    own_column = jnp.where(targets_all // vocab == me, targets_all % vocab, -1)
-    hit_mine = jnp.arange(padded, dtype=jnp.int32)[None, :] == own_column[:, None]
-    dlogit_mine = (
-        (weight_rows / coefficient_aggregate)[:, None]
-        * (jnp.exp(logits_mine - lse_all[:, None]) - hit_mine.astype(f32))
-    ).astype(bf16)
-    head_grad = dense_tn(dlogit_mine, rows_all)
-    sources = from_cores(late)
+    sources = from_cores([(near, 3, 1)] + [(value, 3, 1 + cut) for value in rest])
     table_grad, table_squares = spread_rows(
         lists_of(order), sources, vocab, width, begun, head_grad
     )
 
-    sums_here = jnp.concatenate(
-        [dsh1, dsc1, dg1, dsh2, dsc2, dg2, dfsh, dfsc, dgain_1, dgain_2, dgain_f]
-    )
-    sums_all = lax.all_gather(sums_here.reshape(1, -1, LANES), BOTH, axis=0, tiled=True)
     sums_all = sums_all.reshape(n_dp, reps, -1).sum(1)
     dmods = sums_all[:, : 6 * width]
     dfmods = sums_all[:, 6 * width : 8 * width]

time: 940 us -> 850 us (0.904)
  waiting for transfers between devices: 227 us -> 163 us
  local copies, waits for them, and re-layouts: 157 us -> 129 us
    ppermute x83 -> x76, waiting for transfers between devices: 198 us -> 111 us  [hop(): return lax.ppermute(x, BOTH, pairs)]
    ppermute x0 -> x6, waiting for transfers between devices: none -> 38.4 us  [pass_on(): return lax.ppermute(x, 'dp', pairs)]
    ppermute x6, starting transfers between devices: 28.6 us -> 13.1 us  [step_line(): return lax.ppermute(x, 'dp', pairs)]
    another operation x8 -> x14, other arithmetic: 13.4 us -> 26.2 us
    ppermute x0 -> x6, starting transfers between devices: none -> 12.3 us  [pass_on(): return lax.ppermute(x, 'dp', pairs)]
    slice x10 -> x7, local copies, waits for them, and re-layouts: 16.7 us -> 5.53 us  [the longest x1 2.65 us: local(): near = hop(line_x[:cut], dq=2)]
    ppermute x6, waiting for transfers between devices: 24.7 us -> 13.9 us  [step_line(): return lax.ppermute(x, 'dp', pairs)]
    ppermute x83 -> x76, starting transfers between devices: 79.7 us -> 70.6 us  [hop(): return lax.ppermute(x, BOTH, pairs)]
  transfers between devices with their start and end apart: 96 -> 93, of which waited for: 28 -> 26; matrix products, arithmetic and copies ran while one was open for 38% -> 35% of each run, Pallas kernels for 13% -> 17%
where the time goes in v3:
time: 850 us; the launch traced here: 839 us
  waiting for transfers between devices  163 us (19%)
  Pallas kernels  161 us (19%)
  other arithmetic  131 us (15%)
  local copies, waits for them, and re-layouts  129 us (15%)
  matrix products  121 us (14%)
  starting transfers between devices  109 us (13%)
  between operations  25.1 us (3%)
    ppermute x76, waiting for transfers between devices, hop(): return lax.ppermute(x, BOTH, pairs)  111 us
    ppermute x76, starting transfers between devices, hop(): return lax.ppermute(x, BOTH, pairs)  70.6 us
    pallas_call x3, Pallas kernels, spread_rows(): pl.pallas_call(functools.partial(spread_kernel, groups=groups, arrays=len...  55.7 us
    pallas_call x2, Pallas kernels, mix_rows(): pl.pallas_call(functools.partial(mix_kernel, groups=groups, cands=cands,...  54.4 us
    unnamed x298, local copies, waits for them, and re-layouts  50 us
    dot_general x5, matrix products, dense(): return jnp.dot(a, b, preferred_element_type=f32)  39.1 us
    ppermute x6, waiting for transfers between devices, pass_on(): return lax.ppermute(x, 'dp', pairs)  38.4 us
    dot_general x9, matrix products, dense_tn(): lax.dot_general(a, b, (((0,), (0,)), ((), ())), preferred_element_type=f32)  34.6 us
  transfers between devices with their start and end apart: 93, of which 26 were waited for; matrix products, arithmetic and copies ran while one was open for 35% of the time, Pallas kernels for 17%

profile of v3, /device:TPU:0, one launch (start us, length us, event | category | flops | bytes accessed | tf_op | source)
XLA Modules:
  0.0 839.3 jit_solution(12833764391212905010)
XLA Ops:
  18.0 5.0 collective-permute-start
  24.0 2.6 convert_element_type.210
  40.7 2.9 fusion.80
  56.8 16.3 %reduce-window.6 = s32[32,32,128]{2,1,0:T(8,128)S(1)} reduce-window(s32[32,32,128]{2,1,0:T(8,128)} %fusion.54, s32[]{:T(128)} %constant.670.clone.1), window={size=1x1x128 pad=0_0x0_0x127_0}, to_apply=%region_2.3 | reduce-window | flops 16646144 | bytes 1048580 | tf_op jit(solution)/shard_map/reduce-window
  74.7 12.2 %collective-permute-done.3.refs_4_ = bf16[784,768]{1,0:T(8,128)(2,1)} collective-permute-done((bf16[784,768]{1,0:T(8,128)(2,1)S(1)}, bf16[784,768]{1,0:T(8,128)(2,1)}, u32[]{:S(2)}, u32[]{:S(2)}) %collective-permute-start.3) | collective-permute-done | bytes 1204256 | tf_op jit(solution)/shard_map/ppermute | solution.py:270
  87.9 2.7 collective-permute-start.13
  95.7 26.4 %collective-permute-done.13.refs_12_ = bf16[784,768]{1,0:T(8,128)(2,1)S(1)} collective-permute-done((bf16[784,768]{1,0:T(8,128)(2,1)}, bf16[784,768]{1,0:T(8,128)(2,1)S(1)}, u32[]{:S(2)}, u32[]{:S(2)}) %collective-permute-start.13) | collective-permute-done | bytes 1204256 | tf_op jit(solution)/shard_map/ppermute | solution.py:270
  122.1 6.7 collective-permute-done.14.refs_13_
  134.9 27.1 %shard_map.554 = f32[2,3080,128]{2,1,0:T(8,128)} custom-call(s32[2,1,4096]{2,1,0:T(1,128)} %pad_add_fusion.1.idx_ref, f32[2,1,4096]{2,1,0:T(1,128)} %pad_maximum_fusion.17.mix_ref, bf16[784,768]{1,0:T(8,128)(2,1)} %copy-done.16, bf16[800,768]{1,0:T(8,128)(2,1)} %copy-done.14, bf16[784,768]{1,0:T(8,128)(2,1)} %collective-permute-done.7.refs_2_, ...), custom_call_target="tpu_custom_call" | custom-call | flops 16777216 | bytes 41943040 | tf_op jit(solution)/shard_map/pallas_call | solution.py:405
  169.4 27.2 %shard_map.553 = f32[2,3080,128]{2,1,0:T(8,128)} custom-call(s32[2,1,4096]{2,1,0:T(1,128)} %pad_add_fusion.idx_ref, f32[2,1,4096]{2,1,0:T(1,128)} %pad_maximum_fusion.16.mix_ref, bf16[784,768]{1,0:T(8,128)(2,1)} %copy-done.16, bf16[800,768]{1,0:T(8,128)(2,1)} %copy-done.14, bf16[784,768]{1,0:T(8,128)(2,1)} %collective-permute-done.7.refs_2_, ...), custom_call_target="tpu_custom_call" | custom-call | flops 16777216 | bytes 41943040 | tf_op jit(solution)/shard_map/pallas_call | solution.py:405
  205.0 2.7 reshape.2361
  207.8 15.5 %scatter_custom_fusion = f32[8192]{0:T(1024)S(1)} fusion(s32[4096]{0:T(1024)S(1)} %get-tuple-element.355, f32[4096]{0:T(1024)S(1)} %get-tuple-element.356, f32[]{:T(128)} %constant.683.clone.1), kind=kCustom, calls=%fused_computation.397 | custom fusion | bytes 32772 | tf_op jit(solution)/shard_map/scatter | solution.py:667
  223.4 15.7 %scatter_custom_fusion.1 = f32[8192]{0:T(1024)S(1)} fusion(s32[4096]{0:T(1024)S(1)} %get-tuple-element.355, f32[4096]{0:T(1024)} %exponential_divide_fusion, f32[]{:T(128)} %constant.683.clone.1), kind=kCustom, calls=%fused_computation.395 | custom fusion | bytes 33280 | tf_op jit(solution)/shard_map/scatter | solution.py:667
  239.1 8.3 collective-permute-done.19
  247.4 3.6 fusion.189
  253.4 2.9 multiply_reduce_fusion.10
  261.0 6.4 fusion.18.q_ref.k_ref.v_ref
  267.4 4.8 shard_map.555
  275.4 2.6 constant_dynamic-update-slice_fusion.10
  280.2 2.5 constant_dynamic-update-slice_fusion.7
  288.5 18.7 %shard_map.556 = (bf16[512,768]{1,0:T(8,128)(2,1)S(1)}, f32[512,768]{1,0:T(8,128)}) custom-call(s32[1]{0:T(128)} %dynamic_slice.234.len_ref, s32[1]{0:T(128)} %bitcast.32.core_ref, bf16[512,768]{1,0:T(8,128)(2,1)S(1)} %copy-done.2, bf16[512,768]{1,0:T(8,128)(2,1)S(1)} %copy-done.3, bf16[512,768]{1,0:T(8,128)(2,1)S(1)} %copy-done.7, ...), custom_call_target="tpu_custom_call" | custom-call | flops 1610612736 | bytes 7077888 | tf_op jit(solution)/shard_map/pallas_call | solution.py:161
  307.5 3.4 fusion.188
  312.7 6.0 multiply_convert_fusion.3
  319.1 3.1 constant_dynamic-update-slice_fusion.5
  327.7 3.7 all-to-all-start
  331.4 8.7 %all-gather.10.cloned.1.call-start = ((), (), s32[]{:S(2)}) async-start(), calls=%async_computation.3 | async-start | bytes 1216512 | tf_op jit(solution)/shard_map/all_gather | solution.py:842
  341.5 7.5 fusion.187
  351.6 3.7 collective-permute-start.25
  358.8 5.8 collective-permute-done.26
  364.6 12.3 %fusion.198 = (f32[256]{0:T(256)S(1)}, f32[256,12672]{1,0:T(8,128)}) fusion(bf16[256,768]{1,0:T(8,128)(2,1)S(1)} %pad_maximum_fusion.4, bf16[12672,768]{1,0:T(8,128)(2,1)} %constant_dynamic-update-slice_fusion, pred[12672]{0:T(1024)(128)(4,1)S(1)} %copy-done.103), kind=kOutput, calls=%fused_computation.607 | convolution fusion | flops 4989321216 | bytes 32847232 | tf_op jit(solution)/shard_map/dot_general | solution.py:29
  377.0 6.9 exponential_reduce_fusion
  392.5 15.8 %fusion = f32[256,768]{1,0:T(8,128)S(1)} fusion(bf16[12672,768]{1,0:T(8,128)(2,1)} %constant_dynamic-update-slice_fusion, f32[256,12672]{1,0:T(8,128)} %get-tuple-element.345, f32[256]{0:T(256)S(1)} %reshape.2256, f32[256]{0:T(256)S(1)} %copy-done.118, s32[256]{0:T(256)S(1)} %copy-done.109), kind=kOutput, calls=%fused_computation.19 | convolution fusion | flops 5002297344 | bytes 33229824 | tf_op jit(solution)/shard_map/dot_general | solution.py:25
  413.3 4.8 collective-permute-done.32
  418.1 5.5 collective-permute-done.33
  427.0 3.5 multiply_reduce_fusion
  431.9 7.8 fusion.10
  441.1 6.0 multiply_reduce_fusion.2
  450.9 3.8 fusion.199
  454.7 3.8 convolution_add_fusion
  459.3 11.3 %collective-permute-done.58 = bf16[256,896]{1,0:T(8,128)(2,1)S(1)} collective-permute-done((bf16[256,896]{1,0:T(8,128)(2,1)S(1)}, bf16[256,896]{1,0:T(8,128)(2,1)S(1)}, u32[]{:S(2)}, u32[]{:S(2)}) %collective-permute-start.58) | collective-permute-done | bytes 458784 | tf_op jit(solution)/shard_map/ppermute | solution.py:270
  477.1 3.0 convolution_convert_fusion.do_ref
  481.6 27.5 %shard_map.557 = (bf16[512,768]{1,0:T(8,128)(2,1)S(1)}, f32[512,768]{1,0:T(8,128)}, bf16[512,768]{1,0:T(8,128)(2,1)S(1)}, f32[512,768]{1,0:T(8,128)}, bf16[512,768]{1,0:T(8,128)(2,1)S(1)}) custom-call(s32[1]{0:T(128)} %dynamic_slice.234.len_ref, s32[1]{0:T(128)} %bitcast.32.core_ref, bf16[512,768]{1,0:T(8,128)(2,1)S(1)} %copy-done.2, ...), custom_call_target="tpu_custom_call" | custom-call | flops 4026531840 | bytes 12582912 | tf_op jit(solution)/shard_map/pallas_call | solution.py:239
  528.0 5.3 multiply_reduce_fusion.4
  537.2 6.7 collective-permute-start.45
  553.9 6.2 collective-permute-done.45
  561.1 4.1 collective-permute-done.44
  573.7 12.8 %collective-permute-done.48 = bf16[1,3072,128]{2,1,0:T(8,128)(2,1)S(1)} collective-permute-done((bf16[1,3072,128]{2,1,0:T(8,128)(2,1)}, bf16[1,3072,128]{2,1,0:T(8,128)(2,1)S(1)}, u32[]{:S(2)}, u32[]{:S(2)}) %collective-permute-start.48) | collective-permute-done | bytes 786464 | tf_op jit(solution)/shard_map/ppermute | solution.py:315
  587.3 11.2 %collective-permute-done.54 = bf16[4,2,48,1536]{3,2,0,1:T(8,128)(2,1)S(1)} collective-permute-done((bf16[4,2,48,1536]{3,2,0,1:T(8,128)(2,1)S(1)}, bf16[4,2,48,1536]{3,2,0,1:T(8,128)(2,1)S(1)}, u32[]{:S(2)}, u32[]{:S(2)}) %collective-permute-start.54) | collective-permute-done | bytes 1179680 | tf_op jit(solution)/shard_map/ppermute | solution.py:270
  602.1 15.3 %collective-permute-done.49 = bf16[1,3072,128]{2,1,0:T(8,128)(2,1)S(1)} collective-permute-done((bf16[1,3072,128]{2,1,0:T(8,128)(2,1)S(1)}, bf16[1,3072,128]{2,1,0:T(8,128)(2,1)S(1)}, u32[]{:S(2)}, u32[]{:S(2)}) %collective-permute-start.49) | collective-permute-done | bytes 786464 | tf_op jit(solution)/shard_map/ppermute | solution.py:315
  622.9 2.5 dynamic-slice_bitcast_fusion.5
  627.0 3.5 collective-permute-start.67
  633.0 15.9 %fusion.20.refs_5_ = f32[1584,768]{1,0:T(8,128)} fusion(bf16[2048,896]{1,0:T(8,128)(2,1)} %bitcast.342, s32[2048]{0:T(1024)S(1)} %copy-done.108, f32[2048]{0:T(1024)S(1)} %convert_reduce_fusion, f32[2048]{0:T(1024)S(1)} %copy-done.107, bf16[1572,768]{1,0:T(8,128)(2,1)S(1)} %copy-done.19), kind=kOutput, calls=%fused_computation.46 | convolution fusion | flops 9985130496 | bytes 13596672 | tf_op jit(solution)/shard_map/dot_general | solution.py:33
  648.9 19.8 %shard_map.558.refs_4_ = f32[12608,128]{1,0:T(8,128)} custom-call(s32[14]{0:T(128)} %get-tuple-element.294.cnt_ref, s32[14,256]{1,0:T(8,128)} %get-tuple-element.293.row_ref, s32[14,256]{1,0:T(8,128)} %get-tuple-element.292.pos_ref, f32[14,256]{1,0:T(8,128)} %broadcast_select_fusion.4.mix_ref, bf16[1,3072,128]{2,1,0:T(8,128)(2,1)} %reshape.2262.refs_0_, ...), custom_call_target="tpu_custom_call" | custom-call | flops 3670016 | bytes 18350080 | tf_op jit(solution)/shard_map/pallas_call | solution.py:521
  668.8 10.3 %collective-permute-done.60.refs_0_ = bf16[3,3072,128]{2,1,0:T(8,128)(2,1)} collective-permute-done((bf16[3,3072,128]{2,1,0:T(8,128)(2,1)}, bf16[3,3072,128]{2,1,0:T(8,128)(2,1)}, u32[]{:S(2)}, u32[]{:S(2)}) %collective-permute-start.60) | collective-permute-done | bytes 2359328 | tf_op jit(solution)/shard_map/ppermute | solution.py:270
  682.7 2.7 slice.269
  688.3 3.4 bitcast_add_fusion.4
  691.7 3.6 collective-permute-start.73
  707.0 19.4 %shard_map.559.refs_4_ = f32[12608,128]{1,0:T(8,128)} custom-call(s32[12]{0:T(128)} %get-tuple-element.291.cnt_ref, s32[12,256]{1,0:T(8,128)} %get-tuple-element.290.row_ref, s32[12,256]{1,0:T(8,128)} %get-tuple-element.289.pos_ref, f32[12,256]{1,0:T(8,128)} %broadcast_select_fusion.3.mix_ref, bf16[3,3072,128]{2,1,0:T(8,128)(2,1)} %collective-permute-done.60.refs_0_, ...), custom_call_target="tpu_custom_call" | custom-call | flops 3145728 | bytes 15728640 | tf_op jit(solution)/shard_map/pallas_call | solution.py:521
  739.2 9.1 %collective-permute-done.77 = f32[48,4608]{1,0:T(8,128)S(1)} collective-permute-done((f32[48,4608]{1,0:T(8,128)S(1)}, f32[48,4608]{1,0:T(8,128)S(1)}, u32[]{:S(2)}, u32[]{:S(2)}) %collective-permute-start.77) | collective-permute-done | bytes 884768 | tf_op jit(solution)/shard_map/ppermute | solution.py:280
  748.3 4.8 collective-permute-done.78
  763.8 16.5 %shard_map.560 = (f32[1572,768]{1,0:T(8,128)}, f32[8,128]{1,0:T(8,128)}) custom-call(s32[6]{0:T(128)} %get-tuple-element.315.cnt_ref, s32[6,256]{1,0:T(8,128)} %get-tuple-element.314.row_ref, s32[6,256]{1,0:T(8,128)} %get-tuple-element.313.pos_ref, f32[6,256]{1,0:T(8,128)} %broadcast_select_fusion.5.mix_ref, ...), custom_call_target="tpu_custom_call" | custom-call | flops 1572864 | bytes 7864320 | tf_op jit(solution)/shard_map/pallas_call | solution.py:521
  791.1 3.4 collective-permute-start.84
  796.0 6.7 collective-permute-start.85
  821.1 10.3 %multiply_subtract_fusion = (f32[1572,768]{1,0:T(8,128)}, f32[1572,768]{1,0:T(8,128)}, f32[1572,768]{1,0:T(8,128)}) fusion(f32[1572,768]{1,0:T(8,128)} %param.41, f32[1572,768]{1,0:T(8,128)S(1)} %copy-done.40, f32[]{:T(128)S(6)} %min.3, f32[1572,768]{1,0:T(8,128)} %param.42, f32[1572,768]{1,0:T(8,128)} %param.43), kind=kLoop, calls=%fused_computation.32 | loop fusion | flops 19316736 | bytes 33804292 | tf_op jit(solution)/shard_map/sub | solution.py:258
  (794 shorter events, 254.1 us)
Async XLA Ops:
  7.2 197.8 %all-gather.12.cloned.1.call-start = ((), (), s32[]{:S(2)}) async-start(), calls=%async_computation.4 | async-start | bytes 1723392 | tf_op jit(solution)/shard_map/all_gather | solution.py:592
  11.1 249.9 %all-gather.6.cloned.1.call-start = ((), (), s32[]{:S(2)}) async-start(), calls=%async_computation.1 | async-start | bytes 9732096 | tf_op jit(solution)/shard_map/all_gather | solution.py:592
  14.7 326.8 %all-gather.8.cloned.1.call-start = ((), (), s32[]{:S(2)}) async-start(), calls=%async_computation.2 | async-start | bytes 4866048 | tf_op jit(solution)/shard_map/all_gather | solution.py:592
  18.0 31.4 %collective-permute-start = (f32[64,128]{1,0:T(8,128)}, f32[64,128]{1,0:T(8,128)S(1)}, u32[]{:S(2)}, u32[]{:S(2)}) collective-permute-start(f32[64,128]{1,0:T(8,128)} %get-tuple-element.288), channel_id=1, source_target_pairs={{0,24},{1,25},{2,26},{3,27},{4,28},{5,29},{6,30},{7,31},{8,0},{9,1... | collective-permute-start | bytes 98312 | tf_op jit(solution)/shard_map/ppermute | solution.py:270
  23.0 27.0 %collective-permute-start.1 = (f32[64,128]{1,0:T(8,128)}, f32[64,128]{1,0:T(8,128)S(1)}, u32[]{:S(2)}, u32[]{:S(2)}) collective-permute-start(f32[64,128]{1,0:T(8,128)} %get-tuple-element.288), channel_id=1, source_target_pairs={{0,16},{1,17},{2,18},{3,19},{4,20},{5,21},{6,22},{7,23},{8,24},{9,... | collective-permute-start | bytes 98312 | tf_op jit(solution)/shard_map/ppermute | solution.py:270
  23.0 31.4 %collective-permute-start.2 = (f32[64,128]{1,0:T(8,128)}, f32[64,128]{1,0:T(8,128)}, u32[]{:S(2)}, u32[]{:S(2)}) collective-permute-start(f32[64,128]{1,0:T(8,128)} %get-tuple-element.288), channel_id=1, source_target_pairs={{0,8},{1,9},{2,10},{3,11},{4,12},{5,13},{6,14},{7,15},{8,16},{9,17... | collective-permute-start | bytes 98312 | tf_op jit(solution)/shard_map/ppermute | solution.py:270
  28.1 59.8 %collective-permute-start.5 = (bf16[800,768]{1,0:T(8,128)(2,1)S(1)}, bf16[800,768]{1,0:T(8,128)(2,1)}, u32[]{:S(2)}, u32[]{:S(2)}) collective-permute-start(bf16[800,768]{1,0:T(8,128)(2,1)S(1)} %pad_slice_fusion.refs_1_), channel_id=1, source_target_pairs={{0,2},{1,3},{2,0},{3,1},{4,6},{5,7},{6,4},{7,5},{8,10},{9,11},{10,... | collective-permute-start | bytes 3686408 | tf_op jit(solution)/shard_map/ppermute | solution.py:270
  29.6 58.3 %collective-permute-start.6 = (bf16[800,768]{1,0:T(8,128)(2,1)S(1)}, bf16[800,768]{1,0:T(8,128)(2,1)}, u32[]{:S(2)}, u32[]{:S(2)}) collective-permute-start(bf16[800,768]{1,0:T(8,128)(2,1)S(1)} %pad_slice_fusion.refs_1_), channel_id=1, source_target_pairs={{0,4},{1,5},{2,6},{3,7},{4,0},{5,1},{6,2},{7,3},{8,12},{9,13},{10,... | collective-permute-start | bytes 3686408 | tf_op jit(solution)/shard_map/ppermute | solution.py:270
  49.4 37.4 %collective-permute-start.3 = (bf16[784,768]{1,0:T(8,128)(2,1)S(1)}, bf16[784,768]{1,0:T(8,128)(2,1)}, u32[]{:S(2)}, u32[]{:S(2)}) collective-permute-start(bf16[784,768]{1,0:T(8,128)(2,1)S(1)} %slice.302.refs_0_), channel_id=1, source_target_pairs={{0,2},{1,3},{2,0},{3,1},{4,6},{5,7},{6,4},{7,5},{8,10},{9,11},{10,... | collective-permute-start | bytes 3612680 | tf_op jit(solution)/shard_map/ppermute | solution.py:270
  50.0 37.9 %collective-permute-start.4 = (bf16[784,768]{1,0:T(8,128)(2,1)S(1)}, bf16[784,768]{1,0:T(8,128)(2,1)}, u32[]{:S(2)}, u32[]{:S(2)}) collective-permute-start(bf16[784,768]{1,0:T(8,128)(2,1)S(1)} %slice.302.refs_0_), channel_id=1, source_target_pairs={{0,4},{1,5},{2,6},{3,7},{4,0},{5,1},{6,2},{7,3},{8,12},{9,13},{10,... | collective-permute-start | bytes 3612680 | tf_op jit(solution)/shard_map/ppermute | solution.py:270
  87.9 34.2 %collective-permute-start.13 = (bf16[784,768]{1,0:T(8,128)(2,1)}, bf16[784,768]{1,0:T(8,128)(2,1)S(1)}, u32[]{:S(2)}, u32[]{:S(2)}) collective-permute-start(bf16[784,768]{1,0:T(8,128)(2,1)} %collective-permute-done.3.refs_4_), channel_id=1, source_target_pairs={{0,4},{1,5},{2,6},{3,7},{4,0},{5,1},{6,2},{7,3},{8,12},{9,13},{10,... | collective-permute-start | bytes 3612680 | tf_op jit(solution)/shard_map/ppermute | solution.py:270
  91.1 37.7 %collective-permute-start.14 = (bf16[800,768]{1,0:T(8,128)(2,1)}, bf16[800,768]{1,0:T(8,128)(2,1)S(1)}, u32[]{:S(2)}, u32[]{:S(2)}) collective-permute-start(bf16[800,768]{1,0:T(8,128)(2,1)} %collective-permute-done.6.refs_9_), channel_id=1, source_target_pairs={{0,2},{1,3},{2,0},{3,1},{4,6},{5,7},{6,4},{7,5},{8,10},{9,11},{10,... | collective-permute-start | bytes 3686408 | tf_op jit(solution)/shard_map/ppermute | solution.py:270
  93.9 37.0 %collective-permute-start.12 = (bf16[800,768]{1,0:T(8,128)(2,1)}, bf16[800,768]{1,0:T(8,128)(2,1)S(1)}, u32[]{:S(2)}, u32[]{:S(2)}) collective-permute-start(bf16[800,768]{1,0:T(8,128)(2,1)} %collective-permute-done.6.refs_9_), channel_id=1, source_target_pairs={{0,1},{1,0},{2,3},{3,2},{4,5},{5,4},{6,7},{7,6},{8,9},{9,8},{10,11... | collective-permute-start | bytes 3686408 | tf_op jit(solution)/shard_map/ppermute | solution.py:270
  93.9 36.9 %collective-permute-start.8 = (bf16[800,768]{1,0:T(8,128)(2,1)S(1)}, bf16[800,768]{1,0:T(8,128)(2,1)S(1)}, u32[]{:S(2)}, u32[]{:S(2)}) collective-permute-start(bf16[800,768]{1,0:T(8,128)(2,1)S(1)} %pad_slice_fusion.refs_1_), channel_id=1, source_target_pairs={{0,1},{1,0},{2,3},{3,2},{4,5},{5,4},{6,7},{7,6},{8,9},{9,8},{10,11... | collective-permute-start | bytes 3686408 | tf_op jit(solution)/shard_map/ppermute | solution.py:270
  95.5 35.3 %collective-permute-start.10 = (bf16[800,768]{1,0:T(8,128)(2,1)}, bf16[800,768]{1,0:T(8,128)(2,1)S(1)}, u32[]{:S(2)}, u32[]{:S(2)}) collective-permute-start(bf16[800,768]{1,0:T(8,128)(2,1)} %collective-permute-done.5.refs_5_), channel_id=1, source_target_pairs={{0,1},{1,0},{2,3},{3,2},{4,5},{5,4},{6,7},{7,6},{8,9},{9,8},{10,11... | collective-permute-start | bytes 3686408 | tf_op jit(solution)/shard_map/ppermute | solution.py:270
  165.3 42.4 %collective-permute-start.17 = (bf16[3072,128]{1,0:T(8,128)(2,1)}, bf16[3072,128]{1,0:T(8,128)(2,1)}, u32[]{:S(2)}, u32[]{:S(2)}) collective-permute-start(bf16[3072,128]{1,0:T(8,128)(2,1)} %get-tuple-element.260), channel_id=1, source_target_pairs={{0,8},{1,9},{2,10},{3,11},{4,12},{5,13},{6,14},{7,15},{8,16},{9,17... | collective-permute-start | bytes 2359304 | tf_op jit(solution)/shard_map/ppermute | solution.py:270
  167.8 40.0 %collective-permute-start.18 = (bf16[3072,128]{1,0:T(8,128)(2,1)}, bf16[3072,128]{1,0:T(8,128)(2,1)}, u32[]{:S(2)}, u32[]{:S(2)}) collective-permute-start(bf16[3072,128]{1,0:T(8,128)(2,1)} %get-tuple-element.259), channel_id=1, source_target_pairs={{0,24},{1,25},{2,26},{3,27},{4,28},{5,29},{6,30},{7,31},{8,0},{9,1... | collective-permute-start | bytes 2359304 | tf_op jit(solution)/shard_map/ppermute | solution.py:270
  199.1 48.3 %collective-permute-start.19 = (bf16[3072,128]{1,0:T(8,128)(2,1)}, bf16[3072,128]{1,0:T(8,128)(2,1)}, u32[]{:S(2)}, u32[]{:S(2)}) collective-permute-start(bf16[3072,128]{1,0:T(8,128)(2,1)} %fusion.47), channel_id=1, source_target_pairs={{0,16},{1,17},{2,18},{3,19},{4,20},{5,21},{6,22},{7,23},{8,24},{9,... | collective-permute-start | bytes 2359304 | tf_op jit(solution)/shard_map/ppermute | solution.py:270
  272.3 13.0 %collective-permute-start.20 = (bf16[512,768]{1,0:T(8,128)(2,1)}, bf16[512,768]{1,0:T(8,128)(2,1)S(1)}, u32[]{:S(2)}, u32[]{:S(2)}) collective-permute-start(bf16[512,768]{1,0:T(8,128)(2,1)} %get-tuple-element.126.k_ref), channel_id=1, source_target_pairs={{0,1},{1,0},{2,3},{3,2},{4,5},{5,4},{6,7},{7,6},{8,9},{9,8},{10,11... | collective-permute-start | bytes 2359304 | tf_op jit(solution)/shard_map/ppermute | solution.py:270
  272.4 13.8 %collective-permute-start.21 = (bf16[512,768]{1,0:T(8,128)(2,1)}, bf16[512,768]{1,0:T(8,128)(2,1)}, u32[]{:S(2)}, u32[]{:S(2)}) collective-permute-start(bf16[512,768]{1,0:T(8,128)(2,1)} %get-tuple-element.127.v_ref), channel_id=1, source_target_pairs={{0,1},{1,0},{2,3},{3,2},{4,5},{5,4},{6,7},{7,6},{8,9},{9,8},{10,11... | collective-permute-start | bytes 2359304 | tf_op jit(solution)/shard_map/ppermute | solution.py:270
  275.2 32.0 %collective-permute-start.22 = (bf16[512,768]{1,0:T(8,128)(2,1)}, bf16[512,768]{1,0:T(8,128)(2,1)}, u32[]{:S(2)}, u32[]{:S(2)}) collective-permute-start(bf16[512,768]{1,0:T(8,128)(2,1)} %add_convert_fusion.4), channel_id=1, source_target_pairs={{0,1},{1,0},{2,3},{3,2},{4,5},{5,4},{6,7},{7,6},{8,9},{9,8},{10,11... | collective-permute-start | bytes 2359304 | tf_op jit(solution)/shard_map/ppermute | solution.py:270
  318.8 45.8 %collective-permute-start.28 = (bf16[512,3072]{1,0:T(8,128)(2,1)}, bf16[512,3072]{1,0:T(8,128)(2,1)}, u32[]{:S(2)}, u32[]{:S(2)}) collective-permute-start(bf16[512,3072]{1,0:T(8,128)(2,1)} %get-tuple-element.130), channel_id=1, source_target_pairs={{0,1},{1,0},{2,3},{3,2},{4,5},{5,4},{6,7},{7,6},{8,9},{9,8},{10,11... | collective-permute-start | bytes 9437192 | tf_op jit(solution)/shard_map/ppermute | solution.py:270
  327.7 31.1 %all-to-all-start = ((f32[32,1,512]{2,1,0:T(1,128)}), f32[32,1,512]{2,1,0:T(1,128)S(1)}, u32[]{:S(2)}, u32[]{:S(2)}) async-start(f32[32,1,512]{2,1,0:T(1,128)} %all_to_all.8), calls=%async_computation | async-start | bytes 131072 | tf_op jit(solution)/shard_map/all_to_all | solution.py:746
  331.4 287.9 %all-gather.10.cloned.1.call-start = ((), (), s32[]{:S(2)}) async-start(), calls=%async_computation.3 | async-start | bytes 1216512 | tf_op jit(solution)/shard_map/all_gather | solution.py:842
  408.8 14.8 %collective-permute-start.33 = (f32[64,768]{1,0:T(8,128)S(1)}, f32[64,768]{1,0:T(8,128)S(1)}, u32[]{:S(2)}, u32[]{:S(2)}) collective-permute-start(f32[64,768]{1,0:T(8,128)S(1)} %get-tuple-element.269), channel_id=1, source_target_pairs={{0,16},{1,17},{2,18},{3,19},{4,20},{5,21},{6,22},{7,23},{8,24},{9,... | collective-permute-start | bytes 589832 | tf_op jit(solution)/shard_map/ppermute | solution.py:270
  410.2 13.4 %collective-permute-start.34 = (f32[64,768]{1,0:T(8,128)S(1)}, f32[64,768]{1,0:T(8,128)S(1)}, u32[]{:S(2)}, u32[]{:S(2)}) collective-permute-start(f32[64,768]{1,0:T(8,128)S(1)} %get-tuple-element.268), channel_id=1, source_target_pairs={{0,24},{1,25},{2,26},{3,27},{4,28},{5,29},{6,30},{7,31},{8,0},{9,1... | collective-permute-start | bytes 589832 | tf_op jit(solution)/shard_map/ppermute | solution.py:270
  423.9 34.6 %collective-permute-start.56 = (bf16[256,896]{1,0:T(8,128)(2,1)S(1)}, bf16[256,896]{1,0:T(8,128)(2,1)S(1)}, u32[]{:S(2)}, u32[]{:S(2)}) collective-permute-start(bf16[256,896]{1,0:T(8,128)(2,1)S(1)} %get-tuple-element.271), channel_id=1, source_target_pairs={{0,2},{1,3},{2,0},{3,1},{4,6},{5,7},{6,4},{7,5},{8,10},{9,11},{10,... | collective-permute-start | bytes 1376264 | tf_op jit(solution)/shard_map/ppermute | solution.py:270
  425.4 33.7 %collective-permute-start.57 = (bf16[256,896]{1,0:T(8,128)(2,1)S(1)}, bf16[256,896]{1,0:T(8,128)(2,1)S(1)}, u32[]{:S(2)}, u32[]{:S(2)}) collective-permute-start(bf16[256,896]{1,0:T(8,128)(2,1)S(1)} %get-tuple-element.271), channel_id=1, source_target_pairs={{0,4},{1,5},{2,6},{3,7},{4,0},{5,1},{6,2},{7,3},{8,12},{9,13},{10,... | collective-permute-start | bytes 1376264 | tf_op jit(solution)/shard_map/ppermute | solution.py:270
  439.8 32.4 %collective-permute-start.36 = (bf16[512,1536]{1,0:T(8,128)(2,1)S(1)}, bf16[512,1536]{1,0:T(8,128)(2,1)S(1)}, u32[]{:S(2)}, u32[]{:S(2)}) collective-permute-start(bf16[512,1536]{1,0:T(8,128)(2,1)S(1)} %constant_dynamic-slice_fusion.43), channel_id=1, source_target_pairs={{0,1},{1,0},{2,3},{3,2},{4,5},{5,4},{6,7},{7,6},{8,9},{9,8},{10,11... | collective-permute-start | bytes 4718600 | tf_op jit(solution)/shard_map/ppermute | solution.py:270
  472.1 50.1 %collective-permute-start.59 = (bf16[4,256,896]{2,1,0:T(8,128)(2,1)}, bf16[4,256,896]{2,1,0:T(8,128)(2,1)}, u32[]{:S(2)}, u32[]{:S(2)}) collective-permute-start(bf16[4,256,896]{2,1,0:T(8,128)(2,1)} %pad_maximum_fusion.3), channel_id=1, source_target_pairs={{0,1},{1,0},{2,3},{3,2},{4,5},{5,4},{6,7},{7,6},{8,9},{9,8},{10,11... | collective-permute-start | bytes 5505032 | tf_op jit(solution)/shard_map/ppermute | solution.py:270
  474.8 34.3 %collective-permute-start.39 = (bf16[512,384]{1,0:T(8,128)(2,1)}, bf16[512,384]{1,0:T(8,128)(2,1)}, u32[]{:S(2)}, u32[]{:S(2)}) collective-permute-start(bf16[512,384]{1,0:T(8,128)(2,1)} %constant_dynamic-slice_fusion.42), channel_id=1, source_target_pairs={{0,1},{1,0},{2,3},{3,2},{4,5},{5,4},{6,7},{7,6},{8,9},{9,8},{10,11... | collective-permute-start | bytes 1179656 | tf_op jit(solution)/shard_map/ppermute | solution.py:270
  475.4 37.1 %collective-permute-start.37 = (bf16[4,2,192,384]{3,2,1,0:T(8,128)(2,1)S(1)}, bf16[4,2,192,384]{3,2,1,0:T(8,128)(2,1)}, u32[]{:S(2)}, u32[]{:S(2)}) collective-permute-start(bf16[4,2,192,384]{3,2,1,0:T(8,128)(2,1)S(1)} %fusion.34), channel_id=1, source_target_pairs={{0,4},{1,5},{2,6},{3,7},{4,0},{5,1},{6,2},{7,3},{8,12},{9,13},{10,... | collective-permute-start | bytes 3538952 | tf_op jit(solution)/shard_map/ppermute | solution.py:270
  476.2 36.3 %collective-permute-start.38 = (bf16[4,2,48,1536]{3,2,1,0:T(8,128)(2,1)S(1)}, bf16[4,2,48,1536]{3,2,1,0:T(8,128)(2,1)}, u32[]{:S(2)}, u32[]{:S(2)}) collective-permute-start(bf16[4,2,48,1536]{3,2,1,0:T(8,128)(2,1)S(1)} %fusion.35), channel_id=1, source_target_pairs={{0,2},{1,3},{2,0},{3,1},{4,6},{5,7},{6,4},{7,5},{8,10},{9,11},{10,... | collective-permute-start | bytes 3538952 | tf_op jit(solution)/shard_map/ppermute | solution.py:270
  512.5 12.6 %collective-permute-start.40 = (bf16[512,768]{1,0:T(8,128)(2,1)S(1)}, bf16[512,768]{1,0:T(8,128)(2,1)S(1)}, u32[]{:S(2)}, u32[]{:S(2)}) collective-permute-start(bf16[512,768]{1,0:T(8,128)(2,1)S(1)} %get-tuple-element.149), channel_id=1, source_target_pairs={{0,1},{1,0},{2,3},{3,2},{4,5},{5,4},{6,7},{7,6},{8,9},{9,8},{10,11... | collective-permute-start | bytes 2359304 | tf_op jit(solution)/shard_map/ppermute | solution.py:270
  512.5 13.7 %collective-permute-start.41 = (bf16[512,768]{1,0:T(8,128)(2,1)S(1)}, bf16[512,768]{1,0:T(8,128)(2,1)S(1)}, u32[]{:S(2)}, u32[]{:S(2)}) collective-permute-start(bf16[512,768]{1,0:T(8,128)(2,1)S(1)} %get-tuple-element.151), channel_id=1, source_target_pairs={{0,1},{1,0},{2,3},{3,2},{4,5},{5,4},{6,7},{7,6},{8,9},{9,8},{10,11... | collective-permute-start | bytes 2359304 | tf_op jit(solution)/shard_map/ppermute | solution.py:270
  519.2 17.9 %collective-permute-start.43 = (bf16[4,48,1536]{2,1,0:T(8,128)(2,1)}, bf16[4,48,1536]{2,1,0:T(8,128)(2,1)}, u32[]{:S(2)}, u32[]{:S(2)}) collective-permute-start(bf16[4,48,1536]{2,1,0:T(8,128)(2,1)} %fusion.49), channel_id=1, source_target_pairs={{0,4},{1,5},{2,6},{3,7},{4,0},{5,1},{6,2},{7,3},{8,12},{9,13},{10,... | collective-permute-start | bytes 1769480 | tf_op jit(solution)/shard_map/ppermute | solution.py:270
  520.7 16.5 %collective-permute-start.42 = (bf16[4,192,384]{2,1,0:T(8,128)(2,1)}, bf16[4,192,384]{2,1,0:T(8,128)(2,1)}, u32[]{:S(2)}, u32[]{:S(2)}) collective-permute-start(bf16[4,192,384]{2,1,0:T(8,128)(2,1)} %fusion.48), channel_id=1, source_target_pairs={{0,2},{1,3},{2,0},{3,1},{4,6},{5,7},{6,4},{7,5},{8,10},{9,11},{10,... | collective-permute-start | bytes 1769480 | tf_op jit(solution)/shard_map/ppermute | solution.py:270
  537.2 22.9 %collective-permute-start.45 = (bf16[1,3072,128]{2,1,0:T(8,128)(2,1)}, bf16[1,3072,128]{2,1,0:T(8,128)(2,1)}, u32[]{:S(2)}, u32[]{:S(2)}) collective-permute-start(bf16[1,3072,128]{2,1,0:T(8,128)(2,1)} %reshape.2262.refs_0_), channel_id=1, source_target_pairs={{0,8},{2,10},{4,12},{6,14},{8,16},{10,18},{12,20},{14,22},{16,24},... | collective-permute-start | bytes 2359304 | tf_op jit(solution)/shard_map/ppermute | solution.py:315
  543.9 21.4 %collective-permute-start.44 = (bf16[1,3072,128]{2,1,0:T(8,128)(2,1)}, bf16[1,3072,128]{2,1,0:T(8,128)(2,1)}, u32[]{:S(2)}, u32[]{:S(2)}) collective-permute-start(bf16[1,3072,128]{2,1,0:T(8,128)(2,1)} %reshape.2262.refs_0_), channel_id=1, source_target_pairs={{8,0},{10,2},{12,4},{14,6},{16,8},{18,10},{20,12},{22,14},{24,16},... | collective-permute-start | bytes 2359304 | tf_op jit(solution)/shard_map/ppermute | solution.py:315
  545.2 28.0 %collective-permute-start.51 = (bf16[1,3072,128]{2,1,0:T(8,128)(2,1)}, bf16[1,3072,128]{2,1,0:T(8,128)(2,1)}, u32[]{:S(2)}, u32[]{:S(2)}) collective-permute-start(bf16[1,3072,128]{2,1,0:T(8,128)(2,1)} %reshape.2262.refs_0_), channel_id=1, source_target_pairs={{0,4},{1,5},{2,6},{3,7},{4,0},{5,1},{6,2},{7,3},{8,12},{9,13},{10,... | collective-permute-start | bytes 2359304 | tf_op jit(solution)/shard_map/ppermute | solution.py:270
  545.8 73.5 %collective-permute-start.50 = (bf16[1,3072,128]{2,1,0:T(8,128)(2,1)}, bf16[1,3072,128]{2,1,0:T(8,128)(2,1)}, u32[]{:S(2)}, u32[]{:S(2)}) collective-permute-start(bf16[1,3072,128]{2,1,0:T(8,128)(2,1)} %reshape.2262.refs_0_), channel_id=1, source_target_pairs={{0,2},{1,3},{2,0},{3,1},{4,6},{5,7},{6,4},{7,5},{8,10},{9,11},{10,... | collective-permute-start | bytes 2359304 | tf_op jit(solution)/shard_map/ppermute | solution.py:270
  547.3 19.2 %collective-permute-start.53 = (bf16[512,1152]{1,0:T(8,128)(2,1)S(1)}, bf16[512,1152]{1,0:T(8,128)(2,1)S(1)}, u32[]{:S(2)}, u32[]{:S(2)}) collective-permute-start(bf16[512,1152]{1,0:T(8,128)(2,1)S(1)} %constant_dynamic-slice_fusion.41), channel_id=1, source_target_pairs={{0,1},{1,0},{2,3},{3,2},{4,5},{5,4},{6,7},{7,6},{8,9},{9,8},{10,11... | collective-permute-start | bytes 3538952 | tf_op jit(solution)/shard_map/ppermute | solution.py:270
  560.0 13.2 %collective-permute-start.46 = (bf16[1,3072,128]{2,1,0:T(8,128)(2,1)}, bf16[1,3072,128]{2,1,0:T(8,128)(2,1)S(1)}, u32[]{:S(2)}, u32[]{:S(2)}) collective-permute-start(bf16[1,3072,128]{2,1,0:T(8,128)(2,1)} %collective-permute-done.45), channel_id=1, source_target_pairs={{8,16},{10,18},{12,20},{14,22},{16,24},{18,26},{20,28},{22,30},{9,... | collective-permute-start | bytes 2359304 | tf_op jit(solution)/shard_map/ppermute | solution.py:315
  565.3 21.2 %collective-permute-start.48 = (bf16[1,3072,128]{2,1,0:T(8,128)(2,1)}, bf16[1,3072,128]{2,1,0:T(8,128)(2,1)S(1)}, u32[]{:S(2)}, u32[]{:S(2)}) collective-permute-start(bf16[1,3072,128]{2,1,0:T(8,128)(2,1)} %collective-permute-done.44), channel_id=1, source_target_pairs={{8,0},{10,2},{12,4},{14,6},{16,8},{18,10},{20,12},{22,14},{9,1},{1... | collective-permute-start | bytes 2359304 | tf_op jit(solution)/shard_map/ppermute | solution.py:315
  569.8 28.6 %collective-permute-start.54 = (bf16[4,2,48,1536]{3,2,0,1:T(8,128)(2,1)S(1)}, bf16[4,2,48,1536]{3,2,0,1:T(8,128)(2,1)S(1)}, u32[]{:S(2)}, u32[]{:S(2)}) collective-permute-start(bf16[4,2,48,1536]{3,2,0,1:T(8,128)(2,1)S(1)} %fusion.36), channel_id=1, source_target_pairs={{0,4},{1,5},{2,6},{3,7},{4,0},{5,1},{6,2},{7,3},{8,12},{9,13},{10,... | collective-permute-start | bytes 3538952 | tf_op jit(solution)/shard_map/ppermute | solution.py:270
  573.2 52.3 %collective-permute-start.62 = (bf16[1,3072,128]{2,1,0:T(8,128)(2,1)}, bf16[1,3072,128]{2,1,0:T(8,128)(2,1)}, u32[]{:S(2)}, u32[]{:S(2)}) collective-permute-start(bf16[1,3072,128]{2,1,0:T(8,128)(2,1)} %reshape.2262.refs_0_), channel_id=1, source_target_pairs={{0,1},{1,0},{2,3},{3,2},{4,5},{5,4},{6,7},{7,6},{8,9},{9,8},{10,11... | collective-permute-start | bytes 2359304 | tf_op jit(solution)/shard_map/ppermute | solution.py:270
  573.2 46.1 %collective-permute-start.52 = (bf16[1,3072,128]{2,1,0:T(8,128)(2,1)}, bf16[1,3072,128]{2,1,0:T(8,128)(2,1)}, u32[]{:S(2)}, u32[]{:S(2)}) collective-permute-start(bf16[1,3072,128]{2,1,0:T(8,128)(2,1)} %collective-permute-done.51.refs_4_), channel_id=1, source_target_pairs={{0,2},{1,3},{2,0},{3,1},{4,6},{5,7},{6,4},{7,5},{8,10},{9,11},{10,... | collective-permute-start | bytes 2359304 | tf_op jit(solution)/shard_map/ppermute | solution.py:270
  586.5 13.8 %collective-permute-start.47 = (bf16[1,3072,128]{2,1,0:T(8,128)(2,1)S(1)}, bf16[1,3072,128]{2,1,0:T(8,128)(2,1)S(1)}, u32[]{:S(2)}, u32[]{:S(2)}) collective-permute-start(bf16[1,3072,128]{2,1,0:T(8,128)(2,1)S(1)} %collective-permute-done.46), channel_id=1, source_target_pairs={{16,24},{18,26},{20,28},{22,30},{17,25},{19,27},{21,29},{23,31}} | collective-permute-start | bytes 2359304 | tf_op jit(solution)/shard_map/ppermute | solution.py:315
  598.5 19.0 %collective-permute-start.49 = (bf16[1,3072,128]{2,1,0:T(8,128)(2,1)S(1)}, bf16[1,3072,128]{2,1,0:T(8,128)(2,1)S(1)}, u32[]{:S(2)}, u32[]{:S(2)}) collective-permute-start(bf16[1,3072,128]{2,1,0:T(8,128)(2,1)S(1)} %collective-permute-done.48), channel_id=1, source_target_pairs={{8,0},{10,2},{12,4},{14,6},{9,1},{11,3},{13,5},{15,7}} | collective-permute-start | bytes 2359304 | tf_op jit(solution)/shard_map/ppermute | solution.py:315
  600.3 19.0 %collective-permute-start.55 = (bf16[4,48,1536]{2,1,0:T(8,128)(2,1)S(1)}, bf16[4,48,1536]{2,1,0:T(8,128)(2,1)S(1)}, u32[]{:S(2)}, u32[]{:S(2)}) collective-permute-start(bf16[4,48,1536]{2,1,0:T(8,128)(2,1)S(1)} %fusion.50), channel_id=1, source_target_pairs={{0,2},{1,3},{2,0},{3,1},{4,6},{5,7},{6,4},{7,5},{8,10},{9,11},{10,... | collective-permute-start | bytes 1769480 | tf_op jit(solution)/shard_map/ppermute | solution.py:270
  619.3 29.6 %collective-permute-start.66 = (bf16[3,3072,128]{2,1,0:T(8,128)(2,1)}, bf16[3,3072,128]{2,1,0:T(8,128)(2,1)}, u32[]{:S(2)}, u32[]{:S(2)}) collective-permute-start(bf16[3,3072,128]{2,1,0:T(8,128)(2,1)} %pad_maximum_fusion.2.refs_8_), channel_id=1, source_target_pairs={{0,1},{1,0},{2,3},{3,2},{4,5},{5,4},{6,7},{7,6},{8,9},{9,8},{10,11... | collective-permute-start | bytes 7077896 | tf_op jit(solution)/shard_map/ppermute | solution.py:270
  625.5 53.5 %collective-permute-start.60 = (bf16[3,3072,128]{2,1,0:T(8,128)(2,1)}, bf16[3,3072,128]{2,1,0:T(8,128)(2,1)}, u32[]{:S(2)}, u32[]{:S(2)}) collective-permute-start(bf16[3,3072,128]{2,1,0:T(8,128)(2,1)} %pad_maximum_fusion.2.refs_8_), channel_id=1, source_target_pairs={{0,2},{1,3},{2,0},{3,1},{4,6},{5,7},{6,4},{7,5},{8,10},{9,11},{10,... | collective-permute-start | bytes 7077896 | tf_op jit(solution)/shard_map/ppermute | solution.py:270
  626.1 53.3 %collective-permute-start.61 = (bf16[3,3072,128]{2,1,0:T(8,128)(2,1)}, bf16[3,3072,128]{2,1,0:T(8,128)(2,1)}, u32[]{:S(2)}, u32[]{:S(2)}) collective-permute-start(bf16[3,3072,128]{2,1,0:T(8,128)(2,1)} %pad_maximum_fusion.2.refs_8_), channel_id=1, source_target_pairs={{0,4},{1,5},{2,6},{3,7},{4,0},{5,1},{6,2},{7,3},{8,12},{9,13},{10,... | collective-permute-start | bytes 7077896 | tf_op jit(solution)/shard_map/ppermute | solution.py:270
  627.0 41.8 %collective-permute-start.67 = (f32[48,4608]{1,0:T(8,128)}, f32[48,4608]{1,0:T(8,128)}, u32[]{:S(2)}, u32[]{:S(2)}) collective-permute-start(f32[48,4608]{1,0:T(8,128)} %get-tuple-element.258), channel_id=1, source_target_pairs={{0,8},{2,10},{4,12},{6,14},{1,9},{3,11},{5,13},{7,15}} | collective-permute-start | bytes 2654216 | tf_op jit(solution)/shard_map/ppermute | solution.py:280
  631.4 37.4 %collective-permute-start.68 = (f32[48,4608]{1,0:T(8,128)S(1)}, f32[48,4608]{1,0:T(8,128)}, u32[]{:S(2)}, u32[]{:S(2)}) collective-permute-start(f32[48,4608]{1,0:T(8,128)S(1)} %get-tuple-element.257), channel_id=1, source_target_pairs={{24,16},{26,18},{28,20},{30,22},{25,17},{27,19},{29,21},{31,23}} | collective-permute-start | bytes 2654216 | tf_op jit(solution)/shard_map/ppermute | solution.py:280
  679.4 17.7 %collective-permute-start.71 = (bf16[3,3072,128]{2,1,0:T(8,128)(2,1)}, bf16[3,3072,128]{2,1,0:T(8,128)(2,1)}, u32[]{:S(2)}, u32[]{:S(2)}) collective-permute-start(bf16[3,3072,128]{2,1,0:T(8,128)(2,1)} %collective-permute-done.60.refs_0_), channel_id=1, source_target_pairs={{0,1},{1,0},{2,3},{3,2},{4,5},{5,4},{6,7},{7,6},{8,9},{9,8},{10,11... | collective-permute-start | bytes 7077896 | tf_op jit(solution)/shard_map/ppermute | solution.py:270
  679.7 27.3 %collective-permute-start.72 = (bf16[3,3072,128]{2,1,0:T(8,128)(2,1)}, bf16[3,3072,128]{2,1,0:T(8,128)(2,1)}, u32[]{:S(2)}, u32[]{:S(2)}) collective-permute-start(bf16[3,3072,128]{2,1,0:T(8,128)(2,1)} %collective-permute-done.61.refs_2_), channel_id=1, source_target_pairs={{0,1},{1,0},{2,3},{3,2},{4,5},{5,4},{6,7},{7,6},{8,9},{9,8},{10,11... | collective-permute-start | bytes 7077896 | tf_op jit(solution)/shard_map/ppermute | solution.py:270
  687.5 39.0 %collective-permute-start.69 = (bf16[2,3072,128]{2,1,0:T(8,128)(2,1)}, bf16[2,3072,128]{2,1,0:T(8,128)(2,1)}, u32[]{:S(2)}, u32[]{:S(2)}) collective-permute-start(bf16[2,3072,128]{2,1,0:T(8,128)(2,1)} %slice.269), channel_id=1, source_target_pairs={{0,4},{1,5},{2,6},{3,7},{4,0},{5,1},{6,2},{7,3},{8,12},{9,13},{10,... | collective-permute-start | bytes 4718600 | tf_op jit(solution)/shard_map/ppermute | solution.py:270
  691.7 34.7 %collective-permute-start.73 = (f32[48,4608]{1,0:T(8,128)}, f32[48,4608]{1,0:T(8,128)}, u32[]{:S(2)}, u32[]{:S(2)}) collective-permute-start(f32[48,4608]{1,0:T(8,128)} %get-tuple-element.256), channel_id=1, source_target_pairs={{0,8},{2,10},{4,12},{6,14},{8,16},{10,18},{12,20},{14,22},{1,9},{3... | collective-permute-start | bytes 2654216 | tf_op jit(solution)/shard_map/ppermute | solution.py:280
  695.3 31.1 %collective-permute-start.74 = (f32[48,4608]{1,0:T(8,128)}, f32[48,4608]{1,0:T(8,128)}, u32[]{:S(2)}, u32[]{:S(2)}) collective-permute-start(f32[48,4608]{1,0:T(8,128)} %get-tuple-element.255), channel_id=1, source_target_pairs={{16,8},{18,10},{20,12},{22,14},{24,16},{26,18},{28,20},{30,22},{17... | collective-permute-start | bytes 2654216 | tf_op jit(solution)/shard_map/ppermute | solution.py:280
  697.1 29.3 %collective-permute-start.70 = (bf16[1,3072,128]{2,1,0:T(8,128)(2,1)}, bf16[1,3072,128]{2,1,0:T(8,128)(2,1)}, u32[]{:S(2)}, u32[]{:S(2)}) collective-permute-start(bf16[1,3072,128]{2,1,0:T(8,128)(2,1)} %slice.270), channel_id=1, source_target_pairs={{0,2},{1,3},{2,0},{3,1},{4,6},{5,7},{6,4},{7,5},{8,10},{9,11},{10,... | collective-permute-start | bytes 2359304 | tf_op jit(solution)/shard_map/ppermute | solution.py:270
  728.6 19.7 %collective-permute-start.77 = (f32[48,4608]{1,0:T(8,128)S(1)}, f32[48,4608]{1,0:T(8,128)S(1)}, u32[]{:S(2)}, u32[]{:S(2)}) collective-permute-start(f32[48,4608]{1,0:T(8,128)S(1)} %get-tuple-element.253), channel_id=1, source_target_pairs={{0,8},{2,10},{4,12},{6,14},{8,16},{10,18},{12,20},{14,22},{16,24},... | collective-permute-start | bytes 2654216 | tf_op jit(solution)/shard_map/ppermute | solution.py:280
  730.0 23.1 %collective-permute-start.78 = (f32[48,4608]{1,0:T(8,128)S(1)}, f32[48,4608]{1,0:T(8,128)S(1)}, u32[]{:S(2)}, u32[]{:S(2)}) collective-permute-start(f32[48,4608]{1,0:T(8,128)S(1)} %get-tuple-element.254), channel_id=1, source_target_pairs={{8,0},{10,2},{12,4},{14,6},{16,8},{18,10},{20,12},{22,14},{24,16},... | collective-permute-start | bytes 2654216 | tf_op jit(solution)/shard_map/ppermute | solution.py:280
  737.0 25.4 %collective-permute-start.75 = (bf16[2,3072,128]{2,1,0:T(8,128)(2,1)}, bf16[2,3072,128]{2,1,0:T(8,128)(2,1)S(1)}, u32[]{:S(2)}, u32[]{:S(2)}) collective-permute-start(bf16[2,3072,128]{2,1,0:T(8,128)(2,1)} %collective-permute-done.69.refs_0_), channel_id=1, source_target_pairs={{0,1},{1,0},{2,3},{3,2},{4,5},{5,4},{6,7},{7,6},{8,9},{9,8},{10,11... | collective-permute-start | bytes 4718600 | tf_op jit(solution)/shard_map/ppermute | solution.py:270
  (159 other events, 2006.8 us)
Sparse Core Ops, SparseCore 0:
  11.4 61.5 all-gather.11
  76.5 89.3 all-gather.5
  169.5 101.6 all-gather.7
  547.3 56.5 all-gather.9

commit v4 on v3

--- a/solution.py
+++ b/solution.py
@@ -258,6 +258,28 @@
     return (weight - rate * (step + 0.01 * weight), first, second)
 
 
+def adamw_kernel(clip_ref, *refs, rates):
+    n = len(rates)
+    for k, rate in enumerate(rates):
+        weight, first, second, grad = [ref[...] for ref in refs[4 * k : 4 * k + 4]]
+        outs = refs[4 * n + 3 * k : 4 * n + 3 * k + 3]
+        for out, value in zip(outs, adamw(weight, first, second, clip_ref[0] * grad, rate)):
+            out[...] = value
+
+
+def adamw_all(clip, quads, rates):
+    vmem = pl.BlockSpec(memory_space=pltpu.VMEM)
+    flat = [value for quad in quads for value in quad]
+    shapes = [jax.ShapeDtypeStruct(quad[0].shape, f32) for quad in quads for _ in range(3)]
+    return pl.pallas_call(
+        functools.partial(adamw_kernel, rates=rates),
+        in_specs=[pl.BlockSpec(memory_space=pltpu.SMEM)] + [vmem] * len(flat),
+        out_specs=[vmem] * len(shapes),
+        out_shape=shapes,
+        compiler_params=pltpu.CompilerParams(vmem_limit_bytes=48 * 2**20),
+    )(clip.reshape(1), *flat)
+
+
 def hop(x, dl=0, dq=0, dr=0):
     reps = lax.axis_size("rep")
     lines = lax.axis_size("dp") // PLANE
@@ -355,33 +377,50 @@
     return jnp.sum(every, 0)
 
 
-def mix_kernel(idx_ref, mix_ref, *refs, groups, cands, counts):
-    pieces = refs[: len(counts)]
-    out_ref, tab, stage, sem = refs[-4:]
+def mix_kernel(idx_ref, mix_ref, *refs, groups, cands, counts, keep):
+    n = len(counts)
+    pieces, refs = refs[:n], refs[n:]
+    if keep:
+        out_ref, whole_ref, tab, stage, sem, keep_sem = refs
+    else:
+        out_ref, tab, stage, sem = refs
+    slots = stage.shape[0]
+    bases = [sum(counts[:j]) for j in range(n)]
 
     @pl.when(pl.program_id(0) == 0)
     def _():
+        def slot(j):
+            return stage.at[j % slots, pl.ds(0, counts[j])]
+
         def copy(j):
-            return pltpu.make_async_copy(
-                pieces[j], stage.at[j % 2, pl.ds(0, counts[j])], sem.at[j % 2]
-            )
-
-        copy(0).start()
-        base = 0
-        for j, rows in enumerate(counts):
-            if j + 1 < len(counts):
-                copy(j + 1).start()
+            return pltpu.make_async_copy(pieces[j], slot(j), sem.at[j % slots])
+
+        def store(j):
+            whole = whole_ref.at[pl.ds(bases[j], counts[j])]
+            return pltpu.make_async_copy(slot(j), whole, keep_sem.at[j % slots])
+
+        for j in range(min(2, n)):
+            copy(j).start()
+        for j in range(n):
             copy(j).wait()
-
-            @pl.loop(0, rows // 16)
-            def _(t, j=j, base=base):
-                part = stage[j % 2, pl.ds(pl.multiple_of(t * 16, 16), 16), :].astype(f32)
+            if keep:
+                store(j).start()
+
+            @pl.loop(0, counts[j] // 16)
+            def _(t, j=j):
+                part = stage[j % slots, pl.ds(pl.multiple_of(t * 16, 16), 16), :].astype(f32)
                 for g in range(groups):
-                    tab[pl.ds((base + t * 16) * groups + g, 16, stride=groups), :] = part[
+                    tab[pl.ds((bases[j] + t * 16) * groups + g, 16, stride=groups), :] = part[
                         :, g * LANES : (g + 1) * LANES
                     ]
 
-            base += rows
+            if keep and j >= 2:
+                store(j - 2).wait()
+            if j + 2 < n:
+                copy(j + 2).start()
+        if keep:
+            for j in range(max(0, n - 2), n):
+                store(j).wait()
 
     unroll = 4
 
@@ -397,23 +436,32 @@
             out_ref[0, pl.ds(p * groups, 8), :] = total
 
 
-def mix_rows(idx, mix, pieces, cands):
-    groups = pieces[0].shape[1] // LANES
+def mix_rows(idx, mix, pieces, cands, keep):
+    width = pieces[0].shape[1]
+    groups = width // LANES
     lines, _, entries = idx.shape
     counts = tuple(piece.shape[0] for piece in pieces)
     rows = entries // cands * groups + 8
+    out_specs = [pl.BlockSpec((1, rows, LANES), lambda i: (i, 0, 0))]
+    out_shape = [jax.ShapeDtypeStruct((lines, rows, LANES), f32)]
+    slots = 4
+    scratch = [
+        pltpu.VMEM((sum(counts) * groups + 8, LANES), f32),
+        pltpu.VMEM((slots, max(counts), width), bf16),
+        pltpu.SemaphoreType.DMA((slots,)),
+    ]
+    if keep:
+        out_specs.append(pl.BlockSpec(memory_space=pl.ANY))
+        out_shape.append(jax.ShapeDtypeStruct((sum(counts), width), bf16))
+        scratch.append(pltpu.SemaphoreType.DMA((slots,)))
     return pl.pallas_call(
-        functools.partial(mix_kernel, groups=groups, cands=cands, counts=counts),
+        functools.partial(mix_kernel, groups=groups, cands=cands, counts=counts, keep=keep),
         grid=(lines,),
         in_specs=[pl.BlockSpec((1, 1, entries), lambda i: (i, 0, 0), memory_space=pltpu.SMEM)] * 2
         + [pl.BlockSpec(memory_space=pl.ANY)] * len(pieces),
-        out_specs=pl.BlockSpec((1, rows, LANES), lambda i: (i, 0, 0)),
-        out_shape=jax.ShapeDtypeStruct((lines, rows, LANES), f32),
-        scratch_shapes=[
-            pltpu.VMEM((sum(counts) * groups + 8, LANES), f32),
-            pltpu.VMEM((2, max(counts), groups * LANES), bf16),
-            pltpu.SemaphoreType.DMA((2,)),
-        ],
+        out_specs=out_specs,
+        out_shape=out_shape,
+        scratch_shapes=scratch,
         compiler_params=pltpu.CompilerParams(vmem_limit_bytes=60 * 2**20),
         cost_estimate=pl.CostEstimate(
             flops=lines * entries * 2048, bytes_accessed=40 * 2**20, transcendentals=0
@@ -588,6 +636,9 @@
     groups = width // LANES
     swaps = [(dq, dr) for dq in range(PLANE) for dr in range(reps)]
 
+    def from_me(values):
+        return lax.dynamic_slice_in_dim(jnp.concatenate([values, values], 0), line, lines)
+
     def gather(value, axis=0):
         return lax.all_gather(value.astype(bf16), BOTH, axis=axis, tiled=True)
 
@@ -599,11 +650,7 @@
             [mod_proj, final_proj, time_proj.reshape(few, -1), gains_flat.reshape(few, LANES)], 1
         )
     )
-    wide_all = gather(jnp.concatenate([attn_proj, out_proj, up_proj], 1))
-    down_w = gather(down_proj)
-    qkv_w = wide_all[:, : 3 * width]
-    out_w = wide_all[:, 3 * width : 4 * width]
-    up_w = wide_all[:, 4 * width :]
+    qkv_w = gather(attn_proj)
 
     padded = -(-vocab // 16) * 16
     table_low = jnp.pad(vocab_table.astype(bf16), ((0, padded - vocab), (0, 0)))
@@ -619,8 +666,8 @@
     mixing = jax.nn.softmax(option_scores.reshape(half, cands) / annealed_softness, axis=-1)
     names = (owner * padded + offset).astype(f32).reshape(-1, LANES)
     packed = jnp.concatenate([names, mixing.reshape(-1, LANES)], 0)
-    on_line = jnp.stack([packed] + [hop(packed, dl=-d) for d in range(1, lines)])
-    on_line, owner, offset = lax.optimization_barrier((on_line, owner, offset))
+    groups_of_line = [[l * PLANE + q for l in range(lines)] for q in range(PLANE)]
+    on_line = lax.all_gather(packed, "dp", axis_index_groups=groups_of_line)
     cap = max(2, 2 * half * cands // devices)
     member = (owner[:, None] == jnp.arange(devices, dtype=jnp.int32)[None, :]).astype(jnp.int32)
     slot = jnp.sum((jnp.cumsum(member, 0) - member) * member, 1)
@@ -632,6 +679,7 @@
     for dq in range(PLANE):
         pieces += [first[dq], second[dq]]
         pieces += [hop(first[dq], dr=1), hop(second[dq], dr=1)]
+    on_line = from_me(on_line)
     line_owner = on_line[:, : names.shape[0]].astype(jnp.int32)
     line_mix = on_line[:, names.shape[0] :]
     row_owner = line_owner // padded
@@ -643,21 +691,31 @@
     mix_here = mix_here.reshape(lines, 1, half * cands)
     parts = {}
 
-    def mix_some(which):
+    def mix_some(which, keep):
         out = mix_rows(
             jnp.stack([row_at[d] for d in which]),
             jnp.stack([mix_here[d] for d in which]),
             pieces,
             cands,
+            keep,
         )
         for k, d in enumerate(which):
-            parts[d] = out[k, : half * groups]
-
-    mix_some((1, lines - 1))
-    far_parts = [hop(parts[d].astype(bf16), dl=d) for d in (1, lines - 1)]
-    mix_some(tuple(range(2, lines - 1)) + (0,))
-    for d in range(2, lines - 1):
-        far_parts.append(hop(parts[d].astype(bf16), dl=d))
+            parts[d] = out[0][k, : half * groups]
+        return out[-1]
+
+    outer = (1, lines - 1)
+    mix_some(outer, False)
+    out_up = jnp.concatenate([out_proj, up_proj], 1)
+    parts[1], parts[lines - 1], out_up, down_shard = lax.optimization_barrier(
+        (parts[1], parts[lines - 1], out_up.astype(bf16), down_proj.astype(bf16))
+    )
+    out_up = gather(out_up)
+    down_w = gather(down_shard)
+    out_w, up_w = out_up[:, :width], out_up[:, width:]
+    far_parts = [hop(parts[d].astype(bf16), dl=d) for d in outer]
+    inner = tuple(range(2, lines - 1))
+    plane_table = mix_some(inner + (0,), True)
+    far_parts += [hop(parts[d].astype(bf16), dl=d) for d in inner]
     far_parts[:2], flat_slot, small_all = lax.optimization_barrier(
         (far_parts[:2], flat_slot, small_all)
     )
@@ -729,9 +787,6 @@
         )
         return from_me(mine.reshape(lines, picks))
 
-    def from_me(values):
-        return lax.dynamic_slice_in_dim(jnp.concatenate([values, values], 0), line, lines)
-
     def from_start(values):
         return lax.dynamic_slice_in_dim(
             jnp.concatenate([values, values], 0), (lines - line) % lines, lines
@@ -746,7 +801,6 @@
     asked = lax.all_to_all(asked, BOTH, split_axis=0, concat_axis=0, tiled=True)
     every, act_far, asked = lax.optimization_barrier((every, hop(act_b, dr=1), asked))
     asked, asked_mix = asked[:, :cap].astype(jnp.int32), asked[:, cap:]
-    plane_table = jnp.concatenate(pieces, 0)
     logits = dense_nt(every, plane_table)
     column = jnp.arange(plane_table.shape[0], dtype=jnp.int32)
     exists = (column % padded) < vocab
@@ -787,8 +841,6 @@
     extra = jnp.pad(jnp.stack(pieces_of_lse, 1), ((0, 0), (0, LANES - 3)))
     told = jnp.concatenate([every, extra], 1)
     told_x, told_y = hop(told, dq=1), hop(told, dq=2)
-    told = jnp.stack([told, told_x, told_y, hop(told_x, dq=2)])
-    told = jnp.concatenate([told, hop(told, dr=1)], 0).reshape(-1, width + LANES)
     among = [(chip ^ dq, rep_idx ^ dr) for dr in range(reps) for dq in range(PLANE)]
     targets_all = jnp.concatenate([of_line(loss_target, q, r).reshape(-1) for q, r in among])
     weight_rows = jnp.concatenate([of_line(weight_all, q, r).reshape(-1) for q, r in among])
@@ -805,7 +857,9 @@
     dx1 = dx2 + dn2x
     dg1 = jnp.sum(dx1 * attn, 0)
     dattn = (dx1 * g1).astype(bf16)
-    dattn, g_down, g_up = lax.optimization_barrier((dattn, g_down, g_up))
+    dattn, g_down, g_up, told_x, told_y = lax.optimization_barrier(
+        (dattn, g_down, g_up, told_x, told_y)
+    )
     down_1 = split_blocks(plane_blocks(g_down), 1, 1)
     up_1 = split_blocks(plane_blocks(g_up), 0, 2)
     g_out = chip_product(mixed_b, mixed_far, dattn)
@@ -813,6 +867,7 @@
     dquery, dkey, dkey_far, dvalue, dvalue_far = attend_back(
         length, core, *attended, lse_att, dmixed, *turns
     )
+    told_xy = hop(told_x, dq=2)
     dquery, dkey, dkey_far, dvalue, dvalue_far, down_1, up_1, g_out = lax.optimization_barrier(
         (dquery, dkey, dkey_far, dvalue, dvalue_far, down_1, up_1, g_out)
     )
@@ -837,6 +892,8 @@
     on_line = gather_line(dx0_b)
     own_x, own_y = hop(dx0_b, dq=1), hop(dx0_b, dq=2)
     own_xy = hop(own_y, dq=1)
+    told = jnp.stack([told, told_x, told_y, told_xy])
+    told = jnp.concatenate([told, hop(told, dr=1)], 0).reshape(-1, width + LANES)
     g_last = jnp.concatenate([g_qkv, g_out], 1)
     last_1 = split_blocks(plane_blocks(g_last), 1, 1)
     sums_all = lax.all_gather(sums_here.reshape(1, -1, LANES), BOTH, axis=0, tiled=True)
@@ -904,7 +961,13 @@
     begun = spread_rows(lists_of(order), sources, vocab, width, begun)
     order.clear()
     near, rest, begun, sums = lax.optimization_barrier((near, rest, begun, sums))
+    sources = from_cores([(near, 3, 1)] + [(value, 3, 1 + cut) for value in rest])
+    sources, sums = lax.optimization_barrier((sources, sums))
     sums = reduce_step(blocks, sums, 1)
+    table_grad, table_squares = spread_rows(
+        lists_of(order), sources, vocab, width, begun, head_grad
+    )
+    sums, table_grad, table_squares = lax.optimization_barrier((sums, table_grad, table_squares))
     total = block_at(blocks, 0) + sums[0] + sums[1]
     down_end = tall * pile.shape[3]
     pile = jnp.stack(jnp.split(total[:, :down_end], tall, 1))
@@ -917,10 +980,6 @@
         joined.append(jnp.concatenate([left[:, part], right[:, part]], 1))
         at += columns // 2
     d_up, d_qkv, d_out = joined
-    sources = from_cores([(near, 3, 1)] + [(value, 3, 1 + cut) for value in rest])
-    table_grad, table_squares = spread_rows(
-        lists_of(order), sources, vocab, width, begun, head_grad
-    )
 
     sums_all = sums_all.reshape(n_dp, reps, -1).sum(1)
     dmods = sums_all[:, : 6 * width]
@@ -962,8 +1021,10 @@
     rates = (0.02, 0.02, 0.02, 0.02, 0.02, 0.02, 0.02, 0.02, 0.1)
     grads = (table_grad,) + reduced
     result = [loss_sum, coefficient_aggregate, grad_norm]
-    for weight_now, first_m, second_m, grad, rate in zip(coefficients, moms, sqs, grads, rates):
-        result.extend(adamw(weight_now, first_m, second_m, clip * grad, rate))
+    quads = list(zip(coefficients, moms, sqs, grads))
+    weight_now, first_m, second_m, grad = quads[0]
+    result.extend(adamw(weight_now, first_m, second_m, clip * grad, rates[0]))
+    result.extend(adamw_all(clip, quads[1:], rates[1:]))
     return tuple(result)
 
 

time: 850 us -> 827 us (0.973)
  local copies, waits for them, and re-layouts: 129 us -> 105 us
  blocking collectives: 0 us -> 13.7 us
    unnamed x298 -> x305, local copies, waits for them, and re-layouts: 50 us -> 21.3 us
    ppermute x76 -> x73, waiting for transfers between devices: 111 us -> 127 us  [hop(): return lax.ppermute(x, BOTH, pairs)]
    ppermute x6, waiting for transfers between devices: 13.9 us -> 0.02 us  [step_line(): return lax.ppermute(x, 'dp', pairs)]
    all_gather x0 -> x1, blocking collectives: none -> 13.7 us  [local(): on_line = lax.all_gather(packed, 'dp', axis_index_groups=groups_of_line)]
    all_gather x1, starting transfers between devices: 8.72 us -> 0.22 us  [local(): lax.all_gather(sums_here.reshape(1, -1, LANES), BOTH, axis=0, tiled=True)]
    sub x9 -> x1, other arithmetic: 20.4 us -> 13.4 us  [adamw(): return (weight - rate * (step + 0.01 * weight), first, second)]
    ppermute x76 -> x73, starting transfers between devices: 70.6 us -> 67.2 us  [hop(): return lax.ppermute(x, BOTH, pairs)]
    another operation x15 -> x11, other arithmetic: 28.3 us -> 26.7 us
  transfers between devices with their start and end apart: 93 -> 91, of which waited for: 26 -> 32; matrix products, arithmetic and copies ran while one was open for 35% -> 33% of each run, Pallas kernels for 17% -> 20%
where the time goes in v4:
time: 827 us; the launch traced here: 813 us
  Pallas kernels  166 us (20%)
  waiting for transfers between devices  163 us (20%)
  other arithmetic  126 us (15%)
  matrix products  113 us (14%)
  local copies, waits for them, and re-layouts  105 us (13%)
  starting transfers between devices  101 us (12%)
  between operations  25.5 us (3%)
  blocking collectives  13.7 us (2%)
    ppermute x73, waiting for transfers between devices, hop(): return lax.ppermute(x, BOTH, pairs)  127 us
    ppermute x73, starting transfers between devices, hop(): return lax.ppermute(x, BOTH, pairs)  67.2 us
    pallas_call x2, Pallas kernels, mix_rows(): pl.pallas_call(functools.partial(mix_kernel, groups=groups, cands=cands,...  58.2 us
    pallas_call x3, Pallas kernels, spread_rows(): pl.pallas_call(functools.partial(spread_kernel, groups=groups, arrays=len...  55.6 us
    dot_general x5, matrix products, dense(): return jnp.dot(a, b, preferred_element_type=f32)  39.4 us
    ppermute x6, waiting for transfers between devices, pass_on(): return lax.ppermute(x, 'dp', pairs)  35.8 us
    dot_general x9, matrix products, dense_tn(): lax.dot_general(a, b, (((0,), (0,)), ((), ())), preferred_element_type=f32)  33.3 us
    scatter x2, local copies, waits for them, and re-layouts, local(): empty.at[flat_slot].set(value).reshape(devices, cap)  31.6 us
  transfers between devices with their start and end apart: 91, of which 32 were waited for; matrix products, arithmetic and copies ran while one was open for 33% of the time, Pallas kernels for 20%

profile of v4, /device:TPU:0, one launch (start us, length us, event | category | flops | bytes accessed | tf_op | source)
XLA Modules:
  0.0 813.4 jit_solution(16904345665857227594)
XLA Ops:
  15.5 3.0 collective-permute-start.1
  23.7 18.1 %reduce-window.6 = s32[32,32,128]{2,1,0:T(8,128)} reduce-window(s32[32,32,128]{2,1,0:T(8,128)} %fusion.49, s32[]{:T(128)} %constant.587.clone.1), window={size=1x1x128 pad=0_0x0_0x127_0}, to_apply=%region_2.3 | reduce-window | flops 16646144 | bytes 1048580 | tf_op jit(solution)/shard_map/reduce-window
  47.1 2.8 collective-permute-done.refs_4_
  50.0 25.6 %collective-permute-done.3.refs_9_ = bf16[800,768]{1,0:T(8,128)(2,1)} collective-permute-done((bf16[800,768]{1,0:T(8,128)(2,1)S(1)}, bf16[800,768]{1,0:T(8,128)(2,1)}, u32[]{:S(2)}, u32[]{:S(2)}) %collective-permute-start.3) | collective-permute-done | bytes 1228832 | tf_op jit(solution)/shard_map/ppermute | solution.py:292
  80.3 13.7 %all-gather = f32[256,128]{1,0:T(8,128)S(1)} all-gather(f32[64,128]{1,0:T(8,128)S(1)} %pad_maximum_fusion.14), channel_id=2, replica_groups={{0,8,16,24},{2,10,18,26},{4,12,20,28},{6,14,22,30},{1,9,17,25},{3,11,19..., dimensions={0}, use_global_device_ids=true | all-gather | bytes 163840 | tf_op jit(solution)/shard_map/all_gather | solution.py:670
  95.9 11.6 %collective-permute-done.10.refs_12_ = bf16[784,768]{1,0:T(8,128)(2,1)} collective-permute-done((bf16[784,768]{1,0:T(8,128)(2,1)}, bf16[784,768]{1,0:T(8,128)(2,1)}, u32[]{:S(2)}, u32[]{:S(2)}) %collective-permute-start.10) | collective-permute-done | bytes 1204256 | tf_op jit(solution)/shard_map/ppermute | solution.py:292
  108.0 4.3 collective-permute-done.11.refs_13_
  118.5 27.6 %shard_map.554 = f32[2,3080,128]{2,1,0:T(8,128)} custom-call(s32[2,1,4096]{2,1,0:T(1,128)} %pad_add_fusion.1.idx_ref, f32[2,1,4096]{2,1,0:T(1,128)} %pad_maximum_fusion.16.mix_ref, bf16[784,768]{1,0:T(8,128)(2,1)} %copy-done.46, bf16[800,768]{1,0:T(8,128)(2,1)} %copy-done.45, bf16[784,768]{1,0:T(8,128)(2,1)} %collective-permute-done.4.refs_2_, ...), custom_call_target="tpu_custom_call" | custom-call | flops 16777216 | bytes 41943040 | tf_op jit(solution)/shard_map/pallas_call | solution.py:457
  146.1 3.3 slice_bitcast_fusion
  155.6 2.9 fusion.73
  168.5 2.7 reshape.2363
  171.3 30.6 %shard_map.553 = (f32[2,3080,128]{2,1,0:T(8,128)}, bf16[12672,768]{1,0:T(8,128)(2,1)}) custom-call(s32[2,1,4096]{2,1,0:T(1,128)} %pad_add_fusion.idx_ref, f32[2,1,4096]{2,1,0:T(1,128)} %pad_maximum_fusion.15.mix_ref, bf16[784,768]{1,0:T(8,128)(2,1)} %copy-done.46, bf16[800,768]{1,0:T(8,128)(2,1)} %copy-done.45, ...), custom_call_target="tpu_custom_call" | custom-call | flops 16777216 | bytes 41943040 | tf_op jit(solution)/shard_map/pallas_call | solution.py:457
  205.2 4.7 collective-permute-done.15
  210.0 15.5 %scatter_custom_fusion = f32[8192]{0:T(1024)S(1)} fusion(s32[4096]{0:T(1024)S(1)} %get-tuple-element.418, f32[4096]{0:T(1024)S(1)} %get-tuple-element.419, f32[]{:T(128)} %constant.583.clone.1), kind=kCustom, calls=%fused_computation.355 | custom fusion | bytes 32772 | tf_op jit(solution)/shard_map/scatter | solution.py:725
  225.5 16.0 %scatter_custom_fusion.1 = f32[8192]{0:T(1024)S(1)} fusion(s32[4096]{0:T(1024)S(1)} %get-tuple-element.418, f32[4096]{0:T(1024)S(1)} %exponential_divide_fusion, f32[]{:T(128)} %constant.583.clone.1), kind=kCustom, calls=%fused_computation.353 | custom fusion | bytes 32772 | tf_op jit(solution)/shard_map/scatter | solution.py:725
  243.8 16.8 %collective-permute-done.16 = bf16[3072,128]{1,0:T(8,128)(2,1)} collective-permute-done((bf16[3072,128]{1,0:T(8,128)(2,1)}, bf16[3072,128]{1,0:T(8,128)(2,1)}, u32[]{:S(2)}, u32[]{:S(2)}) %collective-permute-start.16) | collective-permute-done | bytes 786464 | tf_op jit(solution)/shard_map/ppermute | solution.py:292
  260.6 3.5 fusion.170
  266.3 2.9 multiply_reduce_fusion.10
  274.0 6.5 fusion.180.q_ref.k_ref.v_ref
  280.4 4.8 shard_map.555
  292.6 17.4 %shard_map.556 = (bf16[512,768]{1,0:T(8,128)(2,1)S(1)}, f32[512,768]{1,0:T(8,128)}) custom-call(s32[1]{0:T(128)} %dynamic_slice.237.len_ref, s32[1]{0:T(128)} %bitcast.21.core_ref, bf16[512,768]{1,0:T(8,128)(2,1)S(1)} %copy-done.29, bf16[512,768]{1,0:T(8,128)(2,1)S(1)} %copy-done.31, bf16[512,768]{1,0:T(8,128)(2,1)S(1)} %collective-permute-done.17.kf_ref, ...), custom_call_target="tpu_custom_call" | custom-call | flops 1610612736 | bytes 7077888 | tf_op jit(solution)/shard_map/pallas_call | solution.py:161
  310.2 3.9 fusion.169
  316.1 5.8 multiply_convert_fusion.3
  327.3 4.3 all-to-all-start
  333.2 7.5 fusion.168
  350.7 3.6 collective-permute-done.23
  354.4 12.2 %fusion.179 = (f32[256]{0:T(256)S(1)}, f32[256,12672]{1,0:T(8,128)}) fusion(bf16[256,768]{1,0:T(8,128)(2,1)S(1)} %pad_maximum_fusion.4, bf16[12672,768]{1,0:T(8,128)(2,1)} %get-tuple-element.174, pred[12672]{0:T(1024)(128)(4,1)S(1)} %copy-done.108), kind=kOutput, calls=%fused_computation.558 | convolution fusion | flops 4989321216 | bytes 32847232 | tf_op jit(solution)/shard_map/dot_general | solution.py:29
  366.7 6.9 exponential_reduce_fusion
  373.7 3.7 collective-permute-start.26
  384.0 15.8 %fusion = f32[256,768]{1,0:T(8,128)S(1)} fusion(bf16[12672,768]{1,0:T(8,128)(2,1)} %get-tuple-element.174, f32[256,12672]{1,0:T(8,128)} %get-tuple-element.408, f32[256]{0:T(256)S(1)} %reshape.2256, f32[256]{0:T(256)S(1)} %copy-done.125, s32[256]{0:T(256)S(1)} %copy-done.117), kind=kOutput, calls=%fused_computation.19 | convolution fusion | flops 5002297344 | bytes 33229824 | tf_op jit(solution)/shard_map/dot_general | solution.py:25
  400.1 4.0 collective-permute-start.31
  404.8 4.8 collective-permute-done.29
  409.9 8.5 %collective-permute-done.30 = f32[64,768]{1,0:T(8,128)S(1)} collective-permute-done((f32[64,768]{1,0:T(8,128)S(1)}, f32[64,768]{1,0:T(8,128)S(1)}, u32[]{:S(2)}, u32[]{:S(2)}) %collective-permute-start.30) | collective-permute-done | bytes 196640 | tf_op jit(solution)/shard_map/ppermute | solution.py:292
  422.6 3.5 multiply_reduce_fusion
  427.7 8.0 fusion.10
  437.1 3.5 multiply_reduce_fusion.2
  444.8 3.7 fusion.181
  448.5 3.8 convolution_add_fusion
  461.8 3.0 convolution_convert_fusion.do_ref
  464.8 27.5 %shard_map.557 = (bf16[512,768]{1,0:T(8,128)(2,1)S(1)}, f32[512,768]{1,0:T(8,128)}, bf16[512,768]{1,0:T(8,128)(2,1)S(1)}, f32[512,768]{1,0:T(8,128)}, bf16[512,768]{1,0:T(8,128)(2,1)S(1)}) custom-call(s32[1]{0:T(128)} %dynamic_slice.237.len_ref, s32[1]{0:T(128)} %bitcast.21.core_ref, bf16[512,768]{1,0:T(8,128)(2,1)S(1)} %copy-done.30, ...), custom_call_target="tpu_custom_call" | custom-call | flops 4026531840 | bytes 12582912 | tf_op jit(solution)/shard_map/pallas_call | solution.py:239
  497.6 2.7 pad_maximum_fusion.3
  513.2 2.9 multiply_reduce_fusion.4
  520.1 2.7 pad_maximum_fusion.1
  536.4 6.7 collective-permute-done.44
  543.9 4.6 collective-permute-done.43
  560.6 9.1 %collective-permute-done.47 = bf16[1,3072,128]{2,1,0:T(8,128)(2,1)S(1)} collective-permute-done((bf16[1,3072,128]{2,1,0:T(8,128)(2,1)}, bf16[1,3072,128]{2,1,0:T(8,128)(2,1)S(1)}, u32[]{:S(2)}, u32[]{:S(2)}) %collective-permute-start.47) | collective-permute-done | bytes 786464 | tf_op jit(solution)/shard_map/ppermute | solution.py:337
  570.5 11.2 %collective-permute-done.53 = bf16[4,2,48,1536]{3,2,0,1:T(8,128)(2,1)S(1)} collective-permute-done((bf16[4,2,48,1536]{3,2,0,1:T(8,128)(2,1)S(1)}, bf16[4,2,48,1536]{3,2,0,1:T(8,128)(2,1)S(1)}, u32[]{:S(2)}, u32[]{:S(2)}) %collective-permute-start.53) | collective-permute-done | bytes 1179680 | tf_op jit(solution)/shard_map/ppermute | solution.py:292
  585.4 15.3 %collective-permute-done.48 = bf16[1,3072,128]{2,1,0:T(8,128)(2,1)S(1)} collective-permute-done((bf16[1,3072,128]{2,1,0:T(8,128)(2,1)S(1)}, bf16[1,3072,128]{2,1,0:T(8,128)(2,1)S(1)}, u32[]{:S(2)}, u32[]{:S(2)}) %collective-permute-start.48) | collective-permute-done | bytes 786464 | tf_op jit(solution)/shard_map/ppermute | solution.py:337
  602.7 7.8 collective-permute-done.54
  615.1 2.9 dynamic-slice_bitcast_fusion.5
  621.0 5.9 collective-permute-start.64
  626.9 15.9 %fusion.16.refs_5_ = f32[1584,768]{1,0:T(8,128)} fusion(bf16[2048,896]{1,0:T(8,128)(2,1)} %bitcast.339, s32[2048]{0:T(1024)S(1)} %copy-done.112, f32[2048]{0:T(1024)S(1)} %convert_reduce_fusion, f32[2048]{0:T(1024)S(1)} %copy-done.111, bf16[1572,768]{1,0:T(8,128)(2,1)S(1)} %copy-done.40), kind=kOutput, calls=%fused_computation.42 | convolution fusion | flops 9985130496 | bytes 13596672 | tf_op jit(solution)/shard_map/dot_general | solution.py:33
  642.8 19.5 %shard_map.558.refs_4_ = f32[12608,128]{1,0:T(8,128)} custom-call(s32[14]{0:T(128)} %get-tuple-element.357.cnt_ref, s32[14,256]{1,0:T(8,128)} %get-tuple-element.356.row_ref, s32[14,256]{1,0:T(8,128)} %get-tuple-element.355.pos_ref, f32[14,256]{1,0:T(8,128)} %broadcast_select_fusion.4.mix_ref, bf16[1,3072,128]{2,1,0:T(8,128)(2,1)} %reshape.2262.refs_0_, ...), custom_call_target="tpu_custom_call" | custom-call | flops 3670016 | bytes 18350080 | tf_op jit(solution)/shard_map/pallas_call | solution.py:569
  662.4 9.1 %collective-permute-done.58.refs_2_ = bf16[3,3072,128]{2,1,0:T(8,128)(2,1)} collective-permute-done((bf16[3,3072,128]{2,1,0:T(8,128)(2,1)}, bf16[3,3072,128]{2,1,0:T(8,128)(2,1)}, u32[]{:S(2)}, u32[]{:S(2)}) %collective-permute-start.58) | collective-permute-done | bytes 2359328 | tf_op jit(solution)/shard_map/ppermute | solution.py:292
  676.6 3.4 bitcast_add_fusion.4
  681.7 5.3 collective-permute-start.70
  692.8 19.7 %shard_map.559.refs_4_ = f32[12608,128]{1,0:T(8,128)} custom-call(s32[12]{0:T(128)} %get-tuple-element.354.cnt_ref, s32[12,256]{1,0:T(8,128)} %get-tuple-element.353.row_ref, s32[12,256]{1,0:T(8,128)} %get-tuple-element.352.pos_ref, f32[12,256]{1,0:T(8,128)} %broadcast_select_fusion.3.mix_ref, bf16[3,3072,128]{2,1,0:T(8,128)(2,1)} %collective-permute-done.57.refs_0_, ...), custom_call_target="tpu_custom_call" | custom-call | flops 3145728 | bytes 15728640 | tf_op jit(solution)/shard_map/pallas_call | solution.py:569
  721.4 3.4 bitcast_add_fusion.3
  726.1 5.6 collective-permute-start.74
  735.6 16.4 %shard_map.560 = (f32[1572,768]{1,0:T(8,128)}, f32[8,128]{1,0:T(8,128)}) custom-call(s32[6]{0:T(128)} %get-tuple-element.378.cnt_ref, s32[6,256]{1,0:T(8,128)} %get-tuple-element.377.row_ref, s32[6,256]{1,0:T(8,128)} %get-tuple-element.376.pos_ref, f32[6,256]{1,0:T(8,128)} %broadcast_select_fusion.5.mix_ref, ...), custom_call_target="tpu_custom_call" | custom-call | flops 1572864 | bytes 7864320 | tf_op jit(solution)/shard_map/pallas_call | solution.py:569
  765.7 6.4 collective-permute-start.81
  772.2 6.1 collective-permute-start.80
  781.9 3.7 collective-permute-start.82
  789.7 13.4 %multiply_subtract_fusion = (f32[1572,768]{1,0:T(8,128)}, f32[1572,768]{1,0:T(8,128)}, f32[1572,768]{1,0:T(8,128)}) fusion(f32[1572,768]{1,0:T(8,128)} %param.41, f32[1572,768]{1,0:T(8,128)} %get-tuple-element.239, f32[]{:T(128)} %min.3, f32[1572,768]{1,0:T(8,128)} %param.42, f32[1572,768]{1,0:T(8,128)} %param.43), kind=kLoop, calls=%fused_computation.32 | loop fusion | flops 19316736 | bytes 33804292 | tf_op jit(solution)/shard_map/sub | solution.py:258
  (791 shorter events, 219.6 us)
Async XLA Ops:
  7.2 161.3 %all-gather.16.cloned.1.call-start = ((), (), s32[]{:S(2)}) async-start(), calls=%async_computation.5 | async-start | bytes 1723392 | tf_op jit(solution)/shard_map/all_gather | solution.py:643
  11.1 262.9 %all-gather.8.cloned.1.call-start = ((), (), s32[]{:S(2)}) async-start(), calls=%async_computation.1 | async-start | bytes 3649536 | tf_op jit(solution)/shard_map/all_gather | solution.py:643
  12.7 297.4 %all-gather.10.cloned.1.call-start = ((), (), s32[]{:S(2)}) async-start(), calls=%async_computation.2 | async-start | bytes 6082560 | tf_op jit(solution)/shard_map/all_gather | solution.py:643
  15.5 31.6 %collective-permute-start.1 = (bf16[784,768]{1,0:T(8,128)(2,1)S(1)}, bf16[784,768]{1,0:T(8,128)(2,1)}, u32[]{:S(2)}, u32[]{:S(2)}) collective-permute-start(bf16[784,768]{1,0:T(8,128)(2,1)S(1)} %slice.298.refs_0_), channel_id=1, source_target_pairs={{0,4},{1,5},{2,6},{3,7},{4,0},{5,1},{6,2},{7,3},{8,12},{9,13},{10,... | collective-permute-start | bytes 3612680 | tf_op jit(solution)/shard_map/ppermute | solution.py:292
  18.6 31.4 %collective-permute-start = (bf16[784,768]{1,0:T(8,128)(2,1)S(1)}, bf16[784,768]{1,0:T(8,128)(2,1)}, u32[]{:S(2)}, u32[]{:S(2)}) collective-permute-start(bf16[784,768]{1,0:T(8,128)(2,1)S(1)} %slice.298.refs_0_), channel_id=1, source_target_pairs={{0,2},{1,3},{2,0},{3,1},{4,6},{5,7},{6,4},{7,5},{8,10},{9,11},{10,... | collective-permute-start | bytes 3612680 | tf_op jit(solution)/shard_map/ppermute | solution.py:292
  20.2 55.4 %collective-permute-start.3 = (bf16[800,768]{1,0:T(8,128)(2,1)S(1)}, bf16[800,768]{1,0:T(8,128)(2,1)}, u32[]{:S(2)}, u32[]{:S(2)}) collective-permute-start(bf16[800,768]{1,0:T(8,128)(2,1)S(1)} %pad_slice_fusion.refs_1_), channel_id=1, source_target_pairs={{0,4},{1,5},{2,6},{3,7},{4,0},{5,1},{6,2},{7,3},{8,12},{9,13},{10,... | collective-permute-start | bytes 3686408 | tf_op jit(solution)/shard_map/ppermute | solution.py:292
  20.7 57.1 %collective-permute-start.2 = (bf16[800,768]{1,0:T(8,128)(2,1)S(1)}, bf16[800,768]{1,0:T(8,128)(2,1)}, u32[]{:S(2)}, u32[]{:S(2)}) collective-permute-start(bf16[800,768]{1,0:T(8,128)(2,1)S(1)} %pad_slice_fusion.refs_1_), channel_id=1, source_target_pairs={{0,2},{1,3},{2,0},{3,1},{4,6},{5,7},{6,4},{7,5},{8,10},{9,11},{10,... | collective-permute-start | bytes 3686408 | tf_op jit(solution)/shard_map/ppermute | solution.py:292
  77.8 29.7 %collective-permute-start.10 = (bf16[784,768]{1,0:T(8,128)(2,1)}, bf16[784,768]{1,0:T(8,128)(2,1)}, u32[]{:S(2)}, u32[]{:S(2)}) collective-permute-start(bf16[784,768]{1,0:T(8,128)(2,1)} %collective-permute-done.refs_4_), channel_id=1, source_target_pairs={{0,4},{1,5},{2,6},{3,7},{4,0},{5,1},{6,2},{7,3},{8,12},{9,13},{10,... | collective-permute-start | bytes 3612680 | tf_op jit(solution)/shard_map/ppermute | solution.py:292
  78.2 29.4 %collective-permute-start.6 = (bf16[784,768]{1,0:T(8,128)(2,1)}, bf16[784,768]{1,0:T(8,128)(2,1)}, u32[]{:S(2)}, u32[]{:S(2)}) collective-permute-start(bf16[784,768]{1,0:T(8,128)(2,1)} %collective-permute-done.refs_4_), channel_id=1, source_target_pairs={{0,1},{1,0},{2,3},{3,2},{4,5},{5,4},{6,7},{7,6},{8,9},{9,8},{10,11... | collective-permute-start | bytes 3612680 | tf_op jit(solution)/shard_map/ppermute | solution.py:292
  78.2 17.3 %collective-permute-start.4 = (bf16[784,768]{1,0:T(8,128)(2,1)S(1)}, bf16[784,768]{1,0:T(8,128)(2,1)}, u32[]{:S(2)}, u32[]{:S(2)}) collective-permute-start(bf16[784,768]{1,0:T(8,128)(2,1)S(1)} %slice.298.refs_0_), channel_id=1, source_target_pairs={{0,1},{1,0},{2,3},{3,2},{4,5},{5,4},{6,7},{7,6},{8,9},{9,8},{10,11... | collective-permute-start | bytes 3612680 | tf_op jit(solution)/shard_map/ppermute | solution.py:292
  78.7 16.8 %collective-permute-start.8 = (bf16[784,768]{1,0:T(8,128)(2,1)}, bf16[784,768]{1,0:T(8,128)(2,1)}, u32[]{:S(2)}, u32[]{:S(2)}) collective-permute-start(bf16[784,768]{1,0:T(8,128)(2,1)} %collective-permute-done.1.refs_8_), channel_id=1, source_target_pairs={{0,1},{1,0},{2,3},{3,2},{4,5},{5,4},{6,7},{7,6},{8,9},{9,8},{10,11... | collective-permute-start | bytes 3612680 | tf_op jit(solution)/shard_map/ppermute | solution.py:292
  78.7 33.7 %collective-permute-start.11 = (bf16[800,768]{1,0:T(8,128)(2,1)}, bf16[800,768]{1,0:T(8,128)(2,1)}, u32[]{:S(2)}, u32[]{:S(2)}) collective-permute-start(bf16[800,768]{1,0:T(8,128)(2,1)} %collective-permute-done.3.refs_9_), channel_id=1, source_target_pairs={{0,2},{1,3},{2,0},{3,1},{4,6},{5,7},{6,4},{7,5},{8,10},{9,11},{10,... | collective-permute-start | bytes 3686408 | tf_op jit(solution)/shard_map/ppermute | solution.py:292
  95.4 22.0 %collective-permute-start.9 = (bf16[800,768]{1,0:T(8,128)(2,1)}, bf16[800,768]{1,0:T(8,128)(2,1)S(1)}, u32[]{:S(2)}, u32[]{:S(2)}) collective-permute-start(bf16[800,768]{1,0:T(8,128)(2,1)} %collective-permute-done.3.refs_9_), channel_id=1, source_target_pairs={{0,1},{1,0},{2,3},{3,2},{4,5},{5,4},{6,7},{7,6},{8,9},{9,8},{10,11... | collective-permute-start | bytes 3686408 | tf_op jit(solution)/shard_map/ppermute | solution.py:292
  95.4 21.9 %collective-permute-start.5 = (bf16[800,768]{1,0:T(8,128)(2,1)S(1)}, bf16[800,768]{1,0:T(8,128)(2,1)}, u32[]{:S(2)}, u32[]{:S(2)}) collective-permute-start(bf16[800,768]{1,0:T(8,128)(2,1)S(1)} %pad_slice_fusion.refs_1_), channel_id=1, source_target_pairs={{0,1},{1,0},{2,3},{3,2},{4,5},{5,4},{6,7},{7,6},{8,9},{9,8},{10,11... | collective-permute-start | bytes 3686408 | tf_op jit(solution)/shard_map/ppermute | solution.py:292
  107.5 9.9 %collective-permute-start.12 = (bf16[784,768]{1,0:T(8,128)(2,1)}, bf16[784,768]{1,0:T(8,128)(2,1)}, u32[]{:S(2)}, u32[]{:S(2)}) collective-permute-start(bf16[784,768]{1,0:T(8,128)(2,1)} %collective-permute-done.10.refs_12_), channel_id=1, source_target_pairs={{0,1},{1,0},{2,3},{3,2},{4,5},{5,4},{6,7},{7,6},{8,9},{9,8},{10,11... | collective-permute-start | bytes 3612680 | tf_op jit(solution)/shard_map/ppermute | solution.py:292
  149.4 183.8 %all-gather.12.cloned.1.call-start = ((), (), s32[]{:S(2)}) async-start(), calls=%async_computation.3 | async-start | bytes 4866048 | tf_op jit(solution)/shard_map/all_gather | solution.py:643
  162.1 43.1 %collective-permute-start.14 = (bf16[3072,128]{1,0:T(8,128)(2,1)}, bf16[3072,128]{1,0:T(8,128)(2,1)S(1)}, u32[]{:S(2)}, u32[]{:S(2)}) collective-permute-start(bf16[3072,128]{1,0:T(8,128)(2,1)} %get-tuple-element.154), channel_id=1, source_target_pairs={{0,8},{1,9},{2,10},{3,11},{4,12},{5,13},{6,14},{7,15},{8,16},{9,17... | collective-permute-start | bytes 2359304 | tf_op jit(solution)/shard_map/ppermute | solution.py:292
  163.9 46.1 %collective-permute-start.15 = (bf16[3072,128]{1,0:T(8,128)(2,1)}, bf16[3072,128]{1,0:T(8,128)(2,1)}, u32[]{:S(2)}, u32[]{:S(2)}) collective-permute-start(bf16[3072,128]{1,0:T(8,128)(2,1)} %get-tuple-element.155), channel_id=1, source_target_pairs={{0,24},{1,25},{2,26},{3,27},{4,28},{5,29},{6,30},{7,31},{8,0},{9,1... | collective-permute-start | bytes 2359304 | tf_op jit(solution)/shard_map/ppermute | solution.py:292
  204.2 56.3 %collective-permute-start.16 = (bf16[3072,128]{1,0:T(8,128)(2,1)}, bf16[3072,128]{1,0:T(8,128)(2,1)}, u32[]{:S(2)}, u32[]{:S(2)}) collective-permute-start(bf16[3072,128]{1,0:T(8,128)(2,1)} %fusion.42), channel_id=1, source_target_pairs={{0,16},{1,17},{2,18},{3,19},{4,20},{5,21},{6,22},{7,23},{8,24},{9,... | collective-permute-start | bytes 2359304 | tf_op jit(solution)/shard_map/ppermute | solution.py:292
  286.6 23.4 %collective-permute-start.19 = (bf16[512,768]{1,0:T(8,128)(2,1)S(1)}, bf16[512,768]{1,0:T(8,128)(2,1)}, u32[]{:S(2)}, u32[]{:S(2)}) collective-permute-start(bf16[512,768]{1,0:T(8,128)(2,1)S(1)} %add_convert_fusion.4), channel_id=1, source_target_pairs={{0,1},{1,0},{2,3},{3,2},{4,5},{5,4},{6,7},{7,6},{8,9},{9,8},{10,11... | collective-permute-start | bytes 2359304 | tf_op jit(solution)/shard_map/ppermute | solution.py:292
  310.0 11.9 %collective-permute-start.20 = (bf16[512,768]{1,0:T(8,128)(2,1)S(1)}, bf16[512,768]{1,0:T(8,128)(2,1)S(1)}, u32[]{:S(2)}, u32[]{:S(2)}) collective-permute-start(bf16[512,768]{1,0:T(8,128)(2,1)S(1)} %get-tuple-element.168), channel_id=1, source_target_pairs={{0,1},{1,0},{2,3},{3,2},{4,5},{5,4},{6,7},{7,6},{8,9},{9,8},{10,11... | collective-permute-start | bytes 2359304 | tf_op jit(solution)/shard_map/ppermute | solution.py:292
  322.9 31.5 %collective-permute-start.25 = (bf16[512,3072]{1,0:T(8,128)(2,1)}, bf16[512,3072]{1,0:T(8,128)(2,1)}, u32[]{:S(2)}, u32[]{:S(2)}) collective-permute-start(bf16[512,3072]{1,0:T(8,128)(2,1)} %get-tuple-element.170), channel_id=1, source_target_pairs={{0,1},{1,0},{2,3},{3,2},{4,5},{5,4},{6,7},{7,6},{8,9},{9,8},{10,11... | collective-permute-start | bytes 9437192 | tf_op jit(solution)/shard_map/ppermute | solution.py:292
  327.3 21.6 %all-to-all-start = ((f32[32,1,512]{2,1,0:T(1,128)}), f32[32,1,512]{2,1,0:T(1,128)S(1)}, u32[]{:S(2)}, u32[]{:S(2)}) async-start(f32[32,1,512]{2,1,0:T(1,128)} %all_to_all.8), calls=%async_computation | async-start | bytes 131072 | tf_op jit(solution)/shard_map/all_to_all | solution.py:801
  331.6 271.1 %all-gather.14.cloned.1.call-start = ((), (), s32[]{:S(2)}) async-start(), calls=%async_computation.4 | async-start | bytes 1216512 | tf_op jit(solution)/shard_map/all_gather | solution.py:899
  404.1 14.3 %collective-permute-start.30 = (f32[64,768]{1,0:T(8,128)S(1)}, f32[64,768]{1,0:T(8,128)S(1)}, u32[]{:S(2)}, u32[]{:S(2)}) collective-permute-start(f32[64,768]{1,0:T(8,128)S(1)} %get-tuple-element.326), channel_id=1, source_target_pairs={{0,16},{1,17},{2,18},{3,19},{4,20},{5,21},{6,22},{7,23},{8,24},{9,... | collective-permute-start | bytes 589832 | tf_op jit(solution)/shard_map/ppermute | solution.py:292
  419.5 34.3 %collective-permute-start.35 = (bf16[256,896]{1,0:T(8,128)(2,1)S(1)}, bf16[256,896]{1,0:T(8,128)(2,1)S(1)}, u32[]{:S(2)}, u32[]{:S(2)}) collective-permute-start(bf16[256,896]{1,0:T(8,128)(2,1)S(1)} %get-tuple-element.328), channel_id=1, source_target_pairs={{0,4},{1,5},{2,6},{3,7},{4,0},{5,1},{6,2},{7,3},{8,12},{9,13},{10,... | collective-permute-start | bytes 1376264 | tf_op jit(solution)/shard_map/ppermute | solution.py:292
  421.1 32.7 %collective-permute-start.34 = (bf16[256,896]{1,0:T(8,128)(2,1)S(1)}, bf16[256,896]{1,0:T(8,128)(2,1)}, u32[]{:S(2)}, u32[]{:S(2)}) collective-permute-start(bf16[256,896]{1,0:T(8,128)(2,1)S(1)} %get-tuple-element.328), channel_id=1, source_target_pairs={{0,2},{1,3},{2,0},{3,1},{4,6},{5,7},{6,4},{7,5},{8,10},{9,11},{10,... | collective-permute-start | bytes 1376264 | tf_op jit(solution)/shard_map/ppermute | solution.py:292
  427.6 17.1 %collective-permute-start.32 = (bf16[512,384]{1,0:T(8,128)(2,1)S(1)}, bf16[512,384]{1,0:T(8,128)(2,1)S(1)}, u32[]{:S(2)}, u32[]{:S(2)}) collective-permute-start(bf16[512,384]{1,0:T(8,128)(2,1)S(1)} %constant_dynamic-slice_fusion.44), channel_id=1, source_target_pairs={{0,1},{1,0},{2,3},{3,2},{4,5},{5,4},{6,7},{7,6},{8,9},{9,8},{10,11... | collective-permute-start | bytes 1179656 | tf_op jit(solution)/shard_map/ppermute | solution.py:292
  435.8 16.5 %collective-permute-start.33 = (bf16[512,1536]{1,0:T(8,128)(2,1)S(1)}, bf16[512,1536]{1,0:T(8,128)(2,1)S(1)}, u32[]{:S(2)}, u32[]{:S(2)}) collective-permute-start(bf16[512,1536]{1,0:T(8,128)(2,1)S(1)} %constant_dynamic-slice_fusion.43), channel_id=1, source_target_pairs={{0,1},{1,0},{2,3},{3,2},{4,5},{5,4},{6,7},{7,6},{8,9},{9,8},{10,11... | collective-permute-start | bytes 4718600 | tf_op jit(solution)/shard_map/ppermute | solution.py:292
  453.9 39.4 %collective-permute-start.38 = (bf16[512,384]{1,0:T(8,128)(2,1)S(1)}, bf16[512,384]{1,0:T(8,128)(2,1)}, u32[]{:S(2)}, u32[]{:S(2)}) collective-permute-start(bf16[512,384]{1,0:T(8,128)(2,1)S(1)} %constant_dynamic-slice_fusion.42), channel_id=1, source_target_pairs={{0,1},{1,0},{2,3},{3,2},{4,5},{5,4},{6,7},{7,6},{8,9},{9,8},{10,11... | collective-permute-start | bytes 1179656 | tf_op jit(solution)/shard_map/ppermute | solution.py:292
  454.4 43.2 %collective-permute-start.55 = (bf16[256,896]{1,0:T(8,128)(2,1)}, bf16[256,896]{1,0:T(8,128)(2,1)}, u32[]{:S(2)}, u32[]{:S(2)}) collective-permute-start(bf16[256,896]{1,0:T(8,128)(2,1)} %collective-permute-done.34), channel_id=1, source_target_pairs={{0,4},{1,5},{2,6},{3,7},{4,0},{5,1},{6,2},{7,3},{8,12},{9,13},{10,... | collective-permute-start | bytes 1376264 | tf_op jit(solution)/shard_map/ppermute | solution.py:292
  457.9 44.2 %collective-permute-start.36 = (bf16[4,2,192,384]{3,2,1,0:T(8,128)(2,1)S(1)}, bf16[4,2,192,384]{3,2,1,0:T(8,128)(2,1)}, u32[]{:S(2)}, u32[]{:S(2)}) collective-permute-start(bf16[4,2,192,384]{3,2,1,0:T(8,128)(2,1)S(1)} %fusion.29), channel_id=1, source_target_pairs={{0,4},{1,5},{2,6},{3,7},{4,0},{5,1},{6,2},{7,3},{8,12},{9,13},{10,... | collective-permute-start | bytes 3538952 | tf_op jit(solution)/shard_map/ppermute | solution.py:292
  459.4 42.7 %collective-permute-start.37 = (bf16[4,2,48,1536]{3,2,1,0:T(8,128)(2,1)}, bf16[4,2,48,1536]{3,2,1,0:T(8,128)(2,1)}, u32[]{:S(2)}, u32[]{:S(2)}) collective-permute-start(bf16[4,2,48,1536]{3,2,1,0:T(8,128)(2,1)} %fusion.30), channel_id=1, source_target_pairs={{0,2},{1,3},{2,0},{3,1},{4,6},{5,7},{6,4},{7,5},{8,10},{9,11},{10,... | collective-permute-start | bytes 3538952 | tf_op jit(solution)/shard_map/ppermute | solution.py:292
  500.3 56.4 %collective-permute-start.56 = (bf16[4,256,896]{2,1,0:T(8,128)(2,1)}, bf16[4,256,896]{2,1,0:T(8,128)(2,1)}, u32[]{:S(2)}, u32[]{:S(2)}) collective-permute-start(bf16[4,256,896]{2,1,0:T(8,128)(2,1)} %pad_maximum_fusion.3), channel_id=1, source_target_pairs={{0,1},{1,0},{2,3},{3,2},{4,5},{5,4},{6,7},{7,6},{8,9},{9,8},{10,11... | collective-permute-start | bytes 5505032 | tf_op jit(solution)/shard_map/ppermute | solution.py:292
  504.4 18.5 %collective-permute-start.41 = (bf16[4,192,384]{2,1,0:T(8,128)(2,1)S(1)}, bf16[4,192,384]{2,1,0:T(8,128)(2,1)}, u32[]{:S(2)}, u32[]{:S(2)}) collective-permute-start(bf16[4,192,384]{2,1,0:T(8,128)(2,1)S(1)} %fusion.43), channel_id=1, source_target_pairs={{0,2},{1,3},{2,0},{3,1},{4,6},{5,7},{6,4},{7,5},{8,10},{9,11},{10,... | collective-permute-start | bytes 1769480 | tf_op jit(solution)/shard_map/ppermute | solution.py:292
  508.5 15.8 %collective-permute-start.42 = (bf16[4,48,1536]{2,1,0:T(8,128)(2,1)}, bf16[4,48,1536]{2,1,0:T(8,128)(2,1)}, u32[]{:S(2)}, u32[]{:S(2)}) collective-permute-start(bf16[4,48,1536]{2,1,0:T(8,128)(2,1)} %fusion.44), channel_id=1, source_target_pairs={{0,4},{1,5},{2,6},{3,7},{4,0},{5,1},{6,2},{7,3},{8,12},{9,13},{10,... | collective-permute-start | bytes 1769480 | tf_op jit(solution)/shard_map/ppermute | solution.py:292
  524.3 34.2 %collective-permute-start.50 = (bf16[1,3072,128]{2,1,0:T(8,128)(2,1)}, bf16[1,3072,128]{2,1,0:T(8,128)(2,1)}, u32[]{:S(2)}, u32[]{:S(2)}) collective-permute-start(bf16[1,3072,128]{2,1,0:T(8,128)(2,1)} %reshape.2262.refs_0_), channel_id=1, source_target_pairs={{0,4},{1,5},{2,6},{3,7},{4,0},{5,1},{6,2},{7,3},{8,12},{9,13},{10,... | collective-permute-start | bytes 2359304 | tf_op jit(solution)/shard_map/ppermute | solution.py:292
  524.8 18.3 %collective-permute-start.44 = (bf16[1,3072,128]{2,1,0:T(8,128)(2,1)}, bf16[1,3072,128]{2,1,0:T(8,128)(2,1)}, u32[]{:S(2)}, u32[]{:S(2)}) collective-permute-start(bf16[1,3072,128]{2,1,0:T(8,128)(2,1)} %reshape.2262.refs_0_), channel_id=1, source_target_pairs={{0,8},{2,10},{4,12},{6,14},{8,16},{10,18},{12,20},{14,22},{16,24},... | collective-permute-start | bytes 2359304 | tf_op jit(solution)/shard_map/ppermute | solution.py:337
  527.1 21.4 %collective-permute-start.43 = (bf16[1,3072,128]{2,1,0:T(8,128)(2,1)}, bf16[1,3072,128]{2,1,0:T(8,128)(2,1)}, u32[]{:S(2)}, u32[]{:S(2)}) collective-permute-start(bf16[1,3072,128]{2,1,0:T(8,128)(2,1)} %reshape.2262.refs_0_), channel_id=1, source_target_pairs={{8,0},{10,2},{12,4},{14,6},{16,8},{18,10},{20,12},{22,14},{24,16},... | collective-permute-start | bytes 2359304 | tf_op jit(solution)/shard_map/ppermute | solution.py:337
  530.9 18.9 %collective-permute-start.52 = (bf16[512,1152]{1,0:T(8,128)(2,1)S(1)}, bf16[512,1152]{1,0:T(8,128)(2,1)S(1)}, u32[]{:S(2)}, u32[]{:S(2)}) collective-permute-start(bf16[512,1152]{1,0:T(8,128)(2,1)S(1)} %constant_dynamic-slice_fusion.41), channel_id=1, source_target_pairs={{0,1},{1,0},{2,3},{3,2},{4,5},{5,4},{6,7},{7,6},{8,9},{9,8},{10,11... | collective-permute-start | bytes 3538952 | tf_op jit(solution)/shard_map/ppermute | solution.py:292
  543.2 15.9 %collective-permute-start.45 = (bf16[1,3072,128]{2,1,0:T(8,128)(2,1)}, bf16[1,3072,128]{2,1,0:T(8,128)(2,1)S(1)}, u32[]{:S(2)}, u32[]{:S(2)}) collective-permute-start(bf16[1,3072,128]{2,1,0:T(8,128)(2,1)} %collective-permute-done.44), channel_id=1, source_target_pairs={{8,16},{10,18},{12,20},{14,22},{16,24},{18,26},{20,28},{22,30},{9,... | collective-permute-start | bytes 2359304 | tf_op jit(solution)/shard_map/ppermute | solution.py:337
  548.5 21.2 %collective-permute-start.47 = (bf16[1,3072,128]{2,1,0:T(8,128)(2,1)}, bf16[1,3072,128]{2,1,0:T(8,128)(2,1)S(1)}, u32[]{:S(2)}, u32[]{:S(2)}) collective-permute-start(bf16[1,3072,128]{2,1,0:T(8,128)(2,1)} %collective-permute-done.43), channel_id=1, source_target_pairs={{8,0},{10,2},{12,4},{14,6},{16,8},{18,10},{20,12},{22,14},{9,1},{1... | collective-permute-start | bytes 2359304 | tf_op jit(solution)/shard_map/ppermute | solution.py:337
  553.1 28.7 %collective-permute-start.53 = (bf16[4,2,48,1536]{3,2,0,1:T(8,128)(2,1)S(1)}, bf16[4,2,48,1536]{3,2,0,1:T(8,128)(2,1)S(1)}, u32[]{:S(2)}, u32[]{:S(2)}) collective-permute-start(bf16[4,2,48,1536]{3,2,0,1:T(8,128)(2,1)S(1)} %fusion.31), channel_id=1, source_target_pairs={{0,4},{1,5},{2,6},{3,7},{4,0},{5,1},{6,2},{7,3},{8,12},{9,13},{10,... | collective-permute-start | bytes 3538952 | tf_op jit(solution)/shard_map/ppermute | solution.py:292
  556.7 61.3 %collective-permute-start.59 = (bf16[1,3072,128]{2,1,0:T(8,128)(2,1)}, bf16[1,3072,128]{2,1,0:T(8,128)(2,1)}, u32[]{:S(2)}, u32[]{:S(2)}) collective-permute-start(bf16[1,3072,128]{2,1,0:T(8,128)(2,1)} %reshape.2262.refs_0_), channel_id=1, source_target_pairs={{0,1},{1,0},{2,3},{3,2},{4,5},{5,4},{6,7},{7,6},{8,9},{9,8},{10,11... | collective-permute-start | bytes 2359304 | tf_op jit(solution)/shard_map/ppermute | solution.py:292
  558.5 44.1 %collective-permute-start.49 = (bf16[1,3072,128]{2,1,0:T(8,128)(2,1)}, bf16[1,3072,128]{2,1,0:T(8,128)(2,1)}, u32[]{:S(2)}, u32[]{:S(2)}) collective-permute-start(bf16[1,3072,128]{2,1,0:T(8,128)(2,1)} %reshape.2262.refs_0_), channel_id=1, source_target_pairs={{0,2},{1,3},{2,0},{3,1},{4,6},{5,7},{6,4},{7,5},{8,10},{9,11},{10,... | collective-permute-start | bytes 2359304 | tf_op jit(solution)/shard_map/ppermute | solution.py:292
  559.1 43.6 %collective-permute-start.51 = (bf16[1,3072,128]{2,1,0:T(8,128)(2,1)}, bf16[1,3072,128]{2,1,0:T(8,128)(2,1)}, u32[]{:S(2)}, u32[]{:S(2)}) collective-permute-start(bf16[1,3072,128]{2,1,0:T(8,128)(2,1)} %collective-permute-done.50.refs_4_), channel_id=1, source_target_pairs={{0,2},{1,3},{2,0},{3,1},{4,6},{5,7},{6,4},{7,5},{8,10},{9,11},{10,... | collective-permute-start | bytes 2359304 | tf_op jit(solution)/shard_map/ppermute | solution.py:292
  569.7 13.7 %collective-permute-start.46 = (bf16[1,3072,128]{2,1,0:T(8,128)(2,1)S(1)}, bf16[1,3072,128]{2,1,0:T(8,128)(2,1)S(1)}, u32[]{:S(2)}, u32[]{:S(2)}) collective-permute-start(bf16[1,3072,128]{2,1,0:T(8,128)(2,1)S(1)} %collective-permute-done.45), channel_id=1, source_target_pairs={{16,24},{18,26},{20,28},{22,30},{17,25},{19,27},{21,29},{23,31}} | collective-permute-start | bytes 2359304 | tf_op jit(solution)/shard_map/ppermute | solution.py:337
  581.7 19.0 %collective-permute-start.48 = (bf16[1,3072,128]{2,1,0:T(8,128)(2,1)S(1)}, bf16[1,3072,128]{2,1,0:T(8,128)(2,1)S(1)}, u32[]{:S(2)}, u32[]{:S(2)}) collective-permute-start(bf16[1,3072,128]{2,1,0:T(8,128)(2,1)S(1)} %collective-permute-done.47), channel_id=1, source_target_pairs={{8,0},{10,2},{12,4},{14,6},{9,1},{11,3},{13,5},{15,7}} | collective-permute-start | bytes 2359304 | tf_op jit(solution)/shard_map/ppermute | solution.py:337
  583.5 27.0 %collective-permute-start.54 = (bf16[4,48,1536]{2,1,0:T(8,128)(2,1)S(1)}, bf16[4,48,1536]{2,1,0:T(8,128)(2,1)}, u32[]{:S(2)}, u32[]{:S(2)}) collective-permute-start(bf16[4,48,1536]{2,1,0:T(8,128)(2,1)S(1)} %fusion.45), channel_id=1, source_target_pairs={{0,2},{1,3},{2,0},{3,1},{4,6},{5,7},{6,4},{7,5},{8,10},{9,11},{10,... | collective-permute-start | bytes 1769480 | tf_op jit(solution)/shard_map/ppermute | solution.py:292
  611.0 10.0 %collective-permute-start.62 = (bf16[1,3072,128]{2,1,0:T(8,128)(2,1)}, bf16[1,3072,128]{2,1,0:T(8,128)(2,1)}, u32[]{:S(2)}, u32[]{:S(2)}) collective-permute-start(bf16[1,3072,128]{2,1,0:T(8,128)(2,1)} %collective-permute-done.51.refs_6_), channel_id=1, source_target_pairs={{0,1},{1,0},{2,3},{3,2},{4,5},{5,4},{6,7},{7,6},{8,9},{9,8},{10,11... | collective-permute-start | bytes 2359304 | tf_op jit(solution)/shard_map/ppermute | solution.py:292
  611.0 31.8 %collective-permute-start.63 = (bf16[3,3072,128]{2,1,0:T(8,128)(2,1)}, bf16[3,3072,128]{2,1,0:T(8,128)(2,1)}, u32[]{:S(2)}, u32[]{:S(2)}) collective-permute-start(bf16[3,3072,128]{2,1,0:T(8,128)(2,1)} %pad_maximum_fusion.2.refs_8_), channel_id=1, source_target_pairs={{0,1},{1,0},{2,3},{3,2},{4,5},{5,4},{6,7},{7,6},{8,9},{9,8},{10,11... | collective-permute-start | bytes 7077896 | tf_op jit(solution)/shard_map/ppermute | solution.py:292
  618.0 53.5 %collective-permute-start.58 = (bf16[3,3072,128]{2,1,0:T(8,128)(2,1)}, bf16[3,3072,128]{2,1,0:T(8,128)(2,1)}, u32[]{:S(2)}, u32[]{:S(2)}) collective-permute-start(bf16[3,3072,128]{2,1,0:T(8,128)(2,1)} %pad_maximum_fusion.2.refs_8_), channel_id=1, source_target_pairs={{0,4},{1,5},{2,6},{3,7},{4,0},{5,1},{6,2},{7,3},{8,12},{9,13},{10,... | collective-permute-start | bytes 7077896 | tf_op jit(solution)/shard_map/ppermute | solution.py:292
  618.9 53.2 %collective-permute-start.57 = (bf16[3,3072,128]{2,1,0:T(8,128)(2,1)}, bf16[3,3072,128]{2,1,0:T(8,128)(2,1)}, u32[]{:S(2)}, u32[]{:S(2)}) collective-permute-start(bf16[3,3072,128]{2,1,0:T(8,128)(2,1)} %pad_maximum_fusion.2.refs_8_), channel_id=1, source_target_pairs={{0,2},{1,3},{2,0},{3,1},{4,6},{5,7},{6,4},{7,5},{8,10},{9,11},{10,... | collective-permute-start | bytes 7077896 | tf_op jit(solution)/shard_map/ppermute | solution.py:292
  619.4 43.0 %collective-permute-start.65 = (f32[48,4608]{1,0:T(8,128)}, f32[48,4608]{1,0:T(8,128)}, u32[]{:S(2)}, u32[]{:S(2)}) collective-permute-start(f32[48,4608]{1,0:T(8,128)} %get-tuple-element.314), channel_id=1, source_target_pairs={{24,16},{26,18},{28,20},{30,22},{25,17},{27,19},{29,21},{31,23}} | collective-permute-start | bytes 2654216 | tf_op jit(solution)/shard_map/ppermute | solution.py:302
  621.0 41.4 %collective-permute-start.64 = (f32[48,4608]{1,0:T(8,128)}, f32[48,4608]{1,0:T(8,128)}, u32[]{:S(2)}, u32[]{:S(2)}) collective-permute-start(f32[48,4608]{1,0:T(8,128)} %get-tuple-element.315), channel_id=1, source_target_pairs={{0,8},{2,10},{4,12},{6,14},{1,9},{3,11},{5,13},{7,15}} | collective-permute-start | bytes 2654216 | tf_op jit(solution)/shard_map/ppermute | solution.py:302
  672.1 17.1 %collective-permute-start.68 = (bf16[3,3072,128]{2,1,0:T(8,128)(2,1)}, bf16[3,3072,128]{2,1,0:T(8,128)(2,1)S(1)}, u32[]{:S(2)}, u32[]{:S(2)}) collective-permute-start(bf16[3,3072,128]{2,1,0:T(8,128)(2,1)} %collective-permute-done.57.refs_0_), channel_id=1, source_target_pairs={{0,1},{1,0},{2,3},{3,2},{4,5},{5,4},{6,7},{7,6},{8,9},{9,8},{10,11... | collective-permute-start | bytes 7077896 | tf_op jit(solution)/shard_map/ppermute | solution.py:292
  672.3 20.5 %collective-permute-start.69 = (bf16[3,3072,128]{2,1,0:T(8,128)(2,1)}, bf16[3,3072,128]{2,1,0:T(8,128)(2,1)}, u32[]{:S(2)}, u32[]{:S(2)}) collective-permute-start(bf16[3,3072,128]{2,1,0:T(8,128)(2,1)} %collective-permute-done.58.refs_2_), channel_id=1, source_target_pairs={{0,1},{1,0},{2,3},{3,2},{4,5},{5,4},{6,7},{7,6},{8,9},{9,8},{10,11... | collective-permute-start | bytes 7077896 | tf_op jit(solution)/shard_map/ppermute | solution.py:292
  675.5 37.0 %collective-permute-start.66 = (bf16[2,3072,128]{2,1,0:T(8,128)(2,1)}, bf16[2,3072,128]{2,1,0:T(8,128)(2,1)}, u32[]{:S(2)}, u32[]{:S(2)}) collective-permute-start(bf16[2,3072,128]{2,1,0:T(8,128)(2,1)} %slice.263), channel_id=1, source_target_pairs={{0,4},{1,5},{2,6},{3,7},{4,0},{5,1},{6,2},{7,3},{8,12},{9,13},{10,... | collective-permute-start | bytes 4718600 | tf_op jit(solution)/shard_map/ppermute | solution.py:292
  680.0 32.5 %collective-permute-start.71 = (f32[48,4608]{1,0:T(8,128)}, f32[48,4608]{1,0:T(8,128)}, u32[]{:S(2)}, u32[]{:S(2)}) collective-permute-start(f32[48,4608]{1,0:T(8,128)} %get-tuple-element.312), channel_id=1, source_target_pairs={{16,8},{18,10},{20,12},{22,14},{24,16},{26,18},{28,20},{30,22},{17... | collective-permute-start | bytes 2654216 | tf_op jit(solution)/shard_map/ppermute | solution.py:302
  681.7 30.8 %collective-permute-start.70 = (f32[48,4608]{1,0:T(8,128)}, f32[48,4608]{1,0:T(8,128)}, u32[]{:S(2)}, u32[]{:S(2)}) collective-permute-start(f32[48,4608]{1,0:T(8,128)} %get-tuple-element.313), channel_id=1, source_target_pairs={{0,8},{2,10},{4,12},{6,14},{8,16},{10,18},{12,20},{14,22},{1,9},{3... | collective-permute-start | bytes 2654216 | tf_op jit(solution)/shard_map/ppermute | solution.py:302
  689.1 23.4 %collective-permute-start.67 = (bf16[1,3072,128]{2,1,0:T(8,128)(2,1)}, bf16[1,3072,128]{2,1,0:T(8,128)(2,1)}, u32[]{:S(2)}, u32[]{:S(2)}) collective-permute-start(bf16[1,3072,128]{2,1,0:T(8,128)(2,1)} %slice.264), channel_id=1, source_target_pairs={{0,2},{1,3},{2,0},{3,1},{4,6},{5,7},{6,4},{7,5},{8,10},{9,11},{10,... | collective-permute-start | bytes 2359304 | tf_op jit(solution)/shard_map/ppermute | solution.py:292
  724.8 27.2 %collective-permute-start.75 = (f32[48,4608]{1,0:T(8,128)}, f32[48,4608]{1,0:T(8,128)S(1)}, u32[]{:S(2)}, u32[]{:S(2)}) collective-permute-start(f32[48,4608]{1,0:T(8,128)} %get-tuple-element.310), channel_id=1, source_target_pairs={{8,0},{10,2},{12,4},{14,6},{16,8},{18,10},{20,12},{22,14},{24,16},... | collective-permute-start | bytes 2654216 | tf_op jit(solution)/shard_map/ppermute | solution.py:302
  726.1 25.9 %collective-permute-start.74 = (f32[48,4608]{1,0:T(8,128)}, f32[48,4608]{1,0:T(8,128)}, u32[]{:S(2)}, u32[]{:S(2)}) collective-permute-start(f32[48,4608]{1,0:T(8,128)} %get-tuple-element.311), channel_id=1, source_target_pairs={{0,8},{2,10},{4,12},{6,14},{8,16},{10,18},{12,20},{14,22},{16,24},... | collective-permute-start | bytes 2654216 | tf_op jit(solution)/shard_map/ppermute | solution.py:302
  765.7 14.0 %collective-permute-start.81 = (f32[2]{0:T(128)S(1)}, f32[2]{0:T(128)S(1)}, u32[]{:S(2)}, u32[]{:S(2)}) collective-permute-start(f32[2]{0:T(128)S(1)} %fusion.211), channel_id=1, source_target_pairs={{0,6},{1,7},{2,4},{3,5},{4,2},{5,3},{6,0},{7,1},{8,14},{9,15},{10,... | collective-permute-start | bytes 32 | tf_op jit(solution)/shard_map/ppermute | solution.py:292
  (166 other events, 2009.1 us)
Sparse Core Ops, SparseCore 0:
  11.4 61.3 all-gather.15
  76.3 61.5 all-gather.7
  149.5 113.2 all-gather.9
  266.1 64.0 all-gather.11
  529.6 57.7 all-gather.13

commit v5 on v4

--- a/solution.py
+++ b/solution.py
@@ -307,9 +307,10 @@
     return lax.dynamic_slice_in_dim(value, index * size, size, axis=1)
 
 
-def chip_product(left, left_far, right):
+def chip_product(left, left_far, right, far=None):
     rep_idx = lax.axis_index("rep")
-    far = hop(pick_half(right, 1 - rep_idx), dr=1)
+    if far is None:
+        far = hop(pick_half(right, 1 - rep_idx), dr=1)
     return dense_tn(left, pick_half(right, rep_idx)) + dense_tn(left_far, far)
 
 
@@ -322,27 +323,6 @@
     bit = (lax.axis_index("dp") >> axis) & 1
     far = lax.dynamic_index_in_dim(blocks, 1 - bit, place, False).astype(bf16)
     return lax.dynamic_index_in_dim(blocks, bit, place, False), hop(far, dq=1 << axis)
-
-
-def gather_line(value):
-    lines = lax.axis_size("dp") // PLANE
-    line = lax.axis_index("dp") // PLANE
-
-    def pass_on(x, way, k):
-        pairs = []
-        for l in range(lines):
-            if 0 <= l - way * (k - 1) < lines and 0 <= l + way < lines:
-                for q in range(PLANE):
-                    pairs.append((l * PLANE + q, (l + way) * PLANE + q))
-        return lax.ppermute(x, "dp", pairs)
-
-    before, after = [value], [value]
-    for k in range(1, lines):
-        before.append(pass_on(before[-1], 1, k))
-        after.append(pass_on(after[-1], -1, k))
-    return jnp.concatenate(
-        [jnp.where(line + d < lines, after[d], before[lines - d]) for d in range(1, lines)], 0
-    )
 
 
 def block_at(blocks, shift):
@@ -645,10 +625,11 @@
     few = mod_proj.shape[0]
     gains_flat = norm_gains.reshape(-1)
     gains_flat = jnp.pad(gains_flat, (0, few * LANES - gains_flat.size))
-    small_all = gather(
+    small_all = lax.all_gather(
         jnp.concatenate(
             [mod_proj, final_proj, time_proj.reshape(few, -1), gains_flat.reshape(few, LANES)], 1
-        )
+        ).astype(bf16),
+        BOTH,
     )
     qkv_w = gather(attn_proj)
 
@@ -672,7 +653,13 @@
     member = (owner[:, None] == jnp.arange(devices, dtype=jnp.int32)[None, :]).astype(jnp.int32)
     slot = jnp.sum((jnp.cumsum(member, 0) - member) * member, 1)
     flat_slot = owner * cap + slot
-    first, second, flat_slot = lax.optimization_barrier((first, second, flat_slot))
+    late_shards = (
+        jnp.concatenate([out_proj, up_proj], 1).astype(bf16),
+        down_proj.astype(bf16),
+    )
+    first, second, flat_slot, late_shards = lax.optimization_barrier(
+        (first, second, flat_slot, late_shards)
+    )
     first[3] = hop(first[1], dq=2)
     second[3] = hop(second[2], dq=1)
     pieces = []
@@ -691,34 +678,75 @@
     mix_here = mix_here.reshape(lines, 1, half * cands)
     parts = {}
 
-    def mix_some(which, keep):
-        out = mix_rows(
-            jnp.stack([row_at[d] for d in which]),
-            jnp.stack([mix_here[d] for d in which]),
-            pieces,
-            cands,
-            keep,
+    outer = (1, lines - 1)
+    inner = tuple(range(2, lines - 1)) + (0,)
+    stacked = [
+        (jnp.stack([row_at[d] for d in which]), jnp.stack([mix_here[d] for d in which]))
+        for which in (outer, inner)
+    ]
+
+    places = jnp.arange(half, dtype=jnp.int32)
+    turns = []
+    for core in (rep_idx, 1 - rep_idx):
+        cosv, sinv = rope_tables(core * half + places, HD)
+        turns += [jnp.tile(cosv, (1, 4)), jnp.concatenate([-sinv, sinv] * 2, 1)]
+    length = lax.dynamic_slice_in_dim(seq_lengths, dp_idx, 1)
+    picks = loss_pick.shape[-1]
+    tau = (time_index.astype(f32) + 1.0) / TSTEPS
+    starts = (jnp.arange(reps, dtype=jnp.int32) * half)[None, :, None]
+    weight_all = jnp.where(
+        loss_pick + starts < seq_lengths[:, None, None], (1.0 / (0.1 + tau))[:, None, None], 0.0
+    )
+    coefficient_aggregate = jnp.sum(weight_all)
+
+    def of_line(values, at_chip, at_core):
+        mine = lax.dynamic_slice(
+            values.reshape(lines, PLANE, reps, picks), (0, at_chip, at_core, 0), (lines, 1, 1, picks)
         )
-        for k, d in enumerate(which):
+        return from_me(mine.reshape(lines, picks))
+
+    def from_start(values):
+        return lax.dynamic_slice_in_dim(
+            jnp.concatenate([values, values], 0), (lines - line) % lines, lines
+        )
+
+    targets = of_line(loss_target, chip, rep_idx).reshape(-1)
+    weight = of_line(weight_all, chip, rep_idx).reshape(-1)
+    my_pick = lax.dynamic_slice(loss_pick, (dp_idx, rep_idx, 0), (1, 1, picks)).reshape(picks)
+    t_owner = targets // vocab
+    t_slot = (((t_owner // reps) % PLANE) ^ chip) * reps + ((t_owner % reps) ^ rep_idx)
+    t_column = jnp.where(
+        t_owner // (reps * PLANE) == line, t_slot * padded + targets % vocab, -1
+    )
+    among = [(chip ^ dq, rep_idx ^ dr) for dr in range(reps) for dq in range(PLANE)]
+    targets_all = jnp.concatenate([of_line(loss_target, q, r).reshape(-1) for q, r in among])
+    weight_rows = jnp.concatenate([of_line(weight_all, q, r).reshape(-1) for q, r in among])
+    line_facts = (turns, length, weight_all, targets, weight, my_pick, t_column)
+    line_facts, targets_all, weight_rows, stacked = lax.optimization_barrier(
+        (line_facts, targets_all, weight_rows, stacked)
+    )
+    turns, length, weight_all, targets, weight, my_pick, t_column = line_facts
+
+    def mix_some(call, keep):
+        out = mix_rows(*stacked[call], pieces, cands, keep)
+        for k, d in enumerate((outer, inner)[call]):
             parts[d] = out[0][k, : half * groups]
         return out[-1]
 
-    outer = (1, lines - 1)
-    mix_some(outer, False)
-    out_up = jnp.concatenate([out_proj, up_proj], 1)
-    parts[1], parts[lines - 1], out_up, down_shard = lax.optimization_barrier(
-        (parts[1], parts[lines - 1], out_up.astype(bf16), down_proj.astype(bf16))
-    )
-    out_up = gather(out_up)
-    down_w = gather(down_shard)
+    mix_some(0, False)
+    parts[1], parts[lines - 1], late_shards = lax.optimization_barrier(
+        (parts[1], parts[lines - 1], late_shards)
+    )
+    out_up = gather(late_shards[0])
+    down_w = gather(late_shards[1])
     out_w, up_w = out_up[:, :width], out_up[:, width:]
     far_parts = [hop(parts[d].astype(bf16), dl=d) for d in outer]
-    inner = tuple(range(2, lines - 1))
-    plane_table = mix_some(inner + (0,), True)
-    far_parts += [hop(parts[d].astype(bf16), dl=d) for d in inner]
+    plane_table = mix_some(1, True)
+    far_parts += [hop(parts[d].astype(bf16), dl=d) for d in inner[:-1]]
     far_parts[:2], flat_slot, small_all = lax.optimization_barrier(
         (far_parts[:2], flat_slot, small_all)
     )
+    small_all = small_all.reshape(devices * few, -1)
     entry = offset * half + jnp.arange(half * cands, dtype=jnp.int32) // cands + 1
     empty = jnp.zeros((devices * cap,), f32)
     lists = [
@@ -726,9 +754,6 @@
         for value in (entry.astype(f32), mixing.reshape(-1))
     ]
     asked = jnp.concatenate(lists, 1)
-    far_parts, asked = lax.optimization_barrier((far_parts, asked))
-    x0 = (parts[0] + sum(far.astype(f32) for far in far_parts)).reshape(half, width)
-
     mod_f = small_all[:, : 6 * width].astype(f32)
     final_f = small_all[:, 6 * width : 8 * width].astype(f32)
     time_f = small_all[:, 8 * width : -LANES].astype(f32).reshape(-1, time_proj.shape[1])
@@ -736,23 +761,21 @@
     gain_f = gain_f.reshape((devices,) + norm_gains.shape)
     gain_f = gain_f.transpose(1, 0, 2).reshape(norm_gains.shape[0], width)
 
-    length = lax.dynamic_slice_in_dim(seq_lengths, dp_idx, 1)
     feats = time_features(time_index, time_f.shape[0])
     cond, silu_back = jax.vjp(jax.nn.silu, exact(feats, time_f))
     my_cond = lax.dynamic_slice_in_dim(cond, dp_idx, 1)
     mods = exact(my_cond, mod_f)
     fmods = exact(my_cond, final_f)
+    far_parts, asked, mods, fmods, gain_f = lax.optimization_barrier(
+        (far_parts, asked, mods, fmods, gain_f)
+    )
     sh1, sc1, g1, sh2, sc2, g2 = jnp.split(mods, 6, -1)
     fsh, fsc = jnp.split(fmods, 2, -1)
+    x0 = (parts[0] + sum(far.astype(f32) for far in far_parts)).reshape(half, width)
 
     n1, r1 = normalize(x0)
     h1b = (n1 * gain_f[0] * (1.0 + sc1) + sh1).astype(bf16)
     qkv = dense(h1b, qkv_w)
-    places = jnp.arange(half, dtype=jnp.int32)
-    turns = []
-    for core in (rep_idx, 1 - rep_idx):
-        cosv, sinv = rope_tables(core * half + places, HD)
-        turns += [jnp.tile(cosv, (1, 4)), jnp.concatenate([-sinv, sinv] * 2, 1)]
     query, keyed, valued = turn_rows(qkv, turns[0], turns[1])
     attended = (query, keyed, hop(keyed, dr=1), valued, hop(valued, dr=1))
     core = rep_idx.reshape(1)
@@ -773,28 +796,6 @@
     nf, rf = normalize(x2)
     final = nf * gain_f[2] * (1.0 + fsc) + fsh
 
-    picks = loss_pick.shape[-1]
-    tau = (time_index.astype(f32) + 1.0) / TSTEPS
-    starts = (jnp.arange(reps, dtype=jnp.int32) * half)[None, :, None]
-    weight_all = jnp.where(
-        loss_pick + starts < seq_lengths[:, None, None], (1.0 / (0.1 + tau))[:, None, None], 0.0
-    )
-    coefficient_aggregate = jnp.sum(weight_all)
-
-    def of_line(values, at_chip, at_core):
-        mine = lax.dynamic_slice(
-            values.reshape(lines, PLANE, reps, picks), (0, at_chip, at_core, 0), (lines, 1, 1, picks)
-        )
-        return from_me(mine.reshape(lines, picks))
-
-    def from_start(values):
-        return lax.dynamic_slice_in_dim(
-            jnp.concatenate([values, values], 0), (lines - line) % lines, lines
-        )
-
-    targets = of_line(loss_target, chip, rep_idx).reshape(-1)
-    weight = of_line(weight_all, chip, rep_idx).reshape(-1)
-    my_pick = lax.dynamic_slice(loss_pick, (dp_idx, rep_idx, 0), (1, 1, picks)).reshape(picks)
     spread = (jnp.arange(half, dtype=jnp.int32)[:, None] == my_pick[None, :]).astype(f32)
     rows_b = jnp.take(final, my_pick, axis=0).astype(bf16)
     every = jnp.concatenate([rows_b] + [hop(rows_b, dl=-d) for d in range(1, lines)], 0)
@@ -804,11 +805,6 @@
     logits = dense_nt(every, plane_table)
     column = jnp.arange(plane_table.shape[0], dtype=jnp.int32)
     exists = (column % padded) < vocab
-    t_owner = targets // vocab
-    t_slot = (((t_owner // reps) % PLANE) ^ chip) * reps + ((t_owner % reps) ^ rep_idx)
-    t_column = jnp.where(
-        t_owner // (reps * PLANE) == line, t_slot * padded + targets % vocab, -1
-    )
     hit = column[None, :] == t_column[:, None]
     logits = jnp.where(exists[None, :], logits, -1e30)
     top = jnp.max(logits, -1)
@@ -841,10 +837,6 @@
     extra = jnp.pad(jnp.stack(pieces_of_lse, 1), ((0, 0), (0, LANES - 3)))
     told = jnp.concatenate([every, extra], 1)
     told_x, told_y = hop(told, dq=1), hop(told, dq=2)
-    among = [(chip ^ dq, rep_idx ^ dr) for dr in range(reps) for dq in range(PLANE)]
-    targets_all = jnp.concatenate([of_line(loss_target, q, r).reshape(-1) for q, r in among])
-    weight_rows = jnp.concatenate([of_line(weight_all, q, r).reshape(-1) for q, r in among])
-
     grad_final = exact(spread, drows)
     dx2, dfsh, dfsc, dgain_f = modulate_back(grad_final, nf, rf, gain_f[2], fsc)
     dg2 = jnp.sum(dx2 * mlp, 0)
@@ -879,27 +871,30 @@
     dh1 = dense_nt(dqkv, qkv_w)
     dn1x, dsh1, dsc1, dgain_1 = modulate_back(dh1, n1, r1, gain_f[0], sc1)
     dx0 = dx1 + dn1x
-    g_qkv = chip_product(h1b, h1_far, dqkv)
 
 
     dx0_b = dx0.astype(bf16).reshape(1, half * groups, LANES)
-    dx0_b, down_2, up_2 = lax.optimization_barrier((dx0_b, down_2, up_2))
+    dqkv_far = hop(pick_half(dqkv, 1 - rep_idx), dr=1)
+    told = jnp.stack([told, told_x, told_y, told_xy])
+    told = jnp.concatenate([told, hop(told, dr=1)], 0).reshape(-1, width + LANES)
+    row_sums = [dsh1, dsc1, dg1, dsh2, dsc2, dg2, dfsh, dfsc, dgain_1, dgain_2, dgain_f]
+    dx0_b, down_2, up_2, dqkv_far, told, row_sums = lax.optimization_barrier(
+        (dx0_b, down_2, up_2, dqkv_far, told, row_sums)
+    )
+    sums_here = jnp.concatenate(row_sums)
+    g_qkv = chip_product(h1b, h1_far, dqkv, dqkv_far)
     others = lines - 1
     cut = -(-2 * others // 3)
-    sums_here = jnp.concatenate(
-        [dsh1, dsc1, dg1, dsh2, dsc2, dg2, dfsh, dfsc, dgain_1, dgain_2, dgain_f]
-    )
-    on_line = gather_line(dx0_b)
+    on_line = jnp.concatenate([hop(dx0_b, dl=-d) for d in range(1, lines)], 0)
     own_x, own_y = hop(dx0_b, dq=1), hop(dx0_b, dq=2)
+    g_last = jnp.concatenate([g_qkv, g_out], 1)
+    own_x, own_y, g_last = lax.optimization_barrier((own_x, own_y, g_last))
     own_xy = hop(own_y, dq=1)
-    told = jnp.stack([told, told_x, told_y, told_xy])
-    told = jnp.concatenate([told, hop(told, dr=1)], 0).reshape(-1, width + LANES)
-    g_last = jnp.concatenate([g_qkv, g_out], 1)
     last_1 = split_blocks(plane_blocks(g_last), 1, 1)
     sums_all = lax.all_gather(sums_here.reshape(1, -1, LANES), BOTH, axis=0, tiled=True)
     last_2 = split_blocks(last_1[0] + last_1[1].astype(f32), 0, 1)
-    on_line, own_x, own_y, own_xy, last_2, told, sums_all = lax.optimization_barrier(
-        (on_line, own_x, own_y, own_xy, last_2, told, sums_all)
+    on_line, own_x, own_y, own_xy, last_2, dx0_b = lax.optimization_barrier(
+        (on_line, own_x, own_y, own_xy, last_2, dx0_b)
     )
     rows_all = told[:, :width]
     lse_all = jnp.sum(told[:, width : width + 3].astype(f32), 1)
@@ -950,8 +945,8 @@
         * (jnp.exp(logits_mine - lse_all[:, None]) - hit_mine.astype(f32))
     ).astype(bf16)
     head_grad = dense_tn(dlogit_mine, rows_all)
-    line_x, line_y, begun, head_grad, sums = lax.optimization_barrier(
-        (line_x, line_y, begun, head_grad, sums)
+    line_x, line_y, begun, head_grad, sums, sums_all = lax.optimization_barrier(
+        (line_x, line_y, begun, head_grad, sums, sums_all)
     )
     for d in range(lines - 2, 1, -1):
         sums = reduce_step(blocks, sums, d)

time: 827 us -> 802 us (0.970)
  waiting for transfers between devices: 163 us -> 129 us
  starting transfers between devices: 101 us -> 113 us
    ppermute x6 -> x0, waiting for transfers between devices: 35.8 us -> none  [pass_on(): return lax.ppermute(x, 'dp', pairs)]
    ppermute x73 -> x76, starting transfers between devices: 67.2 us -> 76.3 us  [hop(): return lax.ppermute(x, BOTH, pairs)]
    ppermute x6, starting transfers between devices: 21.3 us -> 29.8 us  [step_line(): return lax.ppermute(x, 'dp', pairs)]
    another operation x13 -> x11, other arithmetic: 25.7 us -> 22.2 us
    unnamed x305 -> x365, local copies, waits for them, and re-layouts: 21.3 us -> 23.5 us
    ppermute x73 -> x76, waiting for transfers between devices: 127 us -> 125 us  [hop(): return lax.ppermute(x, BOTH, pairs)]
  transfers between devices with their start and end apart: 91 -> 88, of which waited for: 32 -> 26; matrix products, arithmetic and copies ran while one was open for 33% -> 33% of each run, Pallas kernels for 20% -> 20%
where the time goes in v5:
time: 802 us; the launch traced here: 788 us
  Pallas kernels  163 us (20%)
  waiting for transfers between devices  129 us (16%)
  other arithmetic  121 us (15%)
  starting transfers between devices  113 us (14%)
  matrix products  112 us (14%)
  local copies, waits for them, and re-layouts  109 us (14%)
  between operations  25.6 us (3%)
  blocking collectives  13.8 us (2%)
    ppermute x76, waiting for transfers between devices, hop(): return lax.ppermute(x, BOTH, pairs)  125 us
    ppermute x76, starting transfers between devices, hop(): return lax.ppermute(x, BOTH, pairs)  76.3 us
    pallas_call x2, Pallas kernels, mix_rows(): pl.pallas_call(functools.partial(mix_kernel, groups=groups, cands=cands,...  57.8 us
    pallas_call x3, Pallas kernels, spread_rows(): pl.pallas_call(functools.partial(spread_kernel, groups=groups, arrays=len...  53.6 us
    dot_general x5, matrix products, dense(): return jnp.dot(a, b, preferred_element_type=f32)  39.4 us
    dot_general x9, matrix products, dense_tn(): lax.dot_general(a, b, (((0,), (0,)), ((), ())), preferred_element_type=f32)  33.8 us
    scatter x2, local copies, waits for them, and re-layouts, local(): empty.at[flat_slot].set(value).reshape(devices, cap)  31.6 us
    ppermute x6, starting transfers between devices, step_line(): return lax.ppermute(x, 'dp', pairs)  29.8 us
  transfers between devices with their start and end apart: 88, of which 26 were waited for; matrix products, arithmetic and copies ran while one was open for 33% of the time, Pallas kernels for 20%

profile of v5, /device:TPU:0, one launch (start us, length us, event | category | flops | bytes accessed | tf_op | source)
XLA Modules:
  0.0 787.5 jit_solution(6540402125313565907)
XLA Ops:
  11.1 2.6 convert_element_type.217
  13.9 3.0 collective-permute-start
  25.3 16.3 %reduce-window.6 = s32[32,32,128]{2,1,0:T(8,128)S(1)} reduce-window(s32[32,32,128]{2,1,0:T(8,128)} %fusion.49, s32[]{:T(128)} %constant.583.clone.1), window={size=1x1x128 pad=0_0x0_0x127_0}, to_apply=%region_2.3 | reduce-window | flops 16646144 | bytes 1048580 | tf_op jit(solution)/shard_map/reduce-window
  43.0 13.8 %all-gather = f32[256,128]{1,0:T(8,128)S(1)} all-gather(f32[64,128]{1,0:T(8,128)S(1)} %pad_maximum_fusion.15), channel_id=2, replica_groups={{0,8,16,24},{2,10,18,26},{4,12,20,28},{6,14,22,30},{1,9,17,25},{3,11,19..., dimensions={0}, use_global_device_ids=true | all-gather | bytes 163840 | tf_op jit(solution)/shard_map/all_gather | solution.py:651
  58.7 3.6 fusion.73
  83.0 24.7 %collective-permute-done.10.refs_12_ = bf16[784,768]{1,0:T(8,128)(2,1)S(1)} collective-permute-done((bf16[784,768]{1,0:T(8,128)(2,1)}, bf16[784,768]{1,0:T(8,128)(2,1)S(1)}, u32[]{:S(2)}, u32[]{:S(2)}) %collective-permute-start.10) | collective-permute-done | bytes 1204256 | tf_op jit(solution)/shard_map/ppermute | solution.py:292
  107.7 3.8 collective-permute-done.11.refs_13_
  116.9 27.1 %shard_map.554 = f32[2,3080,128]{2,1,0:T(8,128)} custom-call(s32[2,1,4096]{2,1,0:T(1,128)} %pad_add_fusion.idx_ref, f32[2,1,4096]{2,1,0:T(1,128)} %pad_maximum_fusion.16.mix_ref, bf16[784,768]{1,0:T(8,128)(2,1)} %copy-done.50, bf16[800,768]{1,0:T(8,128)(2,1)} %copy-done.49, bf16[784,768]{1,0:T(8,128)(2,1)} %copy-done.58, bf16[800,768]{1,0:T(8,128)(2,1)} %copy-done.55, ...), custom_call_target="tpu_custom_call" | custom-call | flops 16777216 | bytes 41943040 | tf_op jit(solution)/shard_map/pallas_call | solution.py:437
  144.1 3.0 slice_bitcast_fusion
  153.8 30.7 %shard_map.553 = (f32[2,3080,128]{2,1,0:T(8,128)}, bf16[12672,768]{1,0:T(8,128)(2,1)}) custom-call(s32[2,1,4096]{2,1,0:T(1,128)} %pad_add_fusion.1.idx_ref, f32[2,1,4096]{2,1,0:T(1,128)} %pad_maximum_fusion.17.mix_ref, bf16[784,768]{1,0:T(8,128)(2,1)} %copy-done.50, bf16[800,768]{1,0:T(8,128)(2,1)} %copy-done.49, bf16[784,768]{1,0:T(8,128)(2,1)} %copy-done.58, ...), custom_call_target="tpu_custom_call" | custom-call | flops 16777216 | bytes 41943040 | tf_op jit(solution)/shard_map/pallas_call | solution.py:437
  184.5 2.4 fusion.42
  187.5 9.4 %collective-permute-done.15 = bf16[3072,128]{1,0:T(8,128)(2,1)} collective-permute-done((bf16[3072,128]{1,0:T(8,128)(2,1)S(1)}, bf16[3072,128]{1,0:T(8,128)(2,1)}, u32[]{:S(2)}, u32[]{:S(2)}) %collective-permute-start.15) | collective-permute-done | bytes 786464 | tf_op jit(solution)/shard_map/ppermute | solution.py:292
  196.9 2.7 reshape.2018
  199.7 15.5 %scatter_custom_fusion.1 = f32[8192]{0:T(1024)S(1)} fusion(s32[4096]{0:T(1024)S(1)} %get-tuple-element.490, f32[4096]{0:T(1024)S(1)} %exponential_divide_fusion, f32[]{:T(128)} %constant.588.clone.1), kind=kCustom, calls=%fused_computation.351 | custom fusion | bytes 32772 | tf_op jit(solution)/shard_map/scatter | solution.py:753
  215.2 16.0 %scatter_custom_fusion = f32[8192]{0:T(1024)S(1)} fusion(s32[4096]{0:T(1024)S(1)} %get-tuple-element.490, f32[4096]{0:T(1024)S(1)} %get-tuple-element.491, f32[]{:T(128)} %constant.588.clone.1), kind=kCustom, calls=%fused_computation.353 | custom fusion | bytes 32772 | tf_op jit(solution)/shard_map/scatter | solution.py:753
  233.3 14.2 %collective-permute-done.16 = bf16[3072,128]{1,0:T(8,128)(2,1)} collective-permute-done((bf16[3072,128]{1,0:T(8,128)(2,1)}, bf16[3072,128]{1,0:T(8,128)(2,1)}, u32[]{:S(2)}, u32[]{:S(2)}) %collective-permute-start.16) | collective-permute-done | bytes 786464 | tf_op jit(solution)/shard_map/ppermute | solution.py:292
  247.5 3.5 fusion.167
  256.5 6.5 fusion.179.q_ref.k_ref.v_ref
  263.0 4.9 shard_map.555
  275.2 17.4 %shard_map.556 = (bf16[512,768]{1,0:T(8,128)(2,1)S(1)}, f32[512,768]{1,0:T(8,128)}) custom-call(s32[1]{0:T(128)} %dynamic_slice.235.len_ref, s32[1]{0:T(128)} %bitcast.46.core_ref, bf16[512,768]{1,0:T(8,128)(2,1)S(1)} %copy-done.30, bf16[512,768]{1,0:T(8,128)(2,1)S(1)} %copy-done.32, bf16[512,768]{1,0:T(8,128)(2,1)S(1)} %collective-permute-done.17.kf_ref, ...), custom_call_target="tpu_custom_call" | custom-call | flops 1610612736 | bytes 7077888 | tf_op jit(solution)/shard_map/pallas_call | solution.py:161
  293.7 3.9 fusion.166
  299.5 5.8 multiply_convert_fusion.3
  309.4 6.8 all-to-all-start
  316.4 7.5 fusion.165
  328.4 2.6 collective-permute-start.24
  336.0 3.6 collective-permute-done.23
  341.3 12.2 %fusion.178 = (f32[256]{0:T(256)S(1)}, f32[256,12672]{1,0:T(8,128)}) fusion(bf16[256,768]{1,0:T(8,128)(2,1)S(1)} %pad_maximum_fusion.4, bf16[12672,768]{1,0:T(8,128)(2,1)} %get-tuple-element.222, pred[12672]{0:T(1024)(128)(4,1)S(1)} %fusion.89), kind=kOutput, calls=%fused_computation.558 | convolution fusion | flops 4989321216 | bytes 32847232 | tf_op jit(solution)/shard_map/dot_general | solution.py:29
  353.5 6.9 exponential_reduce_fusion
  369.2 15.8 %fusion = f32[256,768]{1,0:T(8,128)S(1)} fusion(bf16[12672,768]{1,0:T(8,128)(2,1)} %get-tuple-element.222, f32[256,12672]{1,0:T(8,128)} %get-tuple-element.480, f32[256]{0:T(256)S(1)} %reshape.2027, f32[256]{0:T(256)S(1)} %copy-done.155, s32[256]{0:T(256)S(1)} %copy-done.148), kind=kOutput, calls=%fused_computation.19 | convolution fusion | flops 5002297344 | bytes 33229824 | tf_op jit(solution)/shard_map/dot_general | solution.py:25
  389.2 3.4 collective-permute-done.31
  392.6 11.1 %collective-permute-done.30 = f32[64,768]{1,0:T(8,128)S(1)} collective-permute-done((f32[64,768]{1,0:T(8,128)S(1)}, f32[64,768]{1,0:T(8,128)S(1)}, u32[]{:S(2)}, u32[]{:S(2)}) %collective-permute-start.30) | collective-permute-done | bytes 196640 | tf_op jit(solution)/shard_map/ppermute | solution.py:292
  409.9 3.4 multiply_reduce_fusion
  414.8 8.9 %fusion.10 = bf16[512,3072]{1,0:T(8,128)(2,1)S(1)} fusion(f32[512,3072]{1,0:T(8,128)} %get-tuple-element.477, bf16[512,768]{1,0:T(8,128)(2,1)S(1)} %multiply_convert_fusion.5, bf16[3072,768]{1,0:T(8,128)(2,1)} %all-gather.13.cloned.1.call-done), kind=kOutput, calls=%fused_computation.29 | convolution fusion | flops 2447376384 | bytes 14942208 | tf_op jit(solution)/shard_map/dot_general | solution.py:29
  423.7 3.6 multiply_reduce_fusion.2
  433.2 3.7 fusion.180
  437.0 3.8 convolution_add_fusion
  451.7 27.6 %shard_map.557 = (bf16[512,768]{1,0:T(8,128)(2,1)S(1)}, f32[512,768]{1,0:T(8,128)}, bf16[512,768]{1,0:T(8,128)(2,1)S(1)}, f32[512,768]{1,0:T(8,128)}, bf16[512,768]{1,0:T(8,128)(2,1)S(1)}) custom-call(s32[1]{0:T(128)} %dynamic_slice.235.len_ref, s32[1]{0:T(128)} %bitcast.46.core_ref, bf16[512,768]{1,0:T(8,128)(2,1)S(1)} %copy-done.31, ...), custom_call_target="tpu_custom_call" | custom-call | flops 4026531840 | bytes 12582912 | tf_op jit(solution)/shard_map/pallas_call | solution.py:239
  498.0 2.9 multiply_reduce_fusion.4
  502.4 2.5 reshape.2030.refs_0_
  504.9 2.5 fusion.32
  511.7 2.8 collective-permute-start.46
  519.5 2.6 convolution_add_fusion.1
  522.8 10.5 %collective-permute-done.49.refs_2_ = bf16[1,3072,128]{2,1,0:T(8,128)(2,1)S(1)} collective-permute-done((bf16[1,3072,128]{2,1,0:T(8,128)(2,1)}, bf16[1,3072,128]{2,1,0:T(8,128)(2,1)S(1)}, u32[]{:S(2)}, u32[]{:S(2)}) %collective-permute-start.49) | collective-permute-done | bytes 786464 | tf_op jit(solution)/shard_map/ppermute | solution.py:292
  542.4 17.6 %collective-permute-done.52 = bf16[4,2,48,1536]{3,2,0,1:T(8,128)(2,1)} collective-permute-done((bf16[4,2,48,1536]{3,2,0,1:T(8,128)(2,1)S(1)}, bf16[4,2,48,1536]{3,2,0,1:T(8,128)(2,1)}, u32[]{:S(2)}, u32[]{:S(2)}) %collective-permute-start.52) | collective-permute-done | bytes 1179680 | tf_op jit(solution)/shard_map/ppermute | solution.py:292
  565.8 3.3 pad_maximum_fusion.2.refs_8_
  569.2 6.7 collective-permute-done.53
  575.9 2.4 collective-permute-start.54
  580.5 2.6 dynamic-slice_bitcast_fusion.5
  584.5 12.8 %collective-permute-start.61 = (f32[48,4608]{1,0:T(8,128)}, f32[48,4608]{1,0:T(8,128)}, u32[]{:S(2)}, u32[]{:S(2)}) collective-permute-start(f32[48,4608]{1,0:T(8,128)} %get-tuple-element.386), channel_id=1, source_target_pairs={{0,8},{2,10},{4,12},{6,14},{1,9},{3,11},{5,13},{7,15}} | collective-permute-start | bytes 2654216 | tf_op jit(solution)/shard_map/ppermute | solution.py:302
  599.9 15.9 %fusion.16.refs_5_ = f32[1584,768]{1,0:T(8,128)} fusion(bf16[2048,896]{1,0:T(8,128)(2,1)} %bitcast.335, s32[2048]{0:T(1024)S(1)} %copy-done.143, f32[2048]{0:T(1024)S(1)} %convert_reduce_fusion, f32[2048]{0:T(1024)S(1)} %copy-done.142, bf16[1572,768]{1,0:T(8,128)(2,1)S(1)} %copy-done.41), kind=kOutput, calls=%fused_computation.42 | convolution fusion | flops 9985130496 | bytes 13596672 | tf_op jit(solution)/shard_map/dot_general | solution.py:33
  615.8 18.7 %shard_map.558.refs_4_ = f32[12608,128]{1,0:T(8,128)} custom-call(s32[14]{0:T(128)} %get-tuple-element.425.cnt_ref, s32[14,256]{1,0:T(8,128)} %get-tuple-element.424.row_ref, s32[14,256]{1,0:T(8,128)} %get-tuple-element.423.pos_ref, f32[14,256]{1,0:T(8,128)} %broadcast_select_fusion.1.mix_ref, bf16[1,3072,128]{2,1,0:T(8,128)(2,1)} %reshape.2030.refs_0_, ...), custom_call_target="tpu_custom_call" | custom-call | flops 3670016 | bytes 18350080 | tf_op jit(solution)/shard_map/pallas_call | solution.py:549
  634.6 4.1 collective-permute-done.55.refs_2_
  642.4 3.4 bitcast_add_fusion.4
  645.7 11.0 %collective-permute-start.67 = (f32[48,4608]{1,0:T(8,128)}, f32[48,4608]{1,0:T(8,128)}, u32[]{:S(2)}, u32[]{:S(2)}) collective-permute-start(f32[48,4608]{1,0:T(8,128)} %get-tuple-element.384), channel_id=1, source_target_pairs={{0,8},{2,10},{4,12},{6,14},{8,16},{10,18},{12,20},{14,22},{1,9},{3... | collective-permute-start | bytes 2654216 | tf_op jit(solution)/shard_map/ppermute | solution.py:302
  665.3 18.8 %shard_map.559.refs_4_ = f32[12608,128]{1,0:T(8,128)} custom-call(s32[12]{0:T(128)} %get-tuple-element.422.cnt_ref, s32[12,256]{1,0:T(8,128)} %get-tuple-element.421.row_ref, s32[12,256]{1,0:T(8,128)} %get-tuple-element.420.pos_ref, f32[12,256]{1,0:T(8,128)} %broadcast_select_fusion.mix_ref, bf16[3,3072,128]{2,1,0:T(8,128)(2,1)} %collective-permute-done.54.refs_0_, ...), custom_call_target="tpu_custom_call" | custom-call | flops 3145728 | bytes 15728640 | tf_op jit(solution)/shard_map/pallas_call | solution.py:549
  684.2 3.5 collective-permute-start.69
  696.1 3.4 bitcast_add_fusion.3
  706.0 16.1 %shard_map.560 = (f32[1572,768]{1,0:T(8,128)}, f32[8,128]{1,0:T(8,128)}) custom-call(s32[6]{0:T(128)} %get-tuple-element.446.cnt_ref, s32[6,256]{1,0:T(8,128)} %get-tuple-element.445.row_ref, s32[6,256]{1,0:T(8,128)} %get-tuple-element.444.pos_ref, f32[6,256]{1,0:T(8,128)} %broadcast_select_fusion.2.mix_ref, ...), custom_call_target="tpu_custom_call" | custom-call | flops 1572864 | bytes 7864320 | tf_op jit(solution)/shard_map/pallas_call | solution.py:549
  722.1 3.3 collective-permute-done.72
  739.1 3.2 collective-permute-start.77
  743.9 2.9 collective-permute-done.78
  746.8 9.8 %collective-permute-start.79 = (f32[2]{0:T(128)S(1)}, f32[2]{0:T(128)S(1)}, u32[]{:S(2)}, u32[]{:S(2)}) collective-permute-start(f32[2]{0:T(128)S(1)} %add_add_fusion), channel_id=1, source_target_pairs={{0,24},{1,25},{2,26},{3,27},{4,28},{5,29},{6,30},{7,31},{8,0},{9,1... | collective-permute-start | bytes 32 | tf_op jit(solution)/shard_map/ppermute | solution.py:292
  758.0 3.1 collective-permute-done.80
  763.9 13.4 %multiply_subtract_fusion = (f32[1572,768]{1,0:T(8,128)}, f32[1572,768]{1,0:T(8,128)}, f32[1572,768]{1,0:T(8,128)}) fusion(f32[1572,768]{1,0:T(8,128)} %param.41, f32[1572,768]{1,0:T(8,128)} %get-tuple-element.309, f32[]{:T(128)} %min.3, f32[1572,768]{1,0:T(8,128)} %param.42, f32[1572,768]{1,0:T(8,128)} %param.43), kind=kLoop, calls=%fused_computation.32 | loop fusion | flops 19316736 | bytes 33804292 | tf_op jit(solution)/shard_map/sub | solution.py:258
  (845 shorter events, 210.4 us)
Async XLA Ops:
  7.2 180.3 %all-gather.7.cloned.1.call-start = ((), (), s32[]{:S(2)}) async-start(), calls=%async_computation.1 | async-start | bytes 1723392 | tf_op jit(solution)/shard_map/all_gather | solution.py:628
  11.0 245.5 %all-gather.9.cloned.1.call-start = ((), (), s32[]{:S(2)}) async-start(), calls=%async_computation.2 | async-start | bytes 3649536 | tf_op jit(solution)/shard_map/all_gather | solution.py:623
  13.9 62.2 %collective-permute-start = (bf16[784,768]{1,0:T(8,128)(2,1)S(1)}, bf16[784,768]{1,0:T(8,128)(2,1)}, u32[]{:S(2)}, u32[]{:S(2)}) collective-permute-start(bf16[784,768]{1,0:T(8,128)(2,1)S(1)} %slice.299.refs_0_), channel_id=1, source_target_pairs={{0,2},{1,3},{2,0},{3,1},{4,6},{5,7},{6,4},{7,5},{8,10},{9,11},{10,... | collective-permute-start | bytes 3612680 | tf_op jit(solution)/shard_map/ppermute | solution.py:292
  16.9 59.2 %collective-permute-start.1 = (bf16[784,768]{1,0:T(8,128)(2,1)S(1)}, bf16[784,768]{1,0:T(8,128)(2,1)}, u32[]{:S(2)}, u32[]{:S(2)}) collective-permute-start(bf16[784,768]{1,0:T(8,128)(2,1)S(1)} %slice.299.refs_0_), channel_id=1, source_target_pairs={{0,4},{1,5},{2,6},{3,7},{4,0},{5,1},{6,2},{7,3},{8,12},{9,13},{10,... | collective-permute-start | bytes 3612680 | tf_op jit(solution)/shard_map/ppermute | solution.py:292
  18.5 57.6 %collective-permute-start.2 = (bf16[800,768]{1,0:T(8,128)(2,1)S(1)}, bf16[800,768]{1,0:T(8,128)(2,1)}, u32[]{:S(2)}, u32[]{:S(2)}) collective-permute-start(bf16[800,768]{1,0:T(8,128)(2,1)S(1)} %pad_slice_fusion.refs_1_), channel_id=1, source_target_pairs={{0,2},{1,3},{2,0},{3,1},{4,6},{5,7},{6,4},{7,5},{8,10},{9,11},{10,... | collective-permute-start | bytes 3686408 | tf_op jit(solution)/shard_map/ppermute | solution.py:292
  19.1 57.0 %collective-permute-start.3 = (bf16[800,768]{1,0:T(8,128)(2,1)S(1)}, bf16[800,768]{1,0:T(8,128)(2,1)}, u32[]{:S(2)}, u32[]{:S(2)}) collective-permute-start(bf16[800,768]{1,0:T(8,128)(2,1)S(1)} %pad_slice_fusion.refs_1_), channel_id=1, source_target_pairs={{0,4},{1,5},{2,6},{3,7},{4,0},{5,1},{6,2},{7,3},{8,12},{9,13},{10,... | collective-permute-start | bytes 3686408 | tf_op jit(solution)/shard_map/ppermute | solution.py:292
  20.3 273.4 %all-gather.11.cloned.1.call-start = ((), (), s32[]{:S(2)}) async-start(), calls=%async_computation.3 | async-start | bytes 6082560 | tf_op jit(solution)/shard_map/all_gather | solution.py:623
  76.2 31.5 %collective-permute-start.10 = (bf16[784,768]{1,0:T(8,128)(2,1)}, bf16[784,768]{1,0:T(8,128)(2,1)S(1)}, u32[]{:S(2)}, u32[]{:S(2)}) collective-permute-start(bf16[784,768]{1,0:T(8,128)(2,1)} %collective-permute-done.refs_4_), channel_id=1, source_target_pairs={{0,4},{1,5},{2,6},{3,7},{4,0},{5,1},{6,2},{7,3},{8,12},{9,13},{10,... | collective-permute-start | bytes 3612680 | tf_op jit(solution)/shard_map/ppermute | solution.py:292
  78.3 33.3 %collective-permute-start.11 = (bf16[800,768]{1,0:T(8,128)(2,1)}, bf16[800,768]{1,0:T(8,128)(2,1)S(1)}, u32[]{:S(2)}, u32[]{:S(2)}) collective-permute-start(bf16[800,768]{1,0:T(8,128)(2,1)} %collective-permute-done.3.refs_9_), channel_id=1, source_target_pairs={{0,2},{1,3},{2,0},{3,1},{4,6},{5,7},{6,4},{7,5},{8,10},{9,11},{10,... | collective-permute-start | bytes 3686408 | tf_op jit(solution)/shard_map/ppermute | solution.py:292
  81.2 33.1 %collective-permute-start.9 = (bf16[800,768]{1,0:T(8,128)(2,1)}, bf16[800,768]{1,0:T(8,128)(2,1)S(1)}, u32[]{:S(2)}, u32[]{:S(2)}) collective-permute-start(bf16[800,768]{1,0:T(8,128)(2,1)} %collective-permute-done.3.refs_9_), channel_id=1, source_target_pairs={{0,1},{1,0},{2,3},{3,2},{4,5},{5,4},{6,7},{7,6},{8,9},{9,8},{10,11... | collective-permute-start | bytes 3686408 | tf_op jit(solution)/shard_map/ppermute | solution.py:292
  82.3 32.1 %collective-permute-start.5 = (bf16[800,768]{1,0:T(8,128)(2,1)S(1)}, bf16[800,768]{1,0:T(8,128)(2,1)S(1)}, u32[]{:S(2)}, u32[]{:S(2)}) collective-permute-start(bf16[800,768]{1,0:T(8,128)(2,1)S(1)} %pad_slice_fusion.refs_1_), channel_id=1, source_target_pairs={{0,1},{1,0},{2,3},{3,2},{4,5},{5,4},{6,7},{7,6},{8,9},{9,8},{10,11... | collective-permute-start | bytes 3686408 | tf_op jit(solution)/shard_map/ppermute | solution.py:292
  82.9 31.4 %collective-permute-start.7 = (bf16[800,768]{1,0:T(8,128)(2,1)}, bf16[800,768]{1,0:T(8,128)(2,1)S(1)}, u32[]{:S(2)}, u32[]{:S(2)}) collective-permute-start(bf16[800,768]{1,0:T(8,128)(2,1)} %collective-permute-done.2.refs_5_), channel_id=1, source_target_pairs={{0,1},{1,0},{2,3},{3,2},{4,5},{5,4},{6,7},{7,6},{8,9},{9,8},{10,11... | collective-permute-start | bytes 3686408 | tf_op jit(solution)/shard_map/ppermute | solution.py:292
  107.7 7.6 collective-permute-start.12
  147.1 169.3 %all-gather.13.cloned.1.call-start = ((), (), s32[]{:S(2)}) async-start(), calls=%async_computation.4 | async-start | bytes 4866048 | tf_op jit(solution)/shard_map/all_gather | solution.py:623
  148.7 38.8 %collective-permute-start.14 = (bf16[3072,128]{1,0:T(8,128)(2,1)}, bf16[3072,128]{1,0:T(8,128)(2,1)S(1)}, u32[]{:S(2)}, u32[]{:S(2)}) collective-permute-start(bf16[3072,128]{1,0:T(8,128)(2,1)} %get-tuple-element.195), channel_id=1, source_target_pairs={{0,8},{1,9},{2,10},{3,11},{4,12},{5,13},{6,14},{7,15},{8,16},{9,17... | collective-permute-start | bytes 2359304 | tf_op jit(solution)/shard_map/ppermute | solution.py:292
  150.4 46.5 %collective-permute-start.15 = (bf16[3072,128]{1,0:T(8,128)(2,1)S(1)}, bf16[3072,128]{1,0:T(8,128)(2,1)}, u32[]{:S(2)}, u32[]{:S(2)}) collective-permute-start(bf16[3072,128]{1,0:T(8,128)(2,1)S(1)} %get-tuple-element.196), channel_id=1, source_target_pairs={{0,24},{1,25},{2,26},{3,27},{4,28},{5,29},{6,30},{7,31},{8,0},{9,1... | collective-permute-start | bytes 2359304 | tf_op jit(solution)/shard_map/ppermute | solution.py:292
  186.9 60.6 %collective-permute-start.16 = (bf16[3072,128]{1,0:T(8,128)(2,1)}, bf16[3072,128]{1,0:T(8,128)(2,1)}, u32[]{:S(2)}, u32[]{:S(2)}) collective-permute-start(bf16[3072,128]{1,0:T(8,128)(2,1)} %fusion.42), channel_id=1, source_target_pairs={{0,16},{1,17},{2,18},{3,19},{4,20},{5,21},{6,22},{7,23},{8,24},{9,... | collective-permute-start | bytes 2359304 | tf_op jit(solution)/shard_map/ppermute | solution.py:292
  268.6 24.0 %collective-permute-start.19 = (bf16[512,768]{1,0:T(8,128)(2,1)}, bf16[512,768]{1,0:T(8,128)(2,1)S(1)}, u32[]{:S(2)}, u32[]{:S(2)}) collective-permute-start(bf16[512,768]{1,0:T(8,128)(2,1)} %copy-done.68), channel_id=1, source_target_pairs={{0,1},{1,0},{2,3},{3,2},{4,5},{5,4},{6,7},{7,6},{8,9},{9,8},{10,11... | collective-permute-start | bytes 2359304 | tf_op jit(solution)/shard_map/ppermute | solution.py:292
  293.5 11.8 %collective-permute-start.20 = (bf16[512,768]{1,0:T(8,128)(2,1)S(1)}, bf16[512,768]{1,0:T(8,128)(2,1)}, u32[]{:S(2)}, u32[]{:S(2)}) collective-permute-start(bf16[512,768]{1,0:T(8,128)(2,1)S(1)} %get-tuple-element.214), channel_id=1, source_target_pairs={{0,1},{1,0},{2,3},{3,2},{4,5},{5,4},{6,7},{7,6},{8,9},{9,8},{10,11... | collective-permute-start | bytes 2359304 | tf_op jit(solution)/shard_map/ppermute | solution.py:292
  306.2 35.0 %collective-permute-start.25 = (bf16[512,3072]{1,0:T(8,128)(2,1)}, bf16[512,3072]{1,0:T(8,128)(2,1)}, u32[]{:S(2)}, u32[]{:S(2)}) collective-permute-start(bf16[512,3072]{1,0:T(8,128)(2,1)} %get-tuple-element.216), channel_id=1, source_target_pairs={{0,1},{1,0},{2,3},{3,2},{4,5},{5,4},{6,7},{7,6},{8,9},{9,8},{10,11... | collective-permute-start | bytes 9437192 | tf_op jit(solution)/shard_map/ppermute | solution.py:292
  309.4 24.6 %all-to-all-start = ((f32[32,1,512]{2,1,0:T(1,128)}), f32[32,1,512]{2,1,0:T(1,128)S(1)}, u32[]{:S(2)}, u32[]{:S(2)}) async-start(f32[32,1,512]{2,1,0:T(1,128)} %all_to_all.8), calls=%async_computation | async-start | bytes 131072 | tf_op jit(solution)/shard_map/all_to_all | solution.py:802
  316.3 318.3 %all-gather.15.cloned.1.call-start = ((), (), s32[]{:S(2)}) async-start(), calls=%async_computation.5 | async-start | bytes 1216512 | tf_op jit(solution)/shard_map/all_gather | solution.py:894
  328.4 7.6 collective-permute-start.24
  331.0 8.5 %collective-permute-start.23 = (bf16[64,768]{1,0:T(8,128)(2,1)S(1)}, bf16[64,768]{1,0:T(8,128)(2,1)S(1)}, u32[]{:S(2)}, u32[]{:S(2)}) collective-permute-start(bf16[64,768]{1,0:T(8,128)(2,1)S(1)} %select_convert_fusion), channel_id=1, source_target_pairs={{0,16},{1,17},{2,18},{3,19},{4,20},{5,21},{6,22},{7,23},{8,24},{9,... | collective-permute-start | bytes 294920 | tf_op jit(solution)/shard_map/ppermute | solution.py:292
  387.2 16.5 %collective-permute-start.30 = (f32[64,768]{1,0:T(8,128)S(1)}, f32[64,768]{1,0:T(8,128)S(1)}, u32[]{:S(2)}, u32[]{:S(2)}) collective-permute-start(f32[64,768]{1,0:T(8,128)S(1)} %get-tuple-element.397), channel_id=1, source_target_pairs={{0,16},{1,17},{2,18},{3,19},{4,20},{5,21},{6,22},{7,23},{8,24},{9,... | collective-permute-start | bytes 589832 | tf_op jit(solution)/shard_map/ppermute | solution.py:292
  387.6 16.1 %collective-permute-start.29 = (f32[64,768]{1,0:T(8,128)S(1)}, f32[64,768]{1,0:T(8,128)S(1)}, u32[]{:S(2)}, u32[]{:S(2)}) collective-permute-start(f32[64,768]{1,0:T(8,128)S(1)} %get-tuple-element.395), channel_id=1, source_target_pairs={{0,8},{1,9},{2,10},{3,11},{4,12},{5,13},{6,14},{7,15},{8,16},{9,17... | collective-permute-start | bytes 589832 | tf_op jit(solution)/shard_map/ppermute | solution.py:292
  406.8 35.6 %collective-permute-start.34 = (bf16[256,896]{1,0:T(8,128)(2,1)S(1)}, bf16[256,896]{1,0:T(8,128)(2,1)S(1)}, u32[]{:S(2)}, u32[]{:S(2)}) collective-permute-start(bf16[256,896]{1,0:T(8,128)(2,1)S(1)} %get-tuple-element.399), channel_id=1, source_target_pairs={{0,2},{1,3},{2,0},{3,1},{4,6},{5,7},{6,4},{7,5},{8,10},{9,11},{10,... | collective-permute-start | bytes 1376264 | tf_op jit(solution)/shard_map/ppermute | solution.py:292
  408.4 33.9 %collective-permute-start.35 = (bf16[256,896]{1,0:T(8,128)(2,1)S(1)}, bf16[256,896]{1,0:T(8,128)(2,1)S(1)}, u32[]{:S(2)}, u32[]{:S(2)}) collective-permute-start(bf16[256,896]{1,0:T(8,128)(2,1)S(1)} %get-tuple-element.399), channel_id=1, source_target_pairs={{0,4},{1,5},{2,6},{3,7},{4,0},{5,1},{6,2},{7,3},{8,12},{9,13},{10,... | collective-permute-start | bytes 1376264 | tf_op jit(solution)/shard_map/ppermute | solution.py:292
  429.8 11.0 %collective-permute-start.33 = (bf16[512,1536]{1,0:T(8,128)(2,1)S(1)}, bf16[512,1536]{1,0:T(8,128)(2,1)S(1)}, u32[]{:S(2)}, u32[]{:S(2)}) collective-permute-start(bf16[512,1536]{1,0:T(8,128)(2,1)S(1)} %constant_dynamic-slice_fusion.15), channel_id=1, source_target_pairs={{0,1},{1,0},{2,3},{3,2},{4,5},{5,4},{6,7},{7,6},{8,9},{9,8},{10,11... | collective-permute-start | bytes 4718600 | tf_op jit(solution)/shard_map/ppermute | solution.py:292
  443.5 41.9 %collective-permute-start.36 = (bf16[4,2,192,384]{3,2,1,0:T(8,128)(2,1)}, bf16[4,2,192,384]{3,2,1,0:T(8,128)(2,1)}, u32[]{:S(2)}, u32[]{:S(2)}) collective-permute-start(bf16[4,2,192,384]{3,2,1,0:T(8,128)(2,1)} %fusion.29), channel_id=1, source_target_pairs={{0,4},{1,5},{2,6},{3,7},{4,0},{5,1},{6,2},{7,3},{8,12},{9,13},{10,... | collective-permute-start | bytes 3538952 | tf_op jit(solution)/shard_map/ppermute | solution.py:292
  446.9 38.6 %collective-permute-start.37 = (bf16[4,2,48,1536]{3,2,1,0:T(8,128)(2,1)}, bf16[4,2,48,1536]{3,2,1,0:T(8,128)(2,1)S(1)}, u32[]{:S(2)}, u32[]{:S(2)}) collective-permute-start(bf16[4,2,48,1536]{3,2,1,0:T(8,128)(2,1)} %fusion.30), channel_id=1, source_target_pairs={{0,2},{1,3},{2,0},{3,1},{4,6},{5,7},{6,4},{7,5},{8,10},{9,11},{10,... | collective-permute-start | bytes 3538952 | tf_op jit(solution)/shard_map/ppermute | solution.py:292
  447.3 32.9 %collective-permute-start.38 = (bf16[512,384]{1,0:T(8,128)(2,1)S(1)}, bf16[512,384]{1,0:T(8,128)(2,1)S(1)}, u32[]{:S(2)}, u32[]{:S(2)}) collective-permute-start(bf16[512,384]{1,0:T(8,128)(2,1)S(1)} %constant_dynamic-slice_fusion.14), channel_id=1, source_target_pairs={{0,1},{1,0},{2,3},{3,2},{4,5},{5,4},{6,7},{7,6},{8,9},{9,8},{10,11... | collective-permute-start | bytes 1179656 | tf_op jit(solution)/shard_map/ppermute | solution.py:292
  447.4 35.2 %collective-permute-start.44 = (bf16[256,896]{1,0:T(8,128)(2,1)S(1)}, bf16[256,896]{1,0:T(8,128)(2,1)S(1)}, u32[]{:S(2)}, u32[]{:S(2)}) collective-permute-start(bf16[256,896]{1,0:T(8,128)(2,1)S(1)} %collective-permute-done.34), channel_id=1, source_target_pairs={{0,4},{1,5},{2,6},{3,7},{4,0},{5,1},{6,2},{7,3},{8,12},{9,13},{10,... | collective-permute-start | bytes 1376264 | tf_op jit(solution)/shard_map/ppermute | solution.py:292
  484.5 22.9 %collective-permute-start.45 = (bf16[4,256,896]{2,1,0:T(8,128)(2,1)}, bf16[4,256,896]{2,1,0:T(8,128)(2,1)}, u32[]{:S(2)}, u32[]{:S(2)}) collective-permute-start(bf16[4,256,896]{2,1,0:T(8,128)(2,1)} %pad_maximum_fusion.3), channel_id=1, source_target_pairs={{0,1},{1,0},{2,3},{3,2},{4,5},{5,4},{6,7},{7,6},{8,9},{9,8},{10,11... | collective-permute-start | bytes 5505032 | tf_op jit(solution)/shard_map/ppermute | solution.py:292
  485.5 8.6 %collective-permute-start.40 = (bf16[512,768]{1,0:T(8,128)(2,1)S(1)}, bf16[512,768]{1,0:T(8,128)(2,1)S(1)}, u32[]{:S(2)}, u32[]{:S(2)}) collective-permute-start(bf16[512,768]{1,0:T(8,128)(2,1)S(1)} %get-tuple-element.246), channel_id=1, source_target_pairs={{0,1},{1,0},{2,3},{3,2},{4,5},{5,4},{6,7},{7,6},{8,9},{9,8},{10,11... | collective-permute-start | bytes 2359304 | tf_op jit(solution)/shard_map/ppermute | solution.py:292
  485.9 8.4 %collective-permute-start.39 = (bf16[512,768]{1,0:T(8,128)(2,1)S(1)}, bf16[512,768]{1,0:T(8,128)(2,1)S(1)}, u32[]{:S(2)}, u32[]{:S(2)}) collective-permute-start(bf16[512,768]{1,0:T(8,128)(2,1)S(1)} %get-tuple-element.244), channel_id=1, source_target_pairs={{0,1},{1,0},{2,3},{3,2},{4,5},{5,4},{6,7},{7,6},{8,9},{9,8},{10,11... | collective-permute-start | bytes 2359304 | tf_op jit(solution)/shard_map/ppermute | solution.py:292
  488.6 20.8 %collective-permute-start.41 = (bf16[4,192,384]{2,1,0:T(8,128)(2,1)}, bf16[4,192,384]{2,1,0:T(8,128)(2,1)}, u32[]{:S(2)}, u32[]{:S(2)}) collective-permute-start(bf16[4,192,384]{2,1,0:T(8,128)(2,1)} %fusion.43), channel_id=1, source_target_pairs={{0,2},{1,3},{2,0},{3,1},{4,6},{5,7},{6,4},{7,5},{8,10},{9,11},{10,... | collective-permute-start | bytes 1769480 | tf_op jit(solution)/shard_map/ppermute | solution.py:292
  491.3 18.1 %collective-permute-start.42 = (bf16[4,48,1536]{2,1,0:T(8,128)(2,1)}, bf16[4,48,1536]{2,1,0:T(8,128)(2,1)}, u32[]{:S(2)}, u32[]{:S(2)}) collective-permute-start(bf16[4,48,1536]{2,1,0:T(8,128)(2,1)} %fusion.44), channel_id=1, source_target_pairs={{0,4},{1,5},{2,6},{3,7},{4,0},{5,1},{6,2},{7,3},{8,12},{9,13},{10,... | collective-permute-start | bytes 1769480 | tf_op jit(solution)/shard_map/ppermute | solution.py:292
  496.4 13.1 %collective-permute-start.43 = (bf16[512,1152]{1,0:T(8,128)(2,1)}, bf16[512,1152]{1,0:T(8,128)(2,1)}, u32[]{:S(2)}, u32[]{:S(2)}) collective-permute-start(bf16[512,1152]{1,0:T(8,128)(2,1)} %constant_dynamic-slice_fusion.13), channel_id=1, source_target_pairs={{0,1},{1,0},{2,3},{3,2},{4,5},{5,4},{6,7},{7,6},{8,9},{9,8},{10,11... | collective-permute-start | bytes 3538952 | tf_op jit(solution)/shard_map/ppermute | solution.py:292
  509.4 54.5 %collective-permute-start.48 = (bf16[1,3072,128]{2,1,0:T(8,128)(2,1)}, bf16[1,3072,128]{2,1,0:T(8,128)(2,1)}, u32[]{:S(2)}, u32[]{:S(2)}) collective-permute-start(bf16[1,3072,128]{2,1,0:T(8,128)(2,1)} %reshape.2030.refs_0_), channel_id=1, source_target_pairs={{0,8},{1,9},{2,10},{3,11},{4,12},{5,13},{6,14},{7,15},{8,16},{9,17... | collective-permute-start | bytes 2359304 | tf_op jit(solution)/shard_map/ppermute | solution.py:292
  509.9 55.9 %collective-permute-start.47 = (bf16[1,3072,128]{2,1,0:T(8,128)(2,1)}, bf16[1,3072,128]{2,1,0:T(8,128)(2,1)}, u32[]{:S(2)}, u32[]{:S(2)}) collective-permute-start(bf16[1,3072,128]{2,1,0:T(8,128)(2,1)} %reshape.2030.refs_0_), channel_id=1, source_target_pairs={{0,16},{1,17},{2,18},{3,19},{4,20},{5,21},{6,22},{7,23},{8,24},{9,... | collective-permute-start | bytes 2359304 | tf_op jit(solution)/shard_map/ppermute | solution.py:292
  511.7 54.1 %collective-permute-start.46 = (bf16[1,3072,128]{2,1,0:T(8,128)(2,1)}, bf16[1,3072,128]{2,1,0:T(8,128)(2,1)}, u32[]{:S(2)}, u32[]{:S(2)}) collective-permute-start(bf16[1,3072,128]{2,1,0:T(8,128)(2,1)} %reshape.2030.refs_0_), channel_id=1, source_target_pairs={{0,24},{1,25},{2,26},{3,27},{4,28},{5,29},{6,30},{7,31},{8,0},{9,1... | collective-permute-start | bytes 2359304 | tf_op jit(solution)/shard_map/ppermute | solution.py:292
  514.6 18.7 %collective-permute-start.49 = (bf16[1,3072,128]{2,1,0:T(8,128)(2,1)}, bf16[1,3072,128]{2,1,0:T(8,128)(2,1)S(1)}, u32[]{:S(2)}, u32[]{:S(2)}) collective-permute-start(bf16[1,3072,128]{2,1,0:T(8,128)(2,1)} %reshape.2030.refs_0_), channel_id=1, source_target_pairs={{0,2},{1,3},{2,0},{3,1},{4,6},{5,7},{6,4},{7,5},{8,10},{9,11},{10,... | collective-permute-start | bytes 2359304 | tf_op jit(solution)/shard_map/ppermute | solution.py:292
  515.0 18.4 %collective-permute-start.50 = (bf16[1,3072,128]{2,1,0:T(8,128)(2,1)}, bf16[1,3072,128]{2,1,0:T(8,128)(2,1)S(1)}, u32[]{:S(2)}, u32[]{:S(2)}) collective-permute-start(bf16[1,3072,128]{2,1,0:T(8,128)(2,1)} %reshape.2030.refs_0_), channel_id=1, source_target_pairs={{0,4},{1,5},{2,6},{3,7},{4,0},{5,1},{6,2},{7,3},{8,12},{9,13},{10,... | collective-permute-start | bytes 2359304 | tf_op jit(solution)/shard_map/ppermute | solution.py:292
  533.6 26.4 %collective-permute-start.52 = (bf16[4,2,48,1536]{3,2,0,1:T(8,128)(2,1)S(1)}, bf16[4,2,48,1536]{3,2,0,1:T(8,128)(2,1)}, u32[]{:S(2)}, u32[]{:S(2)}) collective-permute-start(bf16[4,2,48,1536]{3,2,0,1:T(8,128)(2,1)S(1)} %fusion.31), channel_id=1, source_target_pairs={{0,4},{1,5},{2,6},{3,7},{4,0},{5,1},{6,2},{7,3},{8,12},{9,13},{10,... | collective-permute-start | bytes 3538952 | tf_op jit(solution)/shard_map/ppermute | solution.py:292
  540.9 28.3 %collective-permute-start.51 = (bf16[1,3072,128]{2,1,0:T(8,128)(2,1)S(1)}, bf16[1,3072,128]{2,1,0:T(8,128)(2,1)S(1)}, u32[]{:S(2)}, u32[]{:S(2)}) collective-permute-start(bf16[1,3072,128]{2,1,0:T(8,128)(2,1)S(1)} %copy-done.82), channel_id=1, source_target_pairs={{0,2},{1,3},{2,0},{3,1},{4,6},{5,7},{6,4},{7,5},{8,10},{9,11},{10,... | collective-permute-start | bytes 2359304 | tf_op jit(solution)/shard_map/ppermute | solution.py:292
  562.4 13.4 %collective-permute-start.53 = (bf16[4,48,1536]{2,1,0:T(8,128)(2,1)S(1)}, bf16[4,48,1536]{2,1,0:T(8,128)(2,1)S(1)}, u32[]{:S(2)}, u32[]{:S(2)}) collective-permute-start(bf16[4,48,1536]{2,1,0:T(8,128)(2,1)S(1)} %fusion.45), channel_id=1, source_target_pairs={{0,2},{1,3},{2,0},{3,1},{4,6},{5,7},{6,4},{7,5},{8,10},{9,11},{10,... | collective-permute-start | bytes 1769480 | tf_op jit(solution)/shard_map/ppermute | solution.py:292
  575.9 58.7 %collective-permute-start.54 = (bf16[3,3072,128]{2,1,0:T(8,128)(2,1)}, bf16[3,3072,128]{2,1,0:T(8,128)(2,1)}, u32[]{:S(2)}, u32[]{:S(2)}) collective-permute-start(bf16[3,3072,128]{2,1,0:T(8,128)(2,1)} %pad_maximum_fusion.2.refs_8_), channel_id=1, source_target_pairs={{0,2},{1,3},{2,0},{3,1},{4,6},{5,7},{6,4},{7,5},{8,10},{9,11},{10,... | collective-permute-start | bytes 7077896 | tf_op jit(solution)/shard_map/ppermute | solution.py:292
  578.8 18.5 %collective-permute-start.59 = (bf16[1,3072,128]{2,1,0:T(8,128)(2,1)S(1)}, bf16[1,3072,128]{2,1,0:T(8,128)(2,1)S(1)}, u32[]{:S(2)}, u32[]{:S(2)}) collective-permute-start(bf16[1,3072,128]{2,1,0:T(8,128)(2,1)S(1)} %collective-permute-done.51.refs_6_), channel_id=1, source_target_pairs={{0,1},{1,0},{2,3},{3,2},{4,5},{5,4},{6,7},{7,6},{8,9},{9,8},{10,11... | collective-permute-start | bytes 2359304 | tf_op jit(solution)/shard_map/ppermute | solution.py:292
  583.1 55.6 %collective-permute-start.55 = (bf16[3,3072,128]{2,1,0:T(8,128)(2,1)}, bf16[3,3072,128]{2,1,0:T(8,128)(2,1)}, u32[]{:S(2)}, u32[]{:S(2)}) collective-permute-start(bf16[3,3072,128]{2,1,0:T(8,128)(2,1)} %pad_maximum_fusion.2.refs_8_), channel_id=1, source_target_pairs={{0,4},{1,5},{2,6},{3,7},{4,0},{5,1},{6,2},{7,3},{8,12},{9,13},{10,... | collective-permute-start | bytes 7077896 | tf_op jit(solution)/shard_map/ppermute | solution.py:292
  584.4 31.4 %collective-permute-start.60 = (bf16[3,3072,128]{2,1,0:T(8,128)(2,1)}, bf16[3,3072,128]{2,1,0:T(8,128)(2,1)}, u32[]{:S(2)}, u32[]{:S(2)}) collective-permute-start(bf16[3,3072,128]{2,1,0:T(8,128)(2,1)} %pad_maximum_fusion.2.refs_8_), channel_id=1, source_target_pairs={{0,1},{1,0},{2,3},{3,2},{4,5},{5,4},{6,7},{7,6},{8,9},{9,8},{10,11... | collective-permute-start | bytes 7077896 | tf_op jit(solution)/shard_map/ppermute | solution.py:292
  584.5 50.1 %collective-permute-start.61 = (f32[48,4608]{1,0:T(8,128)}, f32[48,4608]{1,0:T(8,128)}, u32[]{:S(2)}, u32[]{:S(2)}) collective-permute-start(f32[48,4608]{1,0:T(8,128)} %get-tuple-element.386), channel_id=1, source_target_pairs={{0,8},{2,10},{4,12},{6,14},{1,9},{3,11},{5,13},{7,15}} | collective-permute-start | bytes 2654216 | tf_op jit(solution)/shard_map/ppermute | solution.py:302
  598.2 36.4 %collective-permute-start.62 = (f32[48,4608]{1,0:T(8,128)S(1)}, f32[48,4608]{1,0:T(8,128)}, u32[]{:S(2)}, u32[]{:S(2)}) collective-permute-start(f32[48,4608]{1,0:T(8,128)S(1)} %get-tuple-element.385), channel_id=1, source_target_pairs={{24,16},{26,18},{28,20},{30,22},{25,17},{27,19},{29,21},{31,23}} | collective-permute-start | bytes 2654216 | tf_op jit(solution)/shard_map/ppermute | solution.py:302
  638.8 21.9 %collective-permute-start.65 = (bf16[3,3072,128]{2,1,0:T(8,128)(2,1)}, bf16[3,3072,128]{2,1,0:T(8,128)(2,1)}, u32[]{:S(2)}, u32[]{:S(2)}) collective-permute-start(bf16[3,3072,128]{2,1,0:T(8,128)(2,1)} %collective-permute-done.54.refs_0_), channel_id=1, source_target_pairs={{0,1},{1,0},{2,3},{3,2},{4,5},{5,4},{6,7},{7,6},{8,9},{9,8},{10,11... | collective-permute-start | bytes 7077896 | tf_op jit(solution)/shard_map/ppermute | solution.py:292
  639.3 26.1 %collective-permute-start.66 = (bf16[3,3072,128]{2,1,0:T(8,128)(2,1)}, bf16[3,3072,128]{2,1,0:T(8,128)(2,1)}, u32[]{:S(2)}, u32[]{:S(2)}) collective-permute-start(bf16[3,3072,128]{2,1,0:T(8,128)(2,1)} %collective-permute-done.55.refs_2_), channel_id=1, source_target_pairs={{0,1},{1,0},{2,3},{3,2},{4,5},{5,4},{6,7},{7,6},{8,9},{9,8},{10,11... | collective-permute-start | bytes 7077896 | tf_op jit(solution)/shard_map/ppermute | solution.py:292
  641.1 43.1 %collective-permute-start.63 = (bf16[2,3072,128]{2,1,0:T(8,128)(2,1)S(1)}, bf16[2,3072,128]{2,1,0:T(8,128)(2,1)}, u32[]{:S(2)}, u32[]{:S(2)}) collective-permute-start(bf16[2,3072,128]{2,1,0:T(8,128)(2,1)S(1)} %slice.260), channel_id=1, source_target_pairs={{0,4},{1,5},{2,6},{3,7},{4,0},{5,1},{6,2},{7,3},{8,12},{9,13},{10,... | collective-permute-start | bytes 4718600 | tf_op jit(solution)/shard_map/ppermute | solution.py:292
  645.7 38.4 %collective-permute-start.67 = (f32[48,4608]{1,0:T(8,128)}, f32[48,4608]{1,0:T(8,128)}, u32[]{:S(2)}, u32[]{:S(2)}) collective-permute-start(f32[48,4608]{1,0:T(8,128)} %get-tuple-element.384), channel_id=1, source_target_pairs={{0,8},{2,10},{4,12},{6,14},{8,16},{10,18},{12,20},{14,22},{1,9},{3... | collective-permute-start | bytes 2654216 | tf_op jit(solution)/shard_map/ppermute | solution.py:302
  656.8 27.4 %collective-permute-start.68 = (f32[48,4608]{1,0:T(8,128)}, f32[48,4608]{1,0:T(8,128)}, u32[]{:S(2)}, u32[]{:S(2)}) collective-permute-start(f32[48,4608]{1,0:T(8,128)} %get-tuple-element.383), channel_id=1, source_target_pairs={{16,8},{18,10},{20,12},{22,14},{24,16},{26,18},{28,20},{30,22},{17... | collective-permute-start | bytes 2654216 | tf_op jit(solution)/shard_map/ppermute | solution.py:302
  660.7 23.4 %collective-permute-start.64 = (bf16[1,3072,128]{2,1,0:T(8,128)(2,1)}, bf16[1,3072,128]{2,1,0:T(8,128)(2,1)}, u32[]{:S(2)}, u32[]{:S(2)}) collective-permute-start(bf16[1,3072,128]{2,1,0:T(8,128)(2,1)} %slice.261), channel_id=1, source_target_pairs={{0,2},{1,3},{2,0},{3,1},{4,6},{5,7},{6,4},{7,5},{8,10},{9,11},{10,... | collective-permute-start | bytes 2359304 | tf_op jit(solution)/shard_map/ppermute | solution.py:292
  684.2 11.9 %collective-permute-start.69 = (bf16[2,3072,128]{2,1,0:T(8,128)(2,1)}, bf16[2,3072,128]{2,1,0:T(8,128)(2,1)}, u32[]{:S(2)}, u32[]{:S(2)}) collective-permute-start(bf16[2,3072,128]{2,1,0:T(8,128)(2,1)} %collective-permute-done.63.refs_0_), channel_id=1, source_target_pairs={{0,1},{1,0},{2,3},{3,2},{4,5},{5,4},{6,7},{7,6},{8,9},{9,8},{10,11... | collective-permute-start | bytes 4718600 | tf_op jit(solution)/shard_map/ppermute | solution.py:292
  688.4 7.7 collective-permute-start.70
  699.5 22.6 %collective-permute-start.71 = (f32[48,4608]{1,0:T(8,128)}, f32[48,4608]{1,0:T(8,128)S(1)}, u32[]{:S(2)}, u32[]{:S(2)}) collective-permute-start(f32[48,4608]{1,0:T(8,128)} %get-tuple-element.382), channel_id=1, source_target_pairs={{0,8},{2,10},{4,12},{6,14},{8,16},{10,18},{12,20},{14,22},{16,24},... | collective-permute-start | bytes 2654216 | tf_op jit(solution)/shard_map/ppermute | solution.py:302
  700.8 24.6 %collective-permute-start.72 = (f32[48,4608]{1,0:T(8,128)}, f32[48,4608]{1,0:T(8,128)}, u32[]{:S(2)}, u32[]{:S(2)}) collective-permute-start(f32[48,4608]{1,0:T(8,128)} %get-tuple-element.381), channel_id=1, source_target_pairs={{8,0},{10,2},{12,4},{14,6},{16,8},{18,10},{20,12},{22,14},{24,16},... | collective-permute-start | bytes 2654216 | tf_op jit(solution)/shard_map/ppermute | solution.py:302
  746.8 11.1 %collective-permute-start.79 = (f32[2]{0:T(128)S(1)}, f32[2]{0:T(128)S(1)}, u32[]{:S(2)}, u32[]{:S(2)}) collective-permute-start(f32[2]{0:T(128)S(1)} %add_add_fusion), channel_id=1, source_target_pairs={{0,24},{1,25},{2,26},{3,27},{4,28},{5,29},{6,30},{7,31},{8,0},{9,1... | collective-permute-start | bytes 32 | tf_op jit(solution)/shard_map/ppermute | solution.py:292
  (190 other events, 2199.6 us)
Sparse Core Ops, SparseCore 0:
  11.4 61.5 all-gather.6
  75.9 61.2 all-gather.8
  147.2 103.4 all-gather.10
  254.0 62.1 all-gather.12
  536.0 70.4 all-gather.14

commit v6 on v5

--- a/solution.py
+++ b/solution.py
@@ -560,7 +560,9 @@
         scratch_shapes=scratch,
         compiler_params=pltpu.CompilerParams(vmem_limit_bytes=60 * 2**20),
         cost_estimate=pl.CostEstimate(
-            flops=entries * 2048, bytes_accessed=entries * 10240, transcendentals=0
+            flops=entries * 2048,
+            bytes_accessed=entries * (65536 if first else 10240),
+            transcendentals=0,
         ),
     )(*lists, *sources, *extra)
 
@@ -888,16 +890,24 @@
     on_line = jnp.concatenate([hop(dx0_b, dl=-d) for d in range(1, lines)], 0)
     own_x, own_y = hop(dx0_b, dq=1), hop(dx0_b, dq=2)
     g_last = jnp.concatenate([g_qkv, g_out], 1)
-    own_x, own_y, g_last = lax.optimization_barrier((own_x, own_y, g_last))
+    own_x, own_y, g_last, told = lax.optimization_barrier((own_x, own_y, g_last, told))
     own_xy = hop(own_y, dq=1)
     last_1 = split_blocks(plane_blocks(g_last), 1, 1)
     sums_all = lax.all_gather(sums_here.reshape(1, -1, LANES), BOTH, axis=0, tiled=True)
     last_2 = split_blocks(last_1[0] + last_1[1].astype(f32), 0, 1)
-    on_line, own_x, own_y, own_xy, last_2, dx0_b = lax.optimization_barrier(
-        (on_line, own_x, own_y, own_xy, last_2, dx0_b)
-    )
     rows_all = told[:, :width]
     lse_all = jnp.sum(told[:, width : width + 3].astype(f32), 1)
+    logits_mine = dense_nt(rows_all, table_low)
+    own_column = jnp.where(targets_all // vocab == me, targets_all % vocab, -1)
+    hit_mine = jnp.arange(padded, dtype=jnp.int32)[None, :] == own_column[:, None]
+    dlogit_mine = (
+        (weight_rows / coefficient_aggregate)[:, None]
+        * (jnp.exp(logits_mine - lse_all[:, None]) - hit_mine.astype(f32))
+    ).astype(bf16)
+    head_grad = dense_tn(dlogit_mine, rows_all)
+    on_line, own_x, own_y, own_xy, last_2, dx0_b, head_grad = lax.optimization_barrier(
+        (on_line, own_x, own_y, own_xy, last_2, dx0_b, head_grad)
+    )
     line_x, line_y = hop(on_line, dq=1), hop(on_line, dq=2)
     shards = [two[0] + two[1].astype(f32) for two in (down_2, up_2, last_2)]
     both = shards[1].shape[1]
@@ -937,16 +947,8 @@
     sources = from_cores(early)
     begun = spread_rows(lists_of(order), sources, vocab, width)
     order.clear()
-    logits_mine = dense_nt(rows_all, table_low)
-    own_column = jnp.where(targets_all // vocab == me, targets_all % vocab, -1)
-    hit_mine = jnp.arange(padded, dtype=jnp.int32)[None, :] == own_column[:, None]
-    dlogit_mine = (
-        (weight_rows / coefficient_aggregate)[:, None]
-        * (jnp.exp(logits_mine - lse_all[:, None]) - hit_mine.astype(f32))
-    ).astype(bf16)
-    head_grad = dense_tn(dlogit_mine, rows_all)
-    line_x, line_y, begun, head_grad, sums, sums_all = lax.optimization_barrier(
-        (line_x, line_y, begun, head_grad, sums, sums_all)
+    line_x, line_y, begun, sums, sums_all = lax.optimization_barrier(
+        (line_x, line_y, begun, sums, sums_all)
     )
     for d in range(lines - 2, 1, -1):
         sums = reduce_step(blocks, sums, d)

time: 802 us -> 793 us (0.989)
  starting transfers between devices: 113 us -> 90.9 us
  local copies, waits for them, and re-layouts: 109 us -> 126 us
    ppermute x6, starting transfers between devices: 29.8 us -> 11.2 us  [step_line(): return lax.ppermute(x, 'dp', pairs)]
    unnamed x365 -> x313, local copies, waits for them, and re-layouts: 23.5 us -> 37.3 us
  transfers between devices with their start and end apart: 88 -> 88, of which waited for: 26 -> 28; matrix products, arithmetic and copies ran while one was open for 33% -> 35% of each run, Pallas kernels for 20% -> 21%
where the time goes in v6:
time: 793 us; the launch traced here: 780 us
  Pallas kernels  164 us (21%)
  waiting for transfers between devices  130 us (16%)
  local copies, waits for them, and re-layouts  126 us (16%)
  other arithmetic  117 us (15%)
  matrix products  115 us (15%)
  starting transfers between devices  90.9 us (11%)
  between operations  25.5 us (3%)
  blocking collectives  13.8 us (2%)
    ppermute x76, waiting for transfers between devices, hop(): return lax.ppermute(x, BOTH, pairs)  127 us
    ppermute x76, starting transfers between devices, hop(): return lax.ppermute(x, BOTH, pairs)  71.4 us
    pallas_call x2, Pallas kernels, mix_rows(): pl.pallas_call(functools.partial(mix_kernel, groups=groups, cands=cands,...  57.8 us
    pallas_call x3, Pallas kernels, spread_rows(): pl.pallas_call(functools.partial(spread_kernel, groups=groups, arrays=len...  53.8 us
    dot_general x5, matrix products, dense(): return jnp.dot(a, b, preferred_element_type=f32)  39.3 us
    unnamed x313, local copies, waits for them, and re-layouts  37.3 us
    dot_general x9, matrix products, dense_tn(): lax.dot_general(a, b, (((0,), (0,)), ((), ())), preferred_element_type=f32)  35.8 us
    scatter x2, local copies, waits for them, and re-layouts, local(): empty.at[flat_slot].set(value).reshape(devices, cap)  31.4 us
  transfers between devices with their start and end apart: 88, of which 28 were waited for; matrix products, arithmetic and copies ran while one was open for 35% of the time, Pallas kernels for 21%

profile of v6, /device:TPU:0, one launch (start us, length us, event | category | flops | bytes accessed | tf_op | source)
XLA Modules:
  0.0 780.1 jit_solution(17165072517519879392)
XLA Ops:
  11.1 2.6 convert_element_type.217
  13.9 3.0 collective-permute-start
  25.3 16.3 %reduce-window.6 = s32[32,32,128]{2,1,0:T(8,128)S(1)} reduce-window(s32[32,32,128]{2,1,0:T(8,128)} %fusion.49, s32[]{:T(128)} %constant.583.clone.1), window={size=1x1x128 pad=0_0x0_0x127_0}, to_apply=%region_2.3 | reduce-window | flops 16646144 | bytes 1048580 | tf_op jit(solution)/shard_map/reduce-window
  43.0 13.8 %all-gather = f32[256,128]{1,0:T(8,128)S(1)} all-gather(f32[64,128]{1,0:T(8,128)S(1)} %pad_maximum_fusion.15), channel_id=2, replica_groups={{0,8,16,24},{2,10,18,26},{4,12,20,28},{6,14,22,30},{1,9,17,25},{3,11,19..., dimensions={0}, use_global_device_ids=true | all-gather | bytes 163840 | tf_op jit(solution)/shard_map/all_gather | solution.py:653
  58.7 3.6 fusion.73
  83.3 24.4 %collective-permute-done.10.refs_12_ = bf16[784,768]{1,0:T(8,128)(2,1)S(1)} collective-permute-done((bf16[784,768]{1,0:T(8,128)(2,1)}, bf16[784,768]{1,0:T(8,128)(2,1)S(1)}, u32[]{:S(2)}, u32[]{:S(2)}) %collective-permute-start.10) | collective-permute-done | bytes 1204256 | tf_op jit(solution)/shard_map/ppermute | solution.py:292
  107.7 3.9 collective-permute-done.11.refs_13_
  116.8 27.1 %shard_map.554 = f32[2,3080,128]{2,1,0:T(8,128)} custom-call(s32[2,1,4096]{2,1,0:T(1,128)} %pad_add_fusion.idx_ref, f32[2,1,4096]{2,1,0:T(1,128)} %pad_maximum_fusion.16.mix_ref, bf16[784,768]{1,0:T(8,128)(2,1)} %copy-done.48, bf16[800,768]{1,0:T(8,128)(2,1)} %copy-done.47, bf16[784,768]{1,0:T(8,128)(2,1)} %copy-done.58, bf16[800,768]{1,0:T(8,128)(2,1)} %copy-done.55, ...), custom_call_target="tpu_custom_call" | custom-call | flops 16777216 | bytes 41943040 | tf_op jit(solution)/shard_map/pallas_call | solution.py:437
  144.0 3.3 slice_bitcast_fusion
  150.4 2.2 collective-permute-start.15
  153.8 30.7 %shard_map.553 = (f32[2,3080,128]{2,1,0:T(8,128)}, bf16[12672,768]{1,0:T(8,128)(2,1)}) custom-call(s32[2,1,4096]{2,1,0:T(1,128)} %pad_add_fusion.1.idx_ref, f32[2,1,4096]{2,1,0:T(1,128)} %pad_maximum_fusion.17.mix_ref, bf16[784,768]{1,0:T(8,128)(2,1)} %copy-done.48, bf16[800,768]{1,0:T(8,128)(2,1)} %copy-done.47, bf16[784,768]{1,0:T(8,128)(2,1)} %copy-done.58, ...), custom_call_target="tpu_custom_call" | custom-call | flops 16777216 | bytes 41943040 | tf_op jit(solution)/shard_map/pallas_call | solution.py:437
  187.4 9.8 %collective-permute-done.15 = bf16[3072,128]{1,0:T(8,128)(2,1)} collective-permute-done((bf16[3072,128]{1,0:T(8,128)(2,1)}, bf16[3072,128]{1,0:T(8,128)(2,1)}, u32[]{:S(2)}, u32[]{:S(2)}) %collective-permute-start.15) | collective-permute-done | bytes 786464 | tf_op jit(solution)/shard_map/ppermute | solution.py:292
  197.2 2.7 reshape.2018
  200.0 15.9 %scatter_custom_fusion.1 = f32[8192]{0:T(1024)S(1)} fusion(s32[4096]{0:T(1024)S(1)} %get-tuple-element.492, f32[4096]{0:T(1024)S(1)} %exponential_divide_fusion, f32[]{:T(128)} %constant.588.clone.1), kind=kCustom, calls=%fused_computation.351 | custom fusion | bytes 32772 | tf_op jit(solution)/shard_map/scatter | solution.py:755
  215.9 15.5 %scatter_custom_fusion = f32[8192]{0:T(1024)S(1)} fusion(s32[4096]{0:T(1024)S(1)} %get-tuple-element.492, f32[4096]{0:T(1024)S(1)} %get-tuple-element.493, f32[]{:T(128)} %constant.588.clone.1), kind=kCustom, calls=%fused_computation.353 | custom fusion | bytes 32772 | tf_op jit(solution)/shard_map/scatter | solution.py:755
  234.7 12.6 %collective-permute-done.16 = bf16[3072,128]{1,0:T(8,128)(2,1)} collective-permute-done((bf16[3072,128]{1,0:T(8,128)(2,1)S(1)}, bf16[3072,128]{1,0:T(8,128)(2,1)}, u32[]{:S(2)}, u32[]{:S(2)}) %collective-permute-start.16) | collective-permute-done | bytes 786464 | tf_op jit(solution)/shard_map/ppermute | solution.py:292
  247.3 2.5 fusion.167
  257.0 6.4 fusion.179.q_ref.k_ref.v_ref
  263.4 4.8 shard_map.555
  275.5 17.4 %shard_map.556 = (bf16[512,768]{1,0:T(8,128)(2,1)S(1)}, f32[512,768]{1,0:T(8,128)}) custom-call(s32[1]{0:T(128)} %dynamic_slice.235.len_ref, s32[1]{0:T(128)} %bitcast.46.core_ref, bf16[512,768]{1,0:T(8,128)(2,1)S(1)} %copy-done.30, bf16[512,768]{1,0:T(8,128)(2,1)S(1)} %copy-done.32, bf16[512,768]{1,0:T(8,128)(2,1)S(1)} %collective-permute-done.17.kf_ref, ...), custom_call_target="tpu_custom_call" | custom-call | flops 1610612736 | bytes 7077888 | tf_op jit(solution)/shard_map/pallas_call | solution.py:161
  294.0 3.9 fusion.166
  299.9 5.8 multiply_convert_fusion.3
  309.3 8.1 %all-to-all-start = ((f32[32,1,512]{2,1,0:T(1,128)}), f32[32,1,512]{2,1,0:T(1,128)S(1)}, u32[]{:S(2)}, u32[]{:S(2)}) async-start(f32[32,1,512]{2,1,0:T(1,128)} %all_to_all.8), calls=%async_computation | async-start | bytes 131072 | tf_op jit(solution)/shard_map/all_to_all | solution.py:804
  317.6 7.5 fusion.165
  327.4 2.9 collective-permute-start.24
  335.0 3.6 collective-permute-done.23
  338.6 12.4 %fusion.178 = (f32[256]{0:T(256)S(1)}, f32[256,12672]{1,0:T(8,128)}) fusion(bf16[256,768]{1,0:T(8,128)(2,1)S(1)} %pad_maximum_fusion.4, bf16[12672,768]{1,0:T(8,128)(2,1)} %get-tuple-element.223, pred[12672]{0:T(1024)(128)(4,1)S(1)} %fusion.89), kind=kOutput, calls=%fused_computation.558 | convolution fusion | flops 4989321216 | bytes 32847232 | tf_op jit(solution)/shard_map/dot_general | solution.py:29
  351.1 6.8 exponential_reduce_fusion
  358.1 2.6 collective-permute-start.28
  366.8 15.8 %fusion = f32[256,768]{1,0:T(8,128)S(1)} fusion(bf16[12672,768]{1,0:T(8,128)(2,1)} %get-tuple-element.223, f32[256,12672]{1,0:T(8,128)} %get-tuple-element.482, f32[256]{0:T(256)S(1)} %reshape.2027, f32[256]{0:T(256)S(1)} %broadcast_divide_fusion.1, s32[256]{0:T(256)S(1)} %copy-done.124), kind=kOutput, calls=%fused_computation.19 | convolution fusion | flops 5002297344 | bytes 33229824 | tf_op jit(solution)/shard_map/dot_general | solution.py:25
  382.6 2.7 collective-permute-start.31
  386.6 4.1 collective-permute-done.31
  390.6 9.9 %collective-permute-done.30 = f32[64,768]{1,0:T(8,128)S(1)} collective-permute-done((f32[64,768]{1,0:T(8,128)S(1)}, f32[64,768]{1,0:T(8,128)S(1)}, u32[]{:S(2)}, u32[]{:S(2)}) %collective-permute-start.30) | collective-permute-done | bytes 196640 | tf_op jit(solution)/shard_map/ppermute | solution.py:292
  404.8 3.4 multiply_reduce_fusion
  409.5 9.1 %fusion.10 = bf16[512,3072]{1,0:T(8,128)(2,1)S(1)} fusion(f32[512,3072]{1,0:T(8,128)} %get-tuple-element.479, bf16[512,768]{1,0:T(8,128)(2,1)S(1)} %multiply_convert_fusion.5, bf16[3072,768]{1,0:T(8,128)(2,1)} %all-gather.13.cloned.1.call-done), kind=kOutput, calls=%fused_computation.29 | convolution fusion | flops 2447376384 | bytes 14942208 | tf_op jit(solution)/shard_map/dot_general | solution.py:29
  418.7 3.6 multiply_reduce_fusion.2
  427.4 3.7 fusion.180
  431.1 3.8 convolution_add_fusion
  445.7 27.8 %shard_map.557 = (bf16[512,768]{1,0:T(8,128)(2,1)S(1)}, f32[512,768]{1,0:T(8,128)}, bf16[512,768]{1,0:T(8,128)(2,1)S(1)}, f32[512,768]{1,0:T(8,128)}, bf16[512,768]{1,0:T(8,128)(2,1)S(1)}) custom-call(s32[1]{0:T(128)} %dynamic_slice.235.len_ref, s32[1]{0:T(128)} %bitcast.46.core_ref, bf16[512,768]{1,0:T(8,128)(2,1)S(1)} %copy-done.31, ...), custom_call_target="tpu_custom_call" | custom-call | flops 4026531840 | bytes 12582912 | tf_op jit(solution)/shard_map/pallas_call | solution.py:239
  495.3 2.9 multiply_reduce_fusion.4
  501.0 2.9 fusion.32
  508.9 3.0 collective-permute-start.46
  531.7 2.8 convolution_add_fusion.1
  540.5 16.2 %fusion.16.refs_5_ = f32[1584,768]{1,0:T(8,128)} fusion(bf16[2048,896]{1,0:T(8,128)(2,1)} %bitcast.335, s32[2048]{0:T(1024)S(1)} %copy-done.119, f32[2048]{0:T(1024)S(1)} %convert_reduce_fusion, f32[2048]{0:T(1024)S(1)} %copy-done.118, bf16[1572,768]{1,0:T(8,128)(2,1)S(1)} %copy-done.41), kind=kOutput, calls=%fused_computation.42 | convolution fusion | flops 9985130496 | bytes 13596672 | tf_op jit(solution)/shard_map/dot_general | solution.py:33
  556.7 9.0 %collective-permute-done.52 = bf16[4,2,48,1536]{3,2,0,1:T(8,128)(2,1)} collective-permute-done((bf16[4,2,48,1536]{3,2,0,1:T(8,128)(2,1)}, bf16[4,2,48,1536]{3,2,0,1:T(8,128)(2,1)}, u32[]{:S(2)}, u32[]{:S(2)}) %collective-permute-start.52) | collective-permute-done | bytes 1179680 | tf_op jit(solution)/shard_map/ppermute | solution.py:292
  565.6 2.4 bitcast_add_fusion
  571.6 10.5 %collective-permute-done.53 = bf16[4,48,1536]{2,1,0:T(8,128)(2,1)S(1)} collective-permute-done((bf16[4,48,1536]{2,1,0:T(8,128)(2,1)S(1)}, bf16[4,48,1536]{2,1,0:T(8,128)(2,1)S(1)}, u32[]{:S(2)}, u32[]{:S(2)}) %collective-permute-start.53) | collective-permute-done | bytes 589856 | tf_op jit(solution)/shard_map/ppermute | solution.py:292
  586.5 2.2 add_dynamic-update-slice_fusion.1
  590.6 2.5 dynamic-slice_bitcast_fusion.5
  593.1 3.2 collective-permute-start.61
  601.4 18.9 %shard_map.558.refs_4_ = f32[12608,128]{1,0:T(8,128)} custom-call(s32[14]{0:T(128)} %get-tuple-element.427.cnt_ref, s32[14,256]{1,0:T(8,128)} %get-tuple-element.426.row_ref, s32[14,256]{1,0:T(8,128)} %get-tuple-element.425.pos_ref, f32[14,256]{1,0:T(8,128)} %broadcast_select_fusion.1.mix_ref, bf16[1,3072,128]{2,1,0:T(8,128)(2,1)} %reshape.2030.refs_0_, ...), custom_call_target="tpu_custom_call" | custom-call | flops 3670016 | bytes 117440512 | tf_op jit(solution)/shard_map/pallas_call | solution.py:549
  620.3 19.4 %collective-permute-done.54.refs_0_ = bf16[3,3072,128]{2,1,0:T(8,128)(2,1)} collective-permute-done((bf16[3,3072,128]{2,1,0:T(8,128)(2,1)S(1)}, bf16[3,3072,128]{2,1,0:T(8,128)(2,1)}, u32[]{:S(2)}, u32[]{:S(2)}) %collective-permute-start.54) | collective-permute-done | bytes 2359328 | tf_op jit(solution)/shard_map/ppermute | solution.py:292
  641.7 2.7 slice.260
  645.0 3.4 bitcast_add_fusion.4
  658.8 18.7 %shard_map.559.refs_4_ = f32[12608,128]{1,0:T(8,128)} custom-call(s32[12]{0:T(128)} %get-tuple-element.424.cnt_ref, s32[12,256]{1,0:T(8,128)} %get-tuple-element.423.row_ref, s32[12,256]{1,0:T(8,128)} %get-tuple-element.422.pos_ref, f32[12,256]{1,0:T(8,128)} %broadcast_select_fusion.mix_ref, bf16[3,3072,128]{2,1,0:T(8,128)(2,1)} %collective-permute-done.54.refs_0_, ...), custom_call_target="tpu_custom_call" | custom-call | flops 3145728 | bytes 15728640 | tf_op jit(solution)/shard_map/pallas_call | solution.py:549
  677.6 3.4 collective-permute-done.63.refs_0_
  689.8 3.4 bitcast_add_fusion.3
  699.9 16.1 %shard_map.560 = (f32[1572,768]{1,0:T(8,128)}, f32[8,128]{1,0:T(8,128)}) custom-call(s32[6]{0:T(128)} %get-tuple-element.448.cnt_ref, s32[6,256]{1,0:T(8,128)} %get-tuple-element.447.row_ref, s32[6,256]{1,0:T(8,128)} %get-tuple-element.446.pos_ref, f32[6,256]{1,0:T(8,128)} %broadcast_select_fusion.2.mix_ref, ...), custom_call_target="tpu_custom_call" | custom-call | flops 1572864 | bytes 7864320 | tf_op jit(solution)/shard_map/pallas_call | solution.py:549
  716.1 2.2 collective-permute-done.72
  732.0 2.5 collective-permute-start.77
  734.6 4.7 collective-permute-start.78
  742.8 5.9 collective-permute-start.79
  750.0 3.1 collective-permute-done.80
  756.2 13.4 %multiply_subtract_fusion = (f32[1572,768]{1,0:T(8,128)}, f32[1572,768]{1,0:T(8,128)}, f32[1572,768]{1,0:T(8,128)}) fusion(f32[1572,768]{1,0:T(8,128)} %param.41, f32[1572,768]{1,0:T(8,128)} %get-tuple-element.311, f32[]{:T(128)} %min.3, f32[1572,768]{1,0:T(8,128)} %param.42, f32[1572,768]{1,0:T(8,128)} %param.43), kind=kLoop, calls=%fused_computation.32 | loop fusion | flops 19316736 | bytes 33804292 | tf_op jit(solution)/shard_map/sub | solution.py:258
  (793 shorter events, 223.6 us)
Async XLA Ops:
  7.2 179.3 %all-gather.7.cloned.1.call-start = ((), (), s32[]{:S(2)}) async-start(), calls=%async_computation.1 | async-start | bytes 1723392 | tf_op jit(solution)/shard_map/all_gather | solution.py:630
  11.0 245.9 %all-gather.9.cloned.1.call-start = ((), (), s32[]{:S(2)}) async-start(), calls=%async_computation.2 | async-start | bytes 3649536 | tf_op jit(solution)/shard_map/all_gather | solution.py:625
  13.9 62.2 %collective-permute-start = (bf16[784,768]{1,0:T(8,128)(2,1)S(1)}, bf16[784,768]{1,0:T(8,128)(2,1)}, u32[]{:S(2)}, u32[]{:S(2)}) collective-permute-start(bf16[784,768]{1,0:T(8,128)(2,1)S(1)} %slice.299.refs_0_), channel_id=1, source_target_pairs={{0,2},{1,3},{2,0},{3,1},{4,6},{5,7},{6,4},{7,5},{8,10},{9,11},{10,... | collective-permute-start | bytes 3612680 | tf_op jit(solution)/shard_map/ppermute | solution.py:292
  16.9 59.2 %collective-permute-start.1 = (bf16[784,768]{1,0:T(8,128)(2,1)S(1)}, bf16[784,768]{1,0:T(8,128)(2,1)}, u32[]{:S(2)}, u32[]{:S(2)}) collective-permute-start(bf16[784,768]{1,0:T(8,128)(2,1)S(1)} %slice.299.refs_0_), channel_id=1, source_target_pairs={{0,4},{1,5},{2,6},{3,7},{4,0},{5,1},{6,2},{7,3},{8,12},{9,13},{10,... | collective-permute-start | bytes 3612680 | tf_op jit(solution)/shard_map/ppermute | solution.py:292
  18.5 57.5 %collective-permute-start.2 = (bf16[800,768]{1,0:T(8,128)(2,1)S(1)}, bf16[800,768]{1,0:T(8,128)(2,1)}, u32[]{:S(2)}, u32[]{:S(2)}) collective-permute-start(bf16[800,768]{1,0:T(8,128)(2,1)S(1)} %pad_slice_fusion.refs_1_), channel_id=1, source_target_pairs={{0,2},{1,3},{2,0},{3,1},{4,6},{5,7},{6,4},{7,5},{8,10},{9,11},{10,... | collective-permute-start | bytes 3686408 | tf_op jit(solution)/shard_map/ppermute | solution.py:292
  19.1 56.9 %collective-permute-start.3 = (bf16[800,768]{1,0:T(8,128)(2,1)S(1)}, bf16[800,768]{1,0:T(8,128)(2,1)}, u32[]{:S(2)}, u32[]{:S(2)}) collective-permute-start(bf16[800,768]{1,0:T(8,128)(2,1)S(1)} %pad_slice_fusion.refs_1_), channel_id=1, source_target_pairs={{0,4},{1,5},{2,6},{3,7},{4,0},{5,1},{6,2},{7,3},{8,12},{9,13},{10,... | collective-permute-start | bytes 3686408 | tf_op jit(solution)/shard_map/ppermute | solution.py:292
  20.3 273.7 %all-gather.11.cloned.1.call-start = ((), (), s32[]{:S(2)}) async-start(), calls=%async_computation.3 | async-start | bytes 6082560 | tf_op jit(solution)/shard_map/all_gather | solution.py:625
  76.2 31.5 %collective-permute-start.10 = (bf16[784,768]{1,0:T(8,128)(2,1)}, bf16[784,768]{1,0:T(8,128)(2,1)S(1)}, u32[]{:S(2)}, u32[]{:S(2)}) collective-permute-start(bf16[784,768]{1,0:T(8,128)(2,1)} %collective-permute-done.refs_4_), channel_id=1, source_target_pairs={{0,4},{1,5},{2,6},{3,7},{4,0},{5,1},{6,2},{7,3},{8,12},{9,13},{10,... | collective-permute-start | bytes 3612680 | tf_op jit(solution)/shard_map/ppermute | solution.py:292
  78.3 33.3 %collective-permute-start.11 = (bf16[800,768]{1,0:T(8,128)(2,1)}, bf16[800,768]{1,0:T(8,128)(2,1)S(1)}, u32[]{:S(2)}, u32[]{:S(2)}) collective-permute-start(bf16[800,768]{1,0:T(8,128)(2,1)} %collective-permute-done.3.refs_9_), channel_id=1, source_target_pairs={{0,2},{1,3},{2,0},{3,1},{4,6},{5,7},{6,4},{7,5},{8,10},{9,11},{10,... | collective-permute-start | bytes 3686408 | tf_op jit(solution)/shard_map/ppermute | solution.py:292
  81.7 32.7 %collective-permute-start.9 = (bf16[800,768]{1,0:T(8,128)(2,1)}, bf16[800,768]{1,0:T(8,128)(2,1)S(1)}, u32[]{:S(2)}, u32[]{:S(2)}) collective-permute-start(bf16[800,768]{1,0:T(8,128)(2,1)} %collective-permute-done.3.refs_9_), channel_id=1, source_target_pairs={{0,1},{1,0},{2,3},{3,2},{4,5},{5,4},{6,7},{7,6},{8,9},{9,8},{10,11... | collective-permute-start | bytes 3686408 | tf_op jit(solution)/shard_map/ppermute | solution.py:292
  82.7 31.6 %collective-permute-start.5 = (bf16[800,768]{1,0:T(8,128)(2,1)S(1)}, bf16[800,768]{1,0:T(8,128)(2,1)S(1)}, u32[]{:S(2)}, u32[]{:S(2)}) collective-permute-start(bf16[800,768]{1,0:T(8,128)(2,1)S(1)} %pad_slice_fusion.refs_1_), channel_id=1, source_target_pairs={{0,1},{1,0},{2,3},{3,2},{4,5},{5,4},{6,7},{7,6},{8,9},{9,8},{10,11... | collective-permute-start | bytes 3686408 | tf_op jit(solution)/shard_map/ppermute | solution.py:292
  82.8 31.5 %collective-permute-start.7 = (bf16[800,768]{1,0:T(8,128)(2,1)}, bf16[800,768]{1,0:T(8,128)(2,1)S(1)}, u32[]{:S(2)}, u32[]{:S(2)}) collective-permute-start(bf16[800,768]{1,0:T(8,128)(2,1)} %collective-permute-done.2.refs_5_), channel_id=1, source_target_pairs={{0,1},{1,0},{2,3},{3,2},{4,5},{5,4},{6,7},{7,6},{8,9},{9,8},{10,11... | collective-permute-start | bytes 3686408 | tf_op jit(solution)/shard_map/ppermute | solution.py:292
  107.7 7.7 collective-permute-start.12
  147.3 170.2 %all-gather.13.cloned.1.call-start = ((), (), s32[]{:S(2)}) async-start(), calls=%async_computation.4 | async-start | bytes 4866048 | tf_op jit(solution)/shard_map/all_gather | solution.py:625
  148.7 37.9 %collective-permute-start.14 = (bf16[3072,128]{1,0:T(8,128)(2,1)}, bf16[3072,128]{1,0:T(8,128)(2,1)S(1)}, u32[]{:S(2)}, u32[]{:S(2)}) collective-permute-start(bf16[3072,128]{1,0:T(8,128)(2,1)} %get-tuple-element.196), channel_id=1, source_target_pairs={{0,8},{1,9},{2,10},{3,11},{4,12},{5,13},{6,14},{7,15},{8,16},{9,17... | collective-permute-start | bytes 2359304 | tf_op jit(solution)/shard_map/ppermute | solution.py:292
  150.4 46.8 %collective-permute-start.15 = (bf16[3072,128]{1,0:T(8,128)(2,1)}, bf16[3072,128]{1,0:T(8,128)(2,1)}, u32[]{:S(2)}, u32[]{:S(2)}) collective-permute-start(bf16[3072,128]{1,0:T(8,128)(2,1)} %get-tuple-element.197), channel_id=1, source_target_pairs={{0,24},{1,25},{2,26},{3,27},{4,28},{5,29},{6,30},{7,31},{8,0},{9,1... | collective-permute-start | bytes 2359304 | tf_op jit(solution)/shard_map/ppermute | solution.py:292
  186.0 61.3 %collective-permute-start.16 = (bf16[3072,128]{1,0:T(8,128)(2,1)S(1)}, bf16[3072,128]{1,0:T(8,128)(2,1)}, u32[]{:S(2)}, u32[]{:S(2)}) collective-permute-start(bf16[3072,128]{1,0:T(8,128)(2,1)S(1)} %fusion.42), channel_id=1, source_target_pairs={{0,16},{1,17},{2,18},{3,19},{4,20},{5,21},{6,22},{7,23},{8,24},{9,... | collective-permute-start | bytes 2359304 | tf_op jit(solution)/shard_map/ppermute | solution.py:292
  269.7 23.3 %collective-permute-start.19 = (bf16[512,768]{1,0:T(8,128)(2,1)}, bf16[512,768]{1,0:T(8,128)(2,1)S(1)}, u32[]{:S(2)}, u32[]{:S(2)}) collective-permute-start(bf16[512,768]{1,0:T(8,128)(2,1)} %add_convert_fusion.4), channel_id=1, source_target_pairs={{0,1},{1,0},{2,3},{3,2},{4,5},{5,4},{6,7},{7,6},{8,9},{9,8},{10,11... | collective-permute-start | bytes 2359304 | tf_op jit(solution)/shard_map/ppermute | solution.py:292
  293.9 11.8 %collective-permute-start.20 = (bf16[512,768]{1,0:T(8,128)(2,1)S(1)}, bf16[512,768]{1,0:T(8,128)(2,1)}, u32[]{:S(2)}, u32[]{:S(2)}) collective-permute-start(bf16[512,768]{1,0:T(8,128)(2,1)S(1)} %get-tuple-element.215), channel_id=1, source_target_pairs={{0,1},{1,0},{2,3},{3,2},{4,5},{5,4},{6,7},{7,6},{8,9},{9,8},{10,11... | collective-permute-start | bytes 2359304 | tf_op jit(solution)/shard_map/ppermute | solution.py:292
  306.6 32.0 %collective-permute-start.25 = (bf16[512,3072]{1,0:T(8,128)(2,1)}, bf16[512,3072]{1,0:T(8,128)(2,1)}, u32[]{:S(2)}, u32[]{:S(2)}) collective-permute-start(bf16[512,3072]{1,0:T(8,128)(2,1)} %get-tuple-element.217), channel_id=1, source_target_pairs={{0,1},{1,0},{2,3},{3,2},{4,5},{5,4},{6,7},{7,6},{8,9},{9,8},{10,11... | collective-permute-start | bytes 9437192 | tf_op jit(solution)/shard_map/ppermute | solution.py:292
  309.3 24.3 %all-to-all-start = ((f32[32,1,512]{2,1,0:T(1,128)}), f32[32,1,512]{2,1,0:T(1,128)S(1)}, u32[]{:S(2)}, u32[]{:S(2)}) async-start(f32[32,1,512]{2,1,0:T(1,128)} %all_to_all.8), calls=%async_computation | async-start | bytes 131072 | tf_op jit(solution)/shard_map/all_to_all | solution.py:804
  317.4 302.8 %all-gather.15.cloned.1.call-start = ((), (), s32[]{:S(2)}) async-start(), calls=%async_computation.5 | async-start | bytes 1216512 | tf_op jit(solution)/shard_map/all_gather | solution.py:896
  327.4 7.6 collective-permute-start.24
  330.2 8.3 %collective-permute-start.23 = (bf16[64,768]{1,0:T(8,128)(2,1)S(1)}, bf16[64,768]{1,0:T(8,128)(2,1)S(1)}, u32[]{:S(2)}, u32[]{:S(2)}) collective-permute-start(bf16[64,768]{1,0:T(8,128)(2,1)S(1)} %select_convert_fusion), channel_id=1, source_target_pairs={{0,16},{1,17},{2,18},{3,19},{4,20},{5,21},{6,22},{7,23},{8,24},{9,... | collective-permute-start | bytes 294920 | tf_op jit(solution)/shard_map/ppermute | solution.py:292
  382.6 8.1 %collective-permute-start.31 = (f32[64,768]{1,0:T(8,128)S(1)}, f32[64,768]{1,0:T(8,128)S(1)}, u32[]{:S(2)}, u32[]{:S(2)}) collective-permute-start(f32[64,768]{1,0:T(8,128)S(1)} %get-tuple-element.398), channel_id=1, source_target_pairs={{0,24},{1,25},{2,26},{3,27},{4,28},{5,29},{6,30},{7,31},{8,0},{9,1... | collective-permute-start | bytes 589832 | tf_op jit(solution)/shard_map/ppermute | solution.py:292
  385.2 15.3 %collective-permute-start.30 = (f32[64,768]{1,0:T(8,128)S(1)}, f32[64,768]{1,0:T(8,128)S(1)}, u32[]{:S(2)}, u32[]{:S(2)}) collective-permute-start(f32[64,768]{1,0:T(8,128)S(1)} %get-tuple-element.399), channel_id=1, source_target_pairs={{0,16},{1,17},{2,18},{3,19},{4,20},{5,21},{6,22},{7,23},{8,24},{9,... | collective-permute-start | bytes 589832 | tf_op jit(solution)/shard_map/ppermute | solution.py:292
  385.2 15.3 %collective-permute-start.29 = (f32[64,768]{1,0:T(8,128)S(1)}, f32[64,768]{1,0:T(8,128)S(1)}, u32[]{:S(2)}, u32[]{:S(2)}) collective-permute-start(f32[64,768]{1,0:T(8,128)S(1)} %get-tuple-element.397), channel_id=1, source_target_pairs={{0,8},{1,9},{2,10},{3,11},{4,12},{5,13},{6,14},{7,15},{8,16},{9,17... | collective-permute-start | bytes 589832 | tf_op jit(solution)/shard_map/ppermute | solution.py:292
  401.7 34.7 %collective-permute-start.34 = (bf16[256,896]{1,0:T(8,128)(2,1)S(1)}, bf16[256,896]{1,0:T(8,128)(2,1)S(1)}, u32[]{:S(2)}, u32[]{:S(2)}) collective-permute-start(bf16[256,896]{1,0:T(8,128)(2,1)S(1)} %get-tuple-element.401), channel_id=1, source_target_pairs={{0,2},{1,3},{2,0},{3,1},{4,6},{5,7},{6,4},{7,5},{8,10},{9,11},{10,... | collective-permute-start | bytes 1376264 | tf_op jit(solution)/shard_map/ppermute | solution.py:292
  403.3 33.1 %collective-permute-start.35 = (bf16[256,896]{1,0:T(8,128)(2,1)S(1)}, bf16[256,896]{1,0:T(8,128)(2,1)S(1)}, u32[]{:S(2)}, u32[]{:S(2)}) collective-permute-start(bf16[256,896]{1,0:T(8,128)(2,1)S(1)} %get-tuple-element.401), channel_id=1, source_target_pairs={{0,4},{1,5},{2,6},{3,7},{4,0},{5,1},{6,2},{7,3},{8,12},{9,13},{10,... | collective-permute-start | bytes 1376264 | tf_op jit(solution)/shard_map/ppermute | solution.py:292
  423.4 11.6 %collective-permute-start.33 = (bf16[512,1536]{1,0:T(8,128)(2,1)S(1)}, bf16[512,1536]{1,0:T(8,128)(2,1)S(1)}, u32[]{:S(2)}, u32[]{:S(2)}) collective-permute-start(bf16[512,1536]{1,0:T(8,128)(2,1)S(1)} %constant_dynamic-slice_fusion.15), channel_id=1, source_target_pairs={{0,1},{1,0},{2,3},{3,2},{4,5},{5,4},{6,7},{7,6},{8,9},{9,8},{10,11... | collective-permute-start | bytes 4718600 | tf_op jit(solution)/shard_map/ppermute | solution.py:292
  437.6 42.9 %collective-permute-start.36 = (bf16[4,2,192,384]{3,2,1,0:T(8,128)(2,1)}, bf16[4,2,192,384]{3,2,1,0:T(8,128)(2,1)}, u32[]{:S(2)}, u32[]{:S(2)}) collective-permute-start(bf16[4,2,192,384]{3,2,1,0:T(8,128)(2,1)} %fusion.29), channel_id=1, source_target_pairs={{0,4},{1,5},{2,6},{3,7},{4,0},{5,1},{6,2},{7,3},{8,12},{9,13},{10,... | collective-permute-start | bytes 3538952 | tf_op jit(solution)/shard_map/ppermute | solution.py:292
  441.0 39.5 %collective-permute-start.37 = (bf16[4,2,48,1536]{3,2,1,0:T(8,128)(2,1)}, bf16[4,2,48,1536]{3,2,1,0:T(8,128)(2,1)}, u32[]{:S(2)}, u32[]{:S(2)}) collective-permute-start(bf16[4,2,48,1536]{3,2,1,0:T(8,128)(2,1)} %fusion.30), channel_id=1, source_target_pairs={{0,2},{1,3},{2,0},{3,1},{4,6},{5,7},{6,4},{7,5},{8,10},{9,11},{10,... | collective-permute-start | bytes 3538952 | tf_op jit(solution)/shard_map/ppermute | solution.py:292
  441.4 33.0 %collective-permute-start.38 = (bf16[512,384]{1,0:T(8,128)(2,1)S(1)}, bf16[512,384]{1,0:T(8,128)(2,1)S(1)}, u32[]{:S(2)}, u32[]{:S(2)}) collective-permute-start(bf16[512,384]{1,0:T(8,128)(2,1)S(1)} %constant_dynamic-slice_fusion.14), channel_id=1, source_target_pairs={{0,1},{1,0},{2,3},{3,2},{4,5},{5,4},{6,7},{7,6},{8,9},{9,8},{10,11... | collective-permute-start | bytes 1179656 | tf_op jit(solution)/shard_map/ppermute | solution.py:292
  441.5 36.5 %collective-permute-start.44 = (bf16[256,896]{1,0:T(8,128)(2,1)S(1)}, bf16[256,896]{1,0:T(8,128)(2,1)S(1)}, u32[]{:S(2)}, u32[]{:S(2)}) collective-permute-start(bf16[256,896]{1,0:T(8,128)(2,1)S(1)} %collective-permute-done.34), channel_id=1, source_target_pairs={{0,4},{1,5},{2,6},{3,7},{4,0},{5,1},{6,2},{7,3},{8,12},{9,13},{10,... | collective-permute-start | bytes 1376264 | tf_op jit(solution)/shard_map/ppermute | solution.py:292
  479.5 24.4 %collective-permute-start.45 = (bf16[4,256,896]{2,1,0:T(8,128)(2,1)}, bf16[4,256,896]{2,1,0:T(8,128)(2,1)}, u32[]{:S(2)}, u32[]{:S(2)}) collective-permute-start(bf16[4,256,896]{2,1,0:T(8,128)(2,1)} %pad_maximum_fusion.3), channel_id=1, source_target_pairs={{0,1},{1,0},{2,3},{3,2},{4,5},{5,4},{6,7},{7,6},{8,9},{9,8},{10,11... | collective-permute-start | bytes 5505032 | tf_op jit(solution)/shard_map/ppermute | solution.py:292
  480.5 9.9 %collective-permute-start.40 = (bf16[512,768]{1,0:T(8,128)(2,1)S(1)}, bf16[512,768]{1,0:T(8,128)(2,1)S(1)}, u32[]{:S(2)}, u32[]{:S(2)}) collective-permute-start(bf16[512,768]{1,0:T(8,128)(2,1)S(1)} %get-tuple-element.247), channel_id=1, source_target_pairs={{0,1},{1,0},{2,3},{3,2},{4,5},{5,4},{6,7},{7,6},{8,9},{9,8},{10,11... | collective-permute-start | bytes 2359304 | tf_op jit(solution)/shard_map/ppermute | solution.py:292
  480.9 9.7 %collective-permute-start.39 = (bf16[512,768]{1,0:T(8,128)(2,1)S(1)}, bf16[512,768]{1,0:T(8,128)(2,1)S(1)}, u32[]{:S(2)}, u32[]{:S(2)}) collective-permute-start(bf16[512,768]{1,0:T(8,128)(2,1)S(1)} %get-tuple-element.245), channel_id=1, source_target_pairs={{0,1},{1,0},{2,3},{3,2},{4,5},{5,4},{6,7},{7,6},{8,9},{9,8},{10,11... | collective-permute-start | bytes 2359304 | tf_op jit(solution)/shard_map/ppermute | solution.py:292
  483.6 22.2 %collective-permute-start.41 = (bf16[4,192,384]{2,1,0:T(8,128)(2,1)}, bf16[4,192,384]{2,1,0:T(8,128)(2,1)}, u32[]{:S(2)}, u32[]{:S(2)}) collective-permute-start(bf16[4,192,384]{2,1,0:T(8,128)(2,1)} %fusion.43), channel_id=1, source_target_pairs={{0,2},{1,3},{2,0},{3,1},{4,6},{5,7},{6,4},{7,5},{8,10},{9,11},{10,... | collective-permute-start | bytes 1769480 | tf_op jit(solution)/shard_map/ppermute | solution.py:292
  487.7 18.2 %collective-permute-start.42 = (bf16[4,48,1536]{2,1,0:T(8,128)(2,1)}, bf16[4,48,1536]{2,1,0:T(8,128)(2,1)}, u32[]{:S(2)}, u32[]{:S(2)}) collective-permute-start(bf16[4,48,1536]{2,1,0:T(8,128)(2,1)} %fusion.44), channel_id=1, source_target_pairs={{0,4},{1,5},{2,6},{3,7},{4,0},{5,1},{6,2},{7,3},{8,12},{9,13},{10,... | collective-permute-start | bytes 1769480 | tf_op jit(solution)/shard_map/ppermute | solution.py:292
  494.1 11.8 %collective-permute-start.43 = (bf16[512,1152]{1,0:T(8,128)(2,1)}, bf16[512,1152]{1,0:T(8,128)(2,1)}, u32[]{:S(2)}, u32[]{:S(2)}) collective-permute-start(bf16[512,1152]{1,0:T(8,128)(2,1)} %constant_dynamic-slice_fusion.13), channel_id=1, source_target_pairs={{0,1},{1,0},{2,3},{3,2},{4,5},{5,4},{6,7},{7,6},{8,9},{9,8},{10,11... | collective-permute-start | bytes 3538952 | tf_op jit(solution)/shard_map/ppermute | solution.py:292
  505.9 63.7 %collective-permute-start.48 = (bf16[1,3072,128]{2,1,0:T(8,128)(2,1)}, bf16[1,3072,128]{2,1,0:T(8,128)(2,1)}, u32[]{:S(2)}, u32[]{:S(2)}) collective-permute-start(bf16[1,3072,128]{2,1,0:T(8,128)(2,1)} %reshape.2030.refs_0_), channel_id=1, source_target_pairs={{0,8},{1,9},{2,10},{3,11},{4,12},{5,13},{6,14},{7,15},{8,16},{9,17... | collective-permute-start | bytes 2359304 | tf_op jit(solution)/shard_map/ppermute | solution.py:292
  506.9 62.7 %collective-permute-start.47 = (bf16[1,3072,128]{2,1,0:T(8,128)(2,1)}, bf16[1,3072,128]{2,1,0:T(8,128)(2,1)}, u32[]{:S(2)}, u32[]{:S(2)}) collective-permute-start(bf16[1,3072,128]{2,1,0:T(8,128)(2,1)} %reshape.2030.refs_0_), channel_id=1, source_target_pairs={{0,16},{1,17},{2,18},{3,19},{4,20},{5,21},{6,22},{7,23},{8,24},{9,... | collective-permute-start | bytes 2359304 | tf_op jit(solution)/shard_map/ppermute | solution.py:292
  508.9 60.8 %collective-permute-start.46 = (bf16[1,3072,128]{2,1,0:T(8,128)(2,1)}, bf16[1,3072,128]{2,1,0:T(8,128)(2,1)}, u32[]{:S(2)}, u32[]{:S(2)}) collective-permute-start(bf16[1,3072,128]{2,1,0:T(8,128)(2,1)} %reshape.2030.refs_0_), channel_id=1, source_target_pairs={{0,24},{1,25},{2,26},{3,27},{4,28},{5,29},{6,30},{7,31},{8,0},{9,1... | collective-permute-start | bytes 2359304 | tf_op jit(solution)/shard_map/ppermute | solution.py:292
  511.9 23.4 %collective-permute-start.49 = (bf16[1,3072,128]{2,1,0:T(8,128)(2,1)}, bf16[1,3072,128]{2,1,0:T(8,128)(2,1)}, u32[]{:S(2)}, u32[]{:S(2)}) collective-permute-start(bf16[1,3072,128]{2,1,0:T(8,128)(2,1)} %reshape.2030.refs_0_), channel_id=1, source_target_pairs={{0,2},{1,3},{2,0},{3,1},{4,6},{5,7},{6,4},{7,5},{8,10},{9,11},{10,... | collective-permute-start | bytes 2359304 | tf_op jit(solution)/shard_map/ppermute | solution.py:292
  512.3 23.0 %collective-permute-start.50 = (bf16[1,3072,128]{2,1,0:T(8,128)(2,1)}, bf16[1,3072,128]{2,1,0:T(8,128)(2,1)}, u32[]{:S(2)}, u32[]{:S(2)}) collective-permute-start(bf16[1,3072,128]{2,1,0:T(8,128)(2,1)} %reshape.2030.refs_0_), channel_id=1, source_target_pairs={{0,4},{1,5},{2,6},{3,7},{4,0},{5,1},{6,2},{7,3},{8,12},{9,13},{10,... | collective-permute-start | bytes 2359304 | tf_op jit(solution)/shard_map/ppermute | solution.py:292
  535.2 36.4 %collective-permute-start.51 = (bf16[1,3072,128]{2,1,0:T(8,128)(2,1)}, bf16[1,3072,128]{2,1,0:T(8,128)(2,1)}, u32[]{:S(2)}, u32[]{:S(2)}) collective-permute-start(bf16[1,3072,128]{2,1,0:T(8,128)(2,1)} %collective-permute-done.50.refs_4_), channel_id=1, source_target_pairs={{0,2},{1,3},{2,0},{3,1},{4,6},{5,7},{6,4},{7,5},{8,10},{9,11},{10,... | collective-permute-start | bytes 2359304 | tf_op jit(solution)/shard_map/ppermute | solution.py:292
  538.8 26.8 %collective-permute-start.52 = (bf16[4,2,48,1536]{3,2,0,1:T(8,128)(2,1)}, bf16[4,2,48,1536]{3,2,0,1:T(8,128)(2,1)}, u32[]{:S(2)}, u32[]{:S(2)}) collective-permute-start(bf16[4,2,48,1536]{3,2,0,1:T(8,128)(2,1)} %fusion.31), channel_id=1, source_target_pairs={{0,4},{1,5},{2,6},{3,7},{4,0},{5,1},{6,2},{7,3},{8,12},{9,13},{10,... | collective-permute-start | bytes 3538952 | tf_op jit(solution)/shard_map/ppermute | solution.py:292
  568.1 14.1 %collective-permute-start.53 = (bf16[4,48,1536]{2,1,0:T(8,128)(2,1)S(1)}, bf16[4,48,1536]{2,1,0:T(8,128)(2,1)S(1)}, u32[]{:S(2)}, u32[]{:S(2)}) collective-permute-start(bf16[4,48,1536]{2,1,0:T(8,128)(2,1)S(1)} %fusion.45), channel_id=1, source_target_pairs={{0,2},{1,3},{2,0},{3,1},{4,6},{5,7},{6,4},{7,5},{8,10},{9,11},{10,... | collective-permute-start | bytes 1769480 | tf_op jit(solution)/shard_map/ppermute | solution.py:292
  584.4 55.4 %collective-permute-start.54 = (bf16[3,3072,128]{2,1,0:T(8,128)(2,1)S(1)}, bf16[3,3072,128]{2,1,0:T(8,128)(2,1)}, u32[]{:S(2)}, u32[]{:S(2)}) collective-permute-start(bf16[3,3072,128]{2,1,0:T(8,128)(2,1)S(1)} %pad_maximum_fusion.2.refs_8_), channel_id=1, source_target_pairs={{0,2},{1,3},{2,0},{3,1},{4,6},{5,7},{6,4},{7,5},{8,10},{9,11},{10,... | collective-permute-start | bytes 7077896 | tf_op jit(solution)/shard_map/ppermute | solution.py:292
  585.8 55.1 %collective-permute-start.55 = (bf16[3,3072,128]{2,1,0:T(8,128)(2,1)S(1)}, bf16[3,3072,128]{2,1,0:T(8,128)(2,1)}, u32[]{:S(2)}, u32[]{:S(2)}) collective-permute-start(bf16[3,3072,128]{2,1,0:T(8,128)(2,1)S(1)} %pad_maximum_fusion.2.refs_8_), channel_id=1, source_target_pairs={{0,4},{1,5},{2,6},{3,7},{4,0},{5,1},{6,2},{7,3},{8,12},{9,13},{10,... | collective-permute-start | bytes 7077896 | tf_op jit(solution)/shard_map/ppermute | solution.py:292
  586.5 14.8 %collective-permute-start.60 = (bf16[3,3072,128]{2,1,0:T(8,128)(2,1)S(1)}, bf16[3,3072,128]{2,1,0:T(8,128)(2,1)}, u32[]{:S(2)}, u32[]{:S(2)}) collective-permute-start(bf16[3,3072,128]{2,1,0:T(8,128)(2,1)S(1)} %pad_maximum_fusion.2.refs_8_), channel_id=1, source_target_pairs={{0,1},{1,0},{2,3},{3,2},{4,5},{5,4},{6,7},{7,6},{8,9},{9,8},{10,11... | collective-permute-start | bytes 7077896 | tf_op jit(solution)/shard_map/ppermute | solution.py:292
  593.1 27.2 %collective-permute-start.61 = (f32[48,4608]{1,0:T(8,128)}, f32[48,4608]{1,0:T(8,128)}, u32[]{:S(2)}, u32[]{:S(2)}) collective-permute-start(f32[48,4608]{1,0:T(8,128)} %get-tuple-element.388), channel_id=1, source_target_pairs={{0,8},{2,10},{4,12},{6,14},{1,9},{3,11},{5,13},{7,15}} | collective-permute-start | bytes 2654216 | tf_op jit(solution)/shard_map/ppermute | solution.py:302
  596.3 24.0 %collective-permute-start.62 = (f32[48,4608]{1,0:T(8,128)S(1)}, f32[48,4608]{1,0:T(8,128)}, u32[]{:S(2)}, u32[]{:S(2)}) collective-permute-start(f32[48,4608]{1,0:T(8,128)S(1)} %get-tuple-element.387), channel_id=1, source_target_pairs={{24,16},{26,18},{28,20},{30,22},{25,17},{27,19},{29,21},{31,23}} | collective-permute-start | bytes 2654216 | tf_op jit(solution)/shard_map/ppermute | solution.py:302
  640.9 13.2 %collective-permute-start.65 = (bf16[3,3072,128]{2,1,0:T(8,128)(2,1)}, bf16[3,3072,128]{2,1,0:T(8,128)(2,1)S(1)}, u32[]{:S(2)}, u32[]{:S(2)}) collective-permute-start(bf16[3,3072,128]{2,1,0:T(8,128)(2,1)} %collective-permute-done.54.refs_0_), channel_id=1, source_target_pairs={{0,1},{1,0},{2,3},{3,2},{4,5},{5,4},{6,7},{7,6},{8,9},{9,8},{10,11... | collective-permute-start | bytes 7077896 | tf_op jit(solution)/shard_map/ppermute | solution.py:292
  641.1 17.7 %collective-permute-start.66 = (bf16[3,3072,128]{2,1,0:T(8,128)(2,1)}, bf16[3,3072,128]{2,1,0:T(8,128)(2,1)}, u32[]{:S(2)}, u32[]{:S(2)}) collective-permute-start(bf16[3,3072,128]{2,1,0:T(8,128)(2,1)} %collective-permute-done.55.refs_2_), channel_id=1, source_target_pairs={{0,1},{1,0},{2,3},{3,2},{4,5},{5,4},{6,7},{7,6},{8,9},{9,8},{10,11... | collective-permute-start | bytes 7077896 | tf_op jit(solution)/shard_map/ppermute | solution.py:292
  644.4 36.6 %collective-permute-start.63 = (bf16[2,3072,128]{2,1,0:T(8,128)(2,1)}, bf16[2,3072,128]{2,1,0:T(8,128)(2,1)}, u32[]{:S(2)}, u32[]{:S(2)}) collective-permute-start(bf16[2,3072,128]{2,1,0:T(8,128)(2,1)} %slice.260), channel_id=1, source_target_pairs={{0,4},{1,5},{2,6},{3,7},{4,0},{5,1},{6,2},{7,3},{8,12},{9,13},{10,... | collective-permute-start | bytes 4718600 | tf_op jit(solution)/shard_map/ppermute | solution.py:292
  648.4 29.2 %collective-permute-start.67 = (f32[48,4608]{1,0:T(8,128)}, f32[48,4608]{1,0:T(8,128)S(1)}, u32[]{:S(2)}, u32[]{:S(2)}) collective-permute-start(f32[48,4608]{1,0:T(8,128)} %get-tuple-element.386), channel_id=1, source_target_pairs={{0,8},{2,10},{4,12},{6,14},{8,16},{10,18},{12,20},{14,22},{1,9},{3... | collective-permute-start | bytes 2654216 | tf_op jit(solution)/shard_map/ppermute | solution.py:302
  650.3 27.3 %collective-permute-start.68 = (f32[48,4608]{1,0:T(8,128)}, f32[48,4608]{1,0:T(8,128)}, u32[]{:S(2)}, u32[]{:S(2)}) collective-permute-start(f32[48,4608]{1,0:T(8,128)} %get-tuple-element.385), channel_id=1, source_target_pairs={{16,8},{18,10},{20,12},{22,14},{24,16},{26,18},{28,20},{30,22},{17... | collective-permute-start | bytes 2654216 | tf_op jit(solution)/shard_map/ppermute | solution.py:302
  654.2 23.4 %collective-permute-start.64 = (bf16[1,3072,128]{2,1,0:T(8,128)(2,1)}, bf16[1,3072,128]{2,1,0:T(8,128)(2,1)}, u32[]{:S(2)}, u32[]{:S(2)}) collective-permute-start(bf16[1,3072,128]{2,1,0:T(8,128)(2,1)} %slice.261), channel_id=1, source_target_pairs={{0,2},{1,3},{2,0},{3,1},{4,6},{5,7},{6,4},{7,5},{8,10},{9,11},{10,... | collective-permute-start | bytes 2359304 | tf_op jit(solution)/shard_map/ppermute | solution.py:292
  681.0 8.8 %collective-permute-start.69 = (bf16[2,3072,128]{2,1,0:T(8,128)(2,1)}, bf16[2,3072,128]{2,1,0:T(8,128)(2,1)}, u32[]{:S(2)}, u32[]{:S(2)}) collective-permute-start(bf16[2,3072,128]{2,1,0:T(8,128)(2,1)} %collective-permute-done.63.refs_0_), channel_id=1, source_target_pairs={{0,1},{1,0},{2,3},{3,2},{4,5},{5,4},{6,7},{7,6},{8,9},{9,8},{10,11... | collective-permute-start | bytes 4718600 | tf_op jit(solution)/shard_map/ppermute | solution.py:292
  681.7 8.2 %collective-permute-start.70 = (bf16[1,3072,128]{2,1,0:T(8,128)(2,1)}, bf16[1,3072,128]{2,1,0:T(8,128)(2,1)}, u32[]{:S(2)}, u32[]{:S(2)}) collective-permute-start(bf16[1,3072,128]{2,1,0:T(8,128)(2,1)} %collective-permute-done.64.refs_2_), channel_id=1, source_target_pairs={{0,1},{1,0},{2,3},{3,2},{4,5},{5,4},{6,7},{7,6},{8,9},{9,8},{10,11... | collective-permute-start | bytes 2359304 | tf_op jit(solution)/shard_map/ppermute | solution.py:292
  693.2 22.9 %collective-permute-start.71 = (f32[48,4608]{1,0:T(8,128)}, f32[48,4608]{1,0:T(8,128)S(1)}, u32[]{:S(2)}, u32[]{:S(2)}) collective-permute-start(f32[48,4608]{1,0:T(8,128)} %get-tuple-element.384), channel_id=1, source_target_pairs={{0,8},{2,10},{4,12},{6,14},{8,16},{10,18},{12,20},{14,22},{16,24},... | collective-permute-start | bytes 2654216 | tf_op jit(solution)/shard_map/ppermute | solution.py:302
  694.7 23.6 %collective-permute-start.72 = (f32[48,4608]{1,0:T(8,128)}, f32[48,4608]{1,0:T(8,128)}, u32[]{:S(2)}, u32[]{:S(2)}) collective-permute-start(f32[48,4608]{1,0:T(8,128)} %get-tuple-element.383), channel_id=1, source_target_pairs={{8,0},{10,2},{12,4},{14,6},{16,8},{18,10},{20,12},{22,14},{24,16},... | collective-permute-start | bytes 2654216 | tf_op jit(solution)/shard_map/ppermute | solution.py:302
  732.0 7.7 collective-permute-start.77
  (164 other events, 1645.1 us)
Sparse Core Ops, SparseCore 0:
  11.4 61.5 all-gather.6
  75.9 61.2 all-gather.8
  147.4 103.2 all-gather.10
  254.0 61.9 all-gather.12
  531.8 71.0 all-gather.14
